TPU v7x, 256 devices: a whole 4x4x8 slice. The times are simulated.
256 devices in a mesh: dp: 4 (over z_lo), ctx: 16 (over x, y), tp: 4 (over z_hi, core).
Axes of the slice: x: 4, y: 4, z: 8 (z_hi: 2, z_lo: 4; z = z_hi * 4 + z_lo), core: 2. Of those that a mesh axis runs over, the one named last changes fastest.
Arguments:
- conv_input: bfloat16 [4, 4096, 4096], P('dp', 'ctx', 'tp'), may hold values from -6 to 6
- gate_value: bfloat16 [4, 4096, 4096], P('dp', 'ctx', 'tp'), may hold values from -6 to 6
- out_grad: bfloat16 [4, 4096, 4096], P('dp', ('ctx', 'tp')), may hold values from -16 to 16
- out_weight: bfloat16 [4096, 4096], P(None, 'tp'), may hold values from -0.09375 to 0.09375
- filters: bfloat16 [256, 128], P('tp'), may hold values from -0.5 to 0.5
Outputs:
- grad_input: bfloat16 [4, 4096, 4096], P('dp', 'ctx', 'tp')
- grad_gate: bfloat16 [4, 4096, 4096], P('dp', 'ctx', 'tp')
- grad_weight: float32 [4096, 4096], P(('dp', 'ctx'), 'tp')
- grad_filter: float32 [256, 128], P('tp')
All inputs are finite; a program needn't handle non-finite values.
Results may differ from a plain program's by a relative error of at most 0.0049.
Values may be sent and summed in bfloat16 or wider, within the bound.
No kernel may reach another device: no remote copies, remote signals or barrier semaphores. Data moves between devices by JAX's collectives and lax.ppermute only.
A program may use at most 192 MiB of HBM per device.

v0:
```python
import math

import jax
import jax.numpy as jnp
from jax import lax
from jax.sharding import PartitionSpec as P


def shifted(x, axis, by):
    devices = lax.axis_size(axis)
    pairs = [(i, i + by) for i in range(devices) if 0 <= i + by < devices]
    return lax.ppermute(x, axis, pairs)


def band_rows(filter_rows, forward):
    groups, taps_count = filter_rows.shape
    if forward:
        return jnp.concatenate(
            [
                jnp.zeros((groups, 1), filter_rows.dtype),
                filter_rows[:, ::-1],
                jnp.zeros((groups, 2 * taps_count - 1), filter_rows.dtype),
            ],
            1,
        )
    return jnp.concatenate([filter_rows, jnp.zeros((groups, 2 * taps_count), filter_rows.dtype)], 1)


def band(rows_table):
    groups, period = rows_table.shape
    taps_count = period // 3
    flattened = jnp.tile(rows_table, (1, taps_count))[:, : taps_count * (period - 1)]
    return flattened.reshape(groups, taps_count, period - 1)[:, :, : 2 * taps_count]


def blocks(extended, taps_count):
    count = (extended.shape[0] - taps_count) // taps_count
    width = extended.shape[1]
    lower = extended[: count * taps_count].reshape(count, taps_count, width)
    upper = extended[taps_count:].reshape(count, taps_count, width)
    return jnp.concatenate([lower, upper], 1)


def diagonal_sums(products, taps_count):
    groups = products.shape[0]
    padded = jnp.pad(products, ((0, 0), (0, 0), (0, taps_count)))
    flattened = padded.reshape(groups, 3 * taps_count * taps_count)
    flattened = jnp.pad(flattened, ((0, 0), (0, taps_count)))
    skewed = flattened.reshape(groups, taps_count, 3 * taps_count + 1)
    diag_total = jnp.sum(skewed, axis=1)
    return diag_total[:, 1 : taps_count + 1][:, ::-1]


def local(conv_input, gate_value, out_grad, out_weight, filters):
    groups, taps_count = filters.shape
    signal = conv_input[0]
    gating = gate_value[0]
    length, channels = signal.shape
    group_width = channels // groups
    block_count = length // taps_count
    forward_band = band(band_rows(filters, True))
    backward_band = band(band_rows(filters, False))
    previous = shifted(signal[length - taps_count :], "ctx", 1)
    extended = jnp.concatenate([previous, signal], 0)
    windows = blocks(extended, taps_count).reshape(block_count, 2 * taps_count, groups, group_width)
    response = jnp.einsum(
        "gij,bjgc->bigc", forward_band, windows, preferred_element_type=jnp.float32
    ).reshape(length, channels)
    whole_grads = lax.all_gather(out_grad[0], "tp", axis=0, tiled=True)
    gate_grad = jnp.dot(whole_grads, out_weight, preferred_element_type=jnp.float32)
    gated = (response * gating).astype(jnp.bfloat16)
    conv_grad = (gate_grad * gating).astype(jnp.bfloat16)
    grad_gate = (gate_grad * response).astype(jnp.bfloat16)
    following = shifted(conv_grad[:taps_count], "ctx", -1)
    extended_grad = jnp.concatenate([conv_grad, following], 0)
    grad_windows = blocks(extended_grad, taps_count).reshape(
        block_count, 2 * taps_count, groups, group_width
    )
    grad_input = jnp.einsum(
        "gij,bjgc->bigc", backward_band, grad_windows, preferred_element_type=jnp.float32
    )
    grad_input = grad_input.reshape(length, channels).astype(jnp.bfloat16)
    products = jnp.einsum(
        "bigc,bjgc->gij",
        conv_grad.reshape(block_count, taps_count, groups, group_width),
        windows,
        preferred_element_type=jnp.float32,
    )
    filter_local = diagonal_sums(products, taps_count)
    data_count = lax.axis_size("dp")
    context_count = lax.axis_size("ctx")
    tokens_all = data_count * context_count * length
    filter_total = lax.psum(filter_local, ("dp", "ctx"))
    grad_filter = filter_total * (1.0 / math.sqrt(tokens_all * group_width))
    weight_total = lax.psum_scatter(
        lax.dot_general(
            whole_grads, gated, (((0,), (0,)), ((), ())), preferred_element_type=jnp.float32
        ),
        ("dp", "ctx"),
        scatter_dimension=0,
        tiled=True,
    )
    grad_weight = weight_total * (1.0 / math.sqrt(tokens_all))
    return (grad_input[None], grad_gate[None], grad_weight, grad_filter)


def solution(mesh):
    placed = (
        P("dp", "ctx", "tp"),
        P("dp", "ctx", "tp"),
        P("dp", ("ctx", "tp"), None),
        P(None, "tp"),
        P("tp", None),
    )
    return jax.shard_map(
        local,
        mesh=mesh,
        in_specs=placed,
        out_specs=(
            P("dp", "ctx", "tp"),
            P("dp", "ctx", "tp"),
            P(("dp", "ctx"), "tp"),
            P("tp", None),
        ),
        check_vma=False,
    )
```

profile of v0, /device:TPU:0, one launch (start us, length us, event | category | flops | bytes accessed | tf_op | source)
XLA Modules:
  0.0 568.0 jit_solution(8673479331553047106)
XLA Ops:
  7.2 0.7 all-gather.3.cloned.1.call-update
  7.9 1.0 slice_bitcast_fusion.10
  8.9 1.8 collective-permute-start.1
  10.7 1.2 copy.35
  12.0 0.8 rev.6
  13.0 0.5 tile.20
  13.6 4.1 copy.50
  17.7 3.1 slice.43
  20.8 16.8 %reshape.61 = bf16[64,128,383]{2,1,0:T(8,128)(2,1)} reshape(bf16[64,49024]{1,0:T(8,128)(2,1)} %slice.43) | data formatting | bytes 12550144 | tf_op jit(solution)/shard_map/reshape | solution.py:33
  38.2 3.7 fusion.5
  42.9 11.4 %all-gather.3.cloned.1.call-done = bf16[1,256,4096]{2,1,0:T(8,128)(2,1)} async-done(((bf16[1,64,4096]{2,1,0:T(8,128)(2,1)}), bf16[1,256,4096]{2,1,0:T(8,128)(2,1)}) %all-gather.3.cloned.1.call-update) | async-done | bytes 2097168 | tf_op jit(solution)/shard_map/all_gather | solution.py:69
  54.3 9.9 %convolution_bitcast_fusion = f32[4096,1024]{0,1:T(8,128)} fusion(bf16[1,256,4096]{2,1,0:T(8,128)(2,1)} %all-gather.3.cloned.1.call-done, f32[256,1024]{1,0:T(8,128)S(1)} %copy.39, bf16[1,256,1024]{2,1,0:T(8,128)(2,1)} %param.6), kind=kOutput, calls=%fused_computation | convolution fusion | flops 2148270080 | bytes 20447232 | tf_op jit(solution)/shard_map/dot_general | solution.py:96
  64.2 17.4 %copy.47 = f32[4096,1024]{1,0:T(8,128)} copy(f32[4096,1024]{0,1:T(8,128)} %convolution_bitcast_fusion) | data formatting | bytes 33554432
  81.7 0.7 copy-done.2
  82.4 0.5 tile.8
  82.9 4.1 copy.49
  87.0 3.1 slice.41
  90.1 26.4 %reshape.60 = bf16[64,128,383]{2,1,0:T(8,128)(2,1)} reshape(bf16[64,49024]{1,0:T(8,128)(2,1)} %slice.41) | data formatting | bytes 12550144 | tf_op jit(solution)/shard_map/reshape | solution.py:33
  116.5 7.2 %fusion.13 = (bf16[1,256,1024]{2,1,0:T(8,128)(2,1)}, bf16[256,1024]{1,0:T(8,128)(2,1)S(1)}) fusion(f32[256,1024]{1,0:T(8,128)S(1)} %copy.39, bf16[1,256,1024]{2,1,0:T(8,128)(2,1)S(1)} %copy-done.1, bf16[4096,1024]{1,0:T(8,128)(2,1)} %param.8, bf16[1,256,4096]{2,1,0:T(8,128)(2,1)} %all-gather.3.cloned.1.call-done), kind=kOutput, calls=%fused_computation.21 | convolution fusion | flops 2148794368 | bytes 13107200 | tf_op jit(solution)/shard_map/dot_general | solution.py:70
  123.9 1.3 collective-permute-start
  125.3 1.3 convolution_bitcast_fusion.1
  126.7 6.1 %pad.9 = f32[64,128,384]{2,1,0:T(8,128)} pad(f32[64,128,256]{2,1,0:T(8,128)S(1)} %convolution_bitcast_fusion.1, f32[]{:T(128)} %constant.6.clone.1), padding=0_0x0_0x0_128 | pad | bytes 20971524 | tf_op jit(solution)/shard_map/jit(_pad)/pad | solution.py:46
  132.8 16.2 %copy.52 = f32[8,8,128,384]{3,1,2,0:T(8,128)} copy(f32[8,8,128,384]{3,2,1,0:T(8,128)} %bitcast.72) | data formatting | bytes 25165824
  149.1 10.0 %pad.10 = f32[64,49280]{1,0:T(8,128)} pad(f32[64,49152]{1,0:T(8,128)} %bitcast.73, f32[]{:T(128)} %constant.6.clone.1), padding=0_0x0_128 | pad | bytes 25198596 | tf_op jit(solution)/shard_map/jit(_pad)/pad | solution.py:48
  159.0 17.7 %reshape.64 = f32[64,128,385]{2,1,0:T(8,128)} reshape(f32[64,49280]{1,0:T(8,128)} %pad.10) | data formatting | bytes 25231360 | tf_op jit(solution)/shard_map/reshape | solution.py:49
  176.8 8.3 %reduce_sum.9 = f32[64,385]{1,0:T(8,128)S(1)} reduce(f32[64,128,385]{2,1,0:T(8,128)} %reshape.64, f32[]{:T(128)} %constant.6.clone.1), dimensions={1}, to_apply=%region_1.2 | reduce | flops 3129280 | bytes 12714244 | tf_op jit(solution)/shard_map/reduce_sum | solution.py:50
  185.3 366.9 %psum.7 = f32[64,128]{1,0:T(8,128)S(1)} all-reduce(f32[64,128]{1,0:T(8,128)S(1)} %rev.7), channel_id=1, replica_groups=mesh['dp'=4,'ctx'=16,'tp'=4] {'dp','ctx'}, use_global_device_ids=true, to_apply=%region_2.3 | all-reduce | flops 8192 | bytes 65536 | tf_op jit(solution)/shard_map/psum | solution.py:93
  552.2 0.6 broadcast_multiply_fusion.1
  553.3 3.7 fusion.7
  557.8 1.0 copy.42
  558.8 1.1 copy.48
  560.0 0.9 copy.43
  (38 shorter events, 3.8 us)
Async XLA Ops:
  7.2 47.2 %all-gather.3.cloned.1.call-start = ((), (), s32[]{:S(2)}) async-start(), calls=%async_computation.1 | async-start | bytes 2621440 | tf_op jit(solution)/shard_map/all_gather | solution.py:69
  7.9 550.9 %reduce-scatter.4.cloned.1.call-start = ((), (), s32[]{:S(2)}) async-start(), calls=%async_computation.2 | async-start | bytes 17039360
  8.9 28.6 %collective-permute-start.1 = (bf16[128,1024]{1,0:T(8,128)(2,1)S(1)}, bf16[128,1024]{1,0:T(8,128)(2,1)S(1)}, u32[]{:S(2)}, u32[]{:S(2)}) collective-permute-start(bf16[128,1024]{1,0:T(8,128)(2,1)S(1)} %slice_bitcast_fusion.10), channel_id=1, source_target_pairs={{0,4},{4,8},{8,12},{12,16},{16,20},{20,24},{24,28},{28,32},{32,36}... | collective-permute-start | bytes 786440 | tf_op jit(solution)/shard_map/ppermute | solution.py:12
  20.8 16.8 %copy-start = (bf16[1,256,1024]{2,1,0:T(8,128)(2,1)S(1)}, bf16[1,256,1024]{2,1,0:T(8,128)(2,1)}, u32[]{:S(2)}) copy-start(bf16[1,256,1024]{2,1,0:T(8,128)(2,1)} %param.5) | copy-start | bytes 1572868
  81.6 0.7 copy-start.2
  90.1 26.4 %copy-start.1 = (bf16[1,256,1024]{2,1,0:T(8,128)(2,1)S(1)}, bf16[1,256,1024]{2,1,0:T(8,128)(2,1)}, u32[]{:S(2)}) copy-start(bf16[1,256,1024]{2,1,0:T(8,128)(2,1)} %param.6) | copy-start | bytes 1572868
  123.9 429.0 %collective-permute-start = (bf16[128,1024]{1,0:T(8,128)(2,1)S(1)}, bf16[128,1024]{1,0:T(8,128)(2,1)S(1)}, u32[]{:S(2)}, u32[]{:S(2)}) collective-permute-start(bf16[128,1024]{1,0:T(8,128)(2,1)S(1)} %slice.40), channel_id=1, source_target_pairs={{4,0},{8,4},{12,8},{16,12},{20,16},{24,20},{28,24},{32,28},{36,32}... | collective-permute-start | bytes 786440 | tf_op jit(solution)/shard_map/ppermute | solution.py:12
Sparse Core Ops, SparseCore 0:
  9.8 44.4 all-gather.2
  81.8 405.7 reduce-scatter.3
where the time goes:
time: 574 us; the launch traced here: 568 us
  blocking collectives  367 us (64%)
  local copies, waits for them, and re-layouts  136 us (24%)
  matrix products  25.8 us (4%)
  between operations  14.5 us (3%)
  waiting for transfers between devices  12.1 us (2%)
  other arithmetic  9.16 us (2%)
    psum x1, blocking collectives, local(): filter_total = lax.psum(filter_local, ('dp', 'ctx'))  367 us
    unnamed x16, local copies, waits for them, and re-layouts  47 us
    reshape x2, local copies, waits for them, and re-layouts, band(): flattened.reshape(groups, taps_count, period - 1)[:, :, :2 * taps_count]  43.2 us
    reshape x1, local copies, waits for them, and re-layouts, diagonal_sums(): skewed = flattened.reshape(groups, taps_count, 3 * taps_count + 1)  17.7 us
  transfers between devices with their start and end apart: 4, of which 1 were waited for; matrix products, arithmetic and copies ran while one was open for 25% of the time, Pallas kernels for 0%

commit v1 on v0

v1 whole, which is shorter than its diff:
```python
import math

import jax
import jax.numpy as jnp
from jax import lax
from jax.experimental import pallas as pl
from jax.experimental.pallas import tpu as pltpu
from jax.sharding import PartitionSpec as P

F32 = jnp.float32
BF16 = jnp.bfloat16
SIDE = 4
TAPS = 128
GROUP = 16
LANES = 128
PER_TILE = LANES // GROUP
WIDE = 256
PARAMS = pltpu.CompilerParams(vmem_limit_bytes=48 * 1024 * 1024)


def spot():
    ctx = lax.axis_index("ctx")
    tp = lax.axis_index("tp")
    return ctx // SIDE, ctx % SIDE, lax.axis_index("dp"), tp // 2, tp % 2


def moved(x, axis, by):
    if axis == "x":
        pairs = [(i, (i // SIDE + by) % SIDE * SIDE + i % SIDE) for i in range(SIDE * SIDE)]
        return lax.ppermute(x, "ctx", pairs)
    if axis == "y":
        pairs = [(i, i // SIDE * SIDE + (i % SIDE + by) % SIDE) for i in range(SIDE * SIDE)]
        return lax.ppermute(x, "ctx", pairs)
    if axis == "z":
        return lax.ppermute(x, "dp", [(i, (i + by) % SIDE) for i in range(SIDE)])
    if axis == "half":
        return lax.ppermute(x, "tp", [(i, (i + 2) % 4) for i in range(4)])
    return lax.ppermute(x, "tp", [(i, i // 2 * 2 + (i + 1) % 2) for i in range(4)])


def shifted(x, by):
    devices = lax.axis_size("ctx")
    return lax.ppermute(x, "ctx", [(i, i + by) for i in range(devices) if 0 <= i + by < devices])


def full(shape):
    return pl.BlockSpec(shape, lambda i: (0,) * len(shape))


def tile(rows, width):
    return pl.BlockSpec((rows, width), lambda i: (0, i))


def iota(shape, dim):
    return lax.broadcasted_iota(jnp.int32, shape, dim)


def lane_group(shape):
    return iota(shape, len(shape) - 1) % LANES // GROUP


def banded(rows, stack):
    for g in range(PER_TILE):
        first = jnp.broadcast_to(rows[g : g + 1], (TAPS, 2 * TAPS))
        skewed = pltpu.roll(first, 0, 1, stride=1, stride_axis=0)
        stack[g * TAPS : (g + 1) * TAPS, :] = skewed.astype(BF16)


def own_lanes(stacked):
    group = lane_group((TAPS, 2 * LANES))
    chosen = jnp.zeros((TAPS, 2 * LANES), F32)
    for g in range(PER_TILE):
        chosen = jnp.where(group == g, stacked[g * TAPS : (g + 1) * TAPS], chosen)
    return chosen


def two_windows(first, second, third):
    upper = jnp.concatenate([first, second], 1)
    lower = jnp.concatenate([second, third], 1)
    return jnp.concatenate([upper, lower], 0)


def forward_kernel(filters, previous, signal, gating, response, gated, first_rows, stack):
    step = pl.program_id(0)

    @pl.when(step == 0)
    def _():
        place = iota((TAPS, 2 * TAPS), 1) == TAPS - iota((TAPS, 2 * TAPS), 0)
        first_rows[...] = jnp.dot(
            filters[...], place.astype(F32).astype(BF16), preferred_element_type=F32
        )

    banded(first_rows[pl.ds(pl.multiple_of(step * PER_TILE, PER_TILE), PER_TILE), :], stack)
    window = two_windows(previous[...], signal[:TAPS], signal[TAPS:])
    made = own_lanes(jnp.dot(stack[...], window, preferred_element_type=F32))
    for block in range(2):
        rows = slice(block * TAPS, (block + 1) * TAPS)
        part = made[:, block * LANES : (block + 1) * LANES]
        response[rows] = part
        gated[rows] = (part * gating[rows].astype(F32)).astype(BF16)


def forward(filters, previous, signal, gating):
    length, channels = signal.shape
    return pl.pallas_call(
        forward_kernel,
        grid=(channels // LANES,),
        in_specs=[full(filters.shape), tile(TAPS, LANES), tile(length, LANES), tile(length, LANES)],
        out_specs=[tile(length, LANES), tile(length, LANES)],
        out_shape=[
            jax.ShapeDtypeStruct((length, channels), F32),
            jax.ShapeDtypeStruct((length, channels), BF16),
        ],
        scratch_shapes=[
            pltpu.VMEM((filters.shape[0], 2 * TAPS), F32),
            pltpu.VMEM((PER_TILE * TAPS, 2 * TAPS), BF16),
        ],
        compiler_params=PARAMS,
        name="conv_forward",
    )(filters, previous, signal, gating)


def backward_kernel(
    filters, previous, signal, conv_grad, following, grad_input, grad_filter, first_rows, stack
):
    step = pl.program_id(0)

    @pl.when(step == 0)
    def _():
        place = iota((TAPS, 2 * TAPS), 1) == iota((TAPS, 2 * TAPS), 0)
        first_rows[...] = jnp.dot(
            filters[...], place.astype(F32).astype(BF16), preferred_element_type=F32
        )

    banded(first_rows[pl.ds(pl.multiple_of(step * PER_TILE, PER_TILE), PER_TILE), :], stack)
    window = two_windows(conv_grad[:TAPS], conv_grad[TAPS:], following[...])
    made = own_lanes(jnp.dot(stack[...], window, preferred_element_type=F32))
    for block in range(2):
        grad_input[block * TAPS : (block + 1) * TAPS] = made[
            :, block * LANES : (block + 1) * LANES
        ].astype(BF16)
    square = (2 * TAPS, 2 * TAPS)
    turn = iota(square, 0) == (2 * TAPS - iota(square, 1)) % (2 * TAPS)
    inputs = two_windows(previous[...], signal[:TAPS], signal[TAPS:])
    turned = jnp.dot(
        turn.astype(F32).astype(BF16), inputs, preferred_element_type=F32
    ).astype(BF16)
    both = jnp.concatenate([conv_grad[:TAPS], conv_grad[TAPS:]], 1)
    group = lane_group((TAPS, 2 * LANES))
    for g in range(PER_TILE):
        stack[g * TAPS : (g + 1) * TAPS, :] = jnp.where(group == g, both.astype(F32), 0.0).astype(BF16)
    products = lax.dot_general(
        stack[...], turned, (((1,), (1,)), ((), ())), preferred_element_type=F32
    )
    for g in range(PER_TILE):
        skewed = pltpu.roll(products[g * TAPS : (g + 1) * TAPS], 0, 1, stride=1, stride_axis=0)
        grad_filter[g : g + 1, :] = jnp.sum(skewed[:, TAPS:], axis=0, keepdims=True)


def backward(filters, previous, signal, conv_grad, following):
    length, channels = signal.shape
    return pl.pallas_call(
        backward_kernel,
        grid=(channels // LANES,),
        in_specs=[
            full(filters.shape),
            tile(TAPS, LANES),
            tile(length, LANES),
            tile(length, LANES),
            tile(TAPS, LANES),
        ],
        out_specs=[
            tile(length, LANES),
            pl.BlockSpec((PER_TILE, TAPS), lambda i: (i, 0)),
        ],
        out_shape=[
            jax.ShapeDtypeStruct((length, channels), BF16),
            jax.ShapeDtypeStruct(filters.shape, F32),
        ],
        scratch_shapes=[
            pltpu.VMEM((filters.shape[0], 2 * TAPS), F32),
            pltpu.VMEM((PER_TILE * TAPS, 2 * TAPS), BF16),
        ],
        compiler_params=PARAMS,
        name="conv_backward",
    )(filters, previous, signal, conv_grad, following)


def pack_kernel(mine, other, *outs):
    x, y, _, _, core = spot()
    part = mine.shape[0]
    depth = mine.shape[1] // SIDE
    lower = iota((part, LANES), 1) < LANES // 2
    for ref, at in ((mine, core), (other, 1 - core)):
        rows = pl.ds(pl.multiple_of(at * part, part), part)
        for s in range(SIDE):
            to_x = (x + s) % SIDE
            for d in range(2):
                columns = pl.ds(pl.multiple_of(d * depth + to_x * WIDE, WIDE), WIDE)
                outs[s][rows, d * WIDE : (d + 1) * WIDE] = ref[:, columns]
            to_y = (y + s) % SIDE
            upper_half = jnp.broadcast_to(to_y % 2, (part, LANES)) == 1
            for d in range(2):
                for pair in range(SIDE // 2):
                    runs = []
                    for i in range(2):
                        start = (2 + d) * depth + (2 * pair + i) * WIDE + to_y // 2 * LANES
                        runs.append(ref[:, pl.ds(pl.multiple_of(start, LANES), LANES)].astype(F32))
                    first = jnp.where(upper_half, pltpu.roll(runs[0], LANES // 2, 1), runs[0])
                    second = jnp.where(upper_half, runs[1], pltpu.roll(runs[1], LANES // 2, 1))
                    column = (d * 2 + pair) * LANES
                    outs[SIDE + s][rows, column : column + LANES] = jnp.where(
                        lower, first, second
                    ).astype(BF16)


def pack(mine, other):
    part, width = mine.shape
    shape = (2 * part, width // (2 * SIDE))
    outs = pl.pallas_call(
        pack_kernel,
        grid=(1,),
        in_specs=[full(mine.shape)] * 2,
        out_specs=[full(shape)] * (2 * SIDE),
        out_shape=[jax.ShapeDtypeStruct(shape, BF16)] * (2 * SIDE),
        compiler_params=PARAMS,
        name="pack",
    )(mine, other)
    return outs[:SIDE], outs[SIDE:]


def project_kernel(early, early_other, late, late_other, weight, gating, response, conv_grad, grad_gate, rows):
    _, _, _, half, core = spot()
    part = early.shape[0]

    @pl.when(pl.program_id(0) == 0)
    def _():
        for ref, h, c in (
            (early, half, core),
            (early_other, half, 1 - core),
            (late, 1 - half, core),
            (late_other, 1 - half, 1 - core),
        ):
            rows[pl.ds(pl.multiple_of((2 * h + c) * part, part), part), :] = ref[...]

    made = jnp.dot(rows[...], weight[...], preferred_element_type=F32)
    conv_grad[...] = (made * gating[...].astype(F32)).astype(BF16)
    grad_gate[...] = (made * response[...]).astype(BF16)


def project(early, early_other, late, late_other, weight, gating, response):
    length, channels = gating.shape
    depth = weight.shape[0]
    return pl.pallas_call(
        project_kernel,
        grid=(channels // WIDE,),
        in_specs=[full(early.shape)] * 4
        + [tile(depth, WIDE), tile(length, WIDE), tile(length, WIDE)],
        out_specs=[tile(length, WIDE)] * 2,
        out_shape=[jax.ShapeDtypeStruct((length, channels), BF16)] * 2,
        scratch_shapes=[pltpu.VMEM((length, depth), BF16)],
        compiler_params=PARAMS,
        name="project",
    )(early, early_other, late, late_other, weight, gating, response)


def weight_kernel(*refs):
    early_x, late_x, early_y, late_y = (refs[SIDE * i : SIDE * (i + 1)] for i in range(4))
    gated = refs[4 * SIDE]
    gated_x = (gated,) + tuple(refs[4 * SIDE + 1 : 5 * SIDE])
    gated_y = (gated,) + tuple(refs[5 * SIDE : 6 * SIDE - 1])
    outs = refs[6 * SIDE - 1 : 8 * SIDE - 1]
    turned = refs[8 * SIDE - 1 :]
    x, y, _, half, _ = spot()
    run = 64

    @pl.when(pl.program_id(0) == 0)
    def _():
        for into, early, late, me in ((turned[0], early_x, late_x, y), (turned[1], early_y, late_y, x)):
            for s in range(SIDE):
                for ref, h in ((early[s], half), (late[s], 1 - half)):
                    whole = ref[...].T
                    columns = pl.ds(pl.multiple_of(s * 2 * TAPS + h * TAPS, TAPS), TAPS)
                    for d in range(2):
                        for other in range(SIDE):
                            to = (other - me + SIDE) % SIDE
                            rows = pl.ds(pl.multiple_of(to * 2 * run + d * run, run), run)
                            start = (d * SIDE + other) * run
                            into[rows, columns] = whole[start : start + run]

    for which, blocks in ((0, gated_x), (1, gated_y)):
        tokens = jnp.concatenate([ref[...] for ref in blocks], 0)
        made = jnp.dot(turned[which][...], tokens, preferred_element_type=F32)
        for s in range(SIDE):
            out = outs[which * SIDE + s]
            out[...] = made[s * 2 * run : (s + 1) * 2 * run].astype(out.dtype)


def weight_parts(early_x, late_x, early_y, late_y, gated, gated_x, gated_y):
    length, channels = gated.shape
    tokens, width = early_x[0].shape
    rows = width // SIDE
    outs = pl.pallas_call(
        weight_kernel,
        grid=(channels // WIDE,),
        in_specs=[full((tokens, width))] * (4 * SIDE) + [tile(length, WIDE)] * (2 * SIDE - 1),
        out_specs=[tile(rows, WIDE)] * (2 * SIDE),
        out_shape=[
            jax.ShapeDtypeStruct((rows, channels), F32 if s % SIDE == 0 else BF16)
            for s in range(2 * SIDE)
        ],
        scratch_shapes=[pltpu.VMEM((width, SIDE * length), BF16)] * 2,
        compiler_params=PARAMS,
        name="weight_parts",
    )(*early_x, *late_x, *early_y, *late_y, gated, *gated_x, *gated_y)
    return outs[:SIDE], outs[SIDE:]


def gather_sum_kernel(*refs):
    _, _, z, _, _ = spot()
    outs, kept = refs[2 * SIDE : 3 * SIDE], refs[3 * SIDE]
    run = kept.shape[0] // SIDE
    for which in range(2):
        total = refs[which * SIDE][...]
        for s in range(1, SIDE):
            total = total + refs[which * SIDE + s][...].astype(F32)
        for d in range(2):
            to = (2 * which + d - z + SIDE) % SIDE
            kept[pl.ds(pl.multiple_of(to * run, run), run), :] = total[d * run : (d + 1) * run]
    for s in range(SIDE):
        outs[s][...] = kept[s * run : (s + 1) * run, :].astype(outs[s].dtype)


def gather_sum(parts_x, parts_y):
    rows, channels = parts_x[0].shape
    run = rows // 2
    return pl.pallas_call(
        gather_sum_kernel,
        grid=(channels // WIDE,),
        in_specs=[tile(rows, WIDE)] * (2 * SIDE),
        out_specs=[tile(run, WIDE)] * SIDE,
        out_shape=[
            jax.ShapeDtypeStruct((run, channels), F32 if s == 0 else BF16) for s in range(SIDE)
        ],
        scratch_shapes=[pltpu.VMEM((SIDE * run, WIDE), F32)],
        compiler_params=PARAMS,
        name="gather_sum",
    )(*parts_x, *parts_y)


def summed(x, axis):
    others = [moved(x, axis, by) for by in range(1, SIDE)]
    return x + others[0] + others[1] + others[2]


def local(conv_input, gate_value, out_grad, out_weight, filters):
    signal, gating, grads = conv_input[0], gate_value[0], out_grad[0]
    length, channels = signal.shape
    shifts = range(1, SIDE)

    previous = shifted(signal[length - TAPS :], 1)
    late = moved(grads, "half", 1)
    early_other = moved(grads, "core", 1)
    response, gated = forward(filters, previous, signal, gating)
    early_x, early_y = pack(grads, early_other)
    early_x = [early_x[0]] + [moved(early_x[s], "x", s) for s in shifts]
    early_y = [early_y[0]] + [moved(early_y[s], "y", s) for s in shifts]
    gated_x = [moved(gated, "x", s) for s in shifts]
    gated_y = [moved(gated, "y", s) for s in shifts]

    late_other = moved(late, "core", 1)
    late_x, late_y = pack(late, late_other)
    late_x = [late_x[0]] + [moved(late_x[s], "x", s) for s in shifts]
    late_y = [late_y[0]] + [moved(late_y[s], "y", s) for s in shifts]
    conv_grad, grad_gate = project(
        grads, early_other, late, late_other, out_weight, gating, response
    )
    following = shifted(conv_grad[:TAPS], -1)

    parts_x, parts_y = weight_parts(early_x, late_x, early_y, late_y, gated, gated_x, gated_y)
    parts_x = [parts_x[0]] + [moved(parts_x[s], "y", s) for s in shifts]
    parts_y = [parts_y[0]] + [moved(parts_y[s], "x", s) for s in shifts]

    grad_input, filter_local = backward(filters, previous, signal, conv_grad, following)

    chunks = gather_sum(parts_x, parts_y)
    weight_total = chunks[0]
    for s in shifts:
        weight_total = weight_total + moved(chunks[s], "z", s).astype(F32)

    filter_total = summed(summed(summed(filter_local, "x"), "y"), "z")

    tokens_all = lax.axis_size("dp") * lax.axis_size("ctx") * length
    grad_filter = filter_total * (1.0 / math.sqrt(tokens_all * GROUP))
    grad_weight = weight_total * (1.0 / math.sqrt(tokens_all))
    return (grad_input[None], grad_gate[None], grad_weight, grad_filter)


def solution(mesh):
    placed = (
        P("dp", "ctx", "tp"),
        P("dp", "ctx", "tp"),
        P("dp", ("ctx", "tp"), None),
        P(None, "tp"),
        P("tp", None),
    )
    return jax.shard_map(
        local,
        mesh=mesh,
        in_specs=placed,
        out_specs=(
            P("dp", "ctx", "tp"),
            P("dp", "ctx", "tp"),
            P(("dp", "ctx"), "tp"),
            P("tp", None),
        ),
        check_vma=False,
    )
```

time: 574 us -> 151 us (0.26)
  the two profiles are of different devices: /device:TPU:0 before, /device:TPU:2 now
where the time goes in v1:
time: 151 us; the launch traced here: 150 us
  starting transfers between devices  76.1 us (50%)
  waiting for transfers between devices  39.9 us (26%)
  Pallas kernels  24.8 us (16%)
  local copies, waits for them, and re-layouts  6.93 us (5%)
    ppermute x30, starting transfers between devices, moved(): return lax.ppermute(x, 'ctx', pairs)  50.4 us
    ppermute x30, waiting for transfers between devices, moved(): return lax.ppermute(x, 'ctx', pairs)  27.7 us
    ppermute x6, starting transfers between devices, moved(): return lax.ppermute(x, 'dp', [(i, (i + by) % SIDE) for i in range(SIDE)])  12.7 us
    ppermute x2, waiting for transfers between devices, shifted(): lax.ppermute(x, 'ctx', [(i, i + by) for i in range(devices) if 0 <= i + b...  9.23 us
    ppermute x1, starting transfers between devices, moved(): return lax.ppermute(x, 'tp', [(i, (i + 2) % 4) for i in range(4)])  7.28 us
    pallas_call x1, Pallas kernels, backward(): pl.pallas_call(backward_kernel, grid=(channels // LANES,), in_specs=[full...  6.96 us
    pallas_call x1, Pallas kernels, project(): pl.pallas_call(project_kernel, grid=(channels // WIDE,), in_specs=[full(e...  6.45 us
    unnamed x26, local copies, waits for them, and re-layouts  5.95 us
  transfers between devices with their start and end apart: 41, of which 11 were waited for; matrix products, arithmetic and copies ran while one was open for 1% of the time, Pallas kernels for 17%

profile of v1, /device:TPU:2, one launch (start us, length us, event | category | flops | bytes accessed | tf_op | source)
XLA Modules:
  0.0 150.1 jit_solution(17887581441402321100)
XLA Ops:
  0.6 7.3 %collective-permute-start.2 = (bf16[64,4096]{1,0:T(8,128)(2,1)}, bf16[64,4096]{1,0:T(8,128)(2,1)S(1)}, u32[]{:S(2)}, u32[]{:S(2)}) collective-permute-start(bf16[64,4096]{1,0:T(8,128)(2,1)} %bitcast.9), channel_id=1, source_target_pairs={{0,2},{1,3},{2,0},{3,1},{4,6},{5,7},{6,4},{7,5},{8,10},{9,11},{10,... | collective-permute-start | bytes 1572872 | tf_op jit(solution)/shard_map/ppermute | solution.py:37
  8.9 3.5 %collective-permute-start = (bf16[128,1024]{1,0:T(8,128)(2,1)S(1)}, bf16[128,1024]{1,0:T(8,128)(2,1)S(1)}, u32[]{:S(2)}, u32[]{:S(2)}) collective-permute-start(bf16[128,1024]{1,0:T(8,128)(2,1)S(1)} %slice_bitcast_fusion), channel_id=1, source_target_pairs={{0,4},{4,8},{8,12},{12,16},{16,20},{20,24},{24,28},{28,32},{32,36}... | collective-permute-start | bytes 786440 | tf_op jit(solution)/shard_map/ppermute | solution.py:43
  12.4 9.2 %collective-permute-done.previous = bf16[128,1024]{1,0:T(8,128)(2,1)S(1)} collective-permute-done((bf16[128,1024]{1,0:T(8,128)(2,1)S(1)}, bf16[128,1024]{1,0:T(8,128)(2,1)S(1)}, u32[]{:S(2)}, u32[]{:S(2)}) %collective-permute-start) | collective-permute-done | bytes 262176 | tf_op jit(solution)/shard_map/ppermute | solution.py:43
  24.4 3.8 %conv_forward.1 = (f32[256,1024]{1,0:T(8,128)S(1)}, bf16[256,1024]{1,0:T(8,128)(2,1)S(1)}) custom-call(bf16[64,128]{1,0:T(8,128)(2,1)S(1)} %copy-done.6, bf16[128,1024]{1,0:T(8,128)(2,1)S(1)} %collective-permute-done.previous, bf16[256,1024]{1,0:T(8,128)(2,1)S(1)} %bitcast.7, bf16[256,1024]{1,0:T(8,128)(2,1)S(1)} %bitcast.13), custom_call_target="tpu_custom_call" | custom-call | tf_op jit(solution)/shard_map/conv_forward/pallas_call | solution.py:105
  33.5 2.2 %collective-permute-start.7 = (bf16[128,512]{1,0:T(8,128)(2,1)S(1)}, bf16[128,512]{1,0:T(8,128)(2,1)S(1)}, u32[]{:S(2)}, u32[]{:S(2)}) collective-permute-start(bf16[128,512]{1,0:T(8,128)(2,1)S(1)} %get-tuple-element.45), channel_id=1, source_target_pairs={{0,48},{4,52},{8,56},{12,60},{16,0},{20,4},{24,8},{28,12},{32,16},... | collective-permute-start | bytes 393224 | tf_op jit(solution)/shard_map/ppermute | solution.py:30
  38.2 2.1 %collective-permute-done.6.refs_2_ = bf16[128,512]{1,0:T(8,128)(2,1)S(1)} collective-permute-done((bf16[128,512]{1,0:T(8,128)(2,1)S(1)}, bf16[128,512]{1,0:T(8,128)(2,1)S(1)}, u32[]{:S(2)}, u32[]{:S(2)}) %collective-permute-start.6) | collective-permute-done | bytes 131104 | tf_op jit(solution)/shard_map/ppermute | solution.py:30
  41.7 2.2 %collective-permute-start.21 = (bf16[256,1024]{1,0:T(8,128)(2,1)S(1)}, bf16[256,1024]{1,0:T(8,128)(2,1)S(1)}, u32[]{:S(2)}, u32[]{:S(2)}) collective-permute-start(bf16[256,1024]{1,0:T(8,128)(2,1)S(1)} %get-tuple-element.58.refs_16_), channel_id=1, source_target_pairs={{0,8},{4,12},{8,0},{12,4},{16,24},{20,28},{24,16},{28,20},{32,40},... | collective-permute-start | bytes 1572872 | tf_op jit(solution)/shard_map/ppermute | solution.py:33
  45.4 2.8 %collective-permute-done.12.refs_10_ = bf16[128,512]{1,0:T(8,128)(2,1)S(1)} collective-permute-done((bf16[128,512]{1,0:T(8,128)(2,1)S(1)}, bf16[128,512]{1,0:T(8,128)(2,1)S(1)}, u32[]{:S(2)}, u32[]{:S(2)}) %collective-permute-start.12) | collective-permute-done | bytes 131104 | tf_op jit(solution)/shard_map/ppermute | solution.py:33
  49.4 9.5 %collective-permute-done.13.refs_11_ = bf16[128,512]{1,0:T(8,128)(2,1)S(1)} collective-permute-done((bf16[128,512]{1,0:T(8,128)(2,1)S(1)}, bf16[128,512]{1,0:T(8,128)(2,1)S(1)}, u32[]{:S(2)}, u32[]{:S(2)}) %collective-permute-start.13) | collective-permute-done | bytes 131104 | tf_op jit(solution)/shard_map/ppermute | solution.py:33
  58.9 2.2 %collective-permute-start.19 = (bf16[256,1024]{1,0:T(8,128)(2,1)S(1)}, bf16[256,1024]{1,0:T(8,128)(2,1)S(1)}, u32[]{:S(2)}, u32[]{:S(2)}) collective-permute-start(bf16[256,1024]{1,0:T(8,128)(2,1)S(1)} %get-tuple-element.58.refs_16_), channel_id=1, source_target_pairs={{0,48},{4,52},{8,56},{12,60},{16,0},{20,4},{24,8},{28,12},{32,16},... | collective-permute-start | bytes 1572872 | tf_op jit(solution)/shard_map/ppermute | solution.py:30
  61.1 3.9 %collective-permute-start.18 = (bf16[256,1024]{1,0:T(8,128)(2,1)S(1)}, bf16[256,1024]{1,0:T(8,128)(2,1)S(1)}, u32[]{:S(2)}, u32[]{:S(2)}) collective-permute-start(bf16[256,1024]{1,0:T(8,128)(2,1)S(1)} %get-tuple-element.58.refs_16_), channel_id=1, source_target_pairs={{0,32},{4,36},{8,40},{12,44},{16,48},{20,52},{24,56},{28,60},{32,0... | collective-permute-start | bytes 1572872 | tf_op jit(solution)/shard_map/ppermute | solution.py:30
  65.0 2.5 %collective-permute-start.17 = (bf16[256,1024]{1,0:T(8,128)(2,1)S(1)}, bf16[256,1024]{1,0:T(8,128)(2,1)S(1)}, u32[]{:S(2)}, u32[]{:S(2)}) collective-permute-start(bf16[256,1024]{1,0:T(8,128)(2,1)S(1)} %get-tuple-element.58.refs_16_), channel_id=1, source_target_pairs={{0,16},{4,20},{8,24},{12,28},{16,32},{20,36},{24,40},{28,44},{32,4... | collective-permute-start | bytes 1572872 | tf_op jit(solution)/shard_map/ppermute | solution.py:30
  69.6 6.4 %project.1 = (bf16[256,1024]{1,0:T(8,128)(2,1)S(1)}, bf16[256,1024]{1,0:T(8,128)(2,1)}) custom-call(bf16[64,4096]{1,0:T(8,128)(2,1)S(1)} %bitcast.12, bf16[64,4096]{1,0:T(8,128)(2,1)S(1)} %collective-permute-done.1.early_other.other, bf16[64,4096]{1,0:T(8,128)(2,1)S(1)} %collective-permute-done.2.late.mine, ...), custom_call_target="tpu_custom_call" | custom-call | tf_op jit(solution)/shard_map/project/pallas_call | solution.py:254
  76.1 2.2 %collective-permute-start.4 = (bf16[128,1024]{1,0:T(8,128)(2,1)S(1)}, bf16[128,1024]{1,0:T(8,128)(2,1)S(1)}, u32[]{:S(2)}, u32[]{:S(2)}) collective-permute-start(bf16[128,1024]{1,0:T(8,128)(2,1)S(1)} %slice.11), channel_id=1, source_target_pairs={{4,0},{8,4},{12,8},{16,12},{20,16},{24,20},{28,24},{32,28},{36,32}... | collective-permute-start | bytes 786440 | tf_op jit(solution)/shard_map/ppermute | solution.py:43
  79.0 2.6 %collective-permute-start.8 = (bf16[128,512]{1,0:T(8,128)(2,1)S(1)}, bf16[128,512]{1,0:T(8,128)(2,1)S(1)}, u32[]{:S(2)}, u32[]{:S(2)}) collective-permute-start(bf16[128,512]{1,0:T(8,128)(2,1)S(1)} %get-tuple-element.47), channel_id=1, source_target_pairs={{0,16},{4,20},{8,24},{12,28},{16,32},{20,36},{24,40},{28,44},{32,4... | collective-permute-start | bytes 393224 | tf_op jit(solution)/shard_map/ppermute | solution.py:30
  81.6 6.8 %collective-permute-done.18.refs_18_ = bf16[256,1024]{1,0:T(8,128)(2,1)S(1)} collective-permute-done((bf16[256,1024]{1,0:T(8,128)(2,1)S(1)}, bf16[256,1024]{1,0:T(8,128)(2,1)S(1)}, u32[]{:S(2)}, u32[]{:S(2)}) %collective-permute-start.18) | collective-permute-done | bytes 524320 | tf_op jit(solution)/shard_map/ppermute | solution.py:30
  89.8 2.9 %collective-permute-start.15 = (bf16[128,512]{1,0:T(8,128)(2,1)S(1)}, bf16[128,512]{1,0:T(8,128)(2,1)S(1)}, u32[]{:S(2)}, u32[]{:S(2)}) collective-permute-start(bf16[128,512]{1,0:T(8,128)(2,1)S(1)} %get-tuple-element.56), channel_id=1, source_target_pairs={{0,8},{4,12},{8,0},{12,4},{16,24},{20,28},{24,16},{28,20},{32,40},... | collective-permute-start | bytes 393224 | tf_op jit(solution)/shard_map/ppermute | solution.py:33
  92.7 2.3 %collective-permute-start.16 = (bf16[128,512]{1,0:T(8,128)(2,1)S(1)}, bf16[128,512]{1,0:T(8,128)(2,1)S(1)}, u32[]{:S(2)}, u32[]{:S(2)}) collective-permute-start(bf16[128,512]{1,0:T(8,128)(2,1)S(1)} %get-tuple-element.57), channel_id=1, source_target_pairs={{0,12},{4,0},{8,4},{12,8},{16,28},{20,16},{24,20},{28,24},{32,44},... | collective-permute-start | bytes 393224 | tf_op jit(solution)/shard_map/ppermute | solution.py:33
  95.1 7.0 %conv_backward.1 = (bf16[256,1024]{1,0:T(8,128)(2,1)}, f32[64,128]{1,0:T(8,128)S(1)}) custom-call(bf16[64,128]{1,0:T(8,128)(2,1)S(1)} %copy-done.7, bf16[128,1024]{1,0:T(8,128)(2,1)S(1)} %collective-permute-done.previous, bf16[256,1024]{1,0:T(8,128)(2,1)S(1)} %bitcast.8, bf16[256,1024]{1,0:T(8,128)(2,1)S(1)} %get-tuple-element.39.conv_grad, ...), custom_call_target="tpu_custom_call" | custom-call | tf_op jit(solution)/shard_map/conv_backward/pallas_call | solution.py:162
  102.0 2.6 %collective-permute-start.34 = (f32[64,128]{1,0:T(8,128)S(1)}, f32[64,128]{1,0:T(8,128)S(1)}, u32[]{:S(2)}, u32[]{:S(2)}) collective-permute-start(f32[64,128]{1,0:T(8,128)S(1)} %get-tuple-element.71), channel_id=1, source_target_pairs={{0,48},{4,52},{8,56},{12,60},{16,0},{20,4},{24,8},{28,12},{32,16},... | collective-permute-start | bytes 98312 | tf_op jit(solution)/shard_map/ppermute | solution.py:30
  106.8 5.7 %weight_parts.1 = (f32[128,1024]{1,0:T(8,128)S(1)}, bf16[128,1024]{1,0:T(8,128)(2,1)S(1)}, bf16[128,1024]{1,0:T(8,128)(2,1)S(1)}, bf16[128,1024]{1,0:T(8,128)(2,...) custom-call(bf16[128,512]{1,0:T(8,128)(2,1)S(1)} %get-tuple-element., ...), custom_call_target="tpu_custom_call" | custom-call | tf_op jit(solution)/shard_map/weight_parts/pallas_call | solution.py:303
  112.6 3.3 %collective-permute-start.37 = (f32[64,128]{1,0:T(8,128)S(1)}, f32[64,128]{1,0:T(8,128)S(1)}, u32[]{:S(2)}, u32[]{:S(2)}) collective-permute-start(f32[64,128]{1,0:T(8,128)S(1)} %add_add_fusion.1), channel_id=1, source_target_pairs={{0,12},{4,0},{8,4},{12,8},{16,28},{20,16},{24,20},{28,24},{32,44},... | collective-permute-start | bytes 98312 | tf_op jit(solution)/shard_map/ppermute | solution.py:33
  116.9 2.6 %collective-permute-start.24 = (bf16[128,1024]{1,0:T(8,128)(2,1)S(1)}, bf16[128,1024]{1,0:T(8,128)(2,1)S(1)}, u32[]{:S(2)}, u32[]{:S(2)}) collective-permute-start(bf16[128,1024]{1,0:T(8,128)(2,1)S(1)} %get-tuple-element.61), channel_id=1, source_target_pairs={{0,8},{4,12},{8,0},{12,4},{16,24},{20,28},{24,16},{28,20},{32,40},... | collective-permute-start | bytes 786440 | tf_op jit(solution)/shard_map/ppermute | solution.py:33
  119.5 4.9 %collective-permute-start.25 = (bf16[128,1024]{1,0:T(8,128)(2,1)S(1)}, bf16[128,1024]{1,0:T(8,128)(2,1)S(1)}, u32[]{:S(2)}, u32[]{:S(2)}) collective-permute-start(bf16[128,1024]{1,0:T(8,128)(2,1)S(1)} %get-tuple-element.62), channel_id=1, source_target_pairs={{0,12},{4,0},{8,4},{12,8},{16,28},{20,16},{24,20},{28,24},{32,44},... | collective-permute-start | bytes 786440 | tf_op jit(solution)/shard_map/ppermute | solution.py:33
  124.4 3.0 %collective-permute-done.35 = f32[64,128]{1,0:T(8,128)S(1)} collective-permute-done((f32[64,128]{1,0:T(8,128)S(1)}, f32[64,128]{1,0:T(8,128)S(1)}, u32[]{:S(2)}, u32[]{:S(2)}) %collective-permute-start.35) | collective-permute-done | bytes 32800 | tf_op jit(solution)/shard_map/ppermute | solution.py:33
  127.4 2.0 %collective-permute-start.27 = (bf16[128,1024]{1,0:T(8,128)(2,1)S(1)}, bf16[128,1024]{1,0:T(8,128)(2,1)S(1)}, u32[]{:S(2)}, u32[]{:S(2)}) collective-permute-start(bf16[128,1024]{1,0:T(8,128)(2,1)S(1)} %get-tuple-element.65), channel_id=1, source_target_pairs={{0,32},{4,36},{8,40},{12,44},{16,48},{20,52},{24,56},{28,60},{32,0... | collective-permute-start | bytes 786440 | tf_op jit(solution)/shard_map/ppermute | solution.py:30
  129.4 2.3 %collective-permute-start.28 = (bf16[128,1024]{1,0:T(8,128)(2,1)S(1)}, bf16[128,1024]{1,0:T(8,128)(2,1)S(1)}, u32[]{:S(2)}, u32[]{:S(2)}) collective-permute-start(bf16[128,1024]{1,0:T(8,128)(2,1)S(1)} %get-tuple-element.66), channel_id=1, source_target_pairs={{0,48},{4,52},{8,56},{12,60},{16,0},{20,4},{24,8},{28,12},{32,16},... | collective-permute-start | bytes 786440 | tf_op jit(solution)/shard_map/ppermute | solution.py:30
  131.7 2.0 %collective-permute-start.40 = (f32[64,128]{1,0:T(8,128)S(1)}, f32[64,128]{1,0:T(8,128)S(1)}, u32[]{:S(2)}, u32[]{:S(2)}) collective-permute-start(f32[64,128]{1,0:T(8,128)S(1)} %add_add_fusion), channel_id=1, source_target_pairs={{0,192},{64,0},{128,64},{192,128},{1,193},{65,1},{129,65},{193,129... | collective-permute-start | bytes 98312 | tf_op jit(solution)/shard_map/ppermute | solution.py:35
  133.8 2.6 %collective-permute-start.39 = (f32[64,128]{1,0:T(8,128)S(1)}, f32[64,128]{1,0:T(8,128)S(1)}, u32[]{:S(2)}, u32[]{:S(2)}) collective-permute-start(f32[64,128]{1,0:T(8,128)S(1)} %add_add_fusion), channel_id=1, source_target_pairs={{0,128},{64,192},{128,0},{192,64},{1,129},{65,193},{129,1},{193,65... | collective-permute-start | bytes 98312 | tf_op jit(solution)/shard_map/ppermute | solution.py:35
  138.9 3.2 %collective-permute-start.29 = (bf16[64,1024]{1,0:T(8,128)(2,1)S(1)}, bf16[64,1024]{1,0:T(8,128)(2,1)S(1)}, u32[]{:S(2)}, u32[]{:S(2)}) collective-permute-start(bf16[64,1024]{1,0:T(8,128)(2,1)S(1)} %get-tuple-element.68), channel_id=1, source_target_pairs={{0,64},{64,128},{128,192},{192,0},{1,65},{65,129},{129,193},{193,1... | collective-permute-start | bytes 393224 | tf_op jit(solution)/shard_map/ppermute | solution.py:35
  142.9 2.8 %collective-permute-start.31 = (bf16[64,1024]{1,0:T(8,128)(2,1)S(1)}, bf16[64,1024]{1,0:T(8,128)(2,1)S(1)}, u32[]{:S(2)}, u32[]{:S(2)}) collective-permute-start(bf16[64,1024]{1,0:T(8,128)(2,1)S(1)} %get-tuple-element.70), channel_id=1, source_target_pairs={{0,192},{64,0},{128,64},{192,128},{1,193},{65,1},{129,65},{193,129... | collective-permute-start | bytes 393224 | tf_op jit(solution)/shard_map/ppermute | solution.py:35
  146.3 3.0 %collective-permute-done.30 = bf16[64,1024]{1,0:T(8,128)(2,1)S(1)} collective-permute-done((bf16[64,1024]{1,0:T(8,128)(2,1)S(1)}, bf16[64,1024]{1,0:T(8,128)(2,1)S(1)}, u32[]{:S(2)}, u32[]{:S(2)}) %collective-permute-start.30) | collective-permute-done | bytes 131104 | tf_op jit(solution)/shard_map/ppermute | solution.py:35
  (89 shorter events, 27.7 us)
Async XLA Ops:
  0.6 28.6 %collective-permute-start.2 = (bf16[64,4096]{1,0:T(8,128)(2,1)}, bf16[64,4096]{1,0:T(8,128)(2,1)S(1)}, u32[]{:S(2)}, u32[]{:S(2)}) collective-permute-start(bf16[64,4096]{1,0:T(8,128)(2,1)} %bitcast.9), channel_id=1, source_target_pairs={{0,2},{1,3},{2,0},{3,1},{4,6},{5,7},{6,4},{7,5},{8,10},{9,11},{10,... | collective-permute-start | bytes 1572872 | tf_op jit(solution)/shard_map/ppermute | solution.py:37
  7.9 21.3 %collective-permute-start.1 = (bf16[64,4096]{1,0:T(8,128)(2,1)}, bf16[64,4096]{1,0:T(8,128)(2,1)S(1)}, u32[]{:S(2)}, u32[]{:S(2)}) collective-permute-start(bf16[64,4096]{1,0:T(8,128)(2,1)} %bitcast.10), channel_id=1, source_target_pairs={{0,1},{1,0},{2,3},{3,2},{4,5},{5,4},{6,7},{7,6},{8,9},{9,8},{10,11... | collective-permute-start | bytes 1572872 | tf_op jit(solution)/shard_map/ppermute | solution.py:38
  8.9 12.7 %collective-permute-start = (bf16[128,1024]{1,0:T(8,128)(2,1)S(1)}, bf16[128,1024]{1,0:T(8,128)(2,1)S(1)}, u32[]{:S(2)}, u32[]{:S(2)}) collective-permute-start(bf16[128,1024]{1,0:T(8,128)(2,1)S(1)} %slice_bitcast_fusion), channel_id=1, source_target_pairs={{0,4},{4,8},{8,12},{12,16},{16,20},{20,24},{24,28},{28,32},{32,36}... | collective-permute-start | bytes 786440 | tf_op jit(solution)/shard_map/ppermute | solution.py:43
  28.2 32.9 %collective-permute-start.22 = (bf16[256,1024]{1,0:T(8,128)(2,1)S(1)}, bf16[256,1024]{1,0:T(8,128)(2,1)S(1)}, u32[]{:S(2)}, u32[]{:S(2)}) collective-permute-start(bf16[256,1024]{1,0:T(8,128)(2,1)S(1)} %get-tuple-element.58.refs_16_), channel_id=1, source_target_pairs={{0,12},{4,0},{8,4},{12,8},{16,28},{20,16},{24,20},{28,24},{32,44},... | collective-permute-start | bytes 1572872 | tf_op jit(solution)/shard_map/ppermute | solution.py:33
  29.2 35.8 %collective-permute-start.3 = (bf16[64,4096]{1,0:T(8,128)(2,1)S(1)}, bf16[64,4096]{1,0:T(8,128)(2,1)S(1)}, u32[]{:S(2)}, u32[]{:S(2)}) collective-permute-start(bf16[64,4096]{1,0:T(8,128)(2,1)S(1)} %collective-permute-done.2.late.mine), channel_id=1, source_target_pairs={{0,1},{1,0},{2,3},{3,2},{4,5},{5,4},{6,7},{7,6},{8,9},{9,8},{10,11... | collective-permute-start | bytes 1572872 | tf_op jit(solution)/shard_map/ppermute | solution.py:38
  33.5 8.2 %collective-permute-start.7 = (bf16[128,512]{1,0:T(8,128)(2,1)S(1)}, bf16[128,512]{1,0:T(8,128)(2,1)S(1)}, u32[]{:S(2)}, u32[]{:S(2)}) collective-permute-start(bf16[128,512]{1,0:T(8,128)(2,1)S(1)} %get-tuple-element.45), channel_id=1, source_target_pairs={{0,48},{4,52},{8,56},{12,60},{16,0},{20,4},{24,8},{28,12},{32,16},... | collective-permute-start | bytes 393224 | tf_op jit(solution)/shard_map/ppermute | solution.py:30
  41.7 34.4 %collective-permute-start.21 = (bf16[256,1024]{1,0:T(8,128)(2,1)S(1)}, bf16[256,1024]{1,0:T(8,128)(2,1)S(1)}, u32[]{:S(2)}, u32[]{:S(2)}) collective-permute-start(bf16[256,1024]{1,0:T(8,128)(2,1)S(1)} %get-tuple-element.58.refs_16_), channel_id=1, source_target_pairs={{0,8},{4,12},{8,0},{12,4},{16,24},{20,28},{24,16},{28,20},{32,40},... | collective-permute-start | bytes 1572872 | tf_op jit(solution)/shard_map/ppermute | solution.py:33
  44.7 14.2 %collective-permute-start.13 = (bf16[128,512]{1,0:T(8,128)(2,1)S(1)}, bf16[128,512]{1,0:T(8,128)(2,1)S(1)}, u32[]{:S(2)}, u32[]{:S(2)}) collective-permute-start(bf16[128,512]{1,0:T(8,128)(2,1)S(1)} %get-tuple-element.53), channel_id=1, source_target_pairs={{0,12},{4,0},{8,4},{12,8},{16,28},{20,16},{24,20},{28,24},{32,44},... | collective-permute-start | bytes 393224 | tf_op jit(solution)/shard_map/ppermute | solution.py:33
  48.1 30.8 %collective-permute-start.20 = (bf16[256,1024]{1,0:T(8,128)(2,1)S(1)}, bf16[256,1024]{1,0:T(8,128)(2,1)S(1)}, u32[]{:S(2)}, u32[]{:S(2)}) collective-permute-start(bf16[256,1024]{1,0:T(8,128)(2,1)S(1)} %get-tuple-element.58.refs_16_), channel_id=1, source_target_pairs={{0,4},{4,8},{8,12},{12,0},{16,20},{20,24},{24,28},{28,16},{32,36},... | collective-permute-start | bytes 1572872 | tf_op jit(solution)/shard_map/ppermute | solution.py:33
  58.9 22.7 %collective-permute-start.19 = (bf16[256,1024]{1,0:T(8,128)(2,1)S(1)}, bf16[256,1024]{1,0:T(8,128)(2,1)S(1)}, u32[]{:S(2)}, u32[]{:S(2)}) collective-permute-start(bf16[256,1024]{1,0:T(8,128)(2,1)S(1)} %get-tuple-element.58.refs_16_), channel_id=1, source_target_pairs={{0,48},{4,52},{8,56},{12,60},{16,0},{20,4},{24,8},{28,12},{32,16},... | collective-permute-start | bytes 1572872 | tf_op jit(solution)/shard_map/ppermute | solution.py:30
  61.1 27.3 %collective-permute-start.18 = (bf16[256,1024]{1,0:T(8,128)(2,1)S(1)}, bf16[256,1024]{1,0:T(8,128)(2,1)S(1)}, u32[]{:S(2)}, u32[]{:S(2)}) collective-permute-start(bf16[256,1024]{1,0:T(8,128)(2,1)S(1)} %get-tuple-element.58.refs_16_), channel_id=1, source_target_pairs={{0,32},{4,36},{8,40},{12,44},{16,48},{20,52},{24,56},{28,60},{32,0... | collective-permute-start | bytes 1572872 | tf_op jit(solution)/shard_map/ppermute | solution.py:30
  65.0 23.4 %collective-permute-start.17 = (bf16[256,1024]{1,0:T(8,128)(2,1)S(1)}, bf16[256,1024]{1,0:T(8,128)(2,1)S(1)}, u32[]{:S(2)}, u32[]{:S(2)}) collective-permute-start(bf16[256,1024]{1,0:T(8,128)(2,1)S(1)} %get-tuple-element.58.refs_16_), channel_id=1, source_target_pairs={{0,16},{4,20},{8,24},{12,28},{16,32},{20,36},{24,40},{28,44},{32,4... | collective-permute-start | bytes 1572872 | tf_op jit(solution)/shard_map/ppermute | solution.py:30
  76.1 16.6 %collective-permute-start.4 = (bf16[128,1024]{1,0:T(8,128)(2,1)S(1)}, bf16[128,1024]{1,0:T(8,128)(2,1)S(1)}, u32[]{:S(2)}, u32[]{:S(2)}) collective-permute-start(bf16[128,1024]{1,0:T(8,128)(2,1)S(1)} %slice.11), channel_id=1, source_target_pairs={{4,0},{8,4},{12,8},{16,12},{20,16},{24,20},{28,24},{32,28},{36,32}... | collective-permute-start | bytes 786440 | tf_op jit(solution)/shard_map/ppermute | solution.py:43
  79.0 10.8 %collective-permute-start.8 = (bf16[128,512]{1,0:T(8,128)(2,1)S(1)}, bf16[128,512]{1,0:T(8,128)(2,1)S(1)}, u32[]{:S(2)}, u32[]{:S(2)}) collective-permute-start(bf16[128,512]{1,0:T(8,128)(2,1)S(1)} %get-tuple-element.47), channel_id=1, source_target_pairs={{0,16},{4,20},{8,24},{12,28},{16,32},{20,36},{24,40},{28,44},{32,4... | collective-permute-start | bytes 393224 | tf_op jit(solution)/shard_map/ppermute | solution.py:30
  81.6 20.4 %collective-permute-start.9 = (bf16[128,512]{1,0:T(8,128)(2,1)S(1)}, bf16[128,512]{1,0:T(8,128)(2,1)S(1)}, u32[]{:S(2)}, u32[]{:S(2)}) collective-permute-start(bf16[128,512]{1,0:T(8,128)(2,1)S(1)} %get-tuple-element.48), channel_id=1, source_target_pairs={{0,32},{4,36},{8,40},{12,44},{16,48},{20,52},{24,56},{28,60},{32,0... | collective-permute-start | bytes 393224 | tf_op jit(solution)/shard_map/ppermute | solution.py:30
  88.4 16.2 %collective-permute-start.10 = (bf16[128,512]{1,0:T(8,128)(2,1)S(1)}, bf16[128,512]{1,0:T(8,128)(2,1)S(1)}, u32[]{:S(2)}, u32[]{:S(2)}) collective-permute-start(bf16[128,512]{1,0:T(8,128)(2,1)S(1)} %get-tuple-element.49), channel_id=1, source_target_pairs={{0,48},{4,52},{8,56},{12,60},{16,0},{20,4},{24,8},{28,12},{32,16},... | collective-permute-start | bytes 393224 | tf_op jit(solution)/shard_map/ppermute | solution.py:30
  88.4 16.5 %collective-permute-start.14 = (bf16[128,512]{1,0:T(8,128)(2,1)S(1)}, bf16[128,512]{1,0:T(8,128)(2,1)S(1)}, u32[]{:S(2)}, u32[]{:S(2)}) collective-permute-start(bf16[128,512]{1,0:T(8,128)(2,1)S(1)} %get-tuple-element.55), channel_id=1, source_target_pairs={{0,4},{4,8},{8,12},{12,0},{16,20},{20,24},{24,28},{28,16},{32,36},... | collective-permute-start | bytes 393224 | tf_op jit(solution)/shard_map/ppermute | solution.py:33
  89.8 17.0 %collective-permute-start.15 = (bf16[128,512]{1,0:T(8,128)(2,1)S(1)}, bf16[128,512]{1,0:T(8,128)(2,1)S(1)}, u32[]{:S(2)}, u32[]{:S(2)}) collective-permute-start(bf16[128,512]{1,0:T(8,128)(2,1)S(1)} %get-tuple-element.56), channel_id=1, source_target_pairs={{0,8},{4,12},{8,0},{12,4},{16,24},{20,28},{24,16},{28,20},{32,40},... | collective-permute-start | bytes 393224 | tf_op jit(solution)/shard_map/ppermute | solution.py:33
  92.7 14.0 %collective-permute-start.16 = (bf16[128,512]{1,0:T(8,128)(2,1)S(1)}, bf16[128,512]{1,0:T(8,128)(2,1)S(1)}, u32[]{:S(2)}, u32[]{:S(2)}) collective-permute-start(bf16[128,512]{1,0:T(8,128)(2,1)S(1)} %get-tuple-element.57), channel_id=1, source_target_pairs={{0,12},{4,0},{8,4},{12,8},{16,28},{20,16},{24,20},{28,24},{32,44},... | collective-permute-start | bytes 393224 | tf_op jit(solution)/shard_map/ppermute | solution.py:33
  102.0 10.5 %collective-permute-start.34 = (f32[64,128]{1,0:T(8,128)S(1)}, f32[64,128]{1,0:T(8,128)S(1)}, u32[]{:S(2)}, u32[]{:S(2)}) collective-permute-start(f32[64,128]{1,0:T(8,128)S(1)} %get-tuple-element.71), channel_id=1, source_target_pairs={{0,48},{4,52},{8,56},{12,60},{16,0},{20,4},{24,8},{28,12},{32,16},... | collective-permute-start | bytes 98312 | tf_op jit(solution)/shard_map/ppermute | solution.py:30
  104.7 7.9 %collective-permute-start.33 = (f32[64,128]{1,0:T(8,128)S(1)}, f32[64,128]{1,0:T(8,128)S(1)}, u32[]{:S(2)}, u32[]{:S(2)}) collective-permute-start(f32[64,128]{1,0:T(8,128)S(1)} %get-tuple-element.71), channel_id=1, source_target_pairs={{0,32},{4,36},{8,40},{12,44},{16,48},{20,52},{24,56},{28,60},{32,0... | collective-permute-start | bytes 98312 | tf_op jit(solution)/shard_map/ppermute | solution.py:30
  112.5 16.9 %collective-permute-start.23 = (bf16[128,1024]{1,0:T(8,128)(2,1)S(1)}, bf16[128,1024]{1,0:T(8,128)(2,1)S(1)}, u32[]{:S(2)}, u32[]{:S(2)}) collective-permute-start(bf16[128,1024]{1,0:T(8,128)(2,1)S(1)} %get-tuple-element.60), channel_id=1, source_target_pairs={{0,4},{4,8},{8,12},{12,0},{16,20},{20,24},{24,28},{28,16},{32,36},... | collective-permute-start | bytes 786440 | tf_op jit(solution)/shard_map/ppermute | solution.py:33
  115.9 8.5 %collective-permute-start.36 = (f32[64,128]{1,0:T(8,128)S(1)}, f32[64,128]{1,0:T(8,128)S(1)}, u32[]{:S(2)}, u32[]{:S(2)}) collective-permute-start(f32[64,128]{1,0:T(8,128)S(1)} %add_add_fusion.1), channel_id=1, source_target_pairs={{0,8},{4,12},{8,0},{12,4},{16,24},{20,28},{24,16},{28,20},{32,40},... | collective-permute-start | bytes 98312 | tf_op jit(solution)/shard_map/ppermute | solution.py:33
  115.9 11.5 %collective-permute-start.35 = (f32[64,128]{1,0:T(8,128)S(1)}, f32[64,128]{1,0:T(8,128)S(1)}, u32[]{:S(2)}, u32[]{:S(2)}) collective-permute-start(f32[64,128]{1,0:T(8,128)S(1)} %add_add_fusion.1), channel_id=1, source_target_pairs={{0,4},{4,8},{8,12},{12,0},{16,20},{20,24},{24,28},{28,16},{32,36},... | collective-permute-start | bytes 98312 | tf_op jit(solution)/shard_map/ppermute | solution.py:33
  116.9 14.9 %collective-permute-start.24 = (bf16[128,1024]{1,0:T(8,128)(2,1)S(1)}, bf16[128,1024]{1,0:T(8,128)(2,1)S(1)}, u32[]{:S(2)}, u32[]{:S(2)}) collective-permute-start(bf16[128,1024]{1,0:T(8,128)(2,1)S(1)} %get-tuple-element.61), channel_id=1, source_target_pairs={{0,8},{4,12},{8,0},{12,4},{16,24},{20,28},{24,16},{28,20},{32,40},... | collective-permute-start | bytes 786440 | tf_op jit(solution)/shard_map/ppermute | solution.py:33
  119.5 14.3 %collective-permute-start.25 = (bf16[128,1024]{1,0:T(8,128)(2,1)S(1)}, bf16[128,1024]{1,0:T(8,128)(2,1)S(1)}, u32[]{:S(2)}, u32[]{:S(2)}) collective-permute-start(bf16[128,1024]{1,0:T(8,128)(2,1)S(1)} %get-tuple-element.62), channel_id=1, source_target_pairs={{0,12},{4,0},{8,4},{12,8},{16,28},{20,16},{24,20},{28,24},{32,44},... | collective-permute-start | bytes 786440 | tf_op jit(solution)/shard_map/ppermute | solution.py:33
  124.4 12.0 %collective-permute-start.26 = (bf16[128,1024]{1,0:T(8,128)(2,1)S(1)}, bf16[128,1024]{1,0:T(8,128)(2,1)S(1)}, u32[]{:S(2)}, u32[]{:S(2)}) collective-permute-start(bf16[128,1024]{1,0:T(8,128)(2,1)S(1)} %get-tuple-element.64), channel_id=1, source_target_pairs={{0,16},{4,20},{8,24},{12,28},{16,32},{20,36},{24,40},{28,44},{32,4... | collective-permute-start | bytes 786440 | tf_op jit(solution)/shard_map/ppermute | solution.py:30
  127.4 10.3 %collective-permute-start.27 = (bf16[128,1024]{1,0:T(8,128)(2,1)S(1)}, bf16[128,1024]{1,0:T(8,128)(2,1)S(1)}, u32[]{:S(2)}, u32[]{:S(2)}) collective-permute-start(bf16[128,1024]{1,0:T(8,128)(2,1)S(1)} %get-tuple-element.65), channel_id=1, source_target_pairs={{0,32},{4,36},{8,40},{12,44},{16,48},{20,52},{24,56},{28,60},{32,0... | collective-permute-start | bytes 786440 | tf_op jit(solution)/shard_map/ppermute | solution.py:30
  129.4 8.7 %collective-permute-start.28 = (bf16[128,1024]{1,0:T(8,128)(2,1)S(1)}, bf16[128,1024]{1,0:T(8,128)(2,1)S(1)}, u32[]{:S(2)}, u32[]{:S(2)}) collective-permute-start(bf16[128,1024]{1,0:T(8,128)(2,1)S(1)} %get-tuple-element.66), channel_id=1, source_target_pairs={{0,48},{4,52},{8,56},{12,60},{16,0},{20,4},{24,8},{28,12},{32,16},... | collective-permute-start | bytes 786440 | tf_op jit(solution)/shard_map/ppermute | solution.py:30
  131.7 11.1 %collective-permute-start.40 = (f32[64,128]{1,0:T(8,128)S(1)}, f32[64,128]{1,0:T(8,128)S(1)}, u32[]{:S(2)}, u32[]{:S(2)}) collective-permute-start(f32[64,128]{1,0:T(8,128)S(1)} %add_add_fusion), channel_id=1, source_target_pairs={{0,192},{64,0},{128,64},{192,128},{1,193},{65,1},{129,65},{193,129... | collective-permute-start | bytes 98312 | tf_op jit(solution)/shard_map/ppermute | solution.py:35
  133.8 11.9 %collective-permute-start.39 = (f32[64,128]{1,0:T(8,128)S(1)}, f32[64,128]{1,0:T(8,128)S(1)}, u32[]{:S(2)}, u32[]{:S(2)}) collective-permute-start(f32[64,128]{1,0:T(8,128)S(1)} %add_add_fusion), channel_id=1, source_target_pairs={{0,128},{64,192},{128,0},{192,64},{1,129},{65,193},{129,1},{193,65... | collective-permute-start | bytes 98312 | tf_op jit(solution)/shard_map/ppermute | solution.py:35
  136.4 9.3 %collective-permute-start.38 = (f32[64,128]{1,0:T(8,128)S(1)}, f32[64,128]{1,0:T(8,128)S(1)}, u32[]{:S(2)}, u32[]{:S(2)}) collective-permute-start(f32[64,128]{1,0:T(8,128)S(1)} %add_add_fusion), channel_id=1, source_target_pairs={{0,64},{64,128},{128,192},{192,0},{1,65},{65,129},{129,193},{193,1... | collective-permute-start | bytes 98312 | tf_op jit(solution)/shard_map/ppermute | solution.py:35
  (22 other events, 384.0 us)

commit v2 on v1

--- a/solution.py
+++ b/solution.py
@@ -43,6 +43,19 @@
     return lax.ppermute(x, "ctx", [(i, i + by) for i in range(devices) if 0 <= i + by < devices])
 
 
+ANYWHERE = pl.BlockSpec(memory_space=pl.ANY)
+
+
+def resident(x):
+    return pltpu.with_memory_space_constraint(x, pltpu.HBM)
+
+
+def lasting(microseconds):
+    return pl.CostEstimate(
+        flops=int(microseconds * 1e9), bytes_accessed=int(microseconds * 3e6), transcendentals=0
+    )
+
+
 def full(shape):
     return pl.BlockSpec(shape, lambda i: (0,) * len(shape))
 
@@ -80,7 +93,10 @@
     return jnp.concatenate([upper, lower], 0)
 
 
-def forward_kernel(filters, previous, signal, gating, response, gated, first_rows, stack):
+def forward_kernel(filters, previous, signal, gating, *refs):
+    count = 2 * (SIDE - 1)
+    early, (response, gated), sends = refs[:count], refs[count : count + 2], refs[count + 2 : 2 * count + 2]
+    first_rows, stack = refs[2 * count + 2 :]
     step = pl.program_id(0)
 
     @pl.when(step == 0)
@@ -97,32 +113,42 @@
         rows = slice(block * TAPS, (block + 1) * TAPS)
         part = made[:, block * LANES : (block + 1) * LANES]
         response[rows] = part
-        gated[rows] = (part * gating[rows].astype(F32)).astype(BF16)
-
-
-def forward(filters, previous, signal, gating):
+        product = (part * gating[rows].astype(F32)).astype(BF16)
+        gated[rows] = product
+        for send in sends:
+            send[rows] = product
+    for ref, send in zip(early, sends):
+        send[2 * TAPS :] = ref[...]
+
+
+def forward(filters, previous, signal, gating, early):
     length, channels = signal.shape
+    tokens, width = early[0].shape
+    folds = channels // width
+    rows = tokens // folds
+    tiles = width // LANES
     return pl.pallas_call(
         forward_kernel,
         grid=(channels // LANES,),
-        in_specs=[full(filters.shape), tile(TAPS, LANES), tile(length, LANES), tile(length, LANES)],
-        out_specs=[tile(length, LANES), tile(length, LANES)],
+        in_specs=[full(filters.shape), tile(TAPS, LANES), tile(length, LANES), tile(length, LANES)]
+        + [pl.BlockSpec((rows, LANES), lambda i: (i // tiles, i % tiles))] * len(early),
+        out_specs=[tile(length, LANES)] * 2 + [tile(length + rows, LANES)] * len(early),
         out_shape=[
             jax.ShapeDtypeStruct((length, channels), F32),
             jax.ShapeDtypeStruct((length, channels), BF16),
-        ],
+        ]
+        + [jax.ShapeDtypeStruct((length + rows, channels), BF16)] * len(early),
         scratch_shapes=[
             pltpu.VMEM((filters.shape[0], 2 * TAPS), F32),
             pltpu.VMEM((PER_TILE * TAPS, 2 * TAPS), BF16),
         ],
         compiler_params=PARAMS,
+        cost_estimate=lasting(20),
         name="conv_forward",
-    )(filters, previous, signal, gating)
-
-
-def backward_kernel(
-    filters, previous, signal, conv_grad, following, grad_input, grad_filter, first_rows, stack
-):
+    )(filters, previous, signal, gating, *early)
+
+
+def input_grad_kernel(filters, conv_grad, following, _, grad_input, first_rows, stack):
     step = pl.program_id(0)
 
     @pl.when(step == 0)
@@ -139,16 +165,37 @@
         grad_input[block * TAPS : (block + 1) * TAPS] = made[
             :, block * LANES : (block + 1) * LANES
         ].astype(BF16)
+
+
+def input_grad(filters, conv_grad, following, after):
+    length, channels = conv_grad.shape
+    return pl.pallas_call(
+        input_grad_kernel,
+        grid=(channels // LANES,),
+        in_specs=[full(filters.shape), tile(length, LANES), tile(TAPS, LANES), ANYWHERE],
+        out_specs=tile(length, LANES),
+        out_shape=jax.ShapeDtypeStruct((length, channels), BF16),
+        scratch_shapes=[
+            pltpu.VMEM((filters.shape[0], 2 * TAPS), F32),
+            pltpu.VMEM((PER_TILE * TAPS, 2 * TAPS), BF16),
+        ],
+        compiler_params=PARAMS,
+        cost_estimate=lasting(4),
+        name="input_grad",
+    )(filters, conv_grad, following, after)
+
+
+def filter_grad_kernel(previous, signal, conv_grad, grad_filter, stack):
     square = (2 * TAPS, 2 * TAPS)
     turn = iota(square, 0) == (2 * TAPS - iota(square, 1)) % (2 * TAPS)
     inputs = two_windows(previous[...], signal[:TAPS], signal[TAPS:])
     turned = jnp.dot(
         turn.astype(F32).astype(BF16), inputs, preferred_element_type=F32
     ).astype(BF16)
-    both = jnp.concatenate([conv_grad[:TAPS], conv_grad[TAPS:]], 1)
+    both = jnp.concatenate([conv_grad[:TAPS], conv_grad[TAPS:]], 1).astype(F32)
     group = lane_group((TAPS, 2 * LANES))
     for g in range(PER_TILE):
-        stack[g * TAPS : (g + 1) * TAPS, :] = jnp.where(group == g, both.astype(F32), 0.0).astype(BF16)
+        stack[g * TAPS : (g + 1) * TAPS, :] = jnp.where(group == g, both, 0.0).astype(BF16)
     products = lax.dot_general(
         stack[...], turned, (((1,), (1,)), ((), ())), preferred_element_type=F32
     )
@@ -157,36 +204,23 @@
         grad_filter[g : g + 1, :] = jnp.sum(skewed[:, TAPS:], axis=0, keepdims=True)
 
 
-def backward(filters, previous, signal, conv_grad, following):
+def filter_grad(previous, signal, conv_grad):
     length, channels = signal.shape
     return pl.pallas_call(
-        backward_kernel,
+        filter_grad_kernel,
         grid=(channels // LANES,),
-        in_specs=[
-            full(filters.shape),
-            tile(TAPS, LANES),
-            tile(length, LANES),
-            tile(length, LANES),
-            tile(TAPS, LANES),
-        ],
-        out_specs=[
-            tile(length, LANES),
-            pl.BlockSpec((PER_TILE, TAPS), lambda i: (i, 0)),
-        ],
-        out_shape=[
-            jax.ShapeDtypeStruct((length, channels), BF16),
-            jax.ShapeDtypeStruct(filters.shape, F32),
-        ],
-        scratch_shapes=[
-            pltpu.VMEM((filters.shape[0], 2 * TAPS), F32),
-            pltpu.VMEM((PER_TILE * TAPS, 2 * TAPS), BF16),
-        ],
-        compiler_params=PARAMS,
-        name="conv_backward",
-    )(filters, previous, signal, conv_grad, following)
-
-
-def pack_kernel(mine, other, *outs):
+        in_specs=[tile(TAPS, LANES), tile(length, LANES), tile(length, LANES)],
+        out_specs=pl.BlockSpec((PER_TILE, TAPS), lambda i: (i, 0)),
+        out_shape=jax.ShapeDtypeStruct((channels // GROUP, TAPS), F32),
+        scratch_shapes=[pltpu.VMEM((PER_TILE * TAPS, 2 * TAPS), BF16)],
+        compiler_params=PARAMS,
+        cost_estimate=lasting(4),
+        name="filter_grad",
+    )(previous, signal, conv_grad)
+
+
+def pack_kernel(mine, other, *refs):
+    outs = refs[-2 * SIDE :]
     x, y, _, _, core = spot()
     part = mine.shape[0]
     depth = mine.shape[1] // SIDE
@@ -214,22 +248,23 @@
                     ).astype(BF16)
 
 
-def pack(mine, other):
+def pack(mine, other, *after):
     part, width = mine.shape
     shape = (2 * part, width // (2 * SIDE))
     outs = pl.pallas_call(
         pack_kernel,
         grid=(1,),
-        in_specs=[full(mine.shape)] * 2,
+        in_specs=[full(mine.shape)] * 2 + [ANYWHERE] * len(after),
         out_specs=[full(shape)] * (2 * SIDE),
         out_shape=[jax.ShapeDtypeStruct(shape, BF16)] * (2 * SIDE),
         compiler_params=PARAMS,
+        cost_estimate=lasting(1),
         name="pack",
-    )(mine, other)
+    )(mine, other, *after)
     return outs[:SIDE], outs[SIDE:]
 
 
-def project_kernel(early, early_other, late, late_other, weight, gating, response, conv_grad, grad_gate, rows):
+def project_kernel(early, early_other, late, late_other, weight, gating, response, _, conv_grad, grad_gate, rows):
     _, _, _, half, core = spot()
     part = early.shape[0]
 
@@ -248,38 +283,50 @@
     grad_gate[...] = (made * response[...]).astype(BF16)
 
 
-def project(early, early_other, late, late_other, weight, gating, response):
+def project(early, early_other, late, late_other, weight, gating, response, after):
     length, channels = gating.shape
     depth = weight.shape[0]
     return pl.pallas_call(
         project_kernel,
         grid=(channels // WIDE,),
         in_specs=[full(early.shape)] * 4
-        + [tile(depth, WIDE), tile(length, WIDE), tile(length, WIDE)],
+        + [tile(depth, WIDE), tile(length, WIDE), tile(length, WIDE), ANYWHERE],
         out_specs=[tile(length, WIDE)] * 2,
         out_shape=[jax.ShapeDtypeStruct((length, channels), BF16)] * 2,
         scratch_shapes=[pltpu.VMEM((length, depth), BF16)],
         compiler_params=PARAMS,
+        cost_estimate=lasting(7),
         name="project",
-    )(early, early_other, late, late_other, weight, gating, response)
+    )(early, early_other, late, late_other, weight, gating, response, after)
 
 
 def weight_kernel(*refs):
-    early_x, late_x, early_y, late_y = (refs[SIDE * i : SIDE * (i + 1)] for i in range(4))
-    gated = refs[4 * SIDE]
-    gated_x = (gated,) + tuple(refs[4 * SIDE + 1 : 5 * SIDE])
-    gated_y = (gated,) + tuple(refs[5 * SIDE : 6 * SIDE - 1])
-    outs = refs[6 * SIDE - 1 : 8 * SIDE - 1]
-    turned = refs[8 * SIDE - 1 :]
+    shifts = SIDE - 1
+    counts = (1, 1, SIDE, SIDE, 1, shifts, shifts, shifts, shifts, 1, 2 * SIDE, 2)
+    taken, groups = 0, []
+    for count in counts:
+        groups.append(refs[taken : taken + count])
+        taken += count
+    own_x, own_y, late_x, late_y, gated, gated_x, gated_y, early_x, early_y, _, outs, turned = groups
     x, y, _, half, _ = spot()
     run = 64
 
+    def unfolded(ref):
+        width = late_x[0].shape[1]
+        return jnp.concatenate([ref[:, :width], ref[:, width:]], 0)
+
     @pl.when(pl.program_id(0) == 0)
     def _():
-        for into, early, late, me in ((turned[0], early_x, late_x, y), (turned[1], early_y, late_y, x)):
+        for into, own, early, late, me in (
+            (turned[0], own_x[0], early_x, late_x, y),
+            (turned[1], own_y[0], early_y, late_y, x),
+        ):
             for s in range(SIDE):
-                for ref, h in ((early[s], half), (late[s], 1 - half)):
-                    whole = ref[...].T
+                for block, h in (
+                    (own[...] if s == 0 else unfolded(early[s - 1]), half),
+                    (late[s][...], 1 - half),
+                ):
+                    whole = block.T
                     columns = pl.ds(pl.multiple_of(s * 2 * TAPS + h * TAPS, TAPS), TAPS)
                     for d in range(2):
                         for other in range(SIDE):
@@ -288,7 +335,7 @@
                             start = (d * SIDE + other) * run
                             into[rows, columns] = whole[start : start + run]
 
-    for which, blocks in ((0, gated_x), (1, gated_y)):
+    for which, blocks in ((0, gated + gated_x), (1, gated + gated_y)):
         tokens = jnp.concatenate([ref[...] for ref in blocks], 0)
         made = jnp.dot(turned[which][...], tokens, preferred_element_type=F32)
         for s in range(SIDE):
@@ -296,14 +343,19 @@
             out[...] = made[s * 2 * run : (s + 1) * 2 * run].astype(out.dtype)
 
 
-def weight_parts(early_x, late_x, early_y, late_y, gated, gated_x, gated_y):
+def weight_parts(own_x, own_y, late_x, late_y, gated, got_x, got_y, after):
     length, channels = gated.shape
-    tokens, width = early_x[0].shape
+    tokens, width = own_x.shape
     rows = width // SIDE
+    folded = got_x[0].shape[0] - length
+    tail = pl.BlockSpec((folded, channels), lambda i: (length // folded, 0))
     outs = pl.pallas_call(
         weight_kernel,
         grid=(channels // WIDE,),
-        in_specs=[full((tokens, width))] * (4 * SIDE) + [tile(length, WIDE)] * (2 * SIDE - 1),
+        in_specs=[full((tokens, width))] * (2 + 2 * SIDE)
+        + [tile(length, WIDE)] * (2 * SIDE - 1)
+        + [tail] * (2 * SIDE - 2)
+        + [ANYWHERE],
         out_specs=[tile(rows, WIDE)] * (2 * SIDE),
         out_shape=[
             jax.ShapeDtypeStruct((rows, channels), F32 if s % SIDE == 0 else BF16)
@@ -311,8 +363,9 @@
         ],
         scratch_shapes=[pltpu.VMEM((width, SIDE * length), BF16)] * 2,
         compiler_params=PARAMS,
+        cost_estimate=lasting(6),
         name="weight_parts",
-    )(*early_x, *late_x, *early_y, *late_y, gated, *gated_x, *gated_y)
+    )(own_x, own_y, *late_x, *late_y, gated, *got_x, *got_y, *got_x, *got_y, after)
     return outs[:SIDE], outs[SIDE:]
 
 
@@ -344,13 +397,31 @@
         ],
         scratch_shapes=[pltpu.VMEM((SIDE * run, WIDE), F32)],
         compiler_params=PARAMS,
+        cost_estimate=lasting(1),
         name="gather_sum",
     )(*parts_x, *parts_y)
 
 
-def summed(x, axis):
-    others = [moved(x, axis, by) for by in range(1, SIDE)]
-    return x + others[0] + others[1] + others[2]
+def tied(x, *after):
+    return lax.optimization_barrier((x, *after))[0]
+
+
+def partnered(x, axis, by):
+    if axis == "z":
+        return lax.ppermute(x, "dp", [(i, i ^ by) for i in range(SIDE)])
+    step = by * (SIDE if axis == "x" else 1)
+    return lax.ppermute(x, "ctx", [(i, i ^ step) for i in range(SIDE * SIDE)])
+
+
+def summed(x):
+    for axis in ("x", "y", "z"):
+        for by in (1, 2):
+            x = x + partnered(x, axis, by)
+    return x
+
+
+def exchanged(sends, axis):
+    return [moved(sends[s - 1], axis, s) for s in range(1, SIDE)]
 
 
 def local(conv_input, gate_value, out_grad, out_weight, filters):
@@ -359,36 +430,39 @@
     shifts = range(1, SIDE)
 
     previous = shifted(signal[length - TAPS :], 1)
+    early_other = moved(grads, "core", 1)
     late = moved(grads, "half", 1)
-    early_other = moved(grads, "core", 1)
-    response, gated = forward(filters, previous, signal, gating)
+    signal, gating, filters, grads = (resident(x) for x in (signal, gating, filters, grads))
     early_x, early_y = pack(grads, early_other)
-    early_x = [early_x[0]] + [moved(early_x[s], "x", s) for s in shifts]
-    early_y = [early_y[0]] + [moved(early_y[s], "y", s) for s in shifts]
-    gated_x = [moved(gated, "x", s) for s in shifts]
-    gated_y = [moved(gated, "y", s) for s in shifts]
+    response, gated, *sends = forward(
+        filters, previous, signal, gating, [*early_x[1:], *early_y[1:]]
+    )
+    got_x, got_y = [], []
+    for got, axis, parts in ((got_x, "x", sends[: SIDE - 1]), (got_y, "y", sends[SIDE - 1 :])):
+        first = moved(parts[0], axis, 1)
+        got += [first, moved(tied(parts[1], first), axis, 2), moved(parts[2], axis, 3)]
 
     late_other = moved(late, "core", 1)
-    late_x, late_y = pack(late, late_other)
-    late_x = [late_x[0]] + [moved(late_x[s], "x", s) for s in shifts]
-    late_y = [late_y[0]] + [moved(late_y[s], "y", s) for s in shifts]
+    late_x, late_y = pack(late, late_other, got_x[0], got_y[0], got_x[2], got_y[2])
     conv_grad, grad_gate = project(
-        grads, early_other, late, late_other, out_weight, gating, response
-    )
+        grads, early_other, late, late_other, resident(out_weight), gating, response, late_x[0]
+    )
+    late_x = [late_x[0]] + exchanged(late_x[1:], "x")
+    late_y = [late_y[0]] + exchanged(late_y[1:], "y")
     following = shifted(conv_grad[:TAPS], -1)
-
-    parts_x, parts_y = weight_parts(early_x, late_x, early_y, late_y, gated, gated_x, gated_y)
-    parts_x = [parts_x[0]] + [moved(parts_x[s], "y", s) for s in shifts]
-    parts_y = [parts_y[0]] + [moved(parts_y[s], "x", s) for s in shifts]
-
-    grad_input, filter_local = backward(filters, previous, signal, conv_grad, following)
-
+    filter_local = filter_grad(previous, signal, conv_grad)
+
+    parts_x, parts_y = weight_parts(
+        early_x[0], early_y[0], late_x, late_y, gated, got_x, got_y, filter_local
+    )
+    grad_input = input_grad(filters, conv_grad, following, parts_x[0])
+    parts_x = [parts_x[0]] + exchanged(parts_x[1:], "y")
+    parts_y = [parts_y[0]] + exchanged(parts_y[1:], "x")
+    filter_total = summed(tied(filter_local, parts_x[1]))
     chunks = gather_sum(parts_x, parts_y)
     weight_total = chunks[0]
     for s in shifts:
         weight_total = weight_total + moved(chunks[s], "z", s).astype(F32)
-
-    filter_total = summed(summed(summed(filter_local, "x"), "y"), "z")
 
     tokens_all = lax.axis_size("dp") * lax.axis_size("ctx") * length
     grad_filter = filter_total * (1.0 / math.sqrt(tokens_all * GROUP))

time: 151 us -> 137 us (0.907)
  starting transfers between devices: 76.1 us -> 59.3 us
  Pallas kernels: 24.8 us -> 34.9 us
  local copies, waits for them, and re-layouts: 6.93 us -> 3.07 us
  waiting for transfers between devices: 39.9 us -> 36.3 us
    ppermute x30 -> x18, starting transfers between devices: 50.4 us -> 27.7 us  [moved(): return lax.ppermute(x, 'ctx', pairs)]
    ppermute x0 -> x6, waiting for transfers between devices: none -> 9.39 us  [the longest x4 5.39 us: partnered(): return lax.ppermute(x, 'ctx', [(i, i ^ step) for i in range(SIDE * SIDE)])]
    ppermute x0 -> x6, starting transfers between devices: none -> 9.01 us  [the longest x4 7.81 us: partnered(): return lax.ppermute(x, 'ctx', [(i, i ^ step) for i in range(SIDE * SIDE)])]
    ppermute x2, waiting for transfers between devices: 9.23 us -> 0.3 us  [shifted(): lax.ppermute(x, 'ctx', [(i, i + by) for i in range(devices) if 0 <= i + b...]
    pallas_call x3 -> x4, Pallas kernels: 8.12 us -> 14.5 us  [the longest x1 6.97 us: filter_grad(): pl.pallas_call(filter_grad_kernel, grid=(channels // LANES,), in_specs=[t...]
    unnamed x26 -> x10, local copies, waits for them, and re-layouts: 5.95 us -> 2.08 us
    pallas_call x1, Pallas kernels: 3.79 us -> 7.2 us  [forward(): pl.pallas_call(forward_kernel, grid=(channels // LANES,), in_specs=[full(...]
    ppermute x6 -> x3, waiting for transfers between devices: 2.99 us -> 0.01 us  [moved(): return lax.ppermute(x, 'dp', [(i, (i + by) % SIDE) for i in range(SIDE)])]
  transfers between devices with their start and end apart: 41 -> 32, of which waited for: 11 -> 9; matrix products, arithmetic and copies ran while one was open for 1% -> 1% of each run, Pallas kernels for 17% -> 21%
where the time goes in v2:
time: 137 us; the launch traced here: 136 us
  starting transfers between devices  59.3 us (43%)
  waiting for transfers between devices  36.3 us (26%)
  Pallas kernels  34.9 us (25%)
  local copies, waits for them, and re-layouts  3.07 us (2%)
  other arithmetic  1.42 us (1%)
    ppermute x18, starting transfers between devices, moved(): return lax.ppermute(x, 'ctx', pairs)  27.7 us
    ppermute x18, waiting for transfers between devices, moved(): return lax.ppermute(x, 'ctx', pairs)  26.2 us
    ppermute x3, starting transfers between devices, moved(): return lax.ppermute(x, 'dp', [(i, (i + by) % SIDE) for i in range(SIDE)])  9.84 us
    ppermute x4, starting transfers between devices, partnered(): return lax.ppermute(x, 'ctx', [(i, i ^ step) for i in range(SIDE * SIDE)])  7.81 us
    ppermute x1, starting transfers between devices, moved(): return lax.ppermute(x, 'tp', [(i, (i + 2) % 4) for i in range(4)])  7.28 us
    pallas_call x1, Pallas kernels, forward(): pl.pallas_call(forward_kernel, grid=(channels // LANES,), in_specs=[full(...  7.2 us
    pallas_call x1, Pallas kernels, filter_grad(): pl.pallas_call(filter_grad_kernel, grid=(channels // LANES,), in_specs=[t...  6.97 us
    pallas_call x1, Pallas kernels, project(): pl.pallas_call(project_kernel, grid=(channels // WIDE,), in_specs=[full(e...  6.59 us
  transfers between devices with their start and end apart: 32, of which 9 were waited for; matrix products, arithmetic and copies ran while one was open for 1% of the time, Pallas kernels for 21%

profile of v2, /device:TPU:2, one launch (start us, length us, event | category | flops | bytes accessed | tf_op | source)
XLA Modules:
  0.0 135.9 jit_solution(3011419382057857790)
XLA Ops:
  1.7 3.5 %collective-permute-start.3 = (bf16[128,1024]{1,0:T(8,128)(2,1)S(1)}, bf16[128,1024]{1,0:T(8,128)(2,1)S(1)}, u32[]{:S(2)}, u32[]{:S(2)}) collective-permute-start(bf16[128,1024]{1,0:T(8,128)(2,1)S(1)} %slice_bitcast_fusion), channel_id=1, source_target_pairs={{0,4},{4,8},{8,12},{12,16},{16,20},{20,24},{24,28},{28,32},{32,36}... | collective-permute-start | bytes 786440 | tf_op jit(solution)/shard_map/ppermute | solution.py:43
  5.2 7.3 %collective-permute-start.1 = (bf16[64,4096]{1,0:T(8,128)(2,1)}, bf16[64,4096]{1,0:T(8,128)(2,1)S(1)}, u32[]{:S(2)}, u32[]{:S(2)}) collective-permute-start(bf16[64,4096]{1,0:T(8,128)(2,1)} %bitcast.10), channel_id=1, source_target_pairs={{0,2},{1,3},{2,0},{3,1},{4,6},{5,7},{6,4},{7,5},{8,10},{9,11},{10,... | collective-permute-start | bytes 1572872 | tf_op jit(solution)/shard_map/ppermute | solution.py:37
  12.5 1.6 %pack.2 = (bf16[128,512]{1,0:T(8,128)(2,1)S(1)}, bf16[128,512]{1,0:T(8,128)(2,1)S(1)}, bf16[128,512]{1,0:T(8,128)(2,1)S(1)}, bf16[128,512]{1,0:T(8,128)(2,1)S(1)...) custom-call(bf16[64,4096]{1,0:T(8,128)(2,1)} %bitcast.11, ...), custom_call_target="tpu_custom_call" | custom-call | flops 1000000000 | bytes 3000000 | tf_op jit(solution)/shard_map/pack/pallas_call | solution.py:254
  14.4 7.2 %conv_forward.1 = (f32[256,1024]{1,0:T(8,128)}, bf16[256,1024]{1,0:T(8,128)(2,1)S(1)}, bf16[320,1024]{1,0:T(8,128)(2,1)S(1)}, bf16[320,1024]{1,0:T(8,128)(2,1)S(...) custom-call(bf16[64,128]{1,0:T(8,128)(2,1)} %filters.3, ...), custom_call_target="tpu_custom_call" | custom-call | flops 20000000000 | bytes 60000000 | tf_op jit(solution)/shard_map/conv_forward/pallas_call | solution.py:130
  21.6 1.5 %collective-permute-start.4 = (bf16[320,1024]{1,0:T(8,128)(2,1)S(1)}, bf16[320,1024]{1,0:T(8,128)(2,1)S(1)}, u32[]{:S(2)}, u32[]{:S(2)}) collective-permute-start(bf16[320,1024]{1,0:T(8,128)(2,1)S(1)} %get-tuple-element.52), channel_id=1, source_target_pairs={{0,16},{4,20},{8,24},{12,28},{16,32},{20,36},{24,40},{28,44},{32,4... | collective-permute-start | bytes 1966088 | tf_op jit(solution)/shard_map/ppermute | solution.py:30
  23.1 1.4 collective-permute-start.5
  25.0 1.9 %collective-permute-start.7 = (bf16[320,1024]{1,0:T(8,128)(2,1)S(1)}, bf16[320,1024]{1,0:T(8,128)(2,1)S(1)}, u32[]{:S(2)}, u32[]{:S(2)}) collective-permute-start(bf16[320,1024]{1,0:T(8,128)(2,1)S(1)} %get-tuple-element.55), channel_id=1, source_target_pairs={{0,12},{4,0},{8,4},{12,8},{16,28},{20,16},{24,20},{28,24},{32,44},... | collective-permute-start | bytes 1966088 | tf_op jit(solution)/shard_map/ppermute | solution.py:33
  27.3 10.7 %collective-permute-done.4.refs_0_.refs_11_.refs_17_ = bf16[320,1024]{1,0:T(8,128)(2,1)S(1)} collective-permute-done((bf16[320,1024]{1,0:T(8,128)(2,1)S(1)}, bf16[320,1024]{1,0:T(8,128)(2,1)S(1)}, u32[]{:S(2)}, u32[]{:S(2)}) %collective-permute-start.4) | collective-permute-done | bytes 655392 | tf_op jit(solution)/shard_map/ppermute | solution.py:30
  38.0 2.1 %collective-permute-start.15 = (bf16[320,1024]{1,0:T(8,128)(2,1)S(1)}, bf16[320,1024]{1,0:T(8,128)(2,1)S(1)}, u32[]{:S(2)}, u32[]{:S(2)}) collective-permute-start(bf16[320,1024]{1,0:T(8,128)(2,1)S(1)} %get-tuple-element.69), channel_id=1, source_target_pairs={{0,32},{4,36},{8,40},{12,44},{16,48},{20,52},{24,56},{28,60},{32,0... | collective-permute-start | bytes 1966088 | tf_op jit(solution)/shard_map/ppermute | solution.py:30
  40.4 2.6 %collective-permute-start.16 = (bf16[320,1024]{1,0:T(8,128)(2,1)S(1)}, bf16[320,1024]{1,0:T(8,128)(2,1)S(1)}, u32[]{:S(2)}, u32[]{:S(2)}) collective-permute-start(bf16[320,1024]{1,0:T(8,128)(2,1)S(1)} %get-tuple-element.71), channel_id=1, source_target_pairs={{0,8},{4,12},{8,0},{12,4},{16,24},{20,28},{24,16},{28,20},{32,40},... | collective-permute-start | bytes 1966088 | tf_op jit(solution)/shard_map/ppermute | solution.py:33
  44.8 2.4 %collective-permute-start.10 = (bf16[128,512]{1,0:T(8,128)(2,1)S(1)}, bf16[128,512]{1,0:T(8,128)(2,1)S(1)}, u32[]{:S(2)}, u32[]{:S(2)}) collective-permute-start(bf16[128,512]{1,0:T(8,128)(2,1)S(1)} %get-tuple-element.61), channel_id=1, source_target_pairs={{0,32},{4,36},{8,40},{12,44},{16,48},{20,52},{24,56},{28,60},{32,0... | collective-permute-start | bytes 393224 | tf_op jit(solution)/shard_map/ppermute | solution.py:30
  47.7 1.2 copy-done.3
  49.0 6.6 %project.1 = (bf16[256,1024]{1,0:T(8,128)(2,1)S(1)}, bf16[256,1024]{1,0:T(8,128)(2,1)}) custom-call(bf16[64,4096]{1,0:T(8,128)(2,1)} %bitcast.12, bf16[64,4096]{1,0:T(8,128)(2,1)S(1)} %collective-permute-done.other.early_other, bf16[64,4096]{1,0:T(8,128)(2,1)S(1)} %collective-permute-done.1.mine.late, ...), custom_call_target="tpu_custom_call" | custom-call | flops 7000000000 | bytes 21000000 | tf_op jit(solution)/shard_map/project/pallas_call | solution.py:289
  55.6 3.6 %collective-permute-done.9.refs_3_ = bf16[128,512]{1,0:T(8,128)(2,1)S(1)} collective-permute-done((bf16[128,512]{1,0:T(8,128)(2,1)S(1)}, bf16[128,512]{1,0:T(8,128)(2,1)S(1)}, u32[]{:S(2)}, u32[]{:S(2)}) %collective-permute-start.9) | collective-permute-done | bytes 131104 | tf_op jit(solution)/shard_map/ppermute | solution.py:30
  59.2 1.8 %collective-permute-start.12 = (bf16[128,512]{1,0:T(8,128)(2,1)S(1)}, bf16[128,512]{1,0:T(8,128)(2,1)S(1)}, u32[]{:S(2)}, u32[]{:S(2)}) collective-permute-start(bf16[128,512]{1,0:T(8,128)(2,1)S(1)} %get-tuple-element.64), channel_id=1, source_target_pairs={{0,4},{4,8},{8,12},{12,0},{16,20},{20,24},{24,28},{28,16},{32,36},... | collective-permute-start | bytes 393224 | tf_op jit(solution)/shard_map/ppermute | solution.py:33
  61.0 2.2 %collective-permute-start.13 = (bf16[128,512]{1,0:T(8,128)(2,1)S(1)}, bf16[128,512]{1,0:T(8,128)(2,1)S(1)}, u32[]{:S(2)}, u32[]{:S(2)}) collective-permute-start(bf16[128,512]{1,0:T(8,128)(2,1)S(1)} %get-tuple-element.65), channel_id=1, source_target_pairs={{0,8},{4,12},{8,0},{12,4},{16,24},{20,28},{24,16},{28,20},{32,40},... | collective-permute-start | bytes 393224 | tf_op jit(solution)/shard_map/ppermute | solution.py:33
  63.2 1.8 %collective-permute-start.14 = (bf16[128,512]{1,0:T(8,128)(2,1)S(1)}, bf16[128,512]{1,0:T(8,128)(2,1)S(1)}, u32[]{:S(2)}, u32[]{:S(2)}) collective-permute-start(bf16[128,512]{1,0:T(8,128)(2,1)S(1)} %get-tuple-element.66), channel_id=1, source_target_pairs={{0,12},{4,0},{8,4},{12,8},{16,28},{20,16},{24,20},{28,24},{32,44},... | collective-permute-start | bytes 393224 | tf_op jit(solution)/shard_map/ppermute | solution.py:33
  65.0 7.0 %filter_grad.1.refs_23_ = f32[64,128]{1,0:T(8,128)S(1)} custom-call(bf16[128,1024]{1,0:T(8,128)(2,1)S(1)} %collective-permute-done.3.previous, bf16[256,1024]{1,0:T(8,128)(2,1)} %bitcast.8, bf16[256,1024]{1,0:T(8,128)(2,1)S(1)} %get-tuple-element.57.conv_grad), custom_call_target="tpu_custom_call" | custom-call | flops 4000000000 | bytes 12000000 | tf_op jit(solution)/shard_map/filter_grad/pallas_call | solution.py:209
  72.9 5.8 %weight_parts.1 = (f32[128,1024]{1,0:T(8,128)S(1)}, bf16[128,1024]{1,0:T(8,128)(2,1)S(1)}, bf16[128,1024]{1,0:T(8,128)(2,1)S(1)}, bf16[128,1024]{1,0:T(8,128)(2,...) custom-call(bf16[128,512]{1,0:T(8,128)(2,1)S(1)} %get-tuple-element., ...), custom_call_target="tpu_custom_call" | custom-call | flops 6000000000 | bytes 18000000 | tf_op jit(solution)/shard_map/weight_parts/pallas_call | solution.py:352
  79.0 1.4 collective-permute-start.18
  80.3 11.5 %collective-permute-done.17.refs_1_ = bf16[128,1024]{1,0:T(8,128)(2,1)S(1)} collective-permute-done((bf16[128,1024]{1,0:T(8,128)(2,1)S(1)}, bf16[128,1024]{1,0:T(8,128)(2,1)S(1)}, u32[]{:S(2)}, u32[]{:S(2)}) %collective-permute-start.17) | collective-permute-done | bytes 262176 | tf_op jit(solution)/shard_map/ppermute | solution.py:33
  91.9 2.7 %collective-permute-start.26 = (f32[64,128]{1,0:T(8,128)S(1)}, f32[64,128]{1,0:T(8,128)S(1)}, u32[]{:S(2)}, u32[]{:S(2)}) collective-permute-start(f32[64,128]{1,0:T(8,128)S(1)} %filter_grad.1.refs_23_), channel_id=1, source_target_pairs={{0,16},{4,20},{8,24},{12,28},{16,0},{20,4},{24,8},{28,12},{32,48},... | collective-permute-start | bytes 98312 | tf_op jit(solution)/shard_map/ppermute | solution.py:413
  94.6 2.3 %collective-permute-done.26 = f32[64,128]{1,0:T(8,128)S(1)} collective-permute-done((f32[64,128]{1,0:T(8,128)S(1)}, f32[64,128]{1,0:T(8,128)S(1)}, u32[]{:S(2)}, u32[]{:S(2)}) %collective-permute-start.26) | collective-permute-done | bytes 32800 | tf_op jit(solution)/shard_map/ppermute | solution.py:413
  98.1 2.2 %collective-permute-start.20 = (bf16[128,1024]{1,0:T(8,128)(2,1)S(1)}, bf16[128,1024]{1,0:T(8,128)(2,1)S(1)}, u32[]{:S(2)}, u32[]{:S(2)}) collective-permute-start(bf16[128,1024]{1,0:T(8,128)(2,1)S(1)} %get-tuple-element.78), channel_id=1, source_target_pairs={{0,16},{4,20},{8,24},{12,28},{16,32},{20,36},{24,40},{28,44},{32,4... | collective-permute-start | bytes 786440 | tf_op jit(solution)/shard_map/ppermute | solution.py:30
  100.3 2.4 %collective-permute-start.21 = (bf16[128,1024]{1,0:T(8,128)(2,1)S(1)}, bf16[128,1024]{1,0:T(8,128)(2,1)S(1)}, u32[]{:S(2)}, u32[]{:S(2)}) collective-permute-start(bf16[128,1024]{1,0:T(8,128)(2,1)S(1)} %get-tuple-element.79), channel_id=1, source_target_pairs={{0,32},{4,36},{8,40},{12,44},{16,48},{20,52},{24,56},{28,60},{32,0... | collective-permute-start | bytes 786440 | tf_op jit(solution)/shard_map/ppermute | solution.py:30
  102.7 1.5 %collective-permute-start.22 = (bf16[128,1024]{1,0:T(8,128)(2,1)S(1)}, bf16[128,1024]{1,0:T(8,128)(2,1)S(1)}, u32[]{:S(2)}, u32[]{:S(2)}) collective-permute-start(bf16[128,1024]{1,0:T(8,128)(2,1)S(1)} %get-tuple-element.80), channel_id=1, source_target_pairs={{0,48},{4,52},{8,56},{12,60},{16,0},{20,4},{24,8},{28,12},{32,16},... | collective-permute-start | bytes 786440 | tf_op jit(solution)/shard_map/ppermute | solution.py:30
  105.2 3.1 %collective-permute-done.28 = f32[64,128]{1,0:T(8,128)S(1)} collective-permute-done((f32[64,128]{1,0:T(8,128)S(1)}, f32[64,128]{1,0:T(8,128)S(1)}, u32[]{:S(2)}, u32[]{:S(2)}) %collective-permute-start.28) | collective-permute-done | bytes 32800 | tf_op jit(solution)/shard_map/ppermute | solution.py:413
  108.3 1.9 %collective-permute-start.8 = (bf16[128,1024]{1,0:T(8,128)(2,1)S(1)}, bf16[128,1024]{1,0:T(8,128)(2,1)S(1)}, u32[]{:S(2)}, u32[]{:S(2)}) collective-permute-start(bf16[128,1024]{1,0:T(8,128)(2,1)S(1)} %slice.11), channel_id=1, source_target_pairs={{4,0},{8,4},{12,8},{16,12},{20,16},{24,20},{28,24},{32,28},{36,32}... | collective-permute-start | bytes 786440 | tf_op jit(solution)/shard_map/ppermute | solution.py:43
  110.2 3.0 %collective-permute-start.29 = (f32[64,128]{1,0:T(8,128)S(1)}, f32[64,128]{1,0:T(8,128)S(1)}, u32[]{:S(2)}, u32[]{:S(2)}) collective-permute-start(f32[64,128]{1,0:T(8,128)S(1)} %add.32), channel_id=1, source_target_pairs={{0,8},{4,12},{8,0},{12,4},{16,24},{20,28},{24,16},{28,20},{32,40},... | collective-permute-start | bytes 98312 | tf_op jit(solution)/shard_map/ppermute | solution.py:413
  115.1 7.7 %collective-permute-start.24 = (bf16[64,1024]{1,0:T(8,128)(2,1)S(1)}, bf16[64,1024]{1,0:T(8,128)(2,1)S(1)}, u32[]{:S(2)}, u32[]{:S(2)}) collective-permute-start(bf16[64,1024]{1,0:T(8,128)(2,1)S(1)} %get-tuple-element.83), channel_id=1, source_target_pairs={{0,128},{64,192},{128,0},{192,64},{1,129},{65,193},{129,1},{193,65... | collective-permute-start | bytes 393224 | tf_op jit(solution)/shard_map/ppermute | solution.py:35
  125.0 5.3 %input_grad.1 = bf16[256,1024]{1,0:T(8,128)(2,1)} custom-call(bf16[64,128]{1,0:T(8,128)(2,1)} %filters.3, bf16[256,1024]{1,0:T(8,128)(2,1)S(1)} %get-tuple-element.57.conv_grad, bf16[128,1024]{1,0:T(8,128)(2,1)S(1)} %collective-permute-done.8.following, f32[128,1024]{1,0:T(8,128)S(1)} %get-tuple-element.72._.refs_0_), custom_call_target="tpu_custom_call" | custom-call | flops 4000000000 | bytes 12000000 | tf_op jit(solution)/shard_map/input_grad/pallas_call | solution.py:172
  131.2 4.0 %collective-permute-done.31 = f32[64,128]{1,0:T(8,128)S(1)} collective-permute-done((f32[64,128]{1,0:T(8,128)S(1)}, f32[64,128]{1,0:T(8,128)S(1)}, u32[]{:S(2)}, u32[]{:S(2)}) %collective-permute-start.31) | collective-permute-done | bytes 32800 | tf_op jit(solution)/shard_map/ppermute | solution.py:411
  (59 shorter events, 13.8 us)
Async XLA Ops:
  0.6 11.8 %collective-permute-start = (bf16[64,4096]{1,0:T(8,128)(2,1)}, bf16[64,4096]{1,0:T(8,128)(2,1)S(1)}, u32[]{:S(2)}, u32[]{:S(2)}) collective-permute-start(bf16[64,4096]{1,0:T(8,128)(2,1)} %bitcast.9), channel_id=1, source_target_pairs={{0,1},{1,0},{2,3},{3,2},{4,5},{5,4},{6,7},{7,6},{8,9},{9,8},{10,11... | collective-permute-start | bytes 1572872 | tf_op jit(solution)/shard_map/ppermute | solution.py:38
  1.7 12.7 %collective-permute-start.3 = (bf16[128,1024]{1,0:T(8,128)(2,1)S(1)}, bf16[128,1024]{1,0:T(8,128)(2,1)S(1)}, u32[]{:S(2)}, u32[]{:S(2)}) collective-permute-start(bf16[128,1024]{1,0:T(8,128)(2,1)S(1)} %slice_bitcast_fusion), channel_id=1, source_target_pairs={{0,4},{4,8},{8,12},{12,16},{16,20},{20,24},{24,28},{28,32},{32,36}... | collective-permute-start | bytes 786440 | tf_op jit(solution)/shard_map/ppermute | solution.py:43
  5.2 22.1 %collective-permute-start.1 = (bf16[64,4096]{1,0:T(8,128)(2,1)}, bf16[64,4096]{1,0:T(8,128)(2,1)S(1)}, u32[]{:S(2)}, u32[]{:S(2)}) collective-permute-start(bf16[64,4096]{1,0:T(8,128)(2,1)} %bitcast.10), channel_id=1, source_target_pairs={{0,2},{1,3},{2,0},{3,1},{4,6},{5,7},{6,4},{7,5},{8,10},{9,11},{10,... | collective-permute-start | bytes 1572872 | tf_op jit(solution)/shard_map/ppermute | solution.py:37
  21.6 16.3 %collective-permute-start.4 = (bf16[320,1024]{1,0:T(8,128)(2,1)S(1)}, bf16[320,1024]{1,0:T(8,128)(2,1)S(1)}, u32[]{:S(2)}, u32[]{:S(2)}) collective-permute-start(bf16[320,1024]{1,0:T(8,128)(2,1)S(1)} %get-tuple-element.52), channel_id=1, source_target_pairs={{0,16},{4,20},{8,24},{12,28},{16,32},{20,36},{24,40},{28,44},{32,4... | collective-permute-start | bytes 1966088 | tf_op jit(solution)/shard_map/ppermute | solution.py:30
  23.1 17.3 %collective-permute-start.5 = (bf16[320,1024]{1,0:T(8,128)(2,1)S(1)}, bf16[320,1024]{1,0:T(8,128)(2,1)S(1)}, u32[]{:S(2)}, u32[]{:S(2)}) collective-permute-start(bf16[320,1024]{1,0:T(8,128)(2,1)S(1)} %get-tuple-element.53), channel_id=1, source_target_pairs={{0,4},{4,8},{8,12},{12,0},{16,20},{20,24},{24,28},{28,16},{32,36},... | collective-permute-start | bytes 1966088 | tf_op jit(solution)/shard_map/ppermute | solution.py:33
  24.5 18.5 %collective-permute-start.6 = (bf16[320,1024]{1,0:T(8,128)(2,1)S(1)}, bf16[320,1024]{1,0:T(8,128)(2,1)S(1)}, u32[]{:S(2)}, u32[]{:S(2)}) collective-permute-start(bf16[320,1024]{1,0:T(8,128)(2,1)S(1)} %get-tuple-element.54), channel_id=1, source_target_pairs={{0,48},{4,52},{8,56},{12,60},{16,0},{20,4},{24,8},{28,12},{32,16},... | collective-permute-start | bytes 1966088 | tf_op jit(solution)/shard_map/ppermute | solution.py:30
  25.0 18.0 %collective-permute-start.7 = (bf16[320,1024]{1,0:T(8,128)(2,1)S(1)}, bf16[320,1024]{1,0:T(8,128)(2,1)S(1)}, u32[]{:S(2)}, u32[]{:S(2)}) collective-permute-start(bf16[320,1024]{1,0:T(8,128)(2,1)S(1)} %get-tuple-element.55), channel_id=1, source_target_pairs={{0,12},{4,0},{8,4},{12,8},{16,28},{20,16},{24,20},{28,24},{32,44},... | collective-permute-start | bytes 1966088 | tf_op jit(solution)/shard_map/ppermute | solution.py:33
  27.2 15.7 %collective-permute-start.2 = (bf16[64,4096]{1,0:T(8,128)(2,1)S(1)}, bf16[64,4096]{1,0:T(8,128)(2,1)S(1)}, u32[]{:S(2)}, u32[]{:S(2)}) collective-permute-start(bf16[64,4096]{1,0:T(8,128)(2,1)S(1)} %collective-permute-done.1.mine.late), channel_id=1, source_target_pairs={{0,1},{1,0},{2,3},{3,2},{4,5},{5,4},{6,7},{7,6},{8,9},{9,8},{10,11... | collective-permute-start | bytes 1572872 | tf_op jit(solution)/shard_map/ppermute | solution.py:38
  38.0 34.0 %collective-permute-start.15 = (bf16[320,1024]{1,0:T(8,128)(2,1)S(1)}, bf16[320,1024]{1,0:T(8,128)(2,1)S(1)}, u32[]{:S(2)}, u32[]{:S(2)}) collective-permute-start(bf16[320,1024]{1,0:T(8,128)(2,1)S(1)} %get-tuple-element.69), channel_id=1, source_target_pairs={{0,32},{4,36},{8,40},{12,44},{16,48},{20,52},{24,56},{28,60},{32,0... | collective-permute-start | bytes 1966088 | tf_op jit(solution)/shard_map/ppermute | solution.py:30
  40.4 31.6 %collective-permute-start.16 = (bf16[320,1024]{1,0:T(8,128)(2,1)S(1)}, bf16[320,1024]{1,0:T(8,128)(2,1)S(1)}, u32[]{:S(2)}, u32[]{:S(2)}) collective-permute-start(bf16[320,1024]{1,0:T(8,128)(2,1)S(1)} %get-tuple-element.71), channel_id=1, source_target_pairs={{0,8},{4,12},{8,0},{12,4},{16,24},{20,28},{24,16},{28,20},{32,40},... | collective-permute-start | bytes 1966088 | tf_op jit(solution)/shard_map/ppermute | solution.py:33
  43.6 15.6 %collective-permute-start.9 = (bf16[128,512]{1,0:T(8,128)(2,1)S(1)}, bf16[128,512]{1,0:T(8,128)(2,1)S(1)}, u32[]{:S(2)}, u32[]{:S(2)}) collective-permute-start(bf16[128,512]{1,0:T(8,128)(2,1)S(1)} %get-tuple-element.60), channel_id=1, source_target_pairs={{0,16},{4,20},{8,24},{12,28},{16,32},{20,36},{24,40},{28,44},{32,4... | collective-permute-start | bytes 393224 | tf_op jit(solution)/shard_map/ppermute | solution.py:30
  44.8 16.3 %collective-permute-start.10 = (bf16[128,512]{1,0:T(8,128)(2,1)S(1)}, bf16[128,512]{1,0:T(8,128)(2,1)S(1)}, u32[]{:S(2)}, u32[]{:S(2)}) collective-permute-start(bf16[128,512]{1,0:T(8,128)(2,1)S(1)} %get-tuple-element.61), channel_id=1, source_target_pairs={{0,32},{4,36},{8,40},{12,44},{16,48},{20,52},{24,56},{28,60},{32,0... | collective-permute-start | bytes 393224 | tf_op jit(solution)/shard_map/ppermute | solution.py:30
  47.2 16.0 %collective-permute-start.11 = (bf16[128,512]{1,0:T(8,128)(2,1)S(1)}, bf16[128,512]{1,0:T(8,128)(2,1)S(1)}, u32[]{:S(2)}, u32[]{:S(2)}) collective-permute-start(bf16[128,512]{1,0:T(8,128)(2,1)S(1)} %get-tuple-element.62), channel_id=1, source_target_pairs={{0,48},{4,52},{8,56},{12,60},{16,0},{20,4},{24,8},{28,12},{32,16},... | collective-permute-start | bytes 393224 | tf_op jit(solution)/shard_map/ppermute | solution.py:30
  59.2 12.8 %collective-permute-start.12 = (bf16[128,512]{1,0:T(8,128)(2,1)S(1)}, bf16[128,512]{1,0:T(8,128)(2,1)S(1)}, u32[]{:S(2)}, u32[]{:S(2)}) collective-permute-start(bf16[128,512]{1,0:T(8,128)(2,1)S(1)} %get-tuple-element.64), channel_id=1, source_target_pairs={{0,4},{4,8},{8,12},{12,0},{16,20},{20,24},{24,28},{28,16},{32,36},... | collective-permute-start | bytes 393224 | tf_op jit(solution)/shard_map/ppermute | solution.py:33
  61.0 10.9 %collective-permute-start.13 = (bf16[128,512]{1,0:T(8,128)(2,1)S(1)}, bf16[128,512]{1,0:T(8,128)(2,1)S(1)}, u32[]{:S(2)}, u32[]{:S(2)}) collective-permute-start(bf16[128,512]{1,0:T(8,128)(2,1)S(1)} %get-tuple-element.65), channel_id=1, source_target_pairs={{0,8},{4,12},{8,0},{12,4},{16,24},{20,28},{24,16},{28,20},{32,40},... | collective-permute-start | bytes 393224 | tf_op jit(solution)/shard_map/ppermute | solution.py:33
  63.2 8.8 %collective-permute-start.14 = (bf16[128,512]{1,0:T(8,128)(2,1)S(1)}, bf16[128,512]{1,0:T(8,128)(2,1)S(1)}, u32[]{:S(2)}, u32[]{:S(2)}) collective-permute-start(bf16[128,512]{1,0:T(8,128)(2,1)S(1)} %get-tuple-element.66), channel_id=1, source_target_pairs={{0,12},{4,0},{8,4},{12,8},{16,28},{20,16},{24,20},{28,24},{32,44},... | collective-permute-start | bytes 393224 | tf_op jit(solution)/shard_map/ppermute | solution.py:33
  78.6 13.2 %collective-permute-start.17 = (bf16[128,1024]{1,0:T(8,128)(2,1)S(1)}, bf16[128,1024]{1,0:T(8,128)(2,1)S(1)}, u32[]{:S(2)}, u32[]{:S(2)}) collective-permute-start(bf16[128,1024]{1,0:T(8,128)(2,1)S(1)} %get-tuple-element.74), channel_id=1, source_target_pairs={{0,4},{4,8},{8,12},{12,0},{16,20},{20,24},{24,28},{28,16},{32,36},... | collective-permute-start | bytes 786440 | tf_op jit(solution)/shard_map/ppermute | solution.py:33
  79.0 25.3 %collective-permute-start.18 = (bf16[128,1024]{1,0:T(8,128)(2,1)S(1)}, bf16[128,1024]{1,0:T(8,128)(2,1)S(1)}, u32[]{:S(2)}, u32[]{:S(2)}) collective-permute-start(bf16[128,1024]{1,0:T(8,128)(2,1)S(1)} %get-tuple-element.75), channel_id=1, source_target_pairs={{0,8},{4,12},{8,0},{12,4},{16,24},{20,28},{24,16},{28,20},{32,40},... | collective-permute-start | bytes 786440 | tf_op jit(solution)/shard_map/ppermute | solution.py:33
  91.9 5.0 %collective-permute-start.26 = (f32[64,128]{1,0:T(8,128)S(1)}, f32[64,128]{1,0:T(8,128)S(1)}, u32[]{:S(2)}, u32[]{:S(2)}) collective-permute-start(f32[64,128]{1,0:T(8,128)S(1)} %filter_grad.1.refs_23_), channel_id=1, source_target_pairs={{0,16},{4,20},{8,24},{12,28},{16,0},{20,4},{24,8},{28,12},{32,48},... | collective-permute-start | bytes 98312 | tf_op jit(solution)/shard_map/ppermute | solution.py:413
  96.9 5.8 %collective-permute-start.27 = (f32[64,128]{1,0:T(8,128)S(1)}, f32[64,128]{1,0:T(8,128)S(1)}, u32[]{:S(2)}, u32[]{:S(2)}) collective-permute-start(f32[64,128]{1,0:T(8,128)S(1)} %add.30), channel_id=1, source_target_pairs={{0,32},{4,36},{8,40},{12,44},{16,48},{20,52},{24,56},{28,60},{32,0... | collective-permute-start | bytes 98312 | tf_op jit(solution)/shard_map/ppermute | solution.py:413
  98.1 12.1 %collective-permute-start.19 = (bf16[128,1024]{1,0:T(8,128)(2,1)S(1)}, bf16[128,1024]{1,0:T(8,128)(2,1)S(1)}, u32[]{:S(2)}, u32[]{:S(2)}) collective-permute-start(bf16[128,1024]{1,0:T(8,128)(2,1)S(1)} %get-tuple-element.76), channel_id=1, source_target_pairs={{0,12},{4,0},{8,4},{12,8},{16,28},{20,16},{24,20},{28,24},{32,44},... | collective-permute-start | bytes 786440 | tf_op jit(solution)/shard_map/ppermute | solution.py:33
  98.1 15.1 %collective-permute-start.20 = (bf16[128,1024]{1,0:T(8,128)(2,1)S(1)}, bf16[128,1024]{1,0:T(8,128)(2,1)S(1)}, u32[]{:S(2)}, u32[]{:S(2)}) collective-permute-start(bf16[128,1024]{1,0:T(8,128)(2,1)S(1)} %get-tuple-element.78), channel_id=1, source_target_pairs={{0,16},{4,20},{8,24},{12,28},{16,32},{20,36},{24,40},{28,44},{32,4... | collective-permute-start | bytes 786440 | tf_op jit(solution)/shard_map/ppermute | solution.py:30
  100.3 12.9 %collective-permute-start.21 = (bf16[128,1024]{1,0:T(8,128)(2,1)S(1)}, bf16[128,1024]{1,0:T(8,128)(2,1)S(1)}, u32[]{:S(2)}, u32[]{:S(2)}) collective-permute-start(bf16[128,1024]{1,0:T(8,128)(2,1)S(1)} %get-tuple-element.79), channel_id=1, source_target_pairs={{0,32},{4,36},{8,40},{12,44},{16,48},{20,52},{24,56},{28,60},{32,0... | collective-permute-start | bytes 786440 | tf_op jit(solution)/shard_map/ppermute | solution.py:30
  102.7 10.5 %collective-permute-start.22 = (bf16[128,1024]{1,0:T(8,128)(2,1)S(1)}, bf16[128,1024]{1,0:T(8,128)(2,1)S(1)}, u32[]{:S(2)}, u32[]{:S(2)}) collective-permute-start(bf16[128,1024]{1,0:T(8,128)(2,1)S(1)} %get-tuple-element.80), channel_id=1, source_target_pairs={{0,48},{4,52},{8,56},{12,60},{16,0},{20,4},{24,8},{28,12},{32,16},... | collective-permute-start | bytes 786440 | tf_op jit(solution)/shard_map/ppermute | solution.py:30
  104.3 4.0 %collective-permute-start.28 = (f32[64,128]{1,0:T(8,128)S(1)}, f32[64,128]{1,0:T(8,128)S(1)}, u32[]{:S(2)}, u32[]{:S(2)}) collective-permute-start(f32[64,128]{1,0:T(8,128)S(1)} %add.31), channel_id=1, source_target_pairs={{0,4},{4,0},{8,12},{12,8},{16,20},{20,16},{24,28},{28,24},{32,36},... | collective-permute-start | bytes 98312 | tf_op jit(solution)/shard_map/ppermute | solution.py:413
  108.3 16.7 %collective-permute-start.8 = (bf16[128,1024]{1,0:T(8,128)(2,1)S(1)}, bf16[128,1024]{1,0:T(8,128)(2,1)S(1)}, u32[]{:S(2)}, u32[]{:S(2)}) collective-permute-start(bf16[128,1024]{1,0:T(8,128)(2,1)S(1)} %slice.11), channel_id=1, source_target_pairs={{4,0},{8,4},{12,8},{16,12},{20,16},{24,20},{28,24},{32,28},{36,32}... | collective-permute-start | bytes 786440 | tf_op jit(solution)/shard_map/ppermute | solution.py:43
  110.2 13.6 %collective-permute-start.29 = (f32[64,128]{1,0:T(8,128)S(1)}, f32[64,128]{1,0:T(8,128)S(1)}, u32[]{:S(2)}, u32[]{:S(2)}) collective-permute-start(f32[64,128]{1,0:T(8,128)S(1)} %add.32), channel_id=1, source_target_pairs={{0,8},{4,12},{8,0},{12,4},{16,24},{20,28},{24,16},{28,20},{32,40},... | collective-permute-start | bytes 98312 | tf_op jit(solution)/shard_map/ppermute | solution.py:413
  114.0 16.4 %collective-permute-start.23 = (bf16[64,1024]{1,0:T(8,128)(2,1)S(1)}, bf16[64,1024]{1,0:T(8,128)(2,1)S(1)}, u32[]{:S(2)}, u32[]{:S(2)}) collective-permute-start(bf16[64,1024]{1,0:T(8,128)(2,1)S(1)} %get-tuple-element.82), channel_id=1, source_target_pairs={{0,64},{64,128},{128,192},{192,0},{1,65},{65,129},{129,193},{193,1... | collective-permute-start | bytes 393224 | tf_op jit(solution)/shard_map/ppermute | solution.py:35
  115.1 15.3 %collective-permute-start.24 = (bf16[64,1024]{1,0:T(8,128)(2,1)S(1)}, bf16[64,1024]{1,0:T(8,128)(2,1)S(1)}, u32[]{:S(2)}, u32[]{:S(2)}) collective-permute-start(bf16[64,1024]{1,0:T(8,128)(2,1)S(1)} %get-tuple-element.83), channel_id=1, source_target_pairs={{0,128},{64,192},{128,0},{192,64},{1,129},{65,193},{129,1},{193,65... | collective-permute-start | bytes 393224 | tf_op jit(solution)/shard_map/ppermute | solution.py:35
  122.9 7.6 %collective-permute-start.25 = (bf16[64,1024]{1,0:T(8,128)(2,1)S(1)}, bf16[64,1024]{1,0:T(8,128)(2,1)S(1)}, u32[]{:S(2)}, u32[]{:S(2)}) collective-permute-start(bf16[64,1024]{1,0:T(8,128)(2,1)S(1)} %get-tuple-element.84), channel_id=1, source_target_pairs={{0,192},{64,0},{128,64},{192,128},{1,193},{65,1},{129,65},{193,129... | collective-permute-start | bytes 393224 | tf_op jit(solution)/shard_map/ppermute | solution.py:35
  123.9 6.5 %collective-permute-start.30 = (f32[64,128]{1,0:T(8,128)S(1)}, f32[64,128]{1,0:T(8,128)S(1)}, u32[]{:S(2)}, u32[]{:S(2)}) collective-permute-start(f32[64,128]{1,0:T(8,128)S(1)} %add.33), channel_id=1, source_target_pairs={{0,64},{64,0},{128,192},{192,128},{1,65},{65,1},{129,193},{193,129... | collective-permute-start | bytes 98312 | tf_op jit(solution)/shard_map/ppermute | solution.py:411
  130.3 4.9 %collective-permute-start.31 = (f32[64,128]{1,0:T(8,128)S(1)}, f32[64,128]{1,0:T(8,128)S(1)}, u32[]{:S(2)}, u32[]{:S(2)}) collective-permute-start(f32[64,128]{1,0:T(8,128)S(1)} %add.34), channel_id=1, source_target_pairs={{0,128},{64,192},{128,0},{192,64},{1,129},{65,193},{129,1},{193,65... | collective-permute-start | bytes 98312 | tf_op jit(solution)/shard_map/ppermute | solution.py:411
  (5 other events, 42.4 us)

commit v3 on v0

v3 whole, which is shorter than its diff:
```python
import math

import jax
import jax.numpy as jnp
from jax import lax
from jax.experimental import pallas as pl
from jax.experimental.pallas import tpu as pltpu
from jax.sharding import PartitionSpec as P

F32 = jnp.float32
BF16 = jnp.bfloat16
SIDE = 4
TAPS = 128
GROUP = 16
LANES = 128
PER_TILE = LANES // GROUP
WIDE = 256


def room(mebibytes):
    return pltpu.CompilerParams(vmem_limit_bytes=mebibytes * 1024 * 1024)


def spot():
    ctx = lax.axis_index("ctx")
    tp = lax.axis_index("tp")
    return ctx // SIDE, ctx % SIDE, lax.axis_index("dp"), tp // 2, tp % 2


def moved(x, axis, by):
    if axis == "x":
        pairs = [(i, (i // SIDE + by) % SIDE * SIDE + i % SIDE) for i in range(SIDE * SIDE)]
        return lax.ppermute(x, "ctx", pairs)
    if axis == "y":
        pairs = [(i, i // SIDE * SIDE + (i % SIDE + by) % SIDE) for i in range(SIDE * SIDE)]
        return lax.ppermute(x, "ctx", pairs)
    if axis == "z":
        return lax.ppermute(x, "dp", [(i, (i + by) % SIDE) for i in range(SIDE)])
    if axis == "half":
        return lax.ppermute(x, "tp", [(i, (i + 2) % 4) for i in range(4)])
    return lax.ppermute(x, "tp", [(i, i // 2 * 2 + (i + 1) % 2) for i in range(4)])


def shifted(x, by):
    devices = lax.axis_size("ctx")
    return lax.ppermute(x, "ctx", [(i, i + by) for i in range(devices) if 0 <= i + by < devices])


ANYWHERE = pl.BlockSpec(memory_space=pl.ANY)
HALF = LANES // 2


def resident(x):
    return pltpu.with_memory_space_constraint(x, pltpu.HBM)


def whole(shape, place=None):
    place = place or (0,) * len(shape)
    return pl.BlockSpec(tuple(shape), lambda i: place, pipeline_mode=pl.Buffered(1))


def full(shape):
    return pl.BlockSpec(tuple(shape), lambda i: (0,) * len(shape))


def tile(rows, width):
    return pl.BlockSpec((rows, width), lambda i: (0, i))


def iota(shape, dim):
    return lax.broadcasted_iota(jnp.int32, shape, dim)


def aligned(index, size):
    return pl.ds(pl.multiple_of(index * size, size), size)


def lasting(microseconds):
    return pl.CostEstimate(flops=int(microseconds * 1e9), bytes_accessed=0, transcendentals=0)


def once(kernel, name, ins, outs, scratch=(), after=(), lasts=0):
    def body(*refs):
        kernel(*refs[: len(ins)], *refs[len(ins) + len(after) :])

    specs = [i[1] if isinstance(i, tuple) else whole(i.shape) for i in ins]
    arrays = [i[0] if isinstance(i, tuple) else i for i in ins]
    return pl.pallas_call(
        body,
        grid=(1,),
        in_specs=specs + [ANYWHERE] * len(after),
        out_specs=[whole(shape) for shape, _ in outs],
        out_shape=[jax.ShapeDtypeStruct(shape, dtype) for shape, dtype in outs],
        scratch_shapes=list(scratch),
        compiler_params=room(12),
        cost_estimate=lasting(lasts),
        name=name,
    )(*arrays, *after)


def first_rows(filters, shifted_by):
    lane, tap = iota((TAPS, 2 * TAPS), 1), iota((TAPS, 2 * TAPS), 0)
    place = lane == (TAPS - tap if shifted_by else tap)
    return jnp.dot(filters, place.astype(F32).astype(BF16), preferred_element_type=F32)


def banded(rows, stack):
    for g in range(PER_TILE):
        first = jnp.broadcast_to(rows[g : g + 1], (TAPS, 2 * TAPS))
        skewed = pltpu.roll(first, 0, 1, stride=1, stride_axis=0)
        stack[g * TAPS : (g + 1) * TAPS, :] = skewed.astype(BF16)


def lane_group(shape):
    return iota(shape, len(shape) - 1) % LANES // GROUP


def own_lanes(stacked):
    group = lane_group((TAPS, 2 * LANES))
    chosen = jnp.zeros((TAPS, 2 * LANES), F32)
    for g in range(PER_TILE):
        chosen = jnp.where(group == g, stacked[g * TAPS : (g + 1) * TAPS], chosen)
    return chosen


def two_windows(first, second, third):
    upper = jnp.concatenate([first, second], 1)
    lower = jnp.concatenate([second, third], 1)
    return jnp.concatenate([upper, lower], 0)


def forward_kernel(filters, previous, signal, gating, *refs):
    shifts = SIDE - 1
    early, (response, gated), sends = refs[: 2 * shifts], refs[2 * shifts : 2 * shifts + 2], refs[2 * shifts + 2 : -1]
    stack = refs[-1]
    rows = first_rows(filters[...], True)
    count = signal.shape[1] // LANES
    for i in range(count):
        columns = slice(i * LANES, (i + 1) * LANES)
        which, place = divmod(i, count // 2)
        to = slice(place * LANES, (place + 1) * LANES)
        band = stack.at[i % 2]
        banded(rows[i * PER_TILE : (i + 1) * PER_TILE], band)
        window = two_windows(previous[:, columns], signal[:TAPS, columns], signal[TAPS:, columns])
        made = own_lanes(jnp.dot(band[...], window, preferred_element_type=F32))
        for block in range(2):
            tokens = slice(block * TAPS, (block + 1) * TAPS)
            part = made[:, block * LANES : (block + 1) * LANES]
            response[tokens, columns] = part
            product = (part * gating[tokens, columns].astype(F32)).astype(BF16)
            gated[tokens, columns] = product
            for send in sends[which * shifts : (which + 1) * shifts]:
                send[tokens, to] = product
    for ref, send in zip(early, sends):
        send[2 * TAPS :] = ref[...]


def forward(filters, previous, signal, gating, early):
    length, channels = signal.shape
    rows, width = early[0].shape
    response, gated, *sends = once(
        forward_kernel,
        "conv_forward",
        [filters, previous, signal, gating, *early],
        [((length, channels), F32), ((length, channels), BF16)]
        + [((length + rows, width), BF16)] * len(early),
        [pltpu.VMEM((2, PER_TILE * TAPS, 2 * TAPS), BF16)],
    )
    return response, gated, sends[: SIDE - 1], sends[SIDE - 1 :]


def input_grad_kernel(filters, conv_grad, following, grad_input, stack):
    rows = first_rows(filters[...], False)
    for i in range(conv_grad.shape[1] // LANES):
        columns = slice(i * LANES, (i + 1) * LANES)
        band = stack.at[i % 2]
        banded(rows[i * PER_TILE : (i + 1) * PER_TILE], band)
        window = two_windows(
            conv_grad[:TAPS, columns], conv_grad[TAPS:, columns], following[:, columns]
        )
        made = own_lanes(jnp.dot(band[...], window, preferred_element_type=F32))
        for block in range(2):
            grad_input[block * TAPS : (block + 1) * TAPS, columns] = made[
                :, block * LANES : (block + 1) * LANES
            ].astype(BF16)


def input_grad(filters, conv_grad, following, after):
    return once(
        input_grad_kernel,
        "input_grad",
        [filters, conv_grad, following],
        [(conv_grad.shape, BF16)],
        [pltpu.VMEM((2, PER_TILE * TAPS, 2 * TAPS), BF16)],
        after,
        4,
    )[0]


def filter_grad_kernel(previous, signal, conv_grad, grad_filter, stack):
    square = (2 * TAPS, 2 * TAPS)
    turn = iota(square, 0) == (2 * TAPS - iota(square, 1)) % (2 * TAPS)
    turn = turn.astype(F32).astype(BF16)
    group = lane_group((TAPS, 2 * LANES))
    for i in range(signal.shape[1] // LANES):
        columns = slice(i * LANES, (i + 1) * LANES)
        masked = stack.at[i % 2]
        inputs = two_windows(previous[:, columns], signal[:TAPS, columns], signal[TAPS:, columns])
        turned = jnp.dot(turn, inputs, preferred_element_type=F32).astype(BF16)
        both = jnp.concatenate([conv_grad[:TAPS, columns], conv_grad[TAPS:, columns]], 1)
        both = both.astype(F32)
        for g in range(PER_TILE):
            masked[g * TAPS : (g + 1) * TAPS, :] = jnp.where(group == g, both, 0.0).astype(BF16)
        products = lax.dot_general(
            masked[...], turned, (((1,), (1,)), ((), ())), preferred_element_type=F32
        )
        for g in range(PER_TILE):
            skewed = pltpu.roll(products[g * TAPS : (g + 1) * TAPS], 0, 1, stride=1, stride_axis=0)
            row = i * PER_TILE + g
            grad_filter[row : row + 1, :] = jnp.sum(skewed[:, TAPS:], axis=0, keepdims=True)


def filter_grad(previous, signal, conv_grad, after):
    return once(
        filter_grad_kernel,
        "filter_grad",
        [previous, signal, conv_grad],
        [((signal.shape[1] // GROUP, TAPS), F32)],
        [pltpu.VMEM((2, PER_TILE * TAPS, 2 * TAPS), BF16)],
        after,
        4,
    )[0]


def pack_kernel(mine, *outs):
    x, y, _, _, _ = spot()
    part = mine.shape[0]
    depth = mine.shape[1] // SIDE
    lower = iota((part, LANES), 1) < HALF
    for s in range(SIDE):
        to_x, to_y = (x + s) % SIDE, (y + s) % SIDE
        upper_half = jnp.broadcast_to(to_y % 2, (part, LANES)) == 1
        for d in range(SIDE):
            rows = slice(d // 2 * part, (d // 2 + 1) * part)
            column = d % 2 * WIDE
            start = pl.multiple_of(d * depth + to_x * WIDE, WIDE)
            outs[s][rows, column : column + WIDE] = mine[:, pl.ds(start, WIDE)]
            for pair in range(SIDE // 2):
                runs = []
                for i in range(2):
                    start = d * depth + (2 * pair + i) * WIDE + to_y // 2 * LANES
                    runs.append(mine[:, pl.ds(pl.multiple_of(start, LANES), LANES)].astype(F32))
                first = jnp.where(upper_half, pltpu.roll(runs[0], HALF, 1), runs[0])
                second = jnp.where(upper_half, runs[1], pltpu.roll(runs[1], HALF, 1))
                both = jnp.where(lower, first, second).astype(BF16)
                at = column + pair * LANES
                outs[SIDE + s][rows, at : at + LANES] = both


def pack(mine, after=()):
    part, width = mine.shape
    outs = once(
        pack_kernel, "pack", [mine], [((2 * part, width // (2 * SIDE)), BF16)] * (2 * SIDE), (), after
    )
    return outs[:SIDE], outs[SIDE:]


def turn_into(parts, out, base, me):
    part = parts[0].shape[0] // 2
    for fold in range(2):
        for pair in range(SIDE // 2):
            block = jnp.concatenate(
                [ref[fold * part : (fold + 1) * part] for ref in parts[2 * pair : 2 * pair + 2]], 0
            )
            whole = block.T
            for d in range(2):
                for q in range(SIDE):
                    to = (q - me + SIDE) % SIDE
                    rows = pl.ds(pl.multiple_of(base + to * WIDE + (2 * fold + d) * HALF, HALF), HALF)
                    start = d * WIDE + q * HALF
                    out[rows, pair * LANES : (pair + 1) * LANES] = whole[start : start + HALF]


def turn_early_kernel(*refs):
    x, y, _, _, _ = spot()
    out = refs[-1]
    turn_into(refs[:SIDE], out, 0, y)
    turn_into(refs[SIDE : 2 * SIDE], out, out.shape[0] // 2, x)


def turn_early(own_x, got_x, own_y, got_y, after):
    rows, width = own_x.shape
    count = got_x[0].shape[0] // rows
    tail = whole((rows, width), (count - 1, 0))
    parts = [own_x, *[(got, tail) for got in got_x], own_y, *[(got, tail) for got in got_y]]
    return once(turn_early_kernel, "turn_early", parts, [((4 * width, WIDE), BF16)], (), after)[0]


def turn_late(parts, axis, after=()):
    def kernel(*refs):
        x, y, _, _, _ = spot()
        turn_into(refs[:SIDE], refs[-1], 0, y if axis == "x" else x)

    return once(kernel, "turn_late", parts, [((2 * parts[0].shape[1], WIDE), BF16)], (), after)[0]


def project_kernel(mine, other, weight, gating, response, *refs):
    _, _, _, half, core = spot()
    part = mine.shape[0]
    rows = refs[-1]
    conv_grad, grad_gate = refs[-3:-1]

    @pl.when(pl.program_id(0) == 0)
    def _():
        rows[aligned(core, part), :] = mine[...]
        rows[aligned(1 - core, part), :] = other[...]

    late = len(refs) > 3
    tokens = aligned(1 - half if late else half, TAPS)
    made = jnp.dot(rows[...], weight[...], preferred_element_type=F32)
    made_conv = (made * gating[tokens, :].astype(F32)).astype(BF16)
    made_gate = (made * response[tokens, :]).astype(BF16)
    if late:
        conv_grad[tokens, :] = made_conv
        grad_gate[tokens, :] = made_gate
        conv_grad[aligned(half, TAPS), :] = refs[0][...]
        grad_gate[aligned(half, TAPS), :] = refs[1][...]
    else:
        conv_grad[...] = made_conv
        grad_gate[...] = made_gate


def project(mine, other, weight, gating, response, done=(), after=()):
    length, channels = gating.shape
    depth = weight.shape[0]
    made = length if done else 2 * mine.shape[0]

    def body(*refs):
        kept = 5 + len(done)
        project_kernel(*refs[:kept], *refs[kept + len(after) :])

    return pl.pallas_call(
        body,
        grid=(channels // WIDE,),
        in_specs=[full(mine.shape)] * 2
        + [tile(depth, WIDE), tile(length, WIDE), tile(length, WIDE)]
        + [tile(TAPS, WIDE)] * len(done)
        + [ANYWHERE] * len(after),
        out_specs=[tile(made, WIDE)] * 2,
        out_shape=[jax.ShapeDtypeStruct((made, channels), BF16)] * 2,
        scratch_shapes=[pltpu.VMEM((2 * mine.shape[0], depth), BF16)],
        compiler_params=room(16),
        cost_estimate=lasting(5 if done else 0),
        name="project_late" if done else "project_early",
    )(mine, other, weight, gating, response, *done, *after)


def weight_kernel(early, early_other, late, late_other, gated, *refs):
    _, _, _, half, core = spot()
    got, outs = refs[: SIDE - 1], refs[SIDE - 1 :]
    part = WIDE // SIDE
    tokens = []
    for h, c in ((half, core), (half, 1 - core), (1 - half, core), (1 - half, 1 - core)):
        rows = aligned(2 * h + c, part)
        tokens += [gated[rows, :]] + [ref[rows, :] for ref in got]
    tokens = jnp.concatenate(tokens, 0)
    for s, out in enumerate(outs):
        rows = slice(s * WIDE, (s + 1) * WIDE)
        features = jnp.concatenate([ref[rows] for ref in (early, early_other, late, late_other)], 1)
        out[...] = jnp.dot(features, tokens, preferred_element_type=F32).astype(out.dtype)


def weight_part(which, early, early_other, late, late_other, gated, got, after=()):
    length = gated.shape[0]
    features = late.shape[0]
    width = got[0].shape[1]
    spec = whole((features, WIDE), (which, 0))
    return once(
        weight_kernel,
        "weight_part",
        [
            (early, spec),
            (early_other, spec),
            late,
            late_other,
            (gated, whole((length, width), (0, which))),
            *[(one, whole((length, width))) for one in got],
        ],
        [((features // SIDE, width), F32 if s == 0 else BF16) for s in range(SIDE)],
        (),
        after,
        3,
    )


def first_sum_kernel(*refs):
    _, _, z, _, _ = spot()
    outs, kept = refs[SIDE : 2 * SIDE], refs[2 * SIDE]
    total = refs[0][...]
    for ref in refs[1:SIDE]:
        total = total + ref[...].astype(F32)
    run = kept.shape[0] // SIDE
    for d in range(SIDE):
        kept[aligned((d - z + SIDE) % SIDE, run), :] = total[d * run : (d + 1) * run]
    for s, out in enumerate(outs):
        out[...] = kept[s * run : (s + 1) * run, :].astype(out.dtype)


def first_sum(parts, after=()):
    rows, width = parts[0].shape
    return once(
        first_sum_kernel,
        "first_sum",
        parts,
        [((rows // SIDE, width), F32 if s == 0 else BF16) for s in range(SIDE)],
        [pltpu.VMEM((rows, width), F32)],
        after,
        1,
    )


def last_sum(parts_x, parts_y, scale):
    def kernel(*refs):
        out = refs[-1]
        width = refs[0].shape[1]
        for which in range(2):
            total = refs[which * SIDE][...]
            for ref in refs[which * SIDE + 1 : (which + 1) * SIDE]:
                total = total + ref[...].astype(F32)
            out[:, which * width : (which + 1) * width] = total * scale

    rows, width = parts_x[0].shape
    return once(kernel, "last_sum", [*parts_x, *parts_y], [((rows, 2 * width), F32)])[0]


def tied(x, *after):
    return lax.optimization_barrier((x, *after))[0]


def partnered(x, axis, by):
    if axis == "z":
        return lax.ppermute(x, "dp", [(i, i ^ by) for i in range(SIDE)])
    step = by * (SIDE if axis == "x" else 1)
    return lax.ppermute(x, "ctx", [(i, i ^ step) for i in range(SIDE * SIDE)])


def paired(x, axis, by, after=()):
    return x + partnered(tied(x, *after), axis, by)


def exchanged(parts, axis):
    return [parts[0]] + [moved(parts[s], axis, s) for s in range(1, SIDE)]


def local(conv_input, gate_value, out_grad, out_weight, filters):
    signal, gating, grads = conv_input[0], gate_value[0], out_grad[0]
    length, channels = signal.shape
    halo_sent = signal[length - TAPS :]
    signal, gating, filters, weight = (
        resident(x) for x in (signal, gating, filters, out_weight)
    )
    tokens_all = lax.axis_size("dp") * lax.axis_size("ctx") * length

    late = moved(grads, "half", 1)
    previous = shifted(halo_sent, 1)
    early_other = moved(grads, "core", 1)
    early_x, early_y = pack(resident(grads), (early_other,))
    response, gated, sends_x, sends_y = forward(
        filters, previous, signal, gating, [*early_x[1:], *early_y[1:]]
    )
    got_x, got_y = [], []
    for got, axis, parts in ((got_x, "x", sends_x), (got_y, "y", sends_y)):
        first = moved(parts[0], axis, 1)
        got += [first, moved(tied(parts[1], first), axis, 2), moved(parts[2], axis, 3)]
    conv_early, gate_early = project(resident(grads), early_other, weight, gating, response)

    late_other = moved(tied(late, conv_early, got_x[0], got_y[0], got_x[2], got_y[2]), "core", 1)
    late_x, late_y = pack(late, (late_other,))
    late_x = exchanged(late_x, "x")
    late_y = exchanged(late_y, "y")
    conv_grad, grad_gate = project(
        late,
        late_other,
        weight,
        gating,
        response,
        (conv_early, gate_early),
        (late_x[0],),
    )
    early = turn_early(early_x[0], got_x, early_y[0], got_y, (conv_grad, *late_x[1:], *late_y[1:]))
    early_swap = moved(early, "core", 1)
    turned_x = turn_late(late_x, "x", (early,))
    swap_x = moved(turned_x, "core", 1)
    turned_y = turn_late(late_y, "y", (turned_x,))
    swap_y = moved(turned_y, "core", 1)
    following = shifted(conv_grad[:TAPS], -1)
    filter_local = filter_grad(previous, signal, conv_grad, (turned_y,))
    parts_x = weight_part(
        0, early, early_swap, turned_x, swap_x, gated, got_x, (filter_local,)
    )
    parts_y = weight_part(
        1, early, early_swap, turned_y, swap_y, gated, got_y, (parts_x[0],)
    )
    filter_sum = paired(filter_local, "x", 1)
    filter_sum = paired(filter_sum, "x", 2, (parts_x[0],))
    filter_sum = paired(filter_sum, "y", 1, (parts_y[0],))
    parts_x, parts_y = exchanged(parts_x, "y"), exchanged(parts_y, "x")
    filter_sum = paired(filter_sum, "y", 2, (parts_x[1], parts_x[3]))
    sums_x = first_sum(parts_x)
    filter_sum = paired(filter_sum, "z", 1, (sums_x[0],))
    sums_y = first_sum(parts_y, (sums_x[0],))
    filter_total = paired(filter_sum, "z", 2, (sums_y[0],))
    grad_input = input_grad(filters, conv_grad, following, (sums_y[0],))
    grad_weight = last_sum(
        exchanged(sums_x, "z"), exchanged(sums_y, "z"), 1.0 / math.sqrt(tokens_all)
    )
    grad_filter = filter_total * (1.0 / math.sqrt(tokens_all * GROUP))
    return (grad_input[None], grad_gate[None], grad_weight, grad_filter)


def solution(mesh):
    placed = (
        P("dp", "ctx", "tp"),
        P("dp", "ctx", "tp"),
        P("dp", ("ctx", "tp"), None),
        P(None, "tp"),
        P("tp", None),
    )
    return jax.shard_map(
        local,
        mesh=mesh,
        in_specs=placed,
        out_specs=(
            P("dp", "ctx", "tp"),
            P("dp", "ctx", "tp"),
            P(("dp", "ctx"), "tp"),
            P("tp", None),
        ),
        check_vma=False,
    )
```

time: 574 us -> 123 us (0.21)
  the two profiles are of different devices: /device:TPU:0 before, /device:TPU:2 now
where the time goes in v3:
time: 123 us; the launch traced here: 121 us
  starting transfers between devices  63.7 us (52%)
  Pallas kernels  28.3 us (23%)
  waiting for transfers between devices  26.3 us (21%)
    ppermute x18, starting transfers between devices, moved(): return lax.ppermute(x, 'ctx', pairs)  26.6 us
    pallas_call x13, Pallas kernels, once(): pl.pallas_call(body, grid=(1,), in_specs=specs + [ANYWHERE] * len(after),...  17.3 us
    ppermute x18, waiting for transfers between devices, moved(): return lax.ppermute(x, 'ctx', pairs)  16 us
    ppermute x6, starting transfers between devices, moved(): return lax.ppermute(x, 'dp', [(i, (i + by) % SIDE) for i in range(SIDE)])  14.4 us
    pallas_call x2, Pallas kernels, project(): pl.pallas_call(body, grid=(channels // WIDE,), in_specs=[full(mine.shape)...  11 us
    ppermute x4, waiting for transfers between devices, partnered(): return lax.ppermute(x, 'ctx', [(i, i ^ step) for i in range(SIDE * SIDE)])  8.98 us
    ppermute x1, starting transfers between devices, moved(): return lax.ppermute(x, 'tp', [(i, (i + 2) % 4) for i in range(4)])  7.28 us
    ppermute x2, starting transfers between devices, shifted(): lax.ppermute(x, 'ctx', [(i, i + by) for i in range(devices) if 0 <= i + b...  6.62 us
  transfers between devices with their start and end apart: 38, of which 12 were waited for; matrix products, arithmetic and copies ran while one was open for 1% of the time, Pallas kernels for 23%

profile of v3, /device:TPU:2, one launch (start us, length us, event | category | flops | bytes accessed | tf_op | source)
XLA Modules:
  0.0 120.9 jit_solution(478549743979114710)
XLA Ops:
  1.7 3.5 %collective-permute-start.2 = (bf16[128,1024]{1,0:T(8,128)(2,1)S(1)}, bf16[128,1024]{1,0:T(8,128)(2,1)S(1)}, u32[]{:S(2)}, u32[]{:S(2)}) collective-permute-start(bf16[128,1024]{1,0:T(8,128)(2,1)S(1)} %slice_bitcast_fusion), channel_id=1, source_target_pairs={{0,4},{4,8},{8,12},{12,16},{16,20},{20,24},{24,28},{28,32},{32,36}... | collective-permute-start | bytes 786440 | tf_op jit(solution)/shard_map/ppermute | solution.py:46
  5.2 7.3 %collective-permute-start = (bf16[64,4096]{1,0:T(8,128)(2,1)}, bf16[64,4096]{1,0:T(8,128)(2,1)S(1)}, u32[]{:S(2)}, u32[]{:S(2)}) collective-permute-start(bf16[64,4096]{1,0:T(8,128)(2,1)} %bitcast.8), channel_id=1, source_target_pairs={{0,2},{1,3},{2,0},{3,1},{4,6},{5,7},{6,4},{7,5},{8,10},{9,11},{10,... | collective-permute-start | bytes 1572872 | tf_op jit(solution)/shard_map/ppermute | solution.py:40
  12.5 1.6 %pack.2 = (bf16[128,512]{1,0:T(8,128)(2,1)S(1)}, bf16[128,512]{1,0:T(8,128)(2,1)S(1)}, bf16[128,512]{1,0:T(8,128)(2,1)S(1)}, bf16[128,512]{1,0:T(8,128)(2,1)S(1)...) custom-call(bf16[64,4096]{1,0:T(8,128)(2,1)} %bitcast.9, ...), custom_call_target="tpu_custom_call" | custom-call | tf_op jit(solution)/shard_map/pack/pallas_call | solution.py:88
  14.4 3.5 %conv_forward.1 = (f32[256,1024]{1,0:T(8,128)S(1)}, bf16[256,1024]{1,0:T(8,128)(2,1)S(1)}, bf16[384,512]{1,0:T(8,128)(2,1)S(1)}, bf16[384,512]{1,0:T(8,128)(2,1)...) custom-call(bf16[64,128]{1,0:T(8,128)(2,1)} %refs_0_.3, ...), custom_call_target="tpu_custom_call" | custom-call | tf_op jit(solution)/shard_map/conv_forward/pallas_call | solution.py:88
  17.9 1.4 %collective-permute-start.4 = (bf16[384,512]{1,0:T(8,128)(2,1)S(1)}, bf16[384,512]{1,0:T(8,128)(2,1)S(1)}, u32[]{:S(2)}, u32[]{:S(2)}) collective-permute-start(bf16[384,512]{1,0:T(8,128)(2,1)S(1)} %get-tuple-element.65), channel_id=1, source_target_pairs={{0,4},{4,8},{8,12},{12,0},{16,20},{20,24},{24,28},{28,16},{32,36},... | collective-permute-start | bytes 1179656 | tf_op jit(solution)/shard_map/ppermute | solution.py:36
  19.3 1.5 %collective-permute-start.3 = (bf16[384,512]{1,0:T(8,128)(2,1)S(1)}, bf16[384,512]{1,0:T(8,128)(2,1)S(1)}, u32[]{:S(2)}, u32[]{:S(2)}) collective-permute-start(bf16[384,512]{1,0:T(8,128)(2,1)S(1)} %get-tuple-element.64), channel_id=1, source_target_pairs={{0,16},{4,20},{8,24},{12,28},{16,32},{20,36},{24,40},{28,44},{32,4... | collective-permute-start | bytes 1179656 | tf_op jit(solution)/shard_map/ppermute | solution.py:33
  21.4 1.9 %collective-permute-start.6 = (bf16[384,512]{1,0:T(8,128)(2,1)S(1)}, bf16[384,512]{1,0:T(8,128)(2,1)S(1)}, u32[]{:S(2)}, u32[]{:S(2)}) collective-permute-start(bf16[384,512]{1,0:T(8,128)(2,1)S(1)} %get-tuple-element.67), channel_id=1, source_target_pairs={{0,12},{4,0},{8,4},{12,8},{16,28},{20,16},{24,20},{28,24},{32,44},... | collective-permute-start | bytes 1179656 | tf_op jit(solution)/shard_map/ppermute | solution.py:36
  23.3 5.2 %project_early.1 = (bf16[128,1024]{1,0:T(8,128)(2,1)S(1)}, bf16[128,1024]{1,0:T(8,128)(2,1)S(1)}) custom-call(bf16[64,4096]{1,0:T(8,128)(2,1)} %bitcast.10, bf16[64,4096]{1,0:T(8,128)(2,1)S(1)} %collective-permute-done.1.refs_1_, bf16[4096,1024]{1,0:T(8,128)(2,1)} %refs_2_.3, bf16[256,1024]{1,0:T(8,128)(2,1)} %bitcast.12, ...), custom_call_target="tpu_custom_call" | custom-call | tf_op jit(solution)/shard_map/project_early/pallas_call | solution.py:342
  28.5 1.5 %collective-permute-done.4.refs_5_ = bf16[384,512]{1,0:T(8,128)(2,1)S(1)} collective-permute-done((bf16[384,512]{1,0:T(8,128)(2,1)S(1)}, bf16[384,512]{1,0:T(8,128)(2,1)S(1)}, u32[]{:S(2)}, u32[]{:S(2)}) %collective-permute-start.4) | collective-permute-done | bytes 393248 | tf_op jit(solution)/shard_map/ppermute | solution.py:36
  31.5 2.5 %collective-permute-start.10 = (bf16[384,512]{1,0:T(8,128)(2,1)S(1)}, bf16[384,512]{1,0:T(8,128)(2,1)S(1)}, u32[]{:S(2)}, u32[]{:S(2)}) collective-permute-start(bf16[384,512]{1,0:T(8,128)(2,1)S(1)} %get-tuple-element.77), channel_id=1, source_target_pairs={{0,8},{4,12},{8,0},{12,4},{16,24},{20,28},{24,16},{28,20},{32,40},... | collective-permute-start | bytes 1179656 | tf_op jit(solution)/shard_map/ppermute | solution.py:36
  33.9 2.1 %collective-permute-start.9 = (bf16[384,512]{1,0:T(8,128)(2,1)S(1)}, bf16[384,512]{1,0:T(8,128)(2,1)S(1)}, u32[]{:S(2)}, u32[]{:S(2)}) collective-permute-start(bf16[384,512]{1,0:T(8,128)(2,1)S(1)} %get-tuple-element.74), channel_id=1, source_target_pairs={{0,32},{4,36},{8,40},{12,44},{16,48},{20,52},{24,56},{28,60},{32,0... | collective-permute-start | bytes 1179656 | tf_op jit(solution)/shard_map/ppermute | solution.py:33
  37.8 2.1 %collective-permute-start.12 = (bf16[128,512]{1,0:T(8,128)(2,1)S(1)}, bf16[128,512]{1,0:T(8,128)(2,1)S(1)}, u32[]{:S(2)}, u32[]{:S(2)}) collective-permute-start(bf16[128,512]{1,0:T(8,128)(2,1)S(1)} %get-tuple-element.79), channel_id=1, source_target_pairs={{0,32},{4,36},{8,40},{12,44},{16,48},{20,52},{24,56},{28,60},{32,0... | collective-permute-start | bytes 393224 | tf_op jit(solution)/shard_map/ppermute | solution.py:33
  40.8 3.7 %collective-permute-done.10.refs_6_ = bf16[384,512]{1,0:T(8,128)(2,1)S(1)} collective-permute-done((bf16[384,512]{1,0:T(8,128)(2,1)S(1)}, bf16[384,512]{1,0:T(8,128)(2,1)S(1)}, u32[]{:S(2)}, u32[]{:S(2)}) %collective-permute-start.10) | collective-permute-done | bytes 393248 | tf_op jit(solution)/shard_map/ppermute | solution.py:36
  45.8 1.7 %collective-permute-done.9.refs_2_.refs_6_ = bf16[384,512]{1,0:T(8,128)(2,1)S(1)} collective-permute-done((bf16[384,512]{1,0:T(8,128)(2,1)S(1)}, bf16[384,512]{1,0:T(8,128)(2,1)S(1)}, u32[]{:S(2)}, u32[]{:S(2)}) %collective-permute-start.9) | collective-permute-done | bytes 393248 | tf_op jit(solution)/shard_map/ppermute | solution.py:33
  47.5 1.4 %collective-permute-start.15 = (bf16[128,512]{1,0:T(8,128)(2,1)S(1)}, bf16[128,512]{1,0:T(8,128)(2,1)S(1)}, u32[]{:S(2)}, u32[]{:S(2)}) collective-permute-start(bf16[128,512]{1,0:T(8,128)(2,1)S(1)} %get-tuple-element.82), channel_id=1, source_target_pairs={{0,8},{4,12},{8,0},{12,4},{16,24},{20,28},{24,16},{28,20},{32,40},... | collective-permute-start | bytes 393224 | tf_op jit(solution)/shard_map/ppermute | solution.py:36
  50.0 1.8 %collective-permute-start.16 = (bf16[128,512]{1,0:T(8,128)(2,1)S(1)}, bf16[128,512]{1,0:T(8,128)(2,1)S(1)}, u32[]{:S(2)}, u32[]{:S(2)}) collective-permute-start(bf16[128,512]{1,0:T(8,128)(2,1)S(1)} %get-tuple-element.83), channel_id=1, source_target_pairs={{0,12},{4,0},{8,4},{12,8},{16,28},{20,16},{24,20},{28,24},{32,44},... | collective-permute-start | bytes 393224 | tf_op jit(solution)/shard_map/ppermute | solution.py:36
  51.8 5.8 %project_late.1 = (bf16[256,1024]{1,0:T(8,128)(2,1)S(1)}, bf16[256,1024]{1,0:T(8,128)(2,1)}) custom-call(bf16[64,4096]{1,0:T(8,128)(2,1)S(1)} %collective-permute-done.refs_0_, bf16[64,4096]{1,0:T(8,128)(2,1)S(1)} %collective-permute-done.7.refs_1_, bf16[4096,1024]{1,0:T(8,128)(2,1)} %refs_2_.3, bf16[256,1024]{1,0:T(8,128)(2,1)} %bitcast.13, ...), custom_call_target="tpu_custom_call" | custom-call | flops 5000000000 | tf_op jit(solution)/shard_map/project_late/pallas_call | solution.py:342
  59.1 3.8 %filter_grad.1.refs_8_ = f32[64,128]{1,0:T(8,128)S(1)} custom-call(bf16[128,1024]{1,0:T(8,128)(2,1)S(1)} %collective-permute-done.2.refs_1_.refs_0_, bf16[256,1024]{1,0:T(8,128)(2,1)} %bitcast.15, bf16[256,1024]{1,0:T(8,128)(2,1)S(1)} %get-tuple-element.71.refs_8_.refs_2_.refs_1_, bf16[1024,256]{1,0:T(8,128)(2,1)S(1)} %turn_late.3.refs_3_.refs_2_), custom_call_target="tpu_custom_call" | custom-call | flops 4000000000 | tf_op jit(solution)/shard_map/filter_grad/pallas_call | solution.py:88
  62.9 1.7 %collective-permute-start.32 = (f32[64,128]{1,0:T(8,128)S(1)}, f32[64,128]{1,0:T(8,128)S(1)}, u32[]{:S(2)}, u32[]{:S(2)}) collective-permute-start(f32[64,128]{1,0:T(8,128)S(1)} %filter_grad.1.refs_8_), channel_id=1, source_target_pairs={{0,16},{4,20},{8,24},{12,28},{16,0},{20,4},{24,8},{28,12},{32,48},... | collective-permute-start | bytes 98312 | tf_op jit(solution)/shard_map/ppermute | solution.py:444
  64.6 2.3 %collective-permute-done.32 = f32[64,128]{1,0:T(8,128)S(1)} collective-permute-done((f32[64,128]{1,0:T(8,128)S(1)}, f32[64,128]{1,0:T(8,128)S(1)}, u32[]{:S(2)}, u32[]{:S(2)}) %collective-permute-start.32) | collective-permute-done | bytes 32800 | tf_op jit(solution)/shard_map/ppermute | solution.py:444
  68.2 1.9 %collective-permute-start.33 = (f32[64,128]{1,0:T(8,128)S(1)}, f32[64,128]{1,0:T(8,128)S(1)}, u32[]{:S(2)}, u32[]{:S(2)}) collective-permute-start(f32[64,128]{1,0:T(8,128)S(1)} %add.18), channel_id=1, source_target_pairs={{0,32},{4,36},{8,40},{12,44},{16,48},{20,52},{24,56},{28,60},{32,0... | collective-permute-start | bytes 98312 | tf_op jit(solution)/shard_map/ppermute | solution.py:444
  70.1 3.2 %collective-permute-start.25 = (bf16[256,512]{1,0:T(8,128)(2,1)S(1)}, bf16[256,512]{1,0:T(8,128)(2,1)S(1)}, u32[]{:S(2)}, u32[]{:S(2)}) collective-permute-start(bf16[256,512]{1,0:T(8,128)(2,1)S(1)} %get-tuple-element.93), channel_id=1, source_target_pairs={{0,12},{4,0},{8,4},{12,8},{16,28},{20,16},{24,20},{28,24},{32,44},... | collective-permute-start | bytes 786440 | tf_op jit(solution)/shard_map/ppermute | solution.py:36
  77.1 6.7 %collective-permute-done.34 = f32[64,128]{1,0:T(8,128)S(1)} collective-permute-done((f32[64,128]{1,0:T(8,128)S(1)}, f32[64,128]{1,0:T(8,128)S(1)}, u32[]{:S(2)}, u32[]{:S(2)}) %collective-permute-start.34) | collective-permute-done | bytes 32800 | tf_op jit(solution)/shard_map/ppermute | solution.py:444
  83.7 2.3 %collective-permute-start.21 = (bf16[256,512]{1,0:T(8,128)(2,1)S(1)}, bf16[256,512]{1,0:T(8,128)(2,1)S(1)}, u32[]{:S(2)}, u32[]{:S(2)}) collective-permute-start(bf16[256,512]{1,0:T(8,128)(2,1)S(1)} %get-tuple-element.89), channel_id=1, source_target_pairs={{0,32},{4,36},{8,40},{12,44},{16,48},{20,52},{24,56},{28,60},{32,0... | collective-permute-start | bytes 786440 | tf_op jit(solution)/shard_map/ppermute | solution.py:33
  87.4 3.1 %collective-permute-start.8 = (bf16[128,1024]{1,0:T(8,128)(2,1)S(1)}, bf16[128,1024]{1,0:T(8,128)(2,1)S(1)}, u32[]{:S(2)}, u32[]{:S(2)}) collective-permute-start(bf16[128,1024]{1,0:T(8,128)(2,1)S(1)} %slice.11), channel_id=1, source_target_pairs={{4,0},{8,4},{12,8},{16,12},{20,16},{24,20},{28,24},{32,28},{36,32}... | collective-permute-start | bytes 786440 | tf_op jit(solution)/shard_map/ppermute | solution.py:46
  92.0 2.5 %collective-permute-done.21.refs_2_ = bf16[256,512]{1,0:T(8,128)(2,1)S(1)} collective-permute-done((bf16[256,512]{1,0:T(8,128)(2,1)S(1)}, bf16[256,512]{1,0:T(8,128)(2,1)S(1)}, u32[]{:S(2)}, u32[]{:S(2)}) %collective-permute-start.21) | collective-permute-done | bytes 262176 | tf_op jit(solution)/shard_map/ppermute | solution.py:33
  94.5 3.9 %collective-permute-done.22.refs_3_ = bf16[256,512]{1,0:T(8,128)(2,1)S(1)} collective-permute-done((bf16[256,512]{1,0:T(8,128)(2,1)S(1)}, bf16[256,512]{1,0:T(8,128)(2,1)S(1)}, u32[]{:S(2)}, u32[]{:S(2)}) %collective-permute-start.22) | collective-permute-done | bytes 262176 | tf_op jit(solution)/shard_map/ppermute | solution.py:33
  98.6 6.0 %collective-permute-start.29 = (bf16[64,512]{1,0:T(8,128)(2,1)S(1)}, bf16[64,512]{1,0:T(8,128)(2,1)S(1)}, u32[]{:S(2)}, u32[]{:S(2)}) collective-permute-start(bf16[64,512]{1,0:T(8,128)(2,1)S(1)} %get-tuple-element.100), channel_id=1, source_target_pairs={{0,64},{64,128},{128,192},{192,0},{1,65},{65,129},{129,193},{193,1... | collective-permute-start | bytes 196616 | tf_op jit(solution)/shard_map/ppermute | solution.py:38
  106.0 3.1 %collective-permute-start.31 = (bf16[64,512]{1,0:T(8,128)(2,1)S(1)}, bf16[64,512]{1,0:T(8,128)(2,1)S(1)}, u32[]{:S(2)}, u32[]{:S(2)}) collective-permute-start(bf16[64,512]{1,0:T(8,128)(2,1)S(1)} %get-tuple-element.102), channel_id=1, source_target_pairs={{0,192},{64,0},{128,64},{192,128},{1,193},{65,1},{129,65},{193,129... | collective-permute-start | bytes 196616 | tf_op jit(solution)/shard_map/ppermute | solution.py:38
  110.1 4.1 %collective-permute-start.27 = (bf16[64,512]{1,0:T(8,128)(2,1)S(1)}, bf16[64,512]{1,0:T(8,128)(2,1)S(1)}, u32[]{:S(2)}, u32[]{:S(2)}) collective-permute-start(bf16[64,512]{1,0:T(8,128)(2,1)S(1)} %get-tuple-element.98), channel_id=1, source_target_pairs={{0,128},{64,192},{128,0},{192,64},{1,129},{65,193},{129,1},{193,65... | collective-permute-start | bytes 196616 | tf_op jit(solution)/shard_map/ppermute | solution.py:38
  114.6 1.4 %collective-permute-start.37 = (f32[64,128]{1,0:T(8,128)S(1)}, f32[64,128]{1,0:T(8,128)S(1)}, u32[]{:S(2)}, u32[]{:S(2)}) collective-permute-start(f32[64,128]{1,0:T(8,128)S(1)} %add.22), channel_id=1, source_target_pairs={{0,128},{64,192},{128,0},{192,64},{1,129},{65,193},{129,1},{193,65... | collective-permute-start | bytes 98312 | tf_op jit(solution)/shard_map/ppermute | solution.py:442
  116.0 3.4 %input_grad.1 = bf16[256,1024]{1,0:T(8,128)(2,1)} custom-call(bf16[64,128]{1,0:T(8,128)(2,1)} %refs_0_.3, bf16[256,1024]{1,0:T(8,128)(2,1)S(1)} %get-tuple-element.71.refs_8_.refs_2_.refs_1_, bf16[128,1024]{1,0:T(8,128)(2,1)S(1)} %collective-permute-done.8.refs_2_, f32[64,512]{1,0:T(8,128)S(1)} %get-tuple-element.95.refs_3_.refs_4_), custom_call_target="tpu_custom_call" | custom-call | flops 4000000000 | tf_op jit(solution)/shard_map/input_grad/pallas_call | solution.py:88
  (67 shorter events, 22.2 us)
Async XLA Ops:
  0.6 11.8 %collective-permute-start.1 = (bf16[64,4096]{1,0:T(8,128)(2,1)}, bf16[64,4096]{1,0:T(8,128)(2,1)S(1)}, u32[]{:S(2)}, u32[]{:S(2)}) collective-permute-start(bf16[64,4096]{1,0:T(8,128)(2,1)} %bitcast.7), channel_id=1, source_target_pairs={{0,1},{1,0},{2,3},{3,2},{4,5},{5,4},{6,7},{7,6},{8,9},{9,8},{10,11... | collective-permute-start | bytes 1572872 | tf_op jit(solution)/shard_map/ppermute | solution.py:41
  1.7 12.7 %collective-permute-start.2 = (bf16[128,1024]{1,0:T(8,128)(2,1)S(1)}, bf16[128,1024]{1,0:T(8,128)(2,1)S(1)}, u32[]{:S(2)}, u32[]{:S(2)}) collective-permute-start(bf16[128,1024]{1,0:T(8,128)(2,1)S(1)} %slice_bitcast_fusion), channel_id=1, source_target_pairs={{0,4},{4,8},{8,12},{12,16},{16,20},{20,24},{24,28},{28,32},{32,36}... | collective-permute-start | bytes 786440 | tf_op jit(solution)/shard_map/ppermute | solution.py:46
  5.2 23.3 %collective-permute-start = (bf16[64,4096]{1,0:T(8,128)(2,1)}, bf16[64,4096]{1,0:T(8,128)(2,1)S(1)}, u32[]{:S(2)}, u32[]{:S(2)}) collective-permute-start(bf16[64,4096]{1,0:T(8,128)(2,1)} %bitcast.8), channel_id=1, source_target_pairs={{0,2},{1,3},{2,0},{3,1},{4,6},{5,7},{6,4},{7,5},{8,10},{9,11},{10,... | collective-permute-start | bytes 1572872 | tf_op jit(solution)/shard_map/ppermute | solution.py:40
  17.9 12.0 %collective-permute-start.4 = (bf16[384,512]{1,0:T(8,128)(2,1)S(1)}, bf16[384,512]{1,0:T(8,128)(2,1)S(1)}, u32[]{:S(2)}, u32[]{:S(2)}) collective-permute-start(bf16[384,512]{1,0:T(8,128)(2,1)S(1)} %get-tuple-element.65), channel_id=1, source_target_pairs={{0,4},{4,8},{8,12},{12,0},{16,20},{20,24},{24,28},{28,16},{32,36},... | collective-permute-start | bytes 1179656 | tf_op jit(solution)/shard_map/ppermute | solution.py:36
  19.3 10.7 %collective-permute-start.3 = (bf16[384,512]{1,0:T(8,128)(2,1)S(1)}, bf16[384,512]{1,0:T(8,128)(2,1)S(1)}, u32[]{:S(2)}, u32[]{:S(2)}) collective-permute-start(bf16[384,512]{1,0:T(8,128)(2,1)S(1)} %get-tuple-element.64), channel_id=1, source_target_pairs={{0,16},{4,20},{8,24},{12,28},{16,32},{20,36},{24,40},{28,44},{32,4... | collective-permute-start | bytes 1179656 | tf_op jit(solution)/shard_map/ppermute | solution.py:33
  20.8 10.4 %collective-permute-start.5 = (bf16[384,512]{1,0:T(8,128)(2,1)S(1)}, bf16[384,512]{1,0:T(8,128)(2,1)S(1)}, u32[]{:S(2)}, u32[]{:S(2)}) collective-permute-start(bf16[384,512]{1,0:T(8,128)(2,1)S(1)} %get-tuple-element.66), channel_id=1, source_target_pairs={{0,48},{4,52},{8,56},{12,60},{16,0},{20,4},{24,8},{28,12},{32,16},... | collective-permute-start | bytes 1179656 | tf_op jit(solution)/shard_map/ppermute | solution.py:33
  21.4 10.1 %collective-permute-start.6 = (bf16[384,512]{1,0:T(8,128)(2,1)S(1)}, bf16[384,512]{1,0:T(8,128)(2,1)S(1)}, u32[]{:S(2)}, u32[]{:S(2)}) collective-permute-start(bf16[384,512]{1,0:T(8,128)(2,1)S(1)} %get-tuple-element.67), channel_id=1, source_target_pairs={{0,12},{4,0},{8,4},{12,8},{16,28},{20,16},{24,20},{28,24},{32,44},... | collective-permute-start | bytes 1179656 | tf_op jit(solution)/shard_map/ppermute | solution.py:36
  31.5 13.0 %collective-permute-start.10 = (bf16[384,512]{1,0:T(8,128)(2,1)S(1)}, bf16[384,512]{1,0:T(8,128)(2,1)S(1)}, u32[]{:S(2)}, u32[]{:S(2)}) collective-permute-start(bf16[384,512]{1,0:T(8,128)(2,1)S(1)} %get-tuple-element.77), channel_id=1, source_target_pairs={{0,8},{4,12},{8,0},{12,4},{16,24},{20,28},{24,16},{28,20},{32,40},... | collective-permute-start | bytes 1179656 | tf_op jit(solution)/shard_map/ppermute | solution.py:36
  33.9 13.6 %collective-permute-start.9 = (bf16[384,512]{1,0:T(8,128)(2,1)S(1)}, bf16[384,512]{1,0:T(8,128)(2,1)S(1)}, u32[]{:S(2)}, u32[]{:S(2)}) collective-permute-start(bf16[384,512]{1,0:T(8,128)(2,1)S(1)} %get-tuple-element.74), channel_id=1, source_target_pairs={{0,32},{4,36},{8,40},{12,44},{16,48},{20,52},{24,56},{28,60},{32,0... | collective-permute-start | bytes 1179656 | tf_op jit(solution)/shard_map/ppermute | solution.py:33
  36.6 13.4 %collective-permute-start.11 = (bf16[128,512]{1,0:T(8,128)(2,1)S(1)}, bf16[128,512]{1,0:T(8,128)(2,1)S(1)}, u32[]{:S(2)}, u32[]{:S(2)}) collective-permute-start(bf16[128,512]{1,0:T(8,128)(2,1)S(1)} %get-tuple-element.78), channel_id=1, source_target_pairs={{0,16},{4,20},{8,24},{12,28},{16,32},{20,36},{24,40},{28,44},{32,4... | collective-permute-start | bytes 393224 | tf_op jit(solution)/shard_map/ppermute | solution.py:33
  37.8 19.7 %collective-permute-start.12 = (bf16[128,512]{1,0:T(8,128)(2,1)S(1)}, bf16[128,512]{1,0:T(8,128)(2,1)S(1)}, u32[]{:S(2)}, u32[]{:S(2)}) collective-permute-start(bf16[128,512]{1,0:T(8,128)(2,1)S(1)} %get-tuple-element.79), channel_id=1, source_target_pairs={{0,32},{4,36},{8,40},{12,44},{16,48},{20,52},{24,56},{28,60},{32,0... | collective-permute-start | bytes 393224 | tf_op jit(solution)/shard_map/ppermute | solution.py:33
  40.0 17.6 %collective-permute-start.13 = (bf16[128,512]{1,0:T(8,128)(2,1)S(1)}, bf16[128,512]{1,0:T(8,128)(2,1)S(1)}, u32[]{:S(2)}, u32[]{:S(2)}) collective-permute-start(bf16[128,512]{1,0:T(8,128)(2,1)S(1)} %get-tuple-element.80), channel_id=1, source_target_pairs={{0,48},{4,52},{8,56},{12,60},{16,0},{20,4},{24,8},{28,12},{32,16},... | collective-permute-start | bytes 393224 | tf_op jit(solution)/shard_map/ppermute | solution.py:33
  44.5 13.1 %collective-permute-start.14 = (bf16[128,512]{1,0:T(8,128)(2,1)S(1)}, bf16[128,512]{1,0:T(8,128)(2,1)S(1)}, u32[]{:S(2)}, u32[]{:S(2)}) collective-permute-start(bf16[128,512]{1,0:T(8,128)(2,1)S(1)} %get-tuple-element.81), channel_id=1, source_target_pairs={{0,4},{4,8},{8,12},{12,0},{16,20},{20,24},{24,28},{28,16},{32,36},... | collective-permute-start | bytes 393224 | tf_op jit(solution)/shard_map/ppermute | solution.py:36
  47.5 10.1 %collective-permute-start.15 = (bf16[128,512]{1,0:T(8,128)(2,1)S(1)}, bf16[128,512]{1,0:T(8,128)(2,1)S(1)}, u32[]{:S(2)}, u32[]{:S(2)}) collective-permute-start(bf16[128,512]{1,0:T(8,128)(2,1)S(1)} %get-tuple-element.82), channel_id=1, source_target_pairs={{0,8},{4,12},{8,0},{12,4},{16,24},{20,28},{24,16},{28,20},{32,40},... | collective-permute-start | bytes 393224 | tf_op jit(solution)/shard_map/ppermute | solution.py:36
  50.0 7.6 %collective-permute-start.16 = (bf16[128,512]{1,0:T(8,128)(2,1)S(1)}, bf16[128,512]{1,0:T(8,128)(2,1)S(1)}, u32[]{:S(2)}, u32[]{:S(2)}) collective-permute-start(bf16[128,512]{1,0:T(8,128)(2,1)S(1)} %get-tuple-element.83), channel_id=1, source_target_pairs={{0,12},{4,0},{8,4},{12,8},{16,28},{20,16},{24,20},{28,24},{32,44},... | collective-permute-start | bytes 393224 | tf_op jit(solution)/shard_map/ppermute | solution.py:36
  57.9 9.0 %collective-permute-start.17 = (bf16[2048,256]{1,0:T(8,128)(2,1)S(1)}, bf16[2048,256]{1,0:T(8,128)(2,1)S(1)}, u32[]{:S(2)}, u32[]{:S(2)}) collective-permute-start(bf16[2048,256]{1,0:T(8,128)(2,1)S(1)} %turn_early.1.refs_4_.refs_0_), channel_id=1, source_target_pairs={{0,1},{1,0},{2,3},{3,2},{4,5},{5,4},{6,7},{7,6},{8,9},{9,8},{10,11... | collective-permute-start | bytes 3145736 | tf_op jit(solution)/shard_map/ppermute | solution.py:41
  58.2 8.7 %collective-permute-start.19 = (bf16[1024,256]{1,0:T(8,128)(2,1)S(1)}, bf16[1024,256]{1,0:T(8,128)(2,1)S(1)}, u32[]{:S(2)}, u32[]{:S(2)}) collective-permute-start(bf16[1024,256]{1,0:T(8,128)(2,1)S(1)} %turn_late.2.refs_4_.refs_2_), channel_id=1, source_target_pairs={{0,1},{1,0},{2,3},{3,2},{4,5},{5,4},{6,7},{7,6},{8,9},{9,8},{10,11... | collective-permute-start | bytes 1572872 | tf_op jit(solution)/shard_map/ppermute | solution.py:41
  59.0 14.3 %collective-permute-start.18 = (bf16[1024,256]{1,0:T(8,128)(2,1)S(1)}, bf16[1024,256]{1,0:T(8,128)(2,1)S(1)}, u32[]{:S(2)}, u32[]{:S(2)}) collective-permute-start(bf16[1024,256]{1,0:T(8,128)(2,1)S(1)} %turn_late.3.refs_3_.refs_2_), channel_id=1, source_target_pairs={{0,1},{1,0},{2,3},{3,2},{4,5},{5,4},{6,7},{7,6},{8,9},{9,8},{10,11... | collective-permute-start | bytes 1572872 | tf_op jit(solution)/shard_map/ppermute | solution.py:41
  70.1 15.9 %collective-permute-start.23 = (bf16[256,512]{1,0:T(8,128)(2,1)S(1)}, bf16[256,512]{1,0:T(8,128)(2,1)S(1)}, u32[]{:S(2)}, u32[]{:S(2)}) collective-permute-start(bf16[256,512]{1,0:T(8,128)(2,1)S(1)} %get-tuple-element.91), channel_id=1, source_target_pairs={{0,4},{4,8},{8,12},{12,0},{16,20},{20,24},{24,28},{28,16},{32,36},... | collective-permute-start | bytes 786440 | tf_op jit(solution)/shard_map/ppermute | solution.py:36
  70.1 17.3 %collective-permute-start.25 = (bf16[256,512]{1,0:T(8,128)(2,1)S(1)}, bf16[256,512]{1,0:T(8,128)(2,1)S(1)}, u32[]{:S(2)}, u32[]{:S(2)}) collective-permute-start(bf16[256,512]{1,0:T(8,128)(2,1)S(1)} %get-tuple-element.93), channel_id=1, source_target_pairs={{0,12},{4,0},{8,4},{12,8},{16,28},{20,16},{24,20},{28,24},{32,44},... | collective-permute-start | bytes 786440 | tf_op jit(solution)/shard_map/ppermute | solution.py:36
  73.3 17.2 %collective-permute-start.24 = (bf16[256,512]{1,0:T(8,128)(2,1)S(1)}, bf16[256,512]{1,0:T(8,128)(2,1)S(1)}, u32[]{:S(2)}, u32[]{:S(2)}) collective-permute-start(bf16[256,512]{1,0:T(8,128)(2,1)S(1)} %get-tuple-element.92), channel_id=1, source_target_pairs={{0,8},{4,12},{8,0},{12,4},{16,24},{20,28},{24,16},{28,20},{32,40},... | collective-permute-start | bytes 786440 | tf_op jit(solution)/shard_map/ppermute | solution.py:36
  74.6 9.1 %collective-permute-start.34 = (f32[64,128]{1,0:T(8,128)S(1)}, f32[64,128]{1,0:T(8,128)S(1)}, u32[]{:S(2)}, u32[]{:S(2)}) collective-permute-start(f32[64,128]{1,0:T(8,128)S(1)} %add.19), channel_id=1, source_target_pairs={{0,4},{4,0},{8,12},{12,8},{16,20},{20,16},{24,28},{28,24},{32,36},... | collective-permute-start | bytes 98312 | tf_op jit(solution)/shard_map/ppermute | solution.py:444
  75.8 16.1 %collective-permute-start.20 = (bf16[256,512]{1,0:T(8,128)(2,1)S(1)}, bf16[256,512]{1,0:T(8,128)(2,1)S(1)}, u32[]{:S(2)}, u32[]{:S(2)}) collective-permute-start(bf16[256,512]{1,0:T(8,128)(2,1)S(1)} %get-tuple-element.88), channel_id=1, source_target_pairs={{0,16},{4,20},{8,24},{12,28},{16,32},{20,36},{24,40},{28,44},{32,4... | collective-permute-start | bytes 786440 | tf_op jit(solution)/shard_map/ppermute | solution.py:33
  83.7 10.7 %collective-permute-start.21 = (bf16[256,512]{1,0:T(8,128)(2,1)S(1)}, bf16[256,512]{1,0:T(8,128)(2,1)S(1)}, u32[]{:S(2)}, u32[]{:S(2)}) collective-permute-start(bf16[256,512]{1,0:T(8,128)(2,1)S(1)} %get-tuple-element.89), channel_id=1, source_target_pairs={{0,32},{4,36},{8,40},{12,44},{16,48},{20,52},{24,56},{28,60},{32,0... | collective-permute-start | bytes 786440 | tf_op jit(solution)/shard_map/ppermute | solution.py:33
  86.0 12.4 %collective-permute-start.22 = (bf16[256,512]{1,0:T(8,128)(2,1)S(1)}, bf16[256,512]{1,0:T(8,128)(2,1)S(1)}, u32[]{:S(2)}, u32[]{:S(2)}) collective-permute-start(bf16[256,512]{1,0:T(8,128)(2,1)S(1)} %get-tuple-element.90), channel_id=1, source_target_pairs={{0,48},{4,52},{8,56},{12,60},{16,0},{20,4},{24,8},{28,12},{32,16},... | collective-permute-start | bytes 786440 | tf_op jit(solution)/shard_map/ppermute | solution.py:33
  87.4 22.7 %collective-permute-start.8 = (bf16[128,1024]{1,0:T(8,128)(2,1)S(1)}, bf16[128,1024]{1,0:T(8,128)(2,1)S(1)}, u32[]{:S(2)}, u32[]{:S(2)}) collective-permute-start(bf16[128,1024]{1,0:T(8,128)(2,1)S(1)} %slice.11), channel_id=1, source_target_pairs={{4,0},{8,4},{12,8},{16,12},{20,16},{24,20},{28,24},{32,28},{36,32}... | collective-permute-start | bytes 786440 | tf_op jit(solution)/shard_map/ppermute | solution.py:46
  90.6 14.9 %collective-permute-start.35 = (f32[64,128]{1,0:T(8,128)S(1)}, f32[64,128]{1,0:T(8,128)S(1)}, u32[]{:S(2)}, u32[]{:S(2)}) collective-permute-start(f32[64,128]{1,0:T(8,128)S(1)} %add.20), channel_id=1, source_target_pairs={{0,8},{4,12},{8,0},{12,4},{16,24},{20,28},{24,16},{28,20},{32,40},... | collective-permute-start | bytes 98312 | tf_op jit(solution)/shard_map/ppermute | solution.py:444
  98.6 15.6 %collective-permute-start.29 = (bf16[64,512]{1,0:T(8,128)(2,1)S(1)}, bf16[64,512]{1,0:T(8,128)(2,1)S(1)}, u32[]{:S(2)}, u32[]{:S(2)}) collective-permute-start(bf16[64,512]{1,0:T(8,128)(2,1)S(1)} %get-tuple-element.100), channel_id=1, source_target_pairs={{0,64},{64,128},{128,192},{192,0},{1,65},{65,129},{129,193},{193,1... | collective-permute-start | bytes 196616 | tf_op jit(solution)/shard_map/ppermute | solution.py:38
  104.6 10.0 %collective-permute-start.30 = (bf16[64,512]{1,0:T(8,128)(2,1)S(1)}, bf16[64,512]{1,0:T(8,128)(2,1)S(1)}, u32[]{:S(2)}, u32[]{:S(2)}) collective-permute-start(bf16[64,512]{1,0:T(8,128)(2,1)S(1)} %get-tuple-element.101), channel_id=1, source_target_pairs={{0,128},{64,192},{128,0},{192,64},{1,129},{65,193},{129,1},{193,65... | collective-permute-start | bytes 196616 | tf_op jit(solution)/shard_map/ppermute | solution.py:38
  106.0 13.5 %collective-permute-start.31 = (bf16[64,512]{1,0:T(8,128)(2,1)S(1)}, bf16[64,512]{1,0:T(8,128)(2,1)S(1)}, u32[]{:S(2)}, u32[]{:S(2)}) collective-permute-start(bf16[64,512]{1,0:T(8,128)(2,1)S(1)} %get-tuple-element.102), channel_id=1, source_target_pairs={{0,192},{64,0},{128,64},{192,128},{1,193},{65,1},{129,65},{193,129... | collective-permute-start | bytes 196616 | tf_op jit(solution)/shard_map/ppermute | solution.py:38
  110.1 9.4 %collective-permute-start.26 = (bf16[64,512]{1,0:T(8,128)(2,1)S(1)}, bf16[64,512]{1,0:T(8,128)(2,1)S(1)}, u32[]{:S(2)}, u32[]{:S(2)}) collective-permute-start(bf16[64,512]{1,0:T(8,128)(2,1)S(1)} %get-tuple-element.97), channel_id=1, source_target_pairs={{0,64},{64,128},{128,192},{192,0},{1,65},{65,129},{129,193},{193,1... | collective-permute-start | bytes 196616 | tf_op jit(solution)/shard_map/ppermute | solution.py:38
  110.1 9.3 %collective-permute-start.27 = (bf16[64,512]{1,0:T(8,128)(2,1)S(1)}, bf16[64,512]{1,0:T(8,128)(2,1)S(1)}, u32[]{:S(2)}, u32[]{:S(2)}) collective-permute-start(bf16[64,512]{1,0:T(8,128)(2,1)S(1)} %get-tuple-element.98), channel_id=1, source_target_pairs={{0,128},{64,192},{128,0},{192,64},{1,129},{65,193},{129,1},{193,65... | collective-permute-start | bytes 196616 | tf_op jit(solution)/shard_map/ppermute | solution.py:38
  (6 other events, 30.6 us)

commit v4 on v3

--- a/solution.py
+++ b/solution.py
@@ -130,7 +130,7 @@
 
 
 def forward_kernel(filters, previous, signal, gating, *refs):
-    shifts = SIDE - 1
+    shifts = 2
     early, (response, gated), sends = refs[: 2 * shifts], refs[2 * shifts : 2 * shifts + 2], refs[2 * shifts + 2 : -1]
     stack = refs[-1]
     rows = first_rows(filters[...], True)
@@ -166,7 +166,7 @@
         + [((length + rows, width), BF16)] * len(early),
         [pltpu.VMEM((2, PER_TILE * TAPS, 2 * TAPS), BF16)],
     )
-    return response, gated, sends[: SIDE - 1], sends[SIDE - 1 :]
+    return response, gated, sends[:2], sends[2:]
 
 
 def input_grad_kernel(filters, conv_grad, following, grad_input, stack):
@@ -193,7 +193,6 @@
         [(conv_grad.shape, BF16)],
         [pltpu.VMEM((2, PER_TILE * TAPS, 2 * TAPS), BF16)],
         after,
-        4,
     )[0]
 
 
@@ -265,6 +264,36 @@
     return outs[:SIDE], outs[SIDE:]
 
 
+def relay_kernel(count, mine, *refs):
+    before_x, after_x, before_y, after_y, opposite_x, opposite_y = refs[:6]
+    outs = refs[6 + count :]
+    part = opposite_x.shape[0]
+    pack_kernel(mine, *(out.at[:part] for out in outs))
+    for first, before, opposite, after in (
+        (0, before_x, opposite_x, after_x),
+        (SIDE, before_y, opposite_y, after_y),
+    ):
+        outs[first + 1][part:] = before[:TAPS]
+        outs[first + 2][part:] = opposite[...]
+        outs[first + 3][part:] = after[TAPS : 2 * TAPS]
+
+
+def relay(mine, got_x, got_y, opposite_x, opposite_y, after):
+    rows, width = opposite_x.shape
+    got = [
+        (part, whole((2 * TAPS, width))) for part in (got_x[0], got_x[1], got_y[0], got_y[1])
+    ]
+    shapes = ([(rows, width)] + [(rows + TAPS, width)] * (SIDE - 1)) * 2
+
+    def kernel(*refs):
+        relay_kernel(0, *refs)
+
+    outs = once(
+        kernel, "relay", [mine, *got, opposite_x, opposite_y], [(shape, BF16) for shape in shapes], (), after
+    )
+    return outs[:SIDE], outs[SIDE:]
+
+
 def turn_into(parts, out, base, me):
     part = parts[0].shape[0] // 2
     for fold in range(2):
@@ -272,13 +301,13 @@
             block = jnp.concatenate(
                 [ref[fold * part : (fold + 1) * part] for ref in parts[2 * pair : 2 * pair + 2]], 0
             )
-            whole = block.T
+            transposed = block.T
             for d in range(2):
                 for q in range(SIDE):
                     to = (q - me + SIDE) % SIDE
                     rows = pl.ds(pl.multiple_of(base + to * WIDE + (2 * fold + d) * HALF, HALF), HALF)
                     start = d * WIDE + q * HALF
-                    out[rows, pair * LANES : (pair + 1) * LANES] = whole[start : start + HALF]
+                    out[rows, pair * LANES : (pair + 1) * LANES] = transposed[start : start + HALF]
 
 
 def turn_early_kernel(*refs):
@@ -288,20 +317,24 @@
     turn_into(refs[SIDE : 2 * SIDE], out, out.shape[0] // 2, x)
 
 
-def turn_early(own_x, got_x, own_y, got_y, after):
+def turn_early(own_x, got_x, late_x, own_y, got_y, late_y, after):
     rows, width = own_x.shape
-    count = got_x[0].shape[0] // rows
-    tail = whole((rows, width), (count - 1, 0))
-    parts = [own_x, *[(got, tail) for got in got_x], own_y, *[(got, tail) for got in got_y]]
+    parts = []
+    for own, got, late in ((own_x, got_x, late_x), (own_y, got_y, late_y)):
+        for part in (own, got[0], late[2], got[1]):
+            parts.append((part, whole((rows, width), (part.shape[0] // rows - 1, 0))))
     return once(turn_early_kernel, "turn_early", parts, [((4 * width, WIDE), BF16)], (), after)[0]
 
 
 def turn_late(parts, axis, after=()):
+    rows, width = parts[0].shape
+
     def kernel(*refs):
         x, y, _, _, _ = spot()
         turn_into(refs[:SIDE], refs[-1], 0, y if axis == "x" else x)
 
-    return once(kernel, "turn_late", parts, [((2 * parts[0].shape[1], WIDE), BF16)], (), after)[0]
+    ins = [(part, whole((rows, width))) for part in parts]
+    return once(kernel, "turn_late", ins, [((2 * width, WIDE), BF16)], (), after)[0]
 
 
 def project_kernel(mine, other, weight, gating, response, *refs):
@@ -355,14 +388,17 @@
     )(mine, other, weight, gating, response, *done, *after)
 
 
-def weight_kernel(early, early_other, late, late_other, gated, *refs):
+def weight_kernel(early, early_other, late, late_other, gated, first, third, before, after, *outs):
     _, _, _, half, core = spot()
-    got, outs = refs[: SIDE - 1], refs[SIDE - 1 :]
     part = WIDE // SIDE
     tokens = []
     for h, c in ((half, core), (half, 1 - core), (1 - half, core), (1 - half, 1 - core)):
-        rows = aligned(2 * h + c, part)
-        tokens += [gated[rows, :]] + [ref[rows, :] for ref in got]
+        rows, own_rows = aligned(2 * h + c, part), aligned(c, part)
+        upper = jnp.broadcast_to(h, (part, gated.shape[1])) == 0
+        opposite = jnp.where(
+            upper, before[own_rows, :].astype(F32), after[own_rows, :].astype(F32)
+        ).astype(BF16)
+        tokens += [gated[rows, :], first[rows, :], opposite, third[rows, :]]
     tokens = jnp.concatenate(tokens, 0)
     for s, out in enumerate(outs):
         rows = slice(s * WIDE, (s + 1) * WIDE)
@@ -370,21 +406,24 @@
         out[...] = jnp.dot(features, tokens, preferred_element_type=F32).astype(out.dtype)
 
 
-def weight_part(which, early, early_other, late, late_other, gated, got, after=()):
+def weight_part(which, early, early_other, turned, turned_other, gated, got, late, after=()):
     length = gated.shape[0]
-    features = late.shape[0]
+    features = turned.shape[0]
     width = got[0].shape[1]
     spec = whole((features, WIDE), (which, 0))
+    below = whole((TAPS, width), (1, 0))
     return once(
         weight_kernel,
         "weight_part",
         [
             (early, spec),
             (early_other, spec),
-            late,
-            late_other,
+            turned,
+            turned_other,
             (gated, whole((length, width), (0, which))),
             *[(one, whole((length, width))) for one in got],
+            (late[1], below),
+            (late[3], below),
         ],
         [((features // SIDE, width), F32 if s == 0 else BF16) for s in range(SIDE)],
         (),
@@ -395,42 +434,43 @@
 
 def first_sum_kernel(*refs):
     _, _, z, _, _ = spot()
-    outs, kept = refs[SIDE : 2 * SIDE], refs[2 * SIDE]
-    total = refs[0][...]
-    for ref in refs[1:SIDE]:
-        total = total + ref[...].astype(F32)
+    outs, kept = refs[2 * SIDE : 3 * SIDE], refs[3 * SIDE]
+    width = refs[0].shape[1]
     run = kept.shape[0] // SIDE
-    for d in range(SIDE):
-        kept[aligned((d - z + SIDE) % SIDE, run), :] = total[d * run : (d + 1) * run]
+    for which in range(2):
+        parts = refs[which * SIDE : (which + 1) * SIDE]
+        total = parts[0][...]
+        for ref in parts[1:]:
+            total = total + ref[...].astype(F32)
+        for d in range(SIDE):
+            rows = aligned((d - z + SIDE) % SIDE, run)
+            kept[rows, which * width : (which + 1) * width] = total[d * run : (d + 1) * run]
     for s, out in enumerate(outs):
         out[...] = kept[s * run : (s + 1) * run, :].astype(out.dtype)
 
 
-def first_sum(parts, after=()):
-    rows, width = parts[0].shape
+def first_sum(parts_x, parts_y, after=()):
+    rows, width = parts_x[0].shape
     return once(
         first_sum_kernel,
         "first_sum",
-        parts,
-        [((rows // SIDE, width), F32 if s == 0 else BF16) for s in range(SIDE)],
-        [pltpu.VMEM((rows, width), F32)],
+        [*parts_x, *parts_y],
+        [((rows // SIDE, 2 * width), F32 if s == 0 else BF16) for s in range(SIDE)],
+        [pltpu.VMEM((rows, 2 * width), F32)],
         after,
         1,
     )
 
 
-def last_sum(parts_x, parts_y, scale):
+def last_sum(parts, scale):
     def kernel(*refs):
         out = refs[-1]
-        width = refs[0].shape[1]
-        for which in range(2):
-            total = refs[which * SIDE][...]
-            for ref in refs[which * SIDE + 1 : (which + 1) * SIDE]:
-                total = total + ref[...].astype(F32)
-            out[:, which * width : (which + 1) * width] = total * scale
-
-    rows, width = parts_x[0].shape
-    return once(kernel, "last_sum", [*parts_x, *parts_y], [((rows, 2 * width), F32)])[0]
+        total = refs[0][...]
+        for ref in refs[1:SIDE]:
+            total = total + ref[...].astype(F32)
+        out[...] = total * scale
+
+    return once(kernel, "last_sum", parts, [(parts[0].shape, F32)])[0]
 
 
 def tied(x, *after):
@@ -444,8 +484,8 @@
     return lax.ppermute(x, "ctx", [(i, i ^ step) for i in range(SIDE * SIDE)])
 
 
-def paired(x, axis, by, after=()):
-    return x + partnered(tied(x, *after), axis, by)
+def paired(x, axis, by, before=()):
+    return x + partnered(tied(x, *before), axis, by)
 
 
 def exchanged(parts, axis):
@@ -464,20 +504,17 @@
     late = moved(grads, "half", 1)
     previous = shifted(halo_sent, 1)
     early_other = moved(grads, "core", 1)
-    early_x, early_y = pack(resident(grads), (early_other,))
+    grads = resident(grads)
+    early_x, early_y = pack(grads, (early_other,))
     response, gated, sends_x, sends_y = forward(
-        filters, previous, signal, gating, [*early_x[1:], *early_y[1:]]
-    )
-    got_x, got_y = [], []
-    for got, axis, parts in ((got_x, "x", sends_x), (got_y, "y", sends_y)):
-        first = moved(parts[0], axis, 1)
-        got += [first, moved(tied(parts[1], first), axis, 2), moved(parts[2], axis, 3)]
-    conv_early, gate_early = project(resident(grads), early_other, weight, gating, response)
-
-    late_other = moved(tied(late, conv_early, got_x[0], got_y[0], got_x[2], got_y[2]), "core", 1)
-    late_x, late_y = pack(late, (late_other,))
-    late_x = exchanged(late_x, "x")
-    late_y = exchanged(late_y, "y")
+        filters, previous, signal, gating, [early_x[1], early_x[3], early_y[1], early_y[3]]
+    )
+    got_x = [moved(sends_x[0], "x", 1), moved(sends_x[1], "x", 3)]
+    got_y = [moved(sends_y[0], "y", 1), moved(sends_y[1], "y", 3)]
+    conv_early, gate_early = project(grads, early_other, weight, gating, response)
+
+    late_other = moved(tied(late, conv_early, *got_x, *got_y), "core", 1)
+    late_x, late_y = relay(late, got_x, got_y, early_x[2], early_y[2], (late_other,))
     conv_grad, grad_gate = project(
         late,
         late_other,
@@ -487,7 +524,10 @@
         (conv_early, gate_early),
         (late_x[0],),
     )
-    early = turn_early(early_x[0], got_x, early_y[0], got_y, (conv_grad, *late_x[1:], *late_y[1:]))
+    late_x, late_y = exchanged(late_x, "x"), exchanged(late_y, "y")
+    early = turn_early(
+        early_x[0], got_x, late_x, early_y[0], got_y, late_y, (conv_grad, *late_x[1:], *late_y[1:])
+    )
     early_swap = moved(early, "core", 1)
     turned_x = turn_late(late_x, "x", (early,))
     swap_x = moved(turned_x, "core", 1)
@@ -496,24 +536,21 @@
     following = shifted(conv_grad[:TAPS], -1)
     filter_local = filter_grad(previous, signal, conv_grad, (turned_y,))
     parts_x = weight_part(
-        0, early, early_swap, turned_x, swap_x, gated, got_x, (filter_local,)
-    )
+        0, early, early_swap, turned_x, swap_x, gated, got_x, late_x, (filter_local,)
+    )
+    filter_sum = paired(filter_local, "x", 1, (parts_x[0],))
     parts_y = weight_part(
-        1, early, early_swap, turned_y, swap_y, gated, got_y, (parts_x[0],)
-    )
-    filter_sum = paired(filter_local, "x", 1)
-    filter_sum = paired(filter_sum, "x", 2, (parts_x[0],))
-    filter_sum = paired(filter_sum, "y", 1, (parts_y[0],))
+        1, early, early_swap, turned_y, swap_y, gated, got_y, late_y, (parts_x[0], filter_sum)
+    )
+    filter_sum = paired(filter_sum, "x", 2, (parts_y[0],))
     parts_x, parts_y = exchanged(parts_x, "y"), exchanged(parts_y, "x")
-    filter_sum = paired(filter_sum, "y", 2, (parts_x[1], parts_x[3]))
-    sums_x = first_sum(parts_x)
-    filter_sum = paired(filter_sum, "z", 1, (sums_x[0],))
-    sums_y = first_sum(parts_y, (sums_x[0],))
-    filter_total = paired(filter_sum, "z", 2, (sums_y[0],))
-    grad_input = input_grad(filters, conv_grad, following, (sums_y[0],))
-    grad_weight = last_sum(
-        exchanged(sums_x, "z"), exchanged(sums_y, "z"), 1.0 / math.sqrt(tokens_all)
-    )
+    filter_sum = paired(paired(filter_sum, "y", 1, parts_x[1:]), "y", 2)
+    sums = first_sum(parts_x, parts_y, (filter_sum,))
+    grad_input = input_grad(filters, conv_grad, following, (sums[0],))
+    sums = exchanged(sums, "z")
+    filter_parts = exchanged([tied(filter_sum, sums[1])] * SIDE, "z")
+    filter_total = (filter_parts[0] + filter_parts[2]) + (filter_parts[1] + filter_parts[3])
+    grad_weight = last_sum(sums, 1.0 / math.sqrt(tokens_all))
     grad_filter = filter_total * (1.0 / math.sqrt(tokens_all * GROUP))
     return (grad_input[None], grad_gate[None], grad_weight, grad_filter)
 

time: 123 us -> 118 us (0.959)
  waiting for transfers between devices: 26.3 us -> 17.9 us
  starting transfers between devices: 63.7 us -> 67.4 us
    ppermute x6, starting transfers between devices: 14.4 us -> 22.9 us  [moved(): return lax.ppermute(x, 'dp', [(i, (i + by) % SIDE) for i in range(SIDE)])]
    ppermute x18 -> x16, waiting for transfers between devices: 16 us -> 7.94 us  [moved(): return lax.ppermute(x, 'ctx', pairs)]
    ppermute x18 -> x16, starting transfers between devices: 26.6 us -> 23.9 us  [moved(): return lax.ppermute(x, 'ctx', pairs)]
    ppermute x2 -> x0, starting transfers between devices: 2 us -> none  [partnered(): return lax.ppermute(x, 'dp', [(i, i ^ by) for i in range(SIDE)])]
    ppermute x5, waiting for transfers between devices: 0.01 us -> 1.92 us  [moved(): lax.ppermute(x, 'tp', [(i, i // 2 * 2 + (i + 1) % 2) for i in range(4)])]
    ppermute x4, waiting for transfers between devices: 8.98 us -> 7.44 us  [partnered(): return lax.ppermute(x, 'ctx', [(i, i ^ step) for i in range(SIDE * SIDE)])]
    pallas_call x13 -> x12, Pallas kernels: 17.3 us -> 17.2 us  [once(): pl.pallas_call(body, grid=(1,), in_specs=specs + [ANYWHERE] * len(after),...]
  transfers between devices with their start and end apart: 38 -> 34, of which waited for: 12 -> 11; matrix products, arithmetic and copies ran while one was open for 1% -> 1% of each run, Pallas kernels for 23% -> 24%
where the time goes in v4:
time: 118 us; the launch traced here: 116 us
  starting transfers between devices  67.4 us (57%)
  Pallas kernels  28.2 us (24%)
  waiting for transfers between devices  17.9 us (15%)
    ppermute x16, starting transfers between devices, moved(): return lax.ppermute(x, 'ctx', pairs)  23.9 us
    ppermute x6, starting transfers between devices, moved(): return lax.ppermute(x, 'dp', [(i, (i + by) % SIDE) for i in range(SIDE)])  22.9 us
    pallas_call x12, Pallas kernels, once(): pl.pallas_call(body, grid=(1,), in_specs=specs + [ANYWHERE] * len(after),...  17.2 us
    pallas_call x2, Pallas kernels, project(): pl.pallas_call(body, grid=(channels // WIDE,), in_specs=[full(mine.shape)...  11 us
    ppermute x16, waiting for transfers between devices, moved(): return lax.ppermute(x, 'ctx', pairs)  7.94 us
    ppermute x4, waiting for transfers between devices, partnered(): return lax.ppermute(x, 'ctx', [(i, i ^ step) for i in range(SIDE * SIDE)])  7.44 us
    ppermute x1, starting transfers between devices, moved(): return lax.ppermute(x, 'tp', [(i, (i + 2) % 4) for i in range(4)])  7.28 us
    ppermute x2, starting transfers between devices, shifted(): lax.ppermute(x, 'ctx', [(i, i + by) for i in range(devices) if 0 <= i + b...  6.58 us
  transfers between devices with their start and end apart: 34, of which 11 were waited for; matrix products, arithmetic and copies ran while one was open for 1% of the time, Pallas kernels for 24%

profile of v4, /device:TPU:2, one launch (start us, length us, event | category | flops | bytes accessed | tf_op | source)
XLA Modules:
  0.0 116.0 jit_solution(1849540129832432575)
XLA Ops:
  1.7 3.5 %collective-permute-start.2 = (bf16[128,1024]{1,0:T(8,128)(2,1)S(1)}, bf16[128,1024]{1,0:T(8,128)(2,1)S(1)}, u32[]{:S(2)}, u32[]{:S(2)}) collective-permute-start(bf16[128,1024]{1,0:T(8,128)(2,1)S(1)} %slice_bitcast_fusion), channel_id=1, source_target_pairs={{0,4},{4,8},{8,12},{12,16},{16,20},{20,24},{24,28},{28,32},{32,36}... | collective-permute-start | bytes 786440 | tf_op jit(solution)/shard_map/ppermute | solution.py:46
  5.2 7.3 %collective-permute-start = (bf16[64,4096]{1,0:T(8,128)(2,1)}, bf16[64,4096]{1,0:T(8,128)(2,1)S(1)}, u32[]{:S(2)}, u32[]{:S(2)}) collective-permute-start(bf16[64,4096]{1,0:T(8,128)(2,1)} %bitcast.11), channel_id=1, source_target_pairs={{0,2},{1,3},{2,0},{3,1},{4,6},{5,7},{6,4},{7,5},{8,10},{9,11},{10,... | collective-permute-start | bytes 1572872 | tf_op jit(solution)/shard_map/ppermute | solution.py:40
  12.5 1.6 %pack.1 = (bf16[128,512]{1,0:T(8,128)(2,1)S(1)}, bf16[128,512]{1,0:T(8,128)(2,1)S(1)}, bf16[128,512]{1,0:T(8,128)(2,1)S(1)}, bf16[128,512]{1,0:T(8,128)(2,1)S(1)...) custom-call(bf16[64,4096]{1,0:T(8,128)(2,1)} %bitcast.12, ...), custom_call_target="tpu_custom_call" | custom-call | tf_op jit(solution)/shard_map/pack/pallas_call | solution.py:88
  14.4 3.4 %conv_forward.1 = (f32[256,1024]{1,0:T(8,128)S(1)}, bf16[256,1024]{1,0:T(8,128)(2,1)S(1)}, bf16[384,512]{1,0:T(8,128)(2,1)S(1)}, bf16[384,512]{1,0:T(8,128)(2,1)...) custom-call(bf16[64,128]{1,0:T(8,128)(2,1)} %refs_0_.3, ...), custom_call_target="tpu_custom_call" | custom-call | tf_op jit(solution)/shard_map/conv_forward/pallas_call | solution.py:88
  17.8 1.6 %collective-permute-start.3 = (bf16[384,512]{1,0:T(8,128)(2,1)S(1)}, bf16[384,512]{1,0:T(8,128)(2,1)S(1)}, u32[]{:S(2)}, u32[]{:S(2)}) collective-permute-start(bf16[384,512]{1,0:T(8,128)(2,1)S(1)} %get-tuple-element.53), channel_id=1, source_target_pairs={{0,16},{4,20},{8,24},{12,28},{16,32},{20,36},{24,40},{28,44},{32,4... | collective-permute-start | bytes 1179656 | tf_op jit(solution)/shard_map/ppermute | solution.py:33
  20.0 1.3 %collective-permute-start.5 = (bf16[384,512]{1,0:T(8,128)(2,1)S(1)}, bf16[384,512]{1,0:T(8,128)(2,1)S(1)}, u32[]{:S(2)}, u32[]{:S(2)}) collective-permute-start(bf16[384,512]{1,0:T(8,128)(2,1)S(1)} %get-tuple-element.55), channel_id=1, source_target_pairs={{0,4},{4,8},{8,12},{12,0},{16,20},{20,24},{24,28},{28,16},{32,36},... | collective-permute-start | bytes 1179656 | tf_op jit(solution)/shard_map/ppermute | solution.py:36
  21.3 1.9 %collective-permute-start.6 = (bf16[384,512]{1,0:T(8,128)(2,1)S(1)}, bf16[384,512]{1,0:T(8,128)(2,1)S(1)}, u32[]{:S(2)}, u32[]{:S(2)}) collective-permute-start(bf16[384,512]{1,0:T(8,128)(2,1)S(1)} %get-tuple-element.56), channel_id=1, source_target_pairs={{0,12},{4,0},{8,4},{12,8},{16,28},{20,16},{24,20},{28,24},{32,44},... | collective-permute-start | bytes 1179656 | tf_op jit(solution)/shard_map/ppermute | solution.py:36
  23.2 5.2 %project_early.1 = (bf16[128,1024]{1,0:T(8,128)(2,1)S(1)}, bf16[128,1024]{1,0:T(8,128)(2,1)S(1)}) custom-call(bf16[64,4096]{1,0:T(8,128)(2,1)} %bitcast.13, bf16[64,4096]{1,0:T(8,128)(2,1)S(1)} %collective-permute-done.1.refs_1_, bf16[4096,1024]{1,0:T(8,128)(2,1)} %refs_2_.3, bf16[256,1024]{1,0:T(8,128)(2,1)} %bitcast.8, ...), custom_call_target="tpu_custom_call" | custom-call | tf_op jit(solution)/shard_map/project_early/pallas_call | solution.py:375
  29.9 1.5 %collective-permute-done.5.refs_3_.refs_5_ = bf16[384,512]{1,0:T(8,128)(2,1)S(1)} collective-permute-done((bf16[384,512]{1,0:T(8,128)(2,1)S(1)}, bf16[384,512]{1,0:T(8,128)(2,1)S(1)}, u32[]{:S(2)}, u32[]{:S(2)}) %collective-permute-start.5) | collective-permute-done | bytes 393248 | tf_op jit(solution)/shard_map/ppermute | solution.py:36
  31.4 1.9 %collective-permute-done.7.refs_7_.refs_1_ = bf16[64,4096]{1,0:T(8,128)(2,1)S(1)} collective-permute-done((bf16[64,4096]{1,0:T(8,128)(2,1)S(1)}, bf16[64,4096]{1,0:T(8,128)(2,1)S(1)}, u32[]{:S(2)}, u32[]{:S(2)}) %collective-permute-start.7) | collective-permute-done | bytes 524320 | tf_op jit(solution)/shard_map/ppermute | solution.py:41
  33.9 2.6 %collective-permute-start.10 = (bf16[256,512]{1,0:T(8,128)(2,1)S(1)}, bf16[256,512]{1,0:T(8,128)(2,1)S(1)}, u32[]{:S(2)}, u32[]{:S(2)}) collective-permute-start(bf16[256,512]{1,0:T(8,128)(2,1)S(1)} %get-tuple-element.66), channel_id=1, source_target_pairs={{0,8},{4,12},{8,0},{12,4},{16,24},{20,28},{24,16},{28,20},{32,40},... | collective-permute-start | bytes 786440 | tf_op jit(solution)/shard_map/ppermute | solution.py:36
  38.5 1.3 %collective-permute-start.13 = (bf16[256,512]{1,0:T(8,128)(2,1)S(1)}, bf16[256,512]{1,0:T(8,128)(2,1)S(1)}, u32[]{:S(2)}, u32[]{:S(2)}) collective-permute-start(bf16[256,512]{1,0:T(8,128)(2,1)S(1)} %get-tuple-element.69), channel_id=1, source_target_pairs={{0,4},{4,8},{8,12},{12,0},{16,20},{20,24},{24,28},{28,16},{32,36},... | collective-permute-start | bytes 786440 | tf_op jit(solution)/shard_map/ppermute | solution.py:36
  39.8 1.9 %collective-permute-start.14 = (bf16[256,512]{1,0:T(8,128)(2,1)S(1)}, bf16[256,512]{1,0:T(8,128)(2,1)S(1)}, u32[]{:S(2)}, u32[]{:S(2)}) collective-permute-start(bf16[256,512]{1,0:T(8,128)(2,1)S(1)} %get-tuple-element.70), channel_id=1, source_target_pairs={{0,12},{4,0},{8,4},{12,8},{16,28},{20,16},{24,20},{28,24},{32,44},... | collective-permute-start | bytes 786440 | tf_op jit(solution)/shard_map/ppermute | solution.py:36
  41.7 2.9 %collective-permute-done.10.refs_6_.refs_13_.refs_2_ = bf16[256,512]{1,0:T(8,128)(2,1)S(1)} collective-permute-done((bf16[256,512]{1,0:T(8,128)(2,1)S(1)}, bf16[256,512]{1,0:T(8,128)(2,1)S(1)}, u32[]{:S(2)}, u32[]{:S(2)}) %collective-permute-start.10) | collective-permute-done | bytes 262176 | tf_op jit(solution)/shard_map/ppermute | solution.py:36
  44.6 2.1 %collective-permute-start.9 = (bf16[256,512]{1,0:T(8,128)(2,1)S(1)}, bf16[256,512]{1,0:T(8,128)(2,1)S(1)}, u32[]{:S(2)}, u32[]{:S(2)}) collective-permute-start(bf16[256,512]{1,0:T(8,128)(2,1)S(1)} %get-tuple-element.64), channel_id=1, source_target_pairs={{0,32},{4,36},{8,40},{12,44},{16,48},{20,52},{24,56},{28,60},{32,0... | collective-permute-start | bytes 786440 | tf_op jit(solution)/shard_map/ppermute | solution.py:33
  46.8 5.8 %project_late.1 = (bf16[256,1024]{1,0:T(8,128)(2,1)S(1)}, bf16[256,1024]{1,0:T(8,128)(2,1)}) custom-call(bf16[64,4096]{1,0:T(8,128)(2,1)S(1)} %collective-permute-done.refs_0_, bf16[64,4096]{1,0:T(8,128)(2,1)S(1)} %collective-permute-done.7.refs_7_.refs_1_, bf16[4096,1024]{1,0:T(8,128)(2,1)} %refs_2_.3, bf16[256,1024]{1,0:T(8,128)(2,1)} %bitcast.9, ...), custom_call_target="tpu_custom_call" | custom-call | flops 5000000000 | tf_op jit(solution)/shard_map/project_late/pallas_call | solution.py:375
  54.4 3.8 %filter_grad.1.refs_9_ = f32[64,128]{1,0:T(8,128)S(1)} custom-call(bf16[128,1024]{1,0:T(8,128)(2,1)S(1)} %collective-permute-done.2.refs_1_.refs_0_, bf16[256,1024]{1,0:T(8,128)(2,1)} %bitcast.15, bf16[256,1024]{1,0:T(8,128)(2,1)S(1)} %get-tuple-element.62.refs_8_.refs_2_.refs_1_, bf16[1024,256]{1,0:T(8,128)(2,1)S(1)} %turn_late.3.refs_3_.refs_2_), custom_call_target="tpu_custom_call" | custom-call | flops 4000000000 | tf_op jit(solution)/shard_map/filter_grad/pallas_call | solution.py:88
  58.2 1.3 %weight_part.2 = (f32[256,512]{1,0:T(8,128)S(1)}, bf16[256,512]{1,0:T(8,128)(2,1)S(1)}, bf16[256,512]{1,0:T(8,128)(2,1)S(1)}, bf16[256,512]{1,0:T(8,128)(2,1)S(1)}) custom-call(bf16[2048,256]{1,0:T(8,128)(2,1)S(1)} %turn_early.1.refs_4_.refs_0_, bf16[2048,256]{1,0:T(8,128)(2,1)S(1)} %collective-permute-done.15.refs_1_, ...), custom_call_target="tpu_custom_call" | custom-call | flops 3000000000 | tf_op jit(solution)/shard_map/weight_part/pallas_call | solution.py:88
  59.4 1.8 %collective-permute-start.21 = (f32[64,128]{1,0:T(8,128)S(1)}, f32[64,128]{1,0:T(8,128)S(1)}, u32[]{:S(2)}, u32[]{:S(2)}) collective-permute-start(f32[64,128]{1,0:T(8,128)S(1)} %filter_grad.1.refs_9_), channel_id=1, source_target_pairs={{0,16},{4,20},{8,24},{12,28},{16,0},{20,4},{24,8},{28,12},{32,48},... | collective-permute-start | bytes 98312 | tf_op jit(solution)/shard_map/ppermute | solution.py:484
  61.3 1.3 %collective-permute-start.17 = (bf16[256,512]{1,0:T(8,128)(2,1)S(1)}, bf16[256,512]{1,0:T(8,128)(2,1)S(1)}, u32[]{:S(2)}, u32[]{:S(2)}) collective-permute-start(bf16[256,512]{1,0:T(8,128)(2,1)S(1)} %get-tuple-element.74), channel_id=1, source_target_pairs={{0,4},{4,8},{8,12},{12,0},{16,20},{20,24},{24,28},{28,16},{32,36},... | collective-permute-start | bytes 786440 | tf_op jit(solution)/shard_map/ppermute | solution.py:36
  62.6 3.1 %collective-permute-start.18 = (bf16[256,512]{1,0:T(8,128)(2,1)S(1)}, bf16[256,512]{1,0:T(8,128)(2,1)S(1)}, u32[]{:S(2)}, u32[]{:S(2)}) collective-permute-start(bf16[256,512]{1,0:T(8,128)(2,1)S(1)} %get-tuple-element.75), channel_id=1, source_target_pairs={{0,8},{4,12},{8,0},{12,4},{16,24},{20,28},{24,16},{28,20},{32,40},... | collective-permute-start | bytes 786440 | tf_op jit(solution)/shard_map/ppermute | solution.py:36
  69.5 3.7 %collective-permute-done.25 = f32[64,128]{1,0:T(8,128)S(1)} collective-permute-done((f32[64,128]{1,0:T(8,128)S(1)}, f32[64,128]{1,0:T(8,128)S(1)}, u32[]{:S(2)}, u32[]{:S(2)}) %collective-permute-start.25) | collective-permute-done | bytes 32800 | tf_op jit(solution)/shard_map/ppermute | solution.py:484
  74.2 1.7 %collective-permute-start.24 = (bf16[256,512]{1,0:T(8,128)(2,1)S(1)}, bf16[256,512]{1,0:T(8,128)(2,1)S(1)}, u32[]{:S(2)}, u32[]{:S(2)}) collective-permute-start(bf16[256,512]{1,0:T(8,128)(2,1)S(1)} %get-tuple-element.81), channel_id=1, source_target_pairs={{0,48},{4,52},{8,56},{12,60},{16,0},{20,4},{24,8},{28,12},{32,16},... | collective-permute-start | bytes 786440 | tf_op jit(solution)/shard_map/ppermute | solution.py:33
  75.9 1.8 %collective-permute-done.18.refs_2_ = bf16[256,512]{1,0:T(8,128)(2,1)S(1)} collective-permute-done((bf16[256,512]{1,0:T(8,128)(2,1)S(1)}, bf16[256,512]{1,0:T(8,128)(2,1)S(1)}, u32[]{:S(2)}, u32[]{:S(2)}) %collective-permute-start.18) | collective-permute-done | bytes 262176 | tf_op jit(solution)/shard_map/ppermute | solution.py:36
  78.9 3.1 %collective-permute-start.8 = (bf16[128,1024]{1,0:T(8,128)(2,1)S(1)}, bf16[128,1024]{1,0:T(8,128)(2,1)S(1)}, u32[]{:S(2)}, u32[]{:S(2)}) collective-permute-start(bf16[128,1024]{1,0:T(8,128)(2,1)S(1)} %slice.11), channel_id=1, source_target_pairs={{4,0},{8,4},{12,8},{16,12},{20,16},{24,20},{28,24},{32,28},{36,32}... | collective-permute-start | bytes 786440 | tf_op jit(solution)/shard_map/ppermute | solution.py:46
  82.0 1.8 %collective-permute-start.27 = (f32[64,128]{1,0:T(8,128)S(1)}, f32[64,128]{1,0:T(8,128)S(1)}, u32[]{:S(2)}, u32[]{:S(2)}) collective-permute-start(f32[64,128]{1,0:T(8,128)S(1)} %add.23), channel_id=1, source_target_pairs={{0,8},{4,12},{8,0},{12,4},{16,24},{20,28},{24,16},{28,20},{32,40},... | collective-permute-start | bytes 98312 | tf_op jit(solution)/shard_map/ppermute | solution.py:484
  83.8 3.7 %collective-permute-done.27 = f32[64,128]{1,0:T(8,128)S(1)} collective-permute-done((f32[64,128]{1,0:T(8,128)S(1)}, f32[64,128]{1,0:T(8,128)S(1)}, u32[]{:S(2)}, u32[]{:S(2)}) %collective-permute-start.27) | collective-permute-done | bytes 32800 | tf_op jit(solution)/shard_map/ppermute | solution.py:484
  87.9 6.5 %collective-permute-start.28 = (bf16[64,1024]{1,0:T(8,128)(2,1)S(1)}, bf16[64,1024]{1,0:T(8,128)(2,1)S(1)}, u32[]{:S(2)}, u32[]{:S(2)}) collective-permute-start(bf16[64,1024]{1,0:T(8,128)(2,1)S(1)} %get-tuple-element.86), channel_id=1, source_target_pairs={{0,64},{64,128},{128,192},{192,0},{1,65},{65,129},{129,193},{193,1... | collective-permute-start | bytes 393224 | tf_op jit(solution)/shard_map/ppermute | solution.py:38
  95.3 2.8 %collective-permute-start.30 = (bf16[64,1024]{1,0:T(8,128)(2,1)S(1)}, bf16[64,1024]{1,0:T(8,128)(2,1)S(1)}, u32[]{:S(2)}, u32[]{:S(2)}) collective-permute-start(bf16[64,1024]{1,0:T(8,128)(2,1)S(1)} %get-tuple-element.88), channel_id=1, source_target_pairs={{0,192},{64,0},{128,64},{192,128},{1,193},{65,1},{129,65},{193,129... | collective-permute-start | bytes 393224 | tf_op jit(solution)/shard_map/ppermute | solution.py:38
  98.4 8.9 %collective-permute-start.31 = (f32[64,128]{1,0:T(8,128)S(1)}, f32[64,128]{1,0:T(8,128)S(1)}, u32[]{:S(2)}, u32[]{:S(2)}) collective-permute-start(f32[64,128]{1,0:T(8,128)S(1)} %add.24.refs_8_), channel_id=1, source_target_pairs={{0,128},{64,192},{128,0},{192,64},{1,129},{65,193},{129,1},{193,65... | collective-permute-start | bytes 98312 | tf_op jit(solution)/shard_map/ppermute | solution.py:38
  107.4 3.8 %collective-permute-start.33 = (f32[64,128]{1,0:T(8,128)S(1)}, f32[64,128]{1,0:T(8,128)S(1)}, u32[]{:S(2)}, u32[]{:S(2)}) collective-permute-start(f32[64,128]{1,0:T(8,128)S(1)} %add.24.refs_8_), channel_id=1, source_target_pairs={{0,192},{64,0},{128,64},{192,128},{1,193},{65,1},{129,65},{193,129... | collective-permute-start | bytes 98312 | tf_op jit(solution)/shard_map/ppermute | solution.py:38
  111.2 3.4 %input_grad.1 = bf16[256,1024]{1,0:T(8,128)(2,1)} custom-call(bf16[64,128]{1,0:T(8,128)(2,1)} %refs_0_.3, bf16[256,1024]{1,0:T(8,128)(2,1)S(1)} %get-tuple-element.62.refs_8_.refs_2_.refs_1_, bf16[128,1024]{1,0:T(8,128)(2,1)S(1)} %collective-permute-done.8.refs_2_, f32[64,1024]{1,0:T(8,128)S(1)} %get-tuple-element.84.refs_3_.refs_0_), custom_call_target="tpu_custom_call" | custom-call | tf_op jit(solution)/shard_map/input_grad/pallas_call | solution.py:88
  (57 shorter events, 16.8 us)
Async XLA Ops:
  0.6 11.8 %collective-permute-start.1 = (bf16[64,4096]{1,0:T(8,128)(2,1)}, bf16[64,4096]{1,0:T(8,128)(2,1)S(1)}, u32[]{:S(2)}, u32[]{:S(2)}) collective-permute-start(bf16[64,4096]{1,0:T(8,128)(2,1)} %bitcast.10), channel_id=1, source_target_pairs={{0,1},{1,0},{2,3},{3,2},{4,5},{5,4},{6,7},{7,6},{8,9},{9,8},{10,11... | collective-permute-start | bytes 1572872 | tf_op jit(solution)/shard_map/ppermute | solution.py:41
  1.7 12.7 %collective-permute-start.2 = (bf16[128,1024]{1,0:T(8,128)(2,1)S(1)}, bf16[128,1024]{1,0:T(8,128)(2,1)S(1)}, u32[]{:S(2)}, u32[]{:S(2)}) collective-permute-start(bf16[128,1024]{1,0:T(8,128)(2,1)S(1)} %slice_bitcast_fusion), channel_id=1, source_target_pairs={{0,4},{4,8},{8,12},{12,16},{16,20},{20,24},{24,28},{28,32},{32,36}... | collective-permute-start | bytes 786440 | tf_op jit(solution)/shard_map/ppermute | solution.py:46
  5.2 23.2 %collective-permute-start = (bf16[64,4096]{1,0:T(8,128)(2,1)}, bf16[64,4096]{1,0:T(8,128)(2,1)S(1)}, u32[]{:S(2)}, u32[]{:S(2)}) collective-permute-start(bf16[64,4096]{1,0:T(8,128)(2,1)} %bitcast.11), channel_id=1, source_target_pairs={{0,2},{1,3},{2,0},{3,1},{4,6},{5,7},{6,4},{7,5},{8,10},{9,11},{10,... | collective-permute-start | bytes 1572872 | tf_op jit(solution)/shard_map/ppermute | solution.py:40
  17.8 10.8 %collective-permute-start.3 = (bf16[384,512]{1,0:T(8,128)(2,1)S(1)}, bf16[384,512]{1,0:T(8,128)(2,1)S(1)}, u32[]{:S(2)}, u32[]{:S(2)}) collective-permute-start(bf16[384,512]{1,0:T(8,128)(2,1)S(1)} %get-tuple-element.53), channel_id=1, source_target_pairs={{0,16},{4,20},{8,24},{12,28},{16,32},{20,36},{24,40},{28,44},{32,4... | collective-permute-start | bytes 1179656 | tf_op jit(solution)/shard_map/ppermute | solution.py:33
  19.4 10.4 %collective-permute-start.4 = (bf16[384,512]{1,0:T(8,128)(2,1)S(1)}, bf16[384,512]{1,0:T(8,128)(2,1)S(1)}, u32[]{:S(2)}, u32[]{:S(2)}) collective-permute-start(bf16[384,512]{1,0:T(8,128)(2,1)S(1)} %get-tuple-element.54), channel_id=1, source_target_pairs={{0,48},{4,52},{8,56},{12,60},{16,0},{20,4},{24,8},{28,12},{32,16},... | collective-permute-start | bytes 1179656 | tf_op jit(solution)/shard_map/ppermute | solution.py:33
  20.0 11.4 %collective-permute-start.5 = (bf16[384,512]{1,0:T(8,128)(2,1)S(1)}, bf16[384,512]{1,0:T(8,128)(2,1)S(1)}, u32[]{:S(2)}, u32[]{:S(2)}) collective-permute-start(bf16[384,512]{1,0:T(8,128)(2,1)S(1)} %get-tuple-element.55), channel_id=1, source_target_pairs={{0,4},{4,8},{8,12},{12,0},{16,20},{20,24},{24,28},{28,16},{32,36},... | collective-permute-start | bytes 1179656 | tf_op jit(solution)/shard_map/ppermute | solution.py:36
  21.3 10.1 %collective-permute-start.6 = (bf16[384,512]{1,0:T(8,128)(2,1)S(1)}, bf16[384,512]{1,0:T(8,128)(2,1)S(1)}, u32[]{:S(2)}, u32[]{:S(2)}) collective-permute-start(bf16[384,512]{1,0:T(8,128)(2,1)S(1)} %get-tuple-element.56), channel_id=1, source_target_pairs={{0,12},{4,0},{8,4},{12,8},{16,28},{20,16},{24,20},{28,24},{32,44},... | collective-permute-start | bytes 1179656 | tf_op jit(solution)/shard_map/ppermute | solution.py:36
  33.9 10.7 %collective-permute-start.10 = (bf16[256,512]{1,0:T(8,128)(2,1)S(1)}, bf16[256,512]{1,0:T(8,128)(2,1)S(1)}, u32[]{:S(2)}, u32[]{:S(2)}) collective-permute-start(bf16[256,512]{1,0:T(8,128)(2,1)S(1)} %get-tuple-element.66), channel_id=1, source_target_pairs={{0,8},{4,12},{8,0},{12,4},{16,24},{20,28},{24,16},{28,20},{32,40},... | collective-permute-start | bytes 786440 | tf_op jit(solution)/shard_map/ppermute | solution.py:36
  36.5 16.1 %collective-permute-start.11 = (bf16[256,512]{1,0:T(8,128)(2,1)S(1)}, bf16[256,512]{1,0:T(8,128)(2,1)S(1)}, u32[]{:S(2)}, u32[]{:S(2)}) collective-permute-start(bf16[256,512]{1,0:T(8,128)(2,1)S(1)} %get-tuple-element.67), channel_id=1, source_target_pairs={{0,16},{4,20},{8,24},{12,28},{16,32},{20,36},{24,40},{28,44},{32,4... | collective-permute-start | bytes 786440 | tf_op jit(solution)/shard_map/ppermute | solution.py:33
  37.7 14.9 %collective-permute-start.12 = (bf16[256,512]{1,0:T(8,128)(2,1)S(1)}, bf16[256,512]{1,0:T(8,128)(2,1)S(1)}, u32[]{:S(2)}, u32[]{:S(2)}) collective-permute-start(bf16[256,512]{1,0:T(8,128)(2,1)S(1)} %get-tuple-element.68), channel_id=1, source_target_pairs={{0,48},{4,52},{8,56},{12,60},{16,0},{20,4},{24,8},{28,12},{32,16},... | collective-permute-start | bytes 786440 | tf_op jit(solution)/shard_map/ppermute | solution.py:33
  38.5 14.1 %collective-permute-start.13 = (bf16[256,512]{1,0:T(8,128)(2,1)S(1)}, bf16[256,512]{1,0:T(8,128)(2,1)S(1)}, u32[]{:S(2)}, u32[]{:S(2)}) collective-permute-start(bf16[256,512]{1,0:T(8,128)(2,1)S(1)} %get-tuple-element.69), channel_id=1, source_target_pairs={{0,4},{4,8},{8,12},{12,0},{16,20},{20,24},{24,28},{28,16},{32,36},... | collective-permute-start | bytes 786440 | tf_op jit(solution)/shard_map/ppermute | solution.py:36
  39.8 12.8 %collective-permute-start.14 = (bf16[256,512]{1,0:T(8,128)(2,1)S(1)}, bf16[256,512]{1,0:T(8,128)(2,1)S(1)}, u32[]{:S(2)}, u32[]{:S(2)}) collective-permute-start(bf16[256,512]{1,0:T(8,128)(2,1)S(1)} %get-tuple-element.70), channel_id=1, source_target_pairs={{0,12},{4,0},{8,4},{12,8},{16,28},{20,16},{24,20},{28,24},{32,44},... | collective-permute-start | bytes 786440 | tf_op jit(solution)/shard_map/ppermute | solution.py:36
  44.6 8.2 %collective-permute-start.9 = (bf16[256,512]{1,0:T(8,128)(2,1)S(1)}, bf16[256,512]{1,0:T(8,128)(2,1)S(1)}, u32[]{:S(2)}, u32[]{:S(2)}) collective-permute-start(bf16[256,512]{1,0:T(8,128)(2,1)S(1)} %get-tuple-element.64), channel_id=1, source_target_pairs={{0,32},{4,36},{8,40},{12,44},{16,48},{20,52},{24,56},{28,60},{32,0... | collective-permute-start | bytes 786440 | tf_op jit(solution)/shard_map/ppermute | solution.py:33
  53.2 5.0 %collective-permute-start.15 = (bf16[2048,256]{1,0:T(8,128)(2,1)S(1)}, bf16[2048,256]{1,0:T(8,128)(2,1)S(1)}, u32[]{:S(2)}, u32[]{:S(2)}) collective-permute-start(bf16[2048,256]{1,0:T(8,128)(2,1)S(1)} %turn_early.1.refs_4_.refs_0_), channel_id=1, source_target_pairs={{0,1},{1,0},{2,3},{3,2},{4,5},{5,4},{6,7},{7,6},{8,9},{9,8},{10,11... | collective-permute-start | bytes 3145736 | tf_op jit(solution)/shard_map/ppermute | solution.py:41
  53.5 4.6 %collective-permute-start.16 = (bf16[1024,256]{1,0:T(8,128)(2,1)S(1)}, bf16[1024,256]{1,0:T(8,128)(2,1)S(1)}, u32[]{:S(2)}, u32[]{:S(2)}) collective-permute-start(bf16[1024,256]{1,0:T(8,128)(2,1)S(1)} %turn_late.2.refs_4_.refs_2_), channel_id=1, source_target_pairs={{0,1},{1,0},{2,3},{3,2},{4,5},{5,4},{6,7},{7,6},{8,9},{9,8},{10,11... | collective-permute-start | bytes 1572872 | tf_op jit(solution)/shard_map/ppermute | solution.py:41
  54.3 12.2 %collective-permute-start.20 = (bf16[1024,256]{1,0:T(8,128)(2,1)S(1)}, bf16[1024,256]{1,0:T(8,128)(2,1)S(1)}, u32[]{:S(2)}, u32[]{:S(2)}) collective-permute-start(bf16[1024,256]{1,0:T(8,128)(2,1)S(1)} %turn_late.3.refs_3_.refs_2_), channel_id=1, source_target_pairs={{0,1},{1,0},{2,3},{3,2},{4,5},{5,4},{6,7},{7,6},{8,9},{9,8},{10,11... | collective-permute-start | bytes 1572872 | tf_op jit(solution)/shard_map/ppermute | solution.py:41
  59.4 7.0 %collective-permute-start.21 = (f32[64,128]{1,0:T(8,128)S(1)}, f32[64,128]{1,0:T(8,128)S(1)}, u32[]{:S(2)}, u32[]{:S(2)}) collective-permute-start(f32[64,128]{1,0:T(8,128)S(1)} %filter_grad.1.refs_9_), channel_id=1, source_target_pairs={{0,16},{4,20},{8,24},{12,28},{16,0},{20,4},{24,8},{28,12},{32,48},... | collective-permute-start | bytes 98312 | tf_op jit(solution)/shard_map/ppermute | solution.py:484
  61.3 12.9 %collective-permute-start.17 = (bf16[256,512]{1,0:T(8,128)(2,1)S(1)}, bf16[256,512]{1,0:T(8,128)(2,1)S(1)}, u32[]{:S(2)}, u32[]{:S(2)}) collective-permute-start(bf16[256,512]{1,0:T(8,128)(2,1)S(1)} %get-tuple-element.74), channel_id=1, source_target_pairs={{0,4},{4,8},{8,12},{12,0},{16,20},{20,24},{24,28},{28,16},{32,36},... | collective-permute-start | bytes 786440 | tf_op jit(solution)/shard_map/ppermute | solution.py:36
  62.6 15.1 %collective-permute-start.18 = (bf16[256,512]{1,0:T(8,128)(2,1)S(1)}, bf16[256,512]{1,0:T(8,128)(2,1)S(1)}, u32[]{:S(2)}, u32[]{:S(2)}) collective-permute-start(bf16[256,512]{1,0:T(8,128)(2,1)S(1)} %get-tuple-element.75), channel_id=1, source_target_pairs={{0,8},{4,12},{8,0},{12,4},{16,24},{20,28},{24,16},{28,20},{32,40},... | collective-permute-start | bytes 786440 | tf_op jit(solution)/shard_map/ppermute | solution.py:36
  65.6 12.0 %collective-permute-start.19 = (bf16[256,512]{1,0:T(8,128)(2,1)S(1)}, bf16[256,512]{1,0:T(8,128)(2,1)S(1)}, u32[]{:S(2)}, u32[]{:S(2)}) collective-permute-start(bf16[256,512]{1,0:T(8,128)(2,1)S(1)} %get-tuple-element.76), channel_id=1, source_target_pairs={{0,12},{4,0},{8,4},{12,8},{16,28},{20,16},{24,20},{28,24},{32,44},... | collective-permute-start | bytes 786440 | tf_op jit(solution)/shard_map/ppermute | solution.py:36
  67.7 5.5 %collective-permute-start.25 = (f32[64,128]{1,0:T(8,128)S(1)}, f32[64,128]{1,0:T(8,128)S(1)}, u32[]{:S(2)}, u32[]{:S(2)}) collective-permute-start(f32[64,128]{1,0:T(8,128)S(1)} %add.21.refs_10_), channel_id=1, source_target_pairs={{0,32},{4,36},{8,40},{12,44},{16,48},{20,52},{24,56},{28,60},{32,0... | collective-permute-start | bytes 98312 | tf_op jit(solution)/shard_map/ppermute | solution.py:484
  68.7 18.8 %collective-permute-start.22 = (bf16[256,512]{1,0:T(8,128)(2,1)S(1)}, bf16[256,512]{1,0:T(8,128)(2,1)S(1)}, u32[]{:S(2)}, u32[]{:S(2)}) collective-permute-start(bf16[256,512]{1,0:T(8,128)(2,1)S(1)} %get-tuple-element.79), channel_id=1, source_target_pairs={{0,16},{4,20},{8,24},{12,28},{16,32},{20,36},{24,40},{28,44},{32,4... | collective-permute-start | bytes 786440 | tf_op jit(solution)/shard_map/ppermute | solution.py:33
  73.2 14.3 %collective-permute-start.23 = (bf16[256,512]{1,0:T(8,128)(2,1)S(1)}, bf16[256,512]{1,0:T(8,128)(2,1)S(1)}, u32[]{:S(2)}, u32[]{:S(2)}) collective-permute-start(bf16[256,512]{1,0:T(8,128)(2,1)S(1)} %get-tuple-element.80), channel_id=1, source_target_pairs={{0,32},{4,36},{8,40},{12,44},{16,48},{20,52},{24,56},{28,60},{32,0... | collective-permute-start | bytes 786440 | tf_op jit(solution)/shard_map/ppermute | solution.py:33
  74.2 13.4 %collective-permute-start.24 = (bf16[256,512]{1,0:T(8,128)(2,1)S(1)}, bf16[256,512]{1,0:T(8,128)(2,1)S(1)}, u32[]{:S(2)}, u32[]{:S(2)}) collective-permute-start(bf16[256,512]{1,0:T(8,128)(2,1)S(1)} %get-tuple-element.81), channel_id=1, source_target_pairs={{0,48},{4,52},{8,56},{12,60},{16,0},{20,4},{24,8},{28,12},{32,16},... | collective-permute-start | bytes 786440 | tf_op jit(solution)/shard_map/ppermute | solution.py:33
  78.9 28.5 %collective-permute-start.8 = (bf16[128,1024]{1,0:T(8,128)(2,1)S(1)}, bf16[128,1024]{1,0:T(8,128)(2,1)S(1)}, u32[]{:S(2)}, u32[]{:S(2)}) collective-permute-start(bf16[128,1024]{1,0:T(8,128)(2,1)S(1)} %slice.11), channel_id=1, source_target_pairs={{4,0},{8,4},{12,8},{16,12},{20,16},{24,20},{28,24},{32,28},{36,32}... | collective-permute-start | bytes 786440 | tf_op jit(solution)/shard_map/ppermute | solution.py:46
  82.0 5.5 %collective-permute-start.27 = (f32[64,128]{1,0:T(8,128)S(1)}, f32[64,128]{1,0:T(8,128)S(1)}, u32[]{:S(2)}, u32[]{:S(2)}) collective-permute-start(f32[64,128]{1,0:T(8,128)S(1)} %add.23), channel_id=1, source_target_pairs={{0,8},{4,12},{8,0},{12,4},{16,24},{20,28},{24,16},{28,20},{32,40},... | collective-permute-start | bytes 98312 | tf_op jit(solution)/shard_map/ppermute | solution.py:484
  87.9 10.5 %collective-permute-start.28 = (bf16[64,1024]{1,0:T(8,128)(2,1)S(1)}, bf16[64,1024]{1,0:T(8,128)(2,1)S(1)}, u32[]{:S(2)}, u32[]{:S(2)}) collective-permute-start(bf16[64,1024]{1,0:T(8,128)(2,1)S(1)} %get-tuple-element.86), channel_id=1, source_target_pairs={{0,64},{64,128},{128,192},{192,0},{1,65},{65,129},{129,193},{193,1... | collective-permute-start | bytes 393224 | tf_op jit(solution)/shard_map/ppermute | solution.py:38
  94.5 20.1 %collective-permute-start.29 = (bf16[64,1024]{1,0:T(8,128)(2,1)S(1)}, bf16[64,1024]{1,0:T(8,128)(2,1)S(1)}, u32[]{:S(2)}, u32[]{:S(2)}) collective-permute-start(bf16[64,1024]{1,0:T(8,128)(2,1)S(1)} %get-tuple-element.87), channel_id=1, source_target_pairs={{0,128},{64,192},{128,0},{192,64},{1,129},{65,193},{129,1},{193,65... | collective-permute-start | bytes 393224 | tf_op jit(solution)/shard_map/ppermute | solution.py:38
  95.3 19.3 %collective-permute-start.30 = (bf16[64,1024]{1,0:T(8,128)(2,1)S(1)}, bf16[64,1024]{1,0:T(8,128)(2,1)S(1)}, u32[]{:S(2)}, u32[]{:S(2)}) collective-permute-start(bf16[64,1024]{1,0:T(8,128)(2,1)S(1)} %get-tuple-element.88), channel_id=1, source_target_pairs={{0,192},{64,0},{128,64},{192,128},{1,193},{65,1},{129,65},{193,129... | collective-permute-start | bytes 393224 | tf_op jit(solution)/shard_map/ppermute | solution.py:38
  98.4 17.0 %collective-permute-start.31 = (f32[64,128]{1,0:T(8,128)S(1)}, f32[64,128]{1,0:T(8,128)S(1)}, u32[]{:S(2)}, u32[]{:S(2)}) collective-permute-start(f32[64,128]{1,0:T(8,128)S(1)} %add.24.refs_8_), channel_id=1, source_target_pairs={{0,128},{64,192},{128,0},{192,64},{1,129},{65,193},{129,1},{193,65... | collective-permute-start | bytes 98312 | tf_op jit(solution)/shard_map/ppermute | solution.py:38
  107.4 8.0 %collective-permute-start.32 = (f32[64,128]{1,0:T(8,128)S(1)}, f32[64,128]{1,0:T(8,128)S(1)}, u32[]{:S(2)}, u32[]{:S(2)}) collective-permute-start(f32[64,128]{1,0:T(8,128)S(1)} %add.24.refs_8_), channel_id=1, source_target_pairs={{0,64},{64,128},{128,192},{192,0},{1,65},{65,129},{129,193},{193,1... | collective-permute-start | bytes 98312 | tf_op jit(solution)/shard_map/ppermute | solution.py:38
  107.4 8.0 %collective-permute-start.33 = (f32[64,128]{1,0:T(8,128)S(1)}, f32[64,128]{1,0:T(8,128)S(1)}, u32[]{:S(2)}, u32[]{:S(2)}) collective-permute-start(f32[64,128]{1,0:T(8,128)S(1)} %add.24.refs_8_), channel_id=1, source_target_pairs={{0,192},{64,0},{128,64},{192,128},{1,193},{65,1},{129,65},{193,129... | collective-permute-start | bytes 98312 | tf_op jit(solution)/shard_map/ppermute | solution.py:38
  (2 other events, 6.3 us)

commit v5 on v4

--- a/solution.py
+++ b/solution.py
@@ -388,7 +388,30 @@
     )(mine, other, weight, gating, response, *done, *after)
 
 
-def weight_kernel(early, early_other, late, late_other, gated, first, third, before, after, *outs):
+def high_and_low(x):
+    high = x.astype(BF16).astype(F32)
+    return high, (x - high).astype(BF16).astype(F32)
+
+
+def folded(x, rows):
+    return jnp.concatenate([x[i : i + rows] for i in range(0, x.shape[0], rows)], 1)
+
+
+def unfolded(x):
+    return jnp.concatenate([x[:, i : i + LANES] for i in range(0, x.shape[1], LANES)], 0)
+
+
+def riding(ref, start, rows):
+    pair = ref[start : start + 2 * rows].astype(F32)
+    return unfolded(pair[:rows] + pair[rows:])
+
+
+def four_sum(parts):
+    return (parts[0] + parts[2]) + (parts[1] + parts[3])
+
+
+def weight_kernel(early, early_other, late, late_other, gated, first, third, before, after, *refs):
+    extra, outs = refs[:-SIDE], refs[-SIDE:]
     _, _, _, half, core = spot()
     part = WIDE // SIDE
     tokens = []
@@ -403,10 +426,17 @@
     for s, out in enumerate(outs):
         rows = slice(s * WIDE, (s + 1) * WIDE)
         features = jnp.concatenate([ref[rows] for ref in (early, early_other, late, late_other)], 1)
-        out[...] = jnp.dot(features, tokens, preferred_element_type=F32).astype(out.dtype)
-
-
-def weight_part(which, early, early_other, turned, turned_other, gated, got, late, after=()):
+        out[:WIDE] = jnp.dot(features, tokens, preferred_element_type=F32).astype(out.dtype)
+    if extra:
+        rows = LANES * extra[0].shape[0] // gated.shape[1]
+        pair = jnp.concatenate([folded(part, rows) for part in high_and_low(extra[0][...])], 0)
+        for out in outs[1:]:
+            out[WIDE:] = pair.astype(BF16)
+
+
+def weight_part(
+    which, early, early_other, turned, turned_other, gated, got, late, extra=(), after=()
+):
     length = gated.shape[0]
     features = turned.shape[0]
     width = got[0].shape[1]
@@ -424,17 +454,32 @@
             *[(one, whole((length, width))) for one in got],
             (late[1], below),
             (late[3], below),
+            *extra,
         ],
-        [((features // SIDE, width), F32 if s == 0 else BF16) for s in range(SIDE)],
+        [((features // SIDE, width), F32)]
+        + [((features // SIDE + sum(2 * x.size // width for x in extra), width), BF16)] * (SIDE - 1),
         (),
         after,
         3,
     )
 
 
+def filter_sum_y(own, parts):
+    below = parts[0].shape[0] - WIDE
+    rows = below // 2
+
+    def kernel(*refs):
+        values = [sum(high_and_low(refs[0][...]))]
+        values += [riding(ref, 0, rows) for ref in refs[1:-1]]
+        refs[-1][...] = four_sum(values)
+
+    tails = [(part, whole((below, part.shape[1]), (WIDE // below, 0))) for part in parts]
+    return once(kernel, "filter_sum_y", [own, *tails], [(own.shape, F32)])[0]
+
+
 def first_sum_kernel(*refs):
     _, _, z, _, _ = spot()
-    outs, kept = refs[2 * SIDE : 3 * SIDE], refs[3 * SIDE]
+    extra, outs, own_extra, kept = refs[2 * SIDE], refs[2 * SIDE + 1 : -2], refs[-2], refs[-1]
     width = refs[0].shape[1]
     run = kept.shape[0] // SIDE
     for which in range(2):
@@ -445,32 +490,48 @@
         for d in range(SIDE):
             rows = aligned((d - z + SIDE) % SIDE, run)
             kept[rows, which * width : (which + 1) * width] = total[d * run : (d + 1) * run]
+    high, low = (folded(part, own_extra.shape[0]) for part in high_and_low(extra[...]))
+    own_extra[...] = high + low
     for s, out in enumerate(outs):
-        out[...] = kept[s * run : (s + 1) * run, :].astype(out.dtype)
-
-
-def first_sum(parts_x, parts_y, after=()):
+        out[:run] = kept[s * run : (s + 1) * run, :].astype(out.dtype)
+        if s:
+            out[run:] = jnp.concatenate([high, low], 0).astype(BF16)
+
+
+def first_sum(parts_x, parts_y, extra):
     rows, width = parts_x[0].shape
-    return once(
+    below = LANES * extra.shape[0] // (2 * width)
+    run = rows // SIDE
+    *sums, own_extra = once(
         first_sum_kernel,
         "first_sum",
-        [*parts_x, *parts_y],
-        [((rows // SIDE, 2 * width), F32 if s == 0 else BF16) for s in range(SIDE)],
+        [*[(part, whole((rows, width))) for part in (*parts_x, *parts_y)], extra],
+        [((run, 2 * width), F32)]
+        + [((run + 2 * below, 2 * width), BF16)] * (SIDE - 1)
+        + [((below, 2 * width), F32)],
         [pltpu.VMEM((rows, 2 * width), F32)],
-        after,
+        (),
         1,
     )
-
-
-def last_sum(parts, scale):
+    return sums, own_extra
+
+
+def last_sum(parts, own_extra, filters, scale, filter_scale):
+    rows = parts[0].shape[0]
+    below = own_extra.shape[0]
+
     def kernel(*refs):
-        out = refs[-1]
-        total = refs[0][...]
-        for ref in refs[1:SIDE]:
-            total = total + ref[...].astype(F32)
+        own, others, extra, out, filter_out = refs[0], refs[1:SIDE], refs[SIDE], refs[-2], refs[-1]
+        total = own[...]
+        for ref in others:
+            total = total + ref[:rows].astype(F32)
         out[...] = total * scale
-
-    return once(kernel, "last_sum", parts, [(parts[0].shape, F32)])[0]
+        values = [unfolded(extra[...])] + [riding(ref, rows, below) for ref in others]
+        filter_out[...] = four_sum(values) * filter_scale
+
+    return once(
+        kernel, "last_sum", [*parts, own_extra], [(parts[0].shape, F32), (filters.shape, F32)]
+    )
 
 
 def tied(x, *after):
@@ -538,20 +599,21 @@
     parts_x = weight_part(
         0, early, early_swap, turned_x, swap_x, gated, got_x, late_x, (filter_local,)
     )
-    filter_sum = paired(filter_local, "x", 1, (parts_x[0],))
     parts_y = weight_part(
-        1, early, early_swap, turned_y, swap_y, gated, got_y, late_y, (parts_x[0], filter_sum)
-    )
-    filter_sum = paired(filter_sum, "x", 2, (parts_y[0],))
+        1, early, early_swap, turned_y, swap_y, gated, got_y, late_y, (), (parts_x[0],)
+    )
     parts_x, parts_y = exchanged(parts_x, "y"), exchanged(parts_y, "x")
-    filter_sum = paired(paired(filter_sum, "y", 1, parts_x[1:]), "y", 2)
-    sums = first_sum(parts_x, parts_y, (filter_sum,))
+    filter_sum = filter_sum_y(filter_local, parts_x[1:])
+    filter_sum = paired(paired(filter_sum, "x", 1), "x", 2)
+    sums, own_filter = first_sum(parts_x, parts_y, filter_sum)
     grad_input = input_grad(filters, conv_grad, following, (sums[0],))
-    sums = exchanged(sums, "z")
-    filter_parts = exchanged([tied(filter_sum, sums[1])] * SIDE, "z")
-    filter_total = (filter_parts[0] + filter_parts[2]) + (filter_parts[1] + filter_parts[3])
-    grad_weight = last_sum(sums, 1.0 / math.sqrt(tokens_all))
-    grad_filter = filter_total * (1.0 / math.sqrt(tokens_all * GROUP))
+    grad_weight, grad_filter = last_sum(
+        exchanged(sums, "z"),
+        own_filter,
+        filters,
+        1.0 / math.sqrt(tokens_all),
+        1.0 / math.sqrt(tokens_all * GROUP),
+    )
     return (grad_input[None], grad_gate[None], grad_weight, grad_filter)
 
 

time: 118 us -> 110 us (0.932)
  the two profiles are of different devices: /device:TPU:2 before, /device:TPU:163 now
where the time goes in v5:
time: 110 us
  starting transfers between devices  39.8 us (36%)
  waiting for transfers between devices  39.6 us (36%)
  Pallas kernels  28.3 us (26%)
    ppermute x16, starting transfers between devices, moved(): return lax.ppermute(x, 'ctx', pairs)  21.3 us
    pallas_call x13, Pallas kernels, once(): pl.pallas_call(body, grid=(1,), in_specs=specs + [ANYWHERE] * len(after),...  17.3 us
    pallas_call x2, Pallas kernels, project(): pl.pallas_call(body, grid=(channels // WIDE,), in_specs=[full(mine.shape)...  11 us
    ppermute x3, waiting for transfers between devices, moved(): return lax.ppermute(x, 'dp', [(i, (i + by) % SIDE) for i in range(SIDE)])  11 us
    ppermute x16, waiting for transfers between devices, moved(): return lax.ppermute(x, 'ctx', pairs)  9.66 us
    ppermute x2, starting transfers between devices, shifted(): lax.ppermute(x, 'ctx', [(i, i + by) for i in range(devices) if 0 <= i + b...  8.24 us
    ppermute x2, waiting for transfers between devices, shifted(): lax.ppermute(x, 'ctx', [(i, i + by) for i in range(devices) if 0 <= i + b...  7.84 us
    ppermute x1, waiting for transfers between devices, moved(): return lax.ppermute(x, 'tp', [(i, (i + 2) % 4) for i in range(4)])  7.08 us
  transfers between devices with their start and end apart: 29, of which 10 were waited for; matrix products, arithmetic and copies ran while one was open for 1% of the time, Pallas kernels for 24%

profile of v5, /device:TPU:163, one launch (start us, length us, event | category | flops | bytes accessed | tf_op | source)
XLA Modules:
  0.0 109.5 jit_solution(1572092835963098272)
XLA Ops:
  2.4 3.2 %collective-permute-start.2 = (bf16[128,1024]{1,0:T(8,128)(2,1)S(1)}, bf16[128,1024]{1,0:T(8,128)(2,1)S(1)}, u32[]{:S(2)}, u32[]{:S(2)}) collective-permute-start(bf16[128,1024]{1,0:T(8,128)(2,1)S(1)} %slice_bitcast_fusion), channel_id=1, source_target_pairs={{0,4},{4,8},{8,12},{12,16},{16,20},{20,24},{24,28},{28,32},{32,36}... | collective-permute-start | bytes 786440 | tf_op jit(solution)/shard_map/ppermute | solution.py:46
  5.7 1.6 %pack.1 = (bf16[128,512]{1,0:T(8,128)(2,1)S(1)}, bf16[128,512]{1,0:T(8,128)(2,1)S(1)}, bf16[128,512]{1,0:T(8,128)(2,1)S(1)}, bf16[128,512]{1,0:T(8,128)(2,1)S(1)...) custom-call(bf16[64,4096]{1,0:T(8,128)(2,1)} %bitcast.12, ...), custom_call_target="tpu_custom_call" | custom-call | tf_op jit(solution)/shard_map/pack/pallas_call | solution.py:88
  7.3 7.0 %collective-permute-done.2.refs_1_.refs_0_ = bf16[128,1024]{1,0:T(8,128)(2,1)S(1)} collective-permute-done((bf16[128,1024]{1,0:T(8,128)(2,1)S(1)}, bf16[128,1024]{1,0:T(8,128)(2,1)S(1)}, u32[]{:S(2)}, u32[]{:S(2)}) %collective-permute-start.2) | collective-permute-done | bytes 262176 | tf_op jit(solution)/shard_map/ppermute | solution.py:46
  14.3 3.4 %conv_forward.1 = (f32[256,1024]{1,0:T(8,128)S(1)}, bf16[256,1024]{1,0:T(8,128)(2,1)S(1)}, bf16[384,512]{1,0:T(8,128)(2,1)S(1)}, bf16[384,512]{1,0:T(8,128)(2,1)...) custom-call(bf16[64,128]{1,0:T(8,128)(2,1)} %refs_0_.3, ...), custom_call_target="tpu_custom_call" | custom-call | tf_op jit(solution)/shard_map/conv_forward/pallas_call | solution.py:88
  17.7 1.3 %collective-permute-start.3 = (bf16[384,512]{1,0:T(8,128)(2,1)S(1)}, bf16[384,512]{1,0:T(8,128)(2,1)S(1)}, u32[]{:S(2)}, u32[]{:S(2)}) collective-permute-start(bf16[384,512]{1,0:T(8,128)(2,1)S(1)} %get-tuple-element.52), channel_id=1, source_target_pairs={{0,16},{4,20},{8,24},{12,28},{16,32},{20,36},{24,40},{28,44},{32,4... | collective-permute-start | bytes 1179656 | tf_op jit(solution)/shard_map/ppermute | solution.py:33
  19.3 2.7 %collective-permute-start.6 = (bf16[384,512]{1,0:T(8,128)(2,1)S(1)}, bf16[384,512]{1,0:T(8,128)(2,1)S(1)}, u32[]{:S(2)}, u32[]{:S(2)}) collective-permute-start(bf16[384,512]{1,0:T(8,128)(2,1)S(1)} %get-tuple-element.55), channel_id=1, source_target_pairs={{0,12},{4,0},{8,4},{12,8},{16,28},{20,16},{24,20},{28,24},{32,44},... | collective-permute-start | bytes 1179656 | tf_op jit(solution)/shard_map/ppermute | solution.py:36
  21.9 5.2 %project_early.1 = (bf16[128,1024]{1,0:T(8,128)(2,1)S(1)}, bf16[128,1024]{1,0:T(8,128)(2,1)S(1)}) custom-call(bf16[64,4096]{1,0:T(8,128)(2,1)} %bitcast.13, bf16[64,4096]{1,0:T(8,128)(2,1)S(1)} %collective-permute-done.1.refs_1_, bf16[4096,1024]{1,0:T(8,128)(2,1)} %refs_2_.3, bf16[256,1024]{1,0:T(8,128)(2,1)} %bitcast.8, ...), custom_call_target="tpu_custom_call" | custom-call | tf_op jit(solution)/shard_map/project_early/pallas_call | solution.py:375
  27.2 7.1 %collective-permute-done.refs_0_ = bf16[64,4096]{1,0:T(8,128)(2,1)S(1)} collective-permute-done((bf16[64,4096]{1,0:T(8,128)(2,1)}, bf16[64,4096]{1,0:T(8,128)(2,1)S(1)}, u32[]{:S(2)}, u32[]{:S(2)}) %collective-permute-start) | collective-permute-done | bytes 524320 | tf_op jit(solution)/shard_map/ppermute | solution.py:40
  35.5 1.5 %collective-permute-done.7.refs_7_.refs_1_ = bf16[64,4096]{1,0:T(8,128)(2,1)S(1)} collective-permute-done((bf16[64,4096]{1,0:T(8,128)(2,1)S(1)}, bf16[64,4096]{1,0:T(8,128)(2,1)S(1)}, u32[]{:S(2)}, u32[]{:S(2)}) %collective-permute-start.7) | collective-permute-done | bytes 524320 | tf_op jit(solution)/shard_map/ppermute | solution.py:41
  37.6 2.7 %collective-permute-start.10 = (bf16[256,512]{1,0:T(8,128)(2,1)S(1)}, bf16[256,512]{1,0:T(8,128)(2,1)S(1)}, u32[]{:S(2)}, u32[]{:S(2)}) collective-permute-start(bf16[256,512]{1,0:T(8,128)(2,1)S(1)} %get-tuple-element.65), channel_id=1, source_target_pairs={{0,8},{4,12},{8,0},{12,4},{16,24},{20,28},{24,16},{28,20},{32,40},... | collective-permute-start | bytes 786440 | tf_op jit(solution)/shard_map/ppermute | solution.py:36
  40.3 1.2 %collective-permute-start.11 = (bf16[256,512]{1,0:T(8,128)(2,1)S(1)}, bf16[256,512]{1,0:T(8,128)(2,1)S(1)}, u32[]{:S(2)}, u32[]{:S(2)}) collective-permute-start(bf16[256,512]{1,0:T(8,128)(2,1)S(1)} %get-tuple-element.66), channel_id=1, source_target_pairs={{0,16},{4,20},{8,24},{12,28},{16,32},{20,36},{24,40},{28,44},{32,4... | collective-permute-start | bytes 786440 | tf_op jit(solution)/shard_map/ppermute | solution.py:33
  42.1 2.4 %collective-permute-start.14 = (bf16[256,512]{1,0:T(8,128)(2,1)S(1)}, bf16[256,512]{1,0:T(8,128)(2,1)S(1)}, u32[]{:S(2)}, u32[]{:S(2)}) collective-permute-start(bf16[256,512]{1,0:T(8,128)(2,1)S(1)} %get-tuple-element.69), channel_id=1, source_target_pairs={{0,12},{4,0},{8,4},{12,8},{16,28},{20,16},{24,20},{28,24},{32,44},... | collective-permute-start | bytes 786440 | tf_op jit(solution)/shard_map/ppermute | solution.py:36
  44.5 2.3 %collective-permute-done.10.refs_6_.refs_13_.refs_2_ = bf16[256,512]{1,0:T(8,128)(2,1)S(1)} collective-permute-done((bf16[256,512]{1,0:T(8,128)(2,1)S(1)}, bf16[256,512]{1,0:T(8,128)(2,1)S(1)}, u32[]{:S(2)}, u32[]{:S(2)}) %collective-permute-start.10) | collective-permute-done | bytes 262176 | tf_op jit(solution)/shard_map/ppermute | solution.py:36
  46.7 1.8 %collective-permute-start.9 = (bf16[256,512]{1,0:T(8,128)(2,1)S(1)}, bf16[256,512]{1,0:T(8,128)(2,1)S(1)}, u32[]{:S(2)}, u32[]{:S(2)}) collective-permute-start(bf16[256,512]{1,0:T(8,128)(2,1)S(1)} %get-tuple-element.63), channel_id=1, source_target_pairs={{0,32},{4,36},{8,40},{12,44},{16,48},{20,52},{24,56},{28,60},{32,0... | collective-permute-start | bytes 786440 | tf_op jit(solution)/shard_map/ppermute | solution.py:33
  48.6 5.8 %project_late.1 = (bf16[256,1024]{1,0:T(8,128)(2,1)S(1)}, bf16[256,1024]{1,0:T(8,128)(2,1)}) custom-call(bf16[64,4096]{1,0:T(8,128)(2,1)S(1)} %collective-permute-done.refs_0_, bf16[64,4096]{1,0:T(8,128)(2,1)S(1)} %collective-permute-done.7.refs_7_.refs_1_, bf16[4096,1024]{1,0:T(8,128)(2,1)} %refs_2_.3, bf16[256,1024]{1,0:T(8,128)(2,1)} %bitcast.9, ...), custom_call_target="tpu_custom_call" | custom-call | flops 5000000000 | tf_op jit(solution)/shard_map/project_late/pallas_call | solution.py:375
  54.7 2.6 %collective-permute-start.15 = (bf16[2048,256]{1,0:T(8,128)(2,1)S(1)}, bf16[2048,256]{1,0:T(8,128)(2,1)S(1)}, u32[]{:S(2)}, u32[]{:S(2)}) collective-permute-start(bf16[2048,256]{1,0:T(8,128)(2,1)S(1)} %turn_early.1.refs_4_.refs_0_), channel_id=1, source_target_pairs={{0,1},{1,0},{2,3},{3,2},{4,5},{5,4},{6,7},{7,6},{8,9},{9,8},{10,11... | collective-permute-start | bytes 3145736 | tf_op jit(solution)/shard_map/ppermute | solution.py:41
  58.4 3.8 %filter_grad.1.refs_9_.refs_0_ = f32[64,128]{1,0:T(8,128)S(1)} custom-call(bf16[128,1024]{1,0:T(8,128)(2,1)S(1)} %collective-permute-done.2.refs_1_.refs_0_, bf16[256,1024]{1,0:T(8,128)(2,1)} %bitcast.15, bf16[256,1024]{1,0:T(8,128)(2,1)S(1)} %get-tuple-element.61.refs_8_.refs_2_.refs_1_, bf16[1024,256]{1,0:T(8,128)(2,1)S(1)} %turn_late.3.refs_3_.refs_2_), custom_call_target="tpu_custom_call" | custom-call | flops 4000000000 | tf_op jit(solution)/shard_map/filter_grad/pallas_call | solution.py:88
  62.2 1.3 %weight_part.2 = (f32[256,512]{1,0:T(8,128)S(1)}, bf16[288,512]{1,0:T(8,128)(2,1)S(1)}, bf16[288,512]{1,0:T(8,128)(2,1)S(1)}, bf16[288,512]{1,0:T(8,128)(2,1)S(1)}) custom-call(bf16[2048,256]{1,0:T(8,128)(2,1)S(1)} %turn_early.1.refs_4_.refs_0_, bf16[2048,256]{1,0:T(8,128)(2,1)S(1)} %collective-permute-done.15.refs_1_, ...), custom_call_target="tpu_custom_call" | custom-call | flops 3000000000 | tf_op jit(solution)/shard_map/weight_part/pallas_call | solution.py:88
  63.5 1.4 %collective-permute-start.17 = (bf16[288,512]{1,0:T(8,128)(2,1)S(1)}, bf16[288,512]{1,0:T(8,128)(2,1)S(1)}, u32[]{:S(2)}, u32[]{:S(2)}) collective-permute-start(bf16[288,512]{1,0:T(8,128)(2,1)S(1)} %get-tuple-element.73), channel_id=1, source_target_pairs={{0,4},{4,8},{8,12},{12,0},{16,20},{20,24},{24,28},{28,16},{32,36},... | collective-permute-start | bytes 884744 | tf_op jit(solution)/shard_map/ppermute | solution.py:36
  64.9 2.2 %collective-permute-start.18 = (bf16[288,512]{1,0:T(8,128)(2,1)S(1)}, bf16[288,512]{1,0:T(8,128)(2,1)S(1)}, u32[]{:S(2)}, u32[]{:S(2)}) collective-permute-start(bf16[288,512]{1,0:T(8,128)(2,1)S(1)} %get-tuple-element.74), channel_id=1, source_target_pairs={{0,8},{4,12},{8,0},{12,4},{16,24},{20,28},{24,16},{28,20},{32,40},... | collective-permute-start | bytes 884744 | tf_op jit(solution)/shard_map/ppermute | solution.py:36
  67.1 1.2 %collective-permute-start.19 = (bf16[288,512]{1,0:T(8,128)(2,1)S(1)}, bf16[288,512]{1,0:T(8,128)(2,1)S(1)}, u32[]{:S(2)}, u32[]{:S(2)}) collective-permute-start(bf16[288,512]{1,0:T(8,128)(2,1)S(1)} %get-tuple-element.75), channel_id=1, source_target_pairs={{0,12},{4,0},{8,4},{12,8},{16,28},{20,16},{24,20},{28,24},{32,44},... | collective-permute-start | bytes 884744 | tf_op jit(solution)/shard_map/ppermute | solution.py:36
  68.3 1.3 %weight_part.3 = (f32[256,512]{1,0:T(8,128)S(1)}, bf16[256,512]{1,0:T(8,128)(2,1)S(1)}, bf16[256,512]{1,0:T(8,128)(2,1)S(1)}, bf16[256,512]{1,0:T(8,128)(2,1)S(1)}) custom-call(bf16[2048,256]{1,0:T(8,128)(2,1)S(1)} %turn_early.1.refs_4_.refs_0_, bf16[2048,256]{1,0:T(8,128)(2,1)S(1)} %collective-permute-done.15.refs_1_, ...), custom_call_target="tpu_custom_call" | custom-call | flops 3000000000 | tf_op jit(solution)/shard_map/weight_part/pallas_call | solution.py:88
  69.6 1.3 %collective-permute-start.21 = (bf16[256,512]{1,0:T(8,128)(2,1)S(1)}, bf16[256,512]{1,0:T(8,128)(2,1)S(1)}, u32[]{:S(2)}, u32[]{:S(2)}) collective-permute-start(bf16[256,512]{1,0:T(8,128)(2,1)S(1)} %get-tuple-element.77), channel_id=1, source_target_pairs={{0,16},{4,20},{8,24},{12,28},{16,32},{20,36},{24,40},{28,44},{32,4... | collective-permute-start | bytes 786440 | tf_op jit(solution)/shard_map/ppermute | solution.py:33
  70.9 1.5 %collective-permute-start.22 = (bf16[256,512]{1,0:T(8,128)(2,1)S(1)}, bf16[256,512]{1,0:T(8,128)(2,1)S(1)}, u32[]{:S(2)}, u32[]{:S(2)}) collective-permute-start(bf16[256,512]{1,0:T(8,128)(2,1)S(1)} %get-tuple-element.78), channel_id=1, source_target_pairs={{0,32},{4,36},{8,40},{12,44},{16,48},{20,52},{24,56},{28,60},{32,0... | collective-permute-start | bytes 786440 | tf_op jit(solution)/shard_map/ppermute | solution.py:33
  74.3 6.3 %collective-permute-done.18.refs_2_ = bf16[288,512]{1,0:T(8,128)(2,1)S(1)} collective-permute-done((bf16[288,512]{1,0:T(8,128)(2,1)S(1)}, bf16[288,512]{1,0:T(8,128)(2,1)S(1)}, u32[]{:S(2)}, u32[]{:S(2)}) %collective-permute-start.18) | collective-permute-done | bytes 294944 | tf_op jit(solution)/shard_map/ppermute | solution.py:36
  81.5 2.5 %collective-permute-done.24 = f32[64,128]{1,0:T(8,128)S(1)} collective-permute-done((f32[64,128]{1,0:T(8,128)S(1)}, f32[64,128]{1,0:T(8,128)S(1)}, u32[]{:S(2)}, u32[]{:S(2)}) %collective-permute-start.24) | collective-permute-done | bytes 32800 | tf_op jit(solution)/shard_map/ppermute | solution.py:545
  84.0 1.7 %collective-permute-start.25 = (f32[64,128]{1,0:T(8,128)S(1)}, f32[64,128]{1,0:T(8,128)S(1)}, u32[]{:S(2)}, u32[]{:S(2)}) collective-permute-start(f32[64,128]{1,0:T(8,128)S(1)} %add.6), channel_id=1, source_target_pairs={{0,32},{4,36},{8,40},{12,44},{16,48},{20,52},{24,56},{28,60},{32,0... | collective-permute-start | bytes 98312 | tf_op jit(solution)/shard_map/ppermute | solution.py:545
  85.7 5.0 %collective-permute-start.8 = (bf16[128,1024]{1,0:T(8,128)(2,1)S(1)}, bf16[128,1024]{1,0:T(8,128)(2,1)S(1)}, u32[]{:S(2)}, u32[]{:S(2)}) collective-permute-start(bf16[128,1024]{1,0:T(8,128)(2,1)S(1)} %slice.11), channel_id=1, source_target_pairs={{4,0},{8,4},{12,8},{16,12},{20,16},{24,20},{28,24},{32,28},{36,32}... | collective-permute-start | bytes 786440 | tf_op jit(solution)/shard_map/ppermute | solution.py:46
  91.9 1.6 %collective-permute-start.27 = (bf16[80,1024]{1,0:T(8,128)(2,1)S(1)}, bf16[80,1024]{1,0:T(8,128)(2,1)S(1)}, u32[]{:S(2)}, u32[]{:S(2)}) collective-permute-start(bf16[80,1024]{1,0:T(8,128)(2,1)S(1)} %get-tuple-element.83), channel_id=1, source_target_pairs={{0,128},{64,192},{128,0},{192,64},{1,129},{65,193},{129,1},{193,65... | collective-permute-start | bytes 491528 | tf_op jit(solution)/shard_map/ppermute | solution.py:38
  94.4 3.4 %input_grad.1 = bf16[256,1024]{1,0:T(8,128)(2,1)} custom-call(bf16[64,128]{1,0:T(8,128)(2,1)} %refs_0_.3, bf16[256,1024]{1,0:T(8,128)(2,1)S(1)} %get-tuple-element.61.refs_8_.refs_2_.refs_1_, bf16[128,1024]{1,0:T(8,128)(2,1)S(1)} %collective-permute-done.8.refs_2_, f32[64,1024]{1,0:T(8,128)S(1)} %get-tuple-element.80.refs_3_.refs_0_), custom_call_target="tpu_custom_call" | custom-call | tf_op jit(solution)/shard_map/input_grad/pallas_call | solution.py:88
  97.8 6.0 %collective-permute-done.27.refs_2_ = bf16[80,1024]{1,0:T(8,128)(2,1)S(1)} collective-permute-done((bf16[80,1024]{1,0:T(8,128)(2,1)S(1)}, bf16[80,1024]{1,0:T(8,128)(2,1)S(1)}, u32[]{:S(2)}, u32[]{:S(2)}) %collective-permute-start.27) | collective-permute-done | bytes 163872 | tf_op jit(solution)/shard_map/ppermute | solution.py:38
  103.8 5.0 %collective-permute-done.28.refs_3_ = bf16[80,1024]{1,0:T(8,128)(2,1)S(1)} collective-permute-done((bf16[80,1024]{1,0:T(8,128)(2,1)S(1)}, bf16[80,1024]{1,0:T(8,128)(2,1)S(1)}, u32[]{:S(2)}, u32[]{:S(2)}) %collective-permute-start.28) | collective-permute-done | bytes 163872 | tf_op jit(solution)/shard_map/ppermute | solution.py:38
  (45 shorter events, 11.4 us)
Async XLA Ops:
  0.6 5.1 %collective-permute-start.1 = (bf16[64,4096]{1,0:T(8,128)(2,1)}, bf16[64,4096]{1,0:T(8,128)(2,1)S(1)}, u32[]{:S(2)}, u32[]{:S(2)}) collective-permute-start(bf16[64,4096]{1,0:T(8,128)(2,1)} %bitcast.10), channel_id=1, source_target_pairs={{0,1},{1,0},{2,3},{3,2},{4,5},{5,4},{6,7},{7,6},{8,9},{9,8},{10,11... | collective-permute-start | bytes 1572872 | tf_op jit(solution)/shard_map/ppermute | solution.py:41
  2.4 11.9 %collective-permute-start.2 = (bf16[128,1024]{1,0:T(8,128)(2,1)S(1)}, bf16[128,1024]{1,0:T(8,128)(2,1)S(1)}, u32[]{:S(2)}, u32[]{:S(2)}) collective-permute-start(bf16[128,1024]{1,0:T(8,128)(2,1)S(1)} %slice_bitcast_fusion), channel_id=1, source_target_pairs={{0,4},{4,8},{8,12},{12,16},{16,20},{20,24},{24,28},{28,32},{32,36}... | collective-permute-start | bytes 786440 | tf_op jit(solution)/shard_map/ppermute | solution.py:46
  5.6 28.7 %collective-permute-start = (bf16[64,4096]{1,0:T(8,128)(2,1)}, bf16[64,4096]{1,0:T(8,128)(2,1)S(1)}, u32[]{:S(2)}, u32[]{:S(2)}) collective-permute-start(bf16[64,4096]{1,0:T(8,128)(2,1)} %bitcast.11), channel_id=1, source_target_pairs={{0,2},{1,3},{2,0},{3,1},{4,6},{5,7},{6,4},{7,5},{8,10},{9,11},{10,... | collective-permute-start | bytes 1572872 | tf_op jit(solution)/shard_map/ppermute | solution.py:40
  17.7 16.5 %collective-permute-start.3 = (bf16[384,512]{1,0:T(8,128)(2,1)S(1)}, bf16[384,512]{1,0:T(8,128)(2,1)S(1)}, u32[]{:S(2)}, u32[]{:S(2)}) collective-permute-start(bf16[384,512]{1,0:T(8,128)(2,1)S(1)} %get-tuple-element.52), channel_id=1, source_target_pairs={{0,16},{4,20},{8,24},{12,28},{16,32},{20,36},{24,40},{28,44},{32,4... | collective-permute-start | bytes 1179656 | tf_op jit(solution)/shard_map/ppermute | solution.py:33
  19.0 15.2 %collective-permute-start.4 = (bf16[384,512]{1,0:T(8,128)(2,1)S(1)}, bf16[384,512]{1,0:T(8,128)(2,1)S(1)}, u32[]{:S(2)}, u32[]{:S(2)}) collective-permute-start(bf16[384,512]{1,0:T(8,128)(2,1)S(1)} %get-tuple-element.53), channel_id=1, source_target_pairs={{0,48},{4,52},{8,56},{12,60},{16,0},{20,4},{24,8},{28,12},{32,16},... | collective-permute-start | bytes 1179656 | tf_op jit(solution)/shard_map/ppermute | solution.py:33
  19.3 15.0 %collective-permute-start.5 = (bf16[384,512]{1,0:T(8,128)(2,1)S(1)}, bf16[384,512]{1,0:T(8,128)(2,1)S(1)}, u32[]{:S(2)}, u32[]{:S(2)}) collective-permute-start(bf16[384,512]{1,0:T(8,128)(2,1)S(1)} %get-tuple-element.54), channel_id=1, source_target_pairs={{0,4},{4,8},{8,12},{12,0},{16,20},{20,24},{24,28},{28,16},{32,36},... | collective-permute-start | bytes 1179656 | tf_op jit(solution)/shard_map/ppermute | solution.py:36
  19.3 15.0 %collective-permute-start.6 = (bf16[384,512]{1,0:T(8,128)(2,1)S(1)}, bf16[384,512]{1,0:T(8,128)(2,1)S(1)}, u32[]{:S(2)}, u32[]{:S(2)}) collective-permute-start(bf16[384,512]{1,0:T(8,128)(2,1)S(1)} %get-tuple-element.55), channel_id=1, source_target_pairs={{0,12},{4,0},{8,4},{12,8},{16,28},{20,16},{24,20},{28,24},{32,44},... | collective-permute-start | bytes 1179656 | tf_op jit(solution)/shard_map/ppermute | solution.py:36
  34.3 2.7 %collective-permute-start.7 = (bf16[64,4096]{1,0:T(8,128)(2,1)S(1)}, bf16[64,4096]{1,0:T(8,128)(2,1)S(1)}, u32[]{:S(2)}, u32[]{:S(2)}) collective-permute-start(bf16[64,4096]{1,0:T(8,128)(2,1)S(1)} %collective-permute-done.refs_0_), channel_id=1, source_target_pairs={{0,1},{1,0},{2,3},{3,2},{4,5},{5,4},{6,7},{7,6},{8,9},{9,8},{10,11... | collective-permute-start | bytes 1572872 | tf_op jit(solution)/shard_map/ppermute | solution.py:41
  37.6 9.1 %collective-permute-start.10 = (bf16[256,512]{1,0:T(8,128)(2,1)S(1)}, bf16[256,512]{1,0:T(8,128)(2,1)S(1)}, u32[]{:S(2)}, u32[]{:S(2)}) collective-permute-start(bf16[256,512]{1,0:T(8,128)(2,1)S(1)} %get-tuple-element.65), channel_id=1, source_target_pairs={{0,8},{4,12},{8,0},{12,4},{16,24},{20,28},{24,16},{28,20},{32,40},... | collective-permute-start | bytes 786440 | tf_op jit(solution)/shard_map/ppermute | solution.py:36
  40.3 14.0 %collective-permute-start.11 = (bf16[256,512]{1,0:T(8,128)(2,1)S(1)}, bf16[256,512]{1,0:T(8,128)(2,1)S(1)}, u32[]{:S(2)}, u32[]{:S(2)}) collective-permute-start(bf16[256,512]{1,0:T(8,128)(2,1)S(1)} %get-tuple-element.66), channel_id=1, source_target_pairs={{0,16},{4,20},{8,24},{12,28},{16,32},{20,36},{24,40},{28,44},{32,4... | collective-permute-start | bytes 786440 | tf_op jit(solution)/shard_map/ppermute | solution.py:33
  41.5 12.8 %collective-permute-start.12 = (bf16[256,512]{1,0:T(8,128)(2,1)S(1)}, bf16[256,512]{1,0:T(8,128)(2,1)S(1)}, u32[]{:S(2)}, u32[]{:S(2)}) collective-permute-start(bf16[256,512]{1,0:T(8,128)(2,1)S(1)} %get-tuple-element.67), channel_id=1, source_target_pairs={{0,48},{4,52},{8,56},{12,60},{16,0},{20,4},{24,8},{28,12},{32,16},... | collective-permute-start | bytes 786440 | tf_op jit(solution)/shard_map/ppermute | solution.py:33
  41.8 12.6 %collective-permute-start.13 = (bf16[256,512]{1,0:T(8,128)(2,1)S(1)}, bf16[256,512]{1,0:T(8,128)(2,1)S(1)}, u32[]{:S(2)}, u32[]{:S(2)}) collective-permute-start(bf16[256,512]{1,0:T(8,128)(2,1)S(1)} %get-tuple-element.68), channel_id=1, source_target_pairs={{0,4},{4,8},{8,12},{12,0},{16,20},{20,24},{24,28},{28,16},{32,36},... | collective-permute-start | bytes 786440 | tf_op jit(solution)/shard_map/ppermute | solution.py:36
  42.1 12.3 %collective-permute-start.14 = (bf16[256,512]{1,0:T(8,128)(2,1)S(1)}, bf16[256,512]{1,0:T(8,128)(2,1)S(1)}, u32[]{:S(2)}, u32[]{:S(2)}) collective-permute-start(bf16[256,512]{1,0:T(8,128)(2,1)S(1)} %get-tuple-element.69), channel_id=1, source_target_pairs={{0,12},{4,0},{8,4},{12,8},{16,28},{20,16},{24,20},{28,24},{32,44},... | collective-permute-start | bytes 786440 | tf_op jit(solution)/shard_map/ppermute | solution.py:36
  46.7 7.7 %collective-permute-start.9 = (bf16[256,512]{1,0:T(8,128)(2,1)S(1)}, bf16[256,512]{1,0:T(8,128)(2,1)S(1)}, u32[]{:S(2)}, u32[]{:S(2)}) collective-permute-start(bf16[256,512]{1,0:T(8,128)(2,1)S(1)} %get-tuple-element.63), channel_id=1, source_target_pairs={{0,32},{4,36},{8,40},{12,44},{16,48},{20,52},{24,56},{28,60},{32,0... | collective-permute-start | bytes 786440 | tf_op jit(solution)/shard_map/ppermute | solution.py:33
  54.7 7.5 %collective-permute-start.15 = (bf16[2048,256]{1,0:T(8,128)(2,1)S(1)}, bf16[2048,256]{1,0:T(8,128)(2,1)S(1)}, u32[]{:S(2)}, u32[]{:S(2)}) collective-permute-start(bf16[2048,256]{1,0:T(8,128)(2,1)S(1)} %turn_early.1.refs_4_.refs_0_), channel_id=1, source_target_pairs={{0,1},{1,0},{2,3},{3,2},{4,5},{5,4},{6,7},{7,6},{8,9},{9,8},{10,11... | collective-permute-start | bytes 3145736 | tf_op jit(solution)/shard_map/ppermute | solution.py:41
  57.6 4.7 %collective-permute-start.16 = (bf16[1024,256]{1,0:T(8,128)(2,1)S(1)}, bf16[1024,256]{1,0:T(8,128)(2,1)S(1)}, u32[]{:S(2)}, u32[]{:S(2)}) collective-permute-start(bf16[1024,256]{1,0:T(8,128)(2,1)S(1)} %turn_late.2.refs_4_.refs_2_), channel_id=1, source_target_pairs={{0,1},{1,0},{2,3},{3,2},{4,5},{5,4},{6,7},{7,6},{8,9},{9,8},{10,11... | collective-permute-start | bytes 1572872 | tf_op jit(solution)/shard_map/ppermute | solution.py:41
  57.9 10.5 %collective-permute-start.20 = (bf16[1024,256]{1,0:T(8,128)(2,1)S(1)}, bf16[1024,256]{1,0:T(8,128)(2,1)S(1)}, u32[]{:S(2)}, u32[]{:S(2)}) collective-permute-start(bf16[1024,256]{1,0:T(8,128)(2,1)S(1)} %turn_late.3.refs_3_.refs_2_), channel_id=1, source_target_pairs={{0,1},{1,0},{2,3},{3,2},{4,5},{5,4},{6,7},{7,6},{8,9},{9,8},{10,11... | collective-permute-start | bytes 1572872 | tf_op jit(solution)/shard_map/ppermute | solution.py:41
  63.5 9.9 %collective-permute-start.17 = (bf16[288,512]{1,0:T(8,128)(2,1)S(1)}, bf16[288,512]{1,0:T(8,128)(2,1)S(1)}, u32[]{:S(2)}, u32[]{:S(2)}) collective-permute-start(bf16[288,512]{1,0:T(8,128)(2,1)S(1)} %get-tuple-element.73), channel_id=1, source_target_pairs={{0,4},{4,8},{8,12},{12,0},{16,20},{20,24},{24,28},{28,16},{32,36},... | collective-permute-start | bytes 884744 | tf_op jit(solution)/shard_map/ppermute | solution.py:36
  64.9 15.6 %collective-permute-start.18 = (bf16[288,512]{1,0:T(8,128)(2,1)S(1)}, bf16[288,512]{1,0:T(8,128)(2,1)S(1)}, u32[]{:S(2)}, u32[]{:S(2)}) collective-permute-start(bf16[288,512]{1,0:T(8,128)(2,1)S(1)} %get-tuple-element.74), channel_id=1, source_target_pairs={{0,8},{4,12},{8,0},{12,4},{16,24},{20,28},{24,16},{28,20},{32,40},... | collective-permute-start | bytes 884744 | tf_op jit(solution)/shard_map/ppermute | solution.py:36
  67.1 13.5 %collective-permute-start.19 = (bf16[288,512]{1,0:T(8,128)(2,1)S(1)}, bf16[288,512]{1,0:T(8,128)(2,1)S(1)}, u32[]{:S(2)}, u32[]{:S(2)}) collective-permute-start(bf16[288,512]{1,0:T(8,128)(2,1)S(1)} %get-tuple-element.75), channel_id=1, source_target_pairs={{0,12},{4,0},{8,4},{12,8},{16,28},{20,16},{24,20},{28,24},{32,44},... | collective-permute-start | bytes 884744 | tf_op jit(solution)/shard_map/ppermute | solution.py:36
  69.6 21.2 %collective-permute-start.21 = (bf16[256,512]{1,0:T(8,128)(2,1)S(1)}, bf16[256,512]{1,0:T(8,128)(2,1)S(1)}, u32[]{:S(2)}, u32[]{:S(2)}) collective-permute-start(bf16[256,512]{1,0:T(8,128)(2,1)S(1)} %get-tuple-element.77), channel_id=1, source_target_pairs={{0,16},{4,20},{8,24},{12,28},{16,32},{20,36},{24,40},{28,44},{32,4... | collective-permute-start | bytes 786440 | tf_op jit(solution)/shard_map/ppermute | solution.py:33
  70.9 19.9 %collective-permute-start.22 = (bf16[256,512]{1,0:T(8,128)(2,1)S(1)}, bf16[256,512]{1,0:T(8,128)(2,1)S(1)}, u32[]{:S(2)}, u32[]{:S(2)}) collective-permute-start(bf16[256,512]{1,0:T(8,128)(2,1)S(1)} %get-tuple-element.78), channel_id=1, source_target_pairs={{0,32},{4,36},{8,40},{12,44},{16,48},{20,52},{24,56},{28,60},{32,0... | collective-permute-start | bytes 786440 | tf_op jit(solution)/shard_map/ppermute | solution.py:33
  73.4 17.4 %collective-permute-start.23 = (bf16[256,512]{1,0:T(8,128)(2,1)S(1)}, bf16[256,512]{1,0:T(8,128)(2,1)S(1)}, u32[]{:S(2)}, u32[]{:S(2)}) collective-permute-start(bf16[256,512]{1,0:T(8,128)(2,1)S(1)} %get-tuple-element.79), channel_id=1, source_target_pairs={{0,48},{4,52},{8,56},{12,60},{16,0},{20,4},{24,8},{28,12},{32,16},... | collective-permute-start | bytes 786440 | tf_op jit(solution)/shard_map/ppermute | solution.py:33
  80.6 3.4 %collective-permute-start.24 = (f32[64,128]{1,0:T(8,128)S(1)}, f32[64,128]{1,0:T(8,128)S(1)}, u32[]{:S(2)}, u32[]{:S(2)}) collective-permute-start(f32[64,128]{1,0:T(8,128)S(1)} %filter_sum_y.1), channel_id=1, source_target_pairs={{0,16},{4,20},{8,24},{12,28},{16,0},{20,4},{24,8},{28,12},{32,48},... | collective-permute-start | bytes 98312 | tf_op jit(solution)/shard_map/ppermute | solution.py:545
  84.0 6.8 %collective-permute-start.25 = (f32[64,128]{1,0:T(8,128)S(1)}, f32[64,128]{1,0:T(8,128)S(1)}, u32[]{:S(2)}, u32[]{:S(2)}) collective-permute-start(f32[64,128]{1,0:T(8,128)S(1)} %add.6), channel_id=1, source_target_pairs={{0,32},{4,36},{8,40},{12,44},{16,48},{20,52},{24,56},{28,60},{32,0... | collective-permute-start | bytes 98312 | tf_op jit(solution)/shard_map/ppermute | solution.py:545
  85.7 8.7 %collective-permute-start.8 = (bf16[128,1024]{1,0:T(8,128)(2,1)S(1)}, bf16[128,1024]{1,0:T(8,128)(2,1)S(1)}, u32[]{:S(2)}, u32[]{:S(2)}) collective-permute-start(bf16[128,1024]{1,0:T(8,128)(2,1)S(1)} %slice.11), channel_id=1, source_target_pairs={{4,0},{8,4},{12,8},{16,12},{20,16},{24,20},{28,24},{32,28},{36,32}... | collective-permute-start | bytes 786440 | tf_op jit(solution)/shard_map/ppermute | solution.py:46
  91.2 6.6 %collective-permute-start.26 = (bf16[80,1024]{1,0:T(8,128)(2,1)S(1)}, bf16[80,1024]{1,0:T(8,128)(2,1)S(1)}, u32[]{:S(2)}, u32[]{:S(2)}) collective-permute-start(bf16[80,1024]{1,0:T(8,128)(2,1)S(1)} %get-tuple-element.82), channel_id=1, source_target_pairs={{0,64},{64,128},{128,192},{192,0},{1,65},{65,129},{129,193},{193,1... | collective-permute-start | bytes 491528 | tf_op jit(solution)/shard_map/ppermute | solution.py:38
  91.9 11.9 %collective-permute-start.27 = (bf16[80,1024]{1,0:T(8,128)(2,1)S(1)}, bf16[80,1024]{1,0:T(8,128)(2,1)S(1)}, u32[]{:S(2)}, u32[]{:S(2)}) collective-permute-start(bf16[80,1024]{1,0:T(8,128)(2,1)S(1)} %get-tuple-element.83), channel_id=1, source_target_pairs={{0,128},{64,192},{128,0},{192,64},{1,129},{65,193},{129,1},{193,65... | collective-permute-start | bytes 491528 | tf_op jit(solution)/shard_map/ppermute | solution.py:38
  93.5 15.2 %collective-permute-start.28 = (bf16[80,1024]{1,0:T(8,128)(2,1)S(1)}, bf16[80,1024]{1,0:T(8,128)(2,1)S(1)}, u32[]{:S(2)}, u32[]{:S(2)}) collective-permute-start(bf16[80,1024]{1,0:T(8,128)(2,1)S(1)} %get-tuple-element.84), channel_id=1, source_target_pairs={{0,192},{64,0},{128,64},{192,128},{1,193},{65,1},{129,65},{193,129... | collective-permute-start | bytes 491528 | tf_op jit(solution)/shard_map/ppermute | solution.py:38

commit v6 on v3

v6 whole, which is shorter than its diff:
```python
import math

import jax
import jax.numpy as jnp
from jax import lax
from jax.experimental import pallas as pl
from jax.experimental.pallas import tpu as pltpu
from jax.sharding import PartitionSpec as P

F32 = jnp.float32
BF16 = jnp.bfloat16
SIDE = 4
TAPS = 128
GROUP = 16
LANES = 128
PER_TILE = LANES // GROUP
WIDE = 256


def room(mebibytes):
    return pltpu.CompilerParams(vmem_limit_bytes=mebibytes * 1024 * 1024)


def spot():
    ctx = lax.axis_index("ctx")
    tp = lax.axis_index("tp")
    return ctx // SIDE, ctx % SIDE, lax.axis_index("dp"), tp // 2, tp % 2


def moved(x, axis):
    step = 2 if axis == "half" else 1
    return lax.ppermute(x, "tp", [(i, i ^ step) for i in range(4)])


def in_plane(x, gather, target):
    pairs = []
    for i in range(SIDE * SIDE):
        for j in range(4):
            place_x, place_y = divmod(i, SIDE)
            if (j % 2 == 0) == gather:
                place_x = target(place_x)
            else:
                place_y = target(place_y)
            pairs.append((i * 4 + j, (place_x * SIDE + place_y) * 4 + j))
    return lax.ppermute(x, ("ctx", "tp"), pairs)


def stepped(x, gather, by):
    return in_plane(x, gather, lambda place: (place + by) % SIDE)


def shifted(x, by):
    devices = lax.axis_size("ctx")
    return lax.ppermute(x, "ctx", [(i, i + by) for i in range(devices) if 0 <= i + by < devices])


ANYWHERE = pl.BlockSpec(memory_space=pl.ANY)
HALF = LANES // 2


def resident(x):
    return pltpu.with_memory_space_constraint(x, pltpu.HBM)


def whole(shape, place=None):
    place = place or (0,) * len(shape)
    return pl.BlockSpec(tuple(shape), lambda i: place, pipeline_mode=pl.Buffered(1))


def full(shape):
    return pl.BlockSpec(tuple(shape), lambda i: (0,) * len(shape))


def tile(rows, width):
    return pl.BlockSpec((rows, width), lambda i: (0, i))


def iota(shape, dim):
    return lax.broadcasted_iota(jnp.int32, shape, dim)


def aligned(index, size):
    return pl.ds(pl.multiple_of(index * size, size), size)


def lasting(microseconds):
    return pl.CostEstimate(flops=int(microseconds * 1e9), bytes_accessed=0, transcendentals=0)


def once(kernel, name, ins, outs, scratch=(), after=(), lasts=0):
    def body(*refs):
        kernel(*refs[: len(ins)], *refs[len(ins) + len(after) :])

    specs = [i[1] if isinstance(i, tuple) else whole(i.shape) for i in ins]
    arrays = [i[0] if isinstance(i, tuple) else i for i in ins]
    return pl.pallas_call(
        body,
        grid=(1,),
        in_specs=specs + [ANYWHERE] * len(after),
        out_specs=[whole(shape) for shape, _ in outs],
        out_shape=[jax.ShapeDtypeStruct(shape, dtype) for shape, dtype in outs],
        scratch_shapes=list(scratch),
        compiler_params=room(20),
        cost_estimate=lasting(lasts),
        name=name,
    )(*arrays, *after)


def first_rows(filters, shifted_by):
    lane, tap = iota((TAPS, 2 * TAPS), 1), iota((TAPS, 2 * TAPS), 0)
    place = lane == (TAPS - tap if shifted_by else tap)
    return jnp.dot(filters, place.astype(F32).astype(BF16), preferred_element_type=F32)


def banded(rows, stack):
    for g in range(PER_TILE):
        first = jnp.broadcast_to(rows[g : g + 1], (TAPS, 2 * TAPS))
        skewed = pltpu.roll(first, 0, 1, stride=1, stride_axis=0)
        stack[g * TAPS : (g + 1) * TAPS, :] = skewed.astype(BF16)


def lane_group(shape):
    return iota(shape, len(shape) - 1) % LANES // GROUP


def own_lanes(stacked):
    group = lane_group((TAPS, 2 * LANES))
    chosen = jnp.zeros((TAPS, 2 * LANES), F32)
    for g in range(PER_TILE):
        chosen = jnp.where(group == g, stacked[g * TAPS : (g + 1) * TAPS], chosen)
    return chosen


def two_windows(first, second, third):
    upper = jnp.concatenate([first, second], 1)
    lower = jnp.concatenate([second, third], 1)
    return jnp.concatenate([upper, lower], 0)


def forward_kernel(filters, previous, signal, gating, response, kept, *refs):
    given, gated, stack = refs[:2], refs[2], refs[3]
    _, _, _, _, core = spot()
    rows = first_rows(filters[...], True)
    for i in range(signal.shape[1] // LANES):
        columns = slice(i * LANES, (i + 1) * LANES)
        band = stack.at[i % 2]
        banded(rows[i * PER_TILE : (i + 1) * PER_TILE], band)
        window = two_windows(previous[:, columns], signal[:TAPS, columns], signal[TAPS:, columns])
        made = own_lanes(jnp.dot(band[...], window, preferred_element_type=F32))
        for block in range(2):
            tokens = slice(block * TAPS, (block + 1) * TAPS)
            part = made[:, block * LANES : (block + 1) * LANES]
            response[tokens, columns] = part
            gated[tokens, columns] = (part * gating[tokens, columns].astype(F32)).astype(BF16)
    kept[...] = gated[:, aligned(core, kept.shape[1])]
    for i, out in enumerate(given):
        out[...] = gated[i * TAPS : (i + 1) * TAPS, aligned(1 - core, kept.shape[1])]


def forward(filters, previous, signal, gating):
    length, channels = signal.shape
    quarter = ((TAPS, channels // 2), BF16)
    return once(
        forward_kernel,
        "conv_forward",
        [filters, previous, signal, gating],
        [((length, channels), F32), ((length, channels // 2), BF16), quarter, quarter],
        [
            pltpu.VMEM((length, channels), BF16),
            pltpu.VMEM((2, PER_TILE * TAPS, 2 * TAPS), BF16),
        ],
    )


def join_kernel(kept, upper, lower, gated):
    _, _, _, _, core = spot()
    width = kept.shape[1]
    gated[: 2 * TAPS, aligned(core, width)] = kept[...]
    gated[:TAPS, aligned(1 - core, width)] = upper[...]
    gated[TAPS : 2 * TAPS, aligned(1 - core, width)] = lower[...]
    gated[2 * TAPS :] = gated[: gated.shape[0] - 2 * TAPS]


def join(kept, received, after):
    length, width = kept.shape
    shape = (length + 16, 2 * width)
    return once(join_kernel, "join", [kept, *received], [(shape, BF16)], (), after)[0]


def input_grad_kernel(filters, conv_grad, following, grad_input, stack):
    rows = first_rows(filters[...], False)
    for i in range(conv_grad.shape[1] // LANES):
        columns = slice(i * LANES, (i + 1) * LANES)
        band = stack.at[i % 2]
        banded(rows[i * PER_TILE : (i + 1) * PER_TILE], band)
        window = two_windows(
            conv_grad[:TAPS, columns], conv_grad[TAPS:, columns], following[:, columns]
        )
        made = own_lanes(jnp.dot(band[...], window, preferred_element_type=F32))
        for block in range(2):
            grad_input[block * TAPS : (block + 1) * TAPS, columns] = made[
                :, block * LANES : (block + 1) * LANES
            ].astype(BF16)


def input_grad(filters, conv_grad, following, after):
    return once(
        input_grad_kernel,
        "input_grad",
        [filters, conv_grad, following],
        [(conv_grad.shape, BF16)],
        [pltpu.VMEM((2, PER_TILE * TAPS, 2 * TAPS), BF16)],
        after,
    )[0]


def filter_grad_kernel(previous, signal, conv_grad, grad_filter, stack):
    square = (2 * TAPS, 2 * TAPS)
    turn = iota(square, 0) == (2 * TAPS - iota(square, 1)) % (2 * TAPS)
    turn = turn.astype(F32).astype(BF16)
    group = lane_group((TAPS, 2 * LANES))
    for i in range(signal.shape[1] // LANES):
        columns = slice(i * LANES, (i + 1) * LANES)
        masked = stack.at[i % 2]
        inputs = two_windows(previous[:, columns], signal[:TAPS, columns], signal[TAPS:, columns])
        turned = jnp.dot(turn, inputs, preferred_element_type=F32).astype(BF16)
        both = jnp.concatenate([conv_grad[:TAPS, columns], conv_grad[TAPS:, columns]], 1)
        both = both.astype(F32)
        for g in range(PER_TILE):
            masked[g * TAPS : (g + 1) * TAPS, :] = jnp.where(group == g, both, 0.0).astype(BF16)
        products = lax.dot_general(
            masked[...], turned, (((1,), (1,)), ((), ())), preferred_element_type=F32
        )
        for g in range(PER_TILE):
            skewed = pltpu.roll(products[g * TAPS : (g + 1) * TAPS], 0, 1, stride=1, stride_axis=0)
            row = i * PER_TILE + g
            grad_filter[row : row + 1, :] = jnp.sum(skewed[:, TAPS:], axis=0, keepdims=True)


def filter_grad(previous, signal, conv_grad, after):
    return once(
        filter_grad_kernel,
        "filter_grad",
        [previous, signal, conv_grad],
        [((signal.shape[1] // GROUP, TAPS), F32)],
        [pltpu.VMEM((2, PER_TILE * TAPS, 2 * TAPS), BF16)],
        after,
        4,
    )[0]


def pack_into(mine, other, outs):
    x, y, _, _, core = spot()
    part = mine.shape[0]
    depth = mine.shape[1] // SIDE

    @pl.when(core == 0)
    def _():
        for ref, rows in ((mine, slice(0, part)), (other, slice(part, 2 * part))):
            for s, out in enumerate(outs):
                for d in range(SIDE):
                    start = pl.multiple_of(d * depth + (x + s) % SIDE * WIDE, WIDE)
                    out[rows, d * WIDE : (d + 1) * WIDE] = ref[:, pl.ds(start, WIDE)]

    @pl.when(core == 1)
    def _():
        lower = iota((part, LANES), 1) < HALF
        for ref, rows in ((other, slice(0, part)), (mine, slice(part, 2 * part))):
            for s, out in enumerate(outs):
                to = (y + s) % SIDE
                upper_half = jnp.broadcast_to(to % 2, (part, LANES)) == 1
                for pair in range(2 * SIDE):
                    runs = []
                    for i in range(2):
                        start = pl.multiple_of((2 * pair + i) * WIDE + to // 2 * LANES, LANES)
                        runs.append(ref[:, pl.ds(start, LANES)].astype(F32))
                    first = jnp.where(upper_half, pltpu.roll(runs[0], HALF, 1), runs[0])
                    second = jnp.where(upper_half, runs[1], pltpu.roll(runs[1], HALF, 1))
                    both = jnp.where(lower, first, second).astype(BF16)
                    out[rows, pair * LANES : (pair + 1) * LANES] = both


def pack_kernel(mine, other, *outs):
    pack_into(mine, other, outs)


def pack(mine, other):
    rows, width = mine.shape
    return once(
        pack_kernel, "pack", [mine, other], [((2 * rows, width // SIDE), BF16)] * SIDE
    )


def relay_kernel(mine, other, before, after, opposite, *outs):
    pack_into(mine, other, outs)
    part = opposite.shape[0]
    outs[1][part:] = before[...]
    outs[2][part:] = opposite[...]
    outs[3][part:] = after[...]


def relay(mine, other, got_next, got_last, opposite):
    rows, width = opposite.shape
    return once(
        relay_kernel,
        "relay",
        [
            mine,
            other,
            (got_next, whole((TAPS, width))),
            (got_last, whole((TAPS, width), (1, 0))),
            opposite,
        ],
        [((rows, width), BF16)] + [((rows + TAPS, width), BF16)] * (SIDE - 1),
    )


def project_kernel(mine, other, weight, gating, response, *refs):
    _, _, _, half, core = spot()
    part = mine.shape[0]
    rows = refs[-1]
    conv_grad, grad_gate = refs[-3:-1]

    @pl.when(pl.program_id(0) == 0)
    def _():
        rows[aligned(core, part), :] = mine[...]
        rows[aligned(1 - core, part), :] = other[...]

    late = len(refs) > 3
    tokens = aligned(1 - half if late else half, TAPS)
    made = jnp.dot(rows[...], weight[...], preferred_element_type=F32)
    made_conv = (made * gating[tokens, :].astype(F32)).astype(BF16)
    made_gate = (made * response[tokens, :]).astype(BF16)
    if late:
        conv_grad[tokens, :] = made_conv
        grad_gate[tokens, :] = made_gate
        conv_grad[aligned(half, TAPS), :] = refs[0][...]
        grad_gate[aligned(half, TAPS), :] = refs[1][...]
    else:
        conv_grad[...] = made_conv
        grad_gate[...] = made_gate


def project(mine, other, weight, gating, response, done=(), after=()):
    length, channels = gating.shape
    depth = weight.shape[0]
    made = length if done else 2 * mine.shape[0]

    def body(*refs):
        kept = 5 + len(done)
        project_kernel(*refs[:kept], *refs[kept + len(after) :])

    return pl.pallas_call(
        body,
        grid=(channels // WIDE,),
        in_specs=[full(mine.shape)] * 2
        + [tile(depth, WIDE), tile(length, WIDE), tile(length, WIDE)]
        + [tile(TAPS, WIDE)] * len(done)
        + [ANYWHERE] * len(after),
        out_specs=[tile(made, WIDE)] * 2,
        out_shape=[jax.ShapeDtypeStruct((made, channels), BF16)] * 2,
        scratch_shapes=[pltpu.VMEM((2 * mine.shape[0], depth), BF16)],
        compiler_params=room(16),
        cost_estimate=lasting(5 if done else 0),
        name="project_late" if done else "project_early",
    )(mine, other, weight, gating, response, *done, *after)


def high_and_low(x):
    high = x.astype(BF16).astype(F32)
    return high, (x - high).astype(BF16).astype(F32)


def folded(x, rows):
    return jnp.concatenate([x[i : i + rows] for i in range(0, x.shape[0], rows)], 1)


def unfolded(x):
    return jnp.concatenate([x[:, i : i + LANES] for i in range(0, x.shape[1], LANES)], 0)


def riding(ref, start, rows):
    pair = ref[start : start + 2 * rows].astype(F32)
    return unfolded(pair[:rows] + pair[rows:])


def four_sum(parts):
    return (parts[0] + parts[2]) + (parts[1] + parts[3])


def weight_kernel(*refs):
    early, late = refs[:SIDE], refs[SIDE : 2 * SIDE]
    gated, got_next, before, after, got_last = refs[2 * SIDE : 2 * SIDE + 5]
    outs, turned, tokens = refs[-2 - SIDE : -2], refs[-2], refs[-1]
    x, y, _, half, core = spot()
    me = jnp.where(core == 0, y, x)
    upper = jnp.broadcast_to(half, before.shape) == 0
    opposite = (before[...].astype(F32), after[...].astype(F32))
    for i, (parts, h) in enumerate(((early, half), (late, 1 - half))):
        rows = aligned(h, TAPS)
        halves = opposite if i == 0 else opposite[::-1]
        blocks = (
            gated[rows, :],
            got_next[rows, :],
            jnp.where(upper, *halves).astype(BF16),
            got_last[rows, :],
        )
        for s in range(SIDE):
            at = slice((i * SIDE + s) * TAPS, (i * SIDE + s + 1) * TAPS)
            tokens[at] = blocks[s]
            transposed = parts[s][...].T
            for d in range(SIDE):
                for q in range(SIDE):
                    to = (q - me + SIDE) % SIDE * WIDE + d * HALF
                    start = d * WIDE + q * HALF
                    turned[pl.ds(pl.multiple_of(to, HALF), HALF), at] = transposed[
                        start : start + HALF
                    ]
    for s, out in enumerate(outs):
        features = turned[s * WIDE : (s + 1) * WIDE]
        out[...] = jnp.dot(features, tokens[...], preferred_element_type=F32).astype(out.dtype)


def weight_parts(early, own_late, gated, got, late, after):
    width = gated.shape[1]
    rows = own_late.shape[0]
    length = 2 * rows

    def block(array, start, count=rows):
        return array, whole((count, width), (start // count, 0))

    shape = (width // SIDE, width)
    return once(
        weight_kernel,
        "weight_parts",
        [
            early[0],
            early[1],
            block(late[1], rows),
            early[2],
            own_late,
            *[block(part, 0) for part in late],
            block(gated, 0, length),
            block(got[0], 0, length),
            block(late[0], rows),
            block(late[2], rows),
            block(got[1], 0, length),
        ],
        [(shape, F32)] + [(shape, BF16)] * (SIDE - 1),
        [pltpu.VMEM((width, 2 * SIDE * rows), BF16), pltpu.VMEM((2 * SIDE * rows, width), BF16)],
        after,
        4,
    )


def high_and_low(x):
    high = x.astype(BF16).astype(F32)
    return high, (x - high).astype(BF16).astype(F32)


def folded(x, rows):
    return jnp.concatenate([x[i : i + rows] for i in range(0, x.shape[0], rows)], 1)


def unfolded(x):
    return jnp.concatenate([x[:, i : i + LANES] for i in range(0, x.shape[1], LANES)], 0)


def riding(ref, start, rows):
    pair = ref[start : start + 2 * rows].astype(F32)
    return unfolded(pair[:rows] + pair[rows:])


def four_sum(parts):
    return (parts[0] + parts[2]) + (parts[1] + parts[3])


def first_sum_kernel(*refs):
    _, _, z, _, _ = spot()
    extra, outs, own_extra, kept = refs[SIDE], refs[SIDE + 1 : -2], refs[-2], refs[-1]
    run = kept.shape[0] // SIDE
    total = refs[0][...]
    for ref in refs[1:SIDE]:
        total = total + ref[...].astype(F32)
    for d in range(SIDE):
        kept[aligned((d - z + SIDE) % SIDE, run), :] = total[d * run : (d + 1) * run]
    high, low = (folded(part, own_extra.shape[0]) for part in high_and_low(extra[...]))
    own_extra[...] = high + low
    for s, out in enumerate(outs):
        out[:run] = kept[s * run : (s + 1) * run, :].astype(out.dtype)
        if s:
            out[run:] = jnp.concatenate([high, low], 0).astype(BF16)


def first_sum(parts, extra, after):
    rows, width = parts[0].shape
    below = LANES * extra.shape[0] // width
    run = rows // SIDE
    *sums, own_extra = once(
        first_sum_kernel,
        "first_sum",
        [*parts, extra],
        [((run, width), F32)]
        + [((run + 2 * below, width), BF16)] * (SIDE - 1)
        + [((below, width), F32)],
        [pltpu.VMEM((rows, width), F32)],
        after,
        1,
    )
    return sums, own_extra


def last_sum(parts, own_extra, filters, scale, filter_scale, after):
    rows, width = parts[0].shape
    below = own_extra.shape[0]

    def kernel(*refs):
        own, others, extra = refs[0], refs[1:SIDE], refs[SIDE]
        kept, given, filter_out, summed = refs[SIDE + 1 :]
        _, _, _, _, core = spot()
        total = own[...]
        for ref in others:
            total = total + ref[:rows].astype(F32)
        summed[...] = total * scale
        kept[...] = summed[:, aligned(core, width // 2)]
        given[...] = summed[:, aligned(1 - core, width // 2)]
        values = [unfolded(extra[...])] + [riding(ref, rows, below) for ref in others]
        filter_out[...] = four_sum(values) * filter_scale

    half = ((rows, width // 2), F32)
    return once(
        kernel,
        "last_sum",
        [*parts, own_extra],
        [half, half, (filters.shape, F32)],
        [pltpu.VMEM((rows, width), F32)],
        after,
    )


def beside(kept, received):
    def kernel(first, second, out):
        _, _, _, _, core = spot()
        out[:, aligned(core, first.shape[1])] = first[...]
        out[:, aligned(1 - core, first.shape[1])] = second[...]

    rows, width = kept.shape
    return once(kernel, "beside", [kept, received], [((rows, 2 * width), F32)])[0]


def tied(x, *after):
    return lax.optimization_barrier((x, *after))[0]


def paired(x, gather, by, before=()):
    return x + in_plane(tied(x, *before), gather, lambda place: place ^ by)


def local(conv_input, gate_value, out_grad, out_weight, filters):
    signal, gating, grads = conv_input[0], gate_value[0], out_grad[0]
    length, channels = signal.shape
    halo_sent = signal[length - TAPS :]
    signal, gating, filters, weight = (
        resident(x) for x in (signal, gating, filters, out_weight)
    )
    tokens_all = lax.axis_size("dp") * lax.axis_size("ctx") * length
    shifts = range(1, SIDE)

    late = moved(grads, "half")
    previous = shifted(halo_sent, 1)
    early_other = moved(grads, "core")
    grads = resident(grads)
    early = pack(grads, early_other)
    early_got = [stepped(early[1], True, 1), stepped(early[3], True, 3)]
    response, kept, *given = forward(filters, previous, signal, gating)
    gated = join(kept, [moved(part, "core") for part in given], early_got)
    got = [stepped(gated, True, 1), stepped(gated, True, 3)]
    conv_early, gate_early = project(grads, early_other, weight, gating, response)

    late_other = moved(tied(late, conv_early), "core")
    own_late, *late_sent = relay(late, late_other, *got, early[2])
    conv_grad, grad_gate = project(
        late, late_other, weight, gating, response, (conv_early, gate_early), (own_late,)
    )
    late_got = [stepped(late_sent[s - 1], True, s) for s in shifts]
    following = shifted(conv_grad[:TAPS], -1)
    filter_sum = filter_grad(previous, signal, conv_grad, ())
    parts = weight_parts([early[0], *early_got], own_late, gated, got, late_got, (filter_sum,))

    filter_sum = paired(filter_sum, True, 1)
    filter_sum = paired(filter_sum, True, 2, (parts[0],))
    filter_sum = paired(paired(filter_sum, False, 1), False, 2)
    parts = [parts[0]] + [stepped(parts[s], False, s) for s in shifts]
    sums, own_filter = first_sum(parts, filter_sum, (following,))
    grad_input = input_grad(filters, conv_grad, following, (sums[0],))
    line = [[(i, (i + s) % SIDE) for i in range(SIDE)] for s in shifts]
    sums = [sums[0]] + [lax.ppermute(sums[s], "dp", line[s - 1]) for s in shifts]
    kept, given, grad_filter = last_sum(
        sums,
        own_filter,
        filters,
        1.0 / math.sqrt(tokens_all),
        1.0 / math.sqrt(tokens_all * GROUP),
        (resident(grad_input),),
    )
    grad_weight = beside(kept, moved(given, "core"))
    return (grad_input[None], grad_gate[None], grad_weight, grad_filter)


def solution(mesh):
    placed = (
        P("dp", "ctx", "tp"),
        P("dp", "ctx", "tp"),
        P("dp", ("ctx", "tp"), None),
        P(None, "tp"),
        P("tp", None),
    )
    return jax.shard_map(
        local,
        mesh=mesh,
        in_specs=placed,
        out_specs=(
            P("dp", "ctx", "tp"),
            P("dp", "ctx", "tp"),
            P(("dp", "ctx"), "tp"),
            P("tp", None),
        ),
        check_vma=False,
    )
```

time: 123 us -> 105 us (0.85)
  the two profiles are of different devices: /device:TPU:2 before, /device:TPU:1 now
where the time goes in v6:
time: 105 us
  starting transfers between devices  50.7 us (48%)
  Pallas kernels  29.6 us (28%)
  waiting for transfers between devices  23 us (22%)
    ppermute x14, starting transfers between devices, in_plane(): return lax.ppermute(x, ('ctx', 'tp'), pairs)  22.5 us
    ppermute x6, starting transfers between devices, moved(): return lax.ppermute(x, 'tp', [(i, i ^ step) for i in range(4)])  20.1 us
    pallas_call x10, Pallas kernels, once(): pl.pallas_call(body, grid=(1,), in_specs=specs + [ANYWHERE] * len(after),...  18.6 us
    ppermute x14, waiting for transfers between devices, in_plane(): return lax.ppermute(x, ('ctx', 'tp'), pairs)  16.3 us
    pallas_call x2, Pallas kernels, project(): pl.pallas_call(body, grid=(channels // WIDE,), in_specs=[full(mine.shape)...  11 us
    ppermute x2, starting transfers between devices, shifted(): lax.ppermute(x, 'ctx', [(i, i + by) for i in range(devices) if 0 <= i + b...  4.51 us
    ppermute x6, waiting for transfers between devices, moved(): return lax.ppermute(x, 'tp', [(i, i ^ step) for i in range(4)])  3.78 us
    ppermute x3, starting transfers between devices, local(): lax.ppermute(sums[s], 'dp', line[s - 1])  3.64 us
  transfers between devices with their start and end apart: 25, of which 11 were waited for; matrix products, arithmetic and copies ran while one was open for 1% of the time, Pallas kernels for 22%

profile of v6, /device:TPU:1, one launch (start us, length us, event | category | flops | bytes accessed | tf_op | source)
XLA Modules:
  0.0 105.0 jit_solution(8477968802327111185)
XLA Ops:
  0.6 3.3 %collective-permute-start.1 = (bf16[64,4096]{1,0:T(8,128)(2,1)}, bf16[64,4096]{1,0:T(8,128)(2,1)S(1)}, u32[]{:S(2)}, u32[]{:S(2)}) collective-permute-start(bf16[64,4096]{1,0:T(8,128)(2,1)} %bitcast.8), channel_id=1, source_target_pairs={{0,1},{1,0},{2,3},{3,2},{4,5},{5,4},{6,7},{7,6},{8,9},{9,8},{10,11... | collective-permute-start | bytes 1572872 | tf_op jit(solution)/shard_map/ppermute | solution.py:32
  4.0 5.2 %collective-permute-start = (bf16[64,4096]{1,0:T(8,128)(2,1)}, bf16[64,4096]{1,0:T(8,128)(2,1)S(1)}, u32[]{:S(2)}, u32[]{:S(2)}) collective-permute-start(bf16[64,4096]{1,0:T(8,128)(2,1)} %bitcast.9), channel_id=1, source_target_pairs={{0,2},{1,3},{2,0},{3,1},{4,6},{5,7},{6,4},{7,5},{8,10},{9,11},{10,... | collective-permute-start | bytes 1572872 | tf_op jit(solution)/shard_map/ppermute | solution.py:32
  10.1 3.2 %collective-permute-start.2 = (bf16[128,1024]{1,0:T(8,128)(2,1)S(1)}, bf16[128,1024]{1,0:T(8,128)(2,1)S(1)}, u32[]{:S(2)}, u32[]{:S(2)}) collective-permute-start(bf16[128,1024]{1,0:T(8,128)(2,1)S(1)} %slice_bitcast_fusion), channel_id=1, source_target_pairs={{0,4},{4,8},{8,12},{12,16},{16,20},{20,24},{24,28},{28,32},{32,36}... | collective-permute-start | bytes 786440 | tf_op jit(solution)/shard_map/ppermute | solution.py:54
  13.4 2.0 %pack.1 = (bf16[128,1024]{1,0:T(8,128)(2,1)S(1)}, bf16[128,1024]{1,0:T(8,128)(2,1)S(1)}, bf16[128,1024]{1,0:T(8,128)(2,1)S(1)}, bf16[128,1024]{1,0:T(8,128)(2,1)S(1)}) custom-call(bf16[64,4096]{1,0:T(8,128)(2,1)} %bitcast.10, bf16[64,4096]{1,0:T(8,128)(2,1)S(1)} %collective-permute-done.1.refs_1_), custom_call_target="tpu_custom_call" | custom-call | tf_op jit(solution)/shard_map/pack/pallas_call | solution.py:96
  15.4 1.4 %collective-permute-start.6 = (bf16[128,1024]{1,0:T(8,128)(2,1)S(1)}, bf16[128,1024]{1,0:T(8,128)(2,1)S(1)}, u32[]{:S(2)}, u32[]{:S(2)}) collective-permute-start(bf16[128,1024]{1,0:T(8,128)(2,1)S(1)} %get-tuple-element.41), channel_id=1, source_target_pairs={{0,16},{1,5},{2,18},{3,7},{4,20},{5,9},{6,22},{7,11},{8,24},{9,13}... | collective-permute-start | bytes 786440 | tf_op jit(solution)/shard_map/ppermute | solution.py:45
  16.7 1.4 %collective-permute-start.7 = (bf16[128,1024]{1,0:T(8,128)(2,1)S(1)}, bf16[128,1024]{1,0:T(8,128)(2,1)S(1)}, u32[]{:S(2)}, u32[]{:S(2)}) collective-permute-start(bf16[128,1024]{1,0:T(8,128)(2,1)S(1)} %get-tuple-element.42), channel_id=1, source_target_pairs={{0,48},{1,13},{2,50},{3,15},{4,52},{5,1},{6,54},{7,3},{8,56},{9,5}... | collective-permute-start | bytes 786440 | tf_op jit(solution)/shard_map/ppermute | solution.py:45
  18.6 3.4 %conv_forward.1 = (f32[256,1024]{1,0:T(8,128)S(1)}, bf16[256,512]{1,0:T(8,128)(2,1)S(1)}, bf16[128,512]{1,0:T(8,128)(2,1)S(1)}, bf16[128,512]{1,0:T(8,128)(2,1)S(1)}) custom-call(bf16[64,128]{1,0:T(8,128)(2,1)} %refs_0_.3, bf16[128,1024]{1,0:T(8,128)(2,1)S(1)} %collective-permute-done.2.refs_1_.refs_0_, bf16[256,1024]{1,0:T(8,128)(2,1)} %bitcast.15, ...), custom_call_target="tpu_custom_call" | custom-call | tf_op jit(solution)/shard_map/conv_forward/pallas_call | solution.py:96
  22.1 2.1 %collective-permute-start.4 = (bf16[128,512]{1,0:T(8,128)(2,1)S(1)}, bf16[128,512]{1,0:T(8,128)(2,1)S(1)}, u32[]{:S(2)}, u32[]{:S(2)}) collective-permute-start(bf16[128,512]{1,0:T(8,128)(2,1)S(1)} %get-tuple-element.39), channel_id=1, source_target_pairs={{0,1},{1,0},{2,3},{3,2},{4,5},{5,4},{6,7},{7,6},{8,9},{9,8},{10,11... | collective-permute-start | bytes 393224 | tf_op jit(solution)/shard_map/ppermute | solution.py:32
  25.5 2.3 %collective-permute-start.8 = (bf16[272,1024]{1,0:T(8,128)(2,1)S(1)}, bf16[272,1024]{1,0:T(8,128)(2,1)S(1)}, u32[]{:S(2)}, u32[]{:S(2)}) collective-permute-start(bf16[272,1024]{1,0:T(8,128)(2,1)S(1)} %join.1.refs_8_), channel_id=1, source_target_pairs={{0,16},{1,5},{2,18},{3,7},{4,20},{5,9},{6,22},{7,11},{8,24},{9,13}... | collective-permute-start | bytes 1671176 | tf_op jit(solution)/shard_map/ppermute | solution.py:45
  27.8 1.5 %collective-permute-start.9 = (bf16[272,1024]{1,0:T(8,128)(2,1)S(1)}, bf16[272,1024]{1,0:T(8,128)(2,1)S(1)}, u32[]{:S(2)}, u32[]{:S(2)}) collective-permute-start(bf16[272,1024]{1,0:T(8,128)(2,1)S(1)} %join.1.refs_8_), channel_id=1, source_target_pairs={{0,48},{1,13},{2,50},{3,15},{4,52},{5,1},{6,54},{7,3},{8,56},{9,5}... | collective-permute-start | bytes 1671176 | tf_op jit(solution)/shard_map/ppermute | solution.py:45
  29.3 5.2 %project_early.1 = (bf16[128,1024]{1,0:T(8,128)(2,1)S(1)}, bf16[128,1024]{1,0:T(8,128)(2,1)S(1)}) custom-call(bf16[64,4096]{1,0:T(8,128)(2,1)} %bitcast.11, bf16[64,4096]{1,0:T(8,128)(2,1)S(1)} %collective-permute-done.1.refs_1_, bf16[4096,1024]{1,0:T(8,128)(2,1)} %refs_2_.3, bf16[256,1024]{1,0:T(8,128)(2,1)} %bitcast.13, ...), custom_call_target="tpu_custom_call" | custom-call | tf_op jit(solution)/shard_map/project_early/pallas_call | solution.py:353
  34.6 1.7 %collective-permute-start.3 = (bf16[64,4096]{1,0:T(8,128)(2,1)S(1)}, bf16[64,4096]{1,0:T(8,128)(2,1)S(1)}, u32[]{:S(2)}, u32[]{:S(2)}) collective-permute-start(bf16[64,4096]{1,0:T(8,128)(2,1)S(1)} %collective-permute-done.refs_0_), channel_id=1, source_target_pairs={{0,1},{1,0},{2,3},{3,2},{4,5},{5,4},{6,7},{7,6},{8,9},{9,8},{10,11... | collective-permute-start | bytes 1572872 | tf_op jit(solution)/shard_map/ppermute | solution.py:32
  36.3 1.5 %collective-permute-done.3.refs_1_ = bf16[64,4096]{1,0:T(8,128)(2,1)S(1)} collective-permute-done((bf16[64,4096]{1,0:T(8,128)(2,1)S(1)}, bf16[64,4096]{1,0:T(8,128)(2,1)S(1)}, u32[]{:S(2)}, u32[]{:S(2)}) %collective-permute-start.3) | collective-permute-done | bytes 524320 | tf_op jit(solution)/shard_map/ppermute | solution.py:32
  38.9 2.0 %collective-permute-start.11 = (bf16[256,1024]{1,0:T(8,128)(2,1)S(1)}, bf16[256,1024]{1,0:T(8,128)(2,1)S(1)}, u32[]{:S(2)}, u32[]{:S(2)}) collective-permute-start(bf16[256,1024]{1,0:T(8,128)(2,1)S(1)} %get-tuple-element.47), channel_id=1, source_target_pairs={{0,32},{1,9},{2,34},{3,11},{4,36},{5,13},{6,38},{7,15},{8,40},{9,1... | collective-permute-start | bytes 1572872 | tf_op jit(solution)/shard_map/ppermute | solution.py:45
  41.2 2.3 %collective-permute-start.13 = (bf16[256,1024]{1,0:T(8,128)(2,1)S(1)}, bf16[256,1024]{1,0:T(8,128)(2,1)S(1)}, u32[]{:S(2)}, u32[]{:S(2)}) collective-permute-start(bf16[256,1024]{1,0:T(8,128)(2,1)S(1)} %get-tuple-element.49), channel_id=1, source_target_pairs={{0,48},{1,13},{2,50},{3,15},{4,52},{5,1},{6,54},{7,3},{8,56},{9,5}... | collective-permute-start | bytes 1572872 | tf_op jit(solution)/shard_map/ppermute | solution.py:45
  43.5 5.8 %project_late.1 = (bf16[256,1024]{1,0:T(8,128)(2,1)S(1)}, bf16[256,1024]{1,0:T(8,128)(2,1)}) custom-call(bf16[64,4096]{1,0:T(8,128)(2,1)S(1)} %collective-permute-done.refs_0_, bf16[64,4096]{1,0:T(8,128)(2,1)S(1)} %collective-permute-done.3.refs_1_, bf16[4096,1024]{1,0:T(8,128)(2,1)} %refs_2_.3, bf16[256,1024]{1,0:T(8,128)(2,1)} %bitcast.14, ...), custom_call_target="tpu_custom_call" | custom-call | flops 5000000000 | tf_op jit(solution)/shard_map/project_late/pallas_call | solution.py:353
  49.3 3.8 %filter_grad.1.refs_13_ = f32[64,128]{1,0:T(8,128)S(1)} custom-call(bf16[128,1024]{1,0:T(8,128)(2,1)S(1)} %collective-permute-done.2.refs_1_.refs_0_, bf16[256,1024]{1,0:T(8,128)(2,1)} %bitcast.16, bf16[256,1024]{1,0:T(8,128)(2,1)S(1)} %get-tuple-element.45.refs_2_.refs_1_), custom_call_target="tpu_custom_call" | custom-call | flops 4000000000 | tf_op jit(solution)/shard_map/filter_grad/pallas_call | solution.py:96
  53.1 1.3 %collective-permute-done.12.refs_5_.refs_10_ = bf16[256,1024]{1,0:T(8,128)(2,1)S(1)} collective-permute-done((bf16[256,1024]{1,0:T(8,128)(2,1)S(1)}, bf16[256,1024]{1,0:T(8,128)(2,1)S(1)}, u32[]{:S(2)}, u32[]{:S(2)}) %collective-permute-start.12) | collective-permute-done | bytes 524320 | tf_op jit(solution)/shard_map/ppermute | solution.py:45
  54.4 3.1 %weight_parts.1 = (f32[256,1024]{1,0:T(8,128)S(1)}, bf16[256,1024]{1,0:T(8,128)(2,1)S(1)}, bf16[256,1024]{1,0:T(8,128)(2,1)S(1)}, bf16[256,1024]{1,0:T(8,128)(2,1)S(1)}) custom-call(bf16[128,1024]{1,0:T(8,128)(2,1)S(1)} %get-tuple-element.46.refs_0_, bf16[128,1024]{1,0:T(8,128)(2,1)S(1)} %collective-permute-done.6.refs_3_.refs_1_, ...), custom_call_target="tpu_custom_call" | custom-call | flops 4000000000 | tf_op jit(solution)/shard_map/weight_parts/pallas_call | solution.py:96
  57.5 1.3 %collective-permute-start.14 = (bf16[256,1024]{1,0:T(8,128)(2,1)S(1)}, bf16[256,1024]{1,0:T(8,128)(2,1)S(1)}, u32[]{:S(2)}, u32[]{:S(2)}) collective-permute-start(bf16[256,1024]{1,0:T(8,128)(2,1)S(1)} %get-tuple-element.51), channel_id=1, source_target_pairs={{0,4},{1,17},{2,6},{3,19},{4,8},{5,21},{6,10},{7,23},{8,12},{9,25}... | collective-permute-start | bytes 1572872 | tf_op jit(solution)/shard_map/ppermute | solution.py:45
  58.8 2.5 %collective-permute-start.15 = (bf16[256,1024]{1,0:T(8,128)(2,1)S(1)}, bf16[256,1024]{1,0:T(8,128)(2,1)S(1)}, u32[]{:S(2)}, u32[]{:S(2)}) collective-permute-start(bf16[256,1024]{1,0:T(8,128)(2,1)S(1)} %get-tuple-element.52), channel_id=1, source_target_pairs={{0,8},{1,33},{2,10},{3,35},{4,12},{5,37},{6,14},{7,39},{8,0},{9,41... | collective-permute-start | bytes 1572872 | tf_op jit(solution)/shard_map/ppermute | solution.py:45
  63.7 2.2 %collective-permute-start.17 = (f32[64,128]{1,0:T(8,128)S(1)}, f32[64,128]{1,0:T(8,128)S(1)}, u32[]{:S(2)}, u32[]{:S(2)}) collective-permute-start(f32[64,128]{1,0:T(8,128)S(1)} %filter_grad.1.refs_13_), channel_id=1, source_target_pairs={{0,16},{1,5},{2,18},{3,7},{4,20},{5,1},{6,22},{7,3},{8,24},{9,13},... | collective-permute-start | bytes 98312 | tf_op jit(solution)/shard_map/ppermute | solution.py:45
  65.9 7.5 %collective-permute-done.17 = f32[64,128]{1,0:T(8,128)S(1)} collective-permute-done((f32[64,128]{1,0:T(8,128)S(1)}, f32[64,128]{1,0:T(8,128)S(1)}, u32[]{:S(2)}, u32[]{:S(2)}) %collective-permute-start.17) | collective-permute-done | bytes 32800 | tf_op jit(solution)/shard_map/ppermute | solution.py:45
  73.4 1.8 %collective-permute-start.18 = (f32[64,128]{1,0:T(8,128)S(1)}, f32[64,128]{1,0:T(8,128)S(1)}, u32[]{:S(2)}, u32[]{:S(2)}) collective-permute-start(f32[64,128]{1,0:T(8,128)S(1)} %add.12), channel_id=1, source_target_pairs={{0,32},{1,9},{2,34},{3,11},{4,36},{5,13},{6,38},{7,15},{8,40},{9,1... | collective-permute-start | bytes 98312 | tf_op jit(solution)/shard_map/ppermute | solution.py:45
  75.2 2.5 %collective-permute-done.18 = f32[64,128]{1,0:T(8,128)S(1)} collective-permute-done((f32[64,128]{1,0:T(8,128)S(1)}, f32[64,128]{1,0:T(8,128)S(1)}, u32[]{:S(2)}, u32[]{:S(2)}) %collective-permute-start.18) | collective-permute-done | bytes 32800 | tf_op jit(solution)/shard_map/ppermute | solution.py:45
  78.0 2.7 %collective-permute-done.19 = f32[64,128]{1,0:T(8,128)S(1)} collective-permute-done((f32[64,128]{1,0:T(8,128)S(1)}, f32[64,128]{1,0:T(8,128)S(1)}, u32[]{:S(2)}, u32[]{:S(2)}) %collective-permute-start.19) | collective-permute-done | bytes 32800 | tf_op jit(solution)/shard_map/ppermute | solution.py:45
  80.8 2.0 %collective-permute-start.20 = (f32[64,128]{1,0:T(8,128)S(1)}, f32[64,128]{1,0:T(8,128)S(1)}, u32[]{:S(2)}, u32[]{:S(2)}) collective-permute-start(f32[64,128]{1,0:T(8,128)S(1)} %add.14), channel_id=1, source_target_pairs={{0,8},{1,33},{2,10},{3,35},{4,12},{5,37},{6,14},{7,39},{8,0},{9,41... | collective-permute-start | bytes 98312 | tf_op jit(solution)/shard_map/ppermute | solution.py:45
  82.8 2.2 %collective-permute-done.20 = f32[64,128]{1,0:T(8,128)S(1)} collective-permute-done((f32[64,128]{1,0:T(8,128)S(1)}, f32[64,128]{1,0:T(8,128)S(1)}, u32[]{:S(2)}, u32[]{:S(2)}) %collective-permute-start.20) | collective-permute-done | bytes 32800 | tf_op jit(solution)/shard_map/ppermute | solution.py:45
  87.5 1.6 %collective-permute-start.23 = (bf16[80,1024]{1,0:T(8,128)(2,1)S(1)}, bf16[80,1024]{1,0:T(8,128)(2,1)S(1)}, u32[]{:S(2)}, u32[]{:S(2)}) collective-permute-start(bf16[80,1024]{1,0:T(8,128)(2,1)S(1)} %get-tuple-element.59), channel_id=1, source_target_pairs={{0,192},{64,0},{128,64},{192,128},{1,193},{65,1},{129,65},{193,129... | collective-permute-start | bytes 491528 | tf_op jit(solution)/shard_map/ppermute | solution.py:597
  89.1 3.4 %input_grad.1.refs_5_ = bf16[256,1024]{1,0:T(8,128)(2,1)} custom-call(bf16[64,128]{1,0:T(8,128)(2,1)} %refs_0_.3, bf16[256,1024]{1,0:T(8,128)(2,1)S(1)} %get-tuple-element.45.refs_2_.refs_1_, bf16[128,1024]{1,0:T(8,128)(2,1)S(1)} %collective-permute-done.10.refs_5_.refs_2_, f32[64,1024]{1,0:T(8,128)S(1)} %get-tuple-element.55.refs_3_.refs_0_), custom_call_target="tpu_custom_call" | custom-call | tf_op jit(solution)/shard_map/input_grad/pallas_call | solution.py:96
  92.5 2.4 %collective-permute-done.22.refs_2_ = bf16[80,1024]{1,0:T(8,128)(2,1)S(1)} collective-permute-done((bf16[80,1024]{1,0:T(8,128)(2,1)S(1)}, bf16[80,1024]{1,0:T(8,128)(2,1)S(1)}, u32[]{:S(2)}, u32[]{:S(2)}) %collective-permute-start.22) | collective-permute-done | bytes 163872 | tf_op jit(solution)/shard_map/ppermute | solution.py:597
  95.6 7.7 %collective-permute-start.24 = (f32[64,512]{1,0:T(8,128)S(1)}, f32[64,512]{1,0:T(8,128)S(1)}, u32[]{:S(2)}, u32[]{:S(2)}) collective-permute-start(f32[64,512]{1,0:T(8,128)S(1)} %get-tuple-element.62), channel_id=1, source_target_pairs={{0,1},{1,0},{2,3},{3,2},{4,5},{5,4},{6,7},{7,6},{8,9},{9,8},{10,11... | collective-permute-start | bytes 393224 | tf_op jit(solution)/shard_map/ppermute | solution.py:32
  (36 shorter events, 12.0 us)
Async XLA Ops:
  0.6 12.7 %collective-permute-start.1 = (bf16[64,4096]{1,0:T(8,128)(2,1)}, bf16[64,4096]{1,0:T(8,128)(2,1)S(1)}, u32[]{:S(2)}, u32[]{:S(2)}) collective-permute-start(bf16[64,4096]{1,0:T(8,128)(2,1)} %bitcast.8), channel_id=1, source_target_pairs={{0,1},{1,0},{2,3},{3,2},{4,5},{5,4},{6,7},{7,6},{8,9},{9,8},{10,11... | collective-permute-start | bytes 1572872 | tf_op jit(solution)/shard_map/ppermute | solution.py:32
  4.0 30.6 %collective-permute-start = (bf16[64,4096]{1,0:T(8,128)(2,1)}, bf16[64,4096]{1,0:T(8,128)(2,1)S(1)}, u32[]{:S(2)}, u32[]{:S(2)}) collective-permute-start(bf16[64,4096]{1,0:T(8,128)(2,1)} %bitcast.9), channel_id=1, source_target_pairs={{0,2},{1,3},{2,0},{3,1},{4,6},{5,7},{6,4},{7,5},{8,10},{9,11},{10,... | collective-permute-start | bytes 1572872 | tf_op jit(solution)/shard_map/ppermute | solution.py:32
  10.1 8.5 %collective-permute-start.2 = (bf16[128,1024]{1,0:T(8,128)(2,1)S(1)}, bf16[128,1024]{1,0:T(8,128)(2,1)S(1)}, u32[]{:S(2)}, u32[]{:S(2)}) collective-permute-start(bf16[128,1024]{1,0:T(8,128)(2,1)S(1)} %slice_bitcast_fusion), channel_id=1, source_target_pairs={{0,4},{4,8},{8,12},{12,16},{16,20},{20,24},{24,28},{28,32},{32,36}... | collective-permute-start | bytes 786440 | tf_op jit(solution)/shard_map/ppermute | solution.py:54
  15.4 10.1 %collective-permute-start.6 = (bf16[128,1024]{1,0:T(8,128)(2,1)S(1)}, bf16[128,1024]{1,0:T(8,128)(2,1)S(1)}, u32[]{:S(2)}, u32[]{:S(2)}) collective-permute-start(bf16[128,1024]{1,0:T(8,128)(2,1)S(1)} %get-tuple-element.41), channel_id=1, source_target_pairs={{0,16},{1,5},{2,18},{3,7},{4,20},{5,9},{6,22},{7,11},{8,24},{9,13}... | collective-permute-start | bytes 786440 | tf_op jit(solution)/shard_map/ppermute | solution.py:45
  16.7 8.7 %collective-permute-start.7 = (bf16[128,1024]{1,0:T(8,128)(2,1)S(1)}, bf16[128,1024]{1,0:T(8,128)(2,1)S(1)}, u32[]{:S(2)}, u32[]{:S(2)}) collective-permute-start(bf16[128,1024]{1,0:T(8,128)(2,1)S(1)} %get-tuple-element.42), channel_id=1, source_target_pairs={{0,48},{1,13},{2,50},{3,15},{4,52},{5,1},{6,54},{7,3},{8,56},{9,5}... | collective-permute-start | bytes 786440 | tf_op jit(solution)/shard_map/ppermute | solution.py:45
  22.1 3.1 %collective-permute-start.4 = (bf16[128,512]{1,0:T(8,128)(2,1)S(1)}, bf16[128,512]{1,0:T(8,128)(2,1)S(1)}, u32[]{:S(2)}, u32[]{:S(2)}) collective-permute-start(bf16[128,512]{1,0:T(8,128)(2,1)S(1)} %get-tuple-element.39), channel_id=1, source_target_pairs={{0,1},{1,0},{2,3},{3,2},{4,5},{5,4},{6,7},{7,6},{8,9},{9,8},{10,11... | collective-permute-start | bytes 393224 | tf_op jit(solution)/shard_map/ppermute | solution.py:32
  24.1 1.3 %collective-permute-start.5 = (bf16[128,512]{1,0:T(8,128)(2,1)S(1)}, bf16[128,512]{1,0:T(8,128)(2,1)S(1)}, u32[]{:S(2)}, u32[]{:S(2)}) collective-permute-start(bf16[128,512]{1,0:T(8,128)(2,1)S(1)} %get-tuple-element.40), channel_id=1, source_target_pairs={{0,1},{1,0},{2,3},{3,2},{4,5},{5,4},{6,7},{7,6},{8,9},{9,8},{10,11... | collective-permute-start | bytes 393224 | tf_op jit(solution)/shard_map/ppermute | solution.py:32
  25.5 12.3 %collective-permute-start.8 = (bf16[272,1024]{1,0:T(8,128)(2,1)S(1)}, bf16[272,1024]{1,0:T(8,128)(2,1)S(1)}, u32[]{:S(2)}, u32[]{:S(2)}) collective-permute-start(bf16[272,1024]{1,0:T(8,128)(2,1)S(1)} %join.1.refs_8_), channel_id=1, source_target_pairs={{0,16},{1,5},{2,18},{3,7},{4,20},{5,9},{6,22},{7,11},{8,24},{9,13}... | collective-permute-start | bytes 1671176 | tf_op jit(solution)/shard_map/ppermute | solution.py:45
  27.8 10.0 %collective-permute-start.9 = (bf16[272,1024]{1,0:T(8,128)(2,1)S(1)}, bf16[272,1024]{1,0:T(8,128)(2,1)S(1)}, u32[]{:S(2)}, u32[]{:S(2)}) collective-permute-start(bf16[272,1024]{1,0:T(8,128)(2,1)S(1)} %join.1.refs_8_), channel_id=1, source_target_pairs={{0,48},{1,13},{2,50},{3,15},{4,52},{5,1},{6,54},{7,3},{8,56},{9,5}... | collective-permute-start | bytes 1671176 | tf_op jit(solution)/shard_map/ppermute | solution.py:45
  34.6 3.3 %collective-permute-start.3 = (bf16[64,4096]{1,0:T(8,128)(2,1)S(1)}, bf16[64,4096]{1,0:T(8,128)(2,1)S(1)}, u32[]{:S(2)}, u32[]{:S(2)}) collective-permute-start(bf16[64,4096]{1,0:T(8,128)(2,1)S(1)} %collective-permute-done.refs_0_), channel_id=1, source_target_pairs={{0,1},{1,0},{2,3},{3,2},{4,5},{5,4},{6,7},{7,6},{8,9},{9,8},{10,11... | collective-permute-start | bytes 1572872 | tf_op jit(solution)/shard_map/ppermute | solution.py:32
  38.9 14.2 %collective-permute-start.11 = (bf16[256,1024]{1,0:T(8,128)(2,1)S(1)}, bf16[256,1024]{1,0:T(8,128)(2,1)S(1)}, u32[]{:S(2)}, u32[]{:S(2)}) collective-permute-start(bf16[256,1024]{1,0:T(8,128)(2,1)S(1)} %get-tuple-element.47), channel_id=1, source_target_pairs={{0,32},{1,9},{2,34},{3,11},{4,36},{5,13},{6,38},{7,15},{8,40},{9,1... | collective-permute-start | bytes 1572872 | tf_op jit(solution)/shard_map/ppermute | solution.py:45
  40.8 13.6 %collective-permute-start.12 = (bf16[256,1024]{1,0:T(8,128)(2,1)S(1)}, bf16[256,1024]{1,0:T(8,128)(2,1)S(1)}, u32[]{:S(2)}, u32[]{:S(2)}) collective-permute-start(bf16[256,1024]{1,0:T(8,128)(2,1)S(1)} %get-tuple-element.48), channel_id=1, source_target_pairs={{0,16},{1,5},{2,18},{3,7},{4,20},{5,9},{6,22},{7,11},{8,24},{9,13}... | collective-permute-start | bytes 1572872 | tf_op jit(solution)/shard_map/ppermute | solution.py:45
  41.2 13.2 %collective-permute-start.13 = (bf16[256,1024]{1,0:T(8,128)(2,1)S(1)}, bf16[256,1024]{1,0:T(8,128)(2,1)S(1)}, u32[]{:S(2)}, u32[]{:S(2)}) collective-permute-start(bf16[256,1024]{1,0:T(8,128)(2,1)S(1)} %get-tuple-element.49), channel_id=1, source_target_pairs={{0,48},{1,13},{2,50},{3,15},{4,52},{5,1},{6,54},{7,3},{8,56},{9,5}... | collective-permute-start | bytes 1572872 | tf_op jit(solution)/shard_map/ppermute | solution.py:45
  57.5 27.6 %collective-permute-start.14 = (bf16[256,1024]{1,0:T(8,128)(2,1)S(1)}, bf16[256,1024]{1,0:T(8,128)(2,1)S(1)}, u32[]{:S(2)}, u32[]{:S(2)}) collective-permute-start(bf16[256,1024]{1,0:T(8,128)(2,1)S(1)} %get-tuple-element.51), channel_id=1, source_target_pairs={{0,4},{1,17},{2,6},{3,19},{4,8},{5,21},{6,10},{7,23},{8,12},{9,25}... | collective-permute-start | bytes 1572872 | tf_op jit(solution)/shard_map/ppermute | solution.py:45
  58.8 26.3 %collective-permute-start.15 = (bf16[256,1024]{1,0:T(8,128)(2,1)S(1)}, bf16[256,1024]{1,0:T(8,128)(2,1)S(1)}, u32[]{:S(2)}, u32[]{:S(2)}) collective-permute-start(bf16[256,1024]{1,0:T(8,128)(2,1)S(1)} %get-tuple-element.52), channel_id=1, source_target_pairs={{0,8},{1,33},{2,10},{3,35},{4,12},{5,37},{6,14},{7,39},{8,0},{9,41... | collective-permute-start | bytes 1572872 | tf_op jit(solution)/shard_map/ppermute | solution.py:45
  61.3 23.8 %collective-permute-start.16 = (bf16[256,1024]{1,0:T(8,128)(2,1)S(1)}, bf16[256,1024]{1,0:T(8,128)(2,1)S(1)}, u32[]{:S(2)}, u32[]{:S(2)}) collective-permute-start(bf16[256,1024]{1,0:T(8,128)(2,1)S(1)} %get-tuple-element.53), channel_id=1, source_target_pairs={{0,12},{1,49},{2,14},{3,51},{4,0},{5,53},{6,2},{7,55},{8,4},{9,57}... | collective-permute-start | bytes 1572872 | tf_op jit(solution)/shard_map/ppermute | solution.py:45
  62.4 22.6 %collective-permute-start.10 = (bf16[128,1024]{1,0:T(8,128)(2,1)S(1)}, bf16[128,1024]{1,0:T(8,128)(2,1)S(1)}, u32[]{:S(2)}, u32[]{:S(2)}) collective-permute-start(bf16[128,1024]{1,0:T(8,128)(2,1)S(1)} %slice.11), channel_id=1, source_target_pairs={{4,0},{8,4},{12,8},{16,12},{20,16},{24,20},{28,24},{32,28},{36,32}... | collective-permute-start | bytes 786440 | tf_op jit(solution)/shard_map/ppermute | solution.py:54
  63.7 9.7 %collective-permute-start.17 = (f32[64,128]{1,0:T(8,128)S(1)}, f32[64,128]{1,0:T(8,128)S(1)}, u32[]{:S(2)}, u32[]{:S(2)}) collective-permute-start(f32[64,128]{1,0:T(8,128)S(1)} %filter_grad.1.refs_13_), channel_id=1, source_target_pairs={{0,16},{1,5},{2,18},{3,7},{4,20},{5,1},{6,22},{7,3},{8,24},{9,13},... | collective-permute-start | bytes 98312 | tf_op jit(solution)/shard_map/ppermute | solution.py:45
  73.4 4.3 %collective-permute-start.18 = (f32[64,128]{1,0:T(8,128)S(1)}, f32[64,128]{1,0:T(8,128)S(1)}, u32[]{:S(2)}, u32[]{:S(2)}) collective-permute-start(f32[64,128]{1,0:T(8,128)S(1)} %add.12), channel_id=1, source_target_pairs={{0,32},{1,9},{2,34},{3,11},{4,36},{5,13},{6,38},{7,15},{8,40},{9,1... | collective-permute-start | bytes 98312 | tf_op jit(solution)/shard_map/ppermute | solution.py:45
  77.7 3.1 %collective-permute-start.19 = (f32[64,128]{1,0:T(8,128)S(1)}, f32[64,128]{1,0:T(8,128)S(1)}, u32[]{:S(2)}, u32[]{:S(2)}) collective-permute-start(f32[64,128]{1,0:T(8,128)S(1)} %add.13), channel_id=1, source_target_pairs={{0,4},{1,17},{2,6},{3,19},{4,0},{5,21},{6,2},{7,23},{8,12},{9,25},... | collective-permute-start | bytes 98312 | tf_op jit(solution)/shard_map/ppermute | solution.py:45
  80.8 4.3 %collective-permute-start.20 = (f32[64,128]{1,0:T(8,128)S(1)}, f32[64,128]{1,0:T(8,128)S(1)}, u32[]{:S(2)}, u32[]{:S(2)}) collective-permute-start(f32[64,128]{1,0:T(8,128)S(1)} %add.14), channel_id=1, source_target_pairs={{0,8},{1,33},{2,10},{3,35},{4,12},{5,37},{6,14},{7,39},{8,0},{9,41... | collective-permute-start | bytes 98312 | tf_op jit(solution)/shard_map/ppermute | solution.py:45
  85.5 7.0 %collective-permute-start.21 = (bf16[80,1024]{1,0:T(8,128)(2,1)S(1)}, bf16[80,1024]{1,0:T(8,128)(2,1)S(1)}, u32[]{:S(2)}, u32[]{:S(2)}) collective-permute-start(bf16[80,1024]{1,0:T(8,128)(2,1)S(1)} %get-tuple-element.57), channel_id=1, source_target_pairs={{0,64},{64,128},{128,192},{192,0},{1,65},{65,129},{129,193},{193,1... | collective-permute-start | bytes 491528 | tf_op jit(solution)/shard_map/ppermute | solution.py:597
  86.3 8.6 %collective-permute-start.22 = (bf16[80,1024]{1,0:T(8,128)(2,1)S(1)}, bf16[80,1024]{1,0:T(8,128)(2,1)S(1)}, u32[]{:S(2)}, u32[]{:S(2)}) collective-permute-start(bf16[80,1024]{1,0:T(8,128)(2,1)S(1)} %get-tuple-element.58), channel_id=1, source_target_pairs={{0,128},{64,192},{128,0},{192,64},{1,129},{65,193},{129,1},{193,65... | collective-permute-start | bytes 491528 | tf_op jit(solution)/shard_map/ppermute | solution.py:597
  87.5 7.4 %collective-permute-start.23 = (bf16[80,1024]{1,0:T(8,128)(2,1)S(1)}, bf16[80,1024]{1,0:T(8,128)(2,1)S(1)}, u32[]{:S(2)}, u32[]{:S(2)}) collective-permute-start(bf16[80,1024]{1,0:T(8,128)(2,1)S(1)} %get-tuple-element.59), channel_id=1, source_target_pairs={{0,192},{64,0},{128,64},{192,128},{1,193},{65,1},{129,65},{193,129... | collective-permute-start | bytes 491528 | tf_op jit(solution)/shard_map/ppermute | solution.py:597
  95.6 8.7 %collective-permute-start.24 = (f32[64,512]{1,0:T(8,128)S(1)}, f32[64,512]{1,0:T(8,128)S(1)}, u32[]{:S(2)}, u32[]{:S(2)}) collective-permute-start(f32[64,512]{1,0:T(8,128)S(1)} %get-tuple-element.62), channel_id=1, source_target_pairs={{0,1},{1,0},{2,3},{3,2},{4,5},{5,4},{6,7},{7,6},{8,9},{9,8},{10,11... | collective-permute-start | bytes 393224 | tf_op jit(solution)/shard_map/ppermute | solution.py:32

commit v7 on v6

--- a/solution.py
+++ b/solution.py
@@ -157,7 +157,7 @@
         out[...] = gated[i * TAPS : (i + 1) * TAPS, aligned(1 - core, kept.shape[1])]
 
 
-def forward(filters, previous, signal, gating):
+def forward(filters, previous, signal, gating, after):
     length, channels = signal.shape
     quarter = ((TAPS, channels // 2), BF16)
     return once(
@@ -169,6 +169,7 @@
             pltpu.VMEM((length, channels), BF16),
             pltpu.VMEM((2, PER_TILE * TAPS, 2 * TAPS), BF16),
         ],
+        after,
     )
 
 
@@ -291,16 +292,15 @@
     )
 
 
-def relay_kernel(mine, other, before, after, opposite, *outs):
+def relay_kernel(mine, other, before, after, *outs):
     pack_into(mine, other, outs)
-    part = opposite.shape[0]
+    part = outs[0].shape[0]
     outs[1][part:] = before[...]
-    outs[2][part:] = opposite[...]
     outs[3][part:] = after[...]
 
 
-def relay(mine, other, got_next, got_last, opposite):
-    rows, width = opposite.shape
+def relay(mine, other, got_next, got_last):
+    rows, width = 2 * mine.shape[0], got_next.shape[1]
     return once(
         relay_kernel,
         "relay",
@@ -309,9 +309,8 @@
             other,
             (got_next, whole((TAPS, width))),
             (got_last, whole((TAPS, width), (1, 0))),
-            opposite,
         ],
-        [((rows, width), BF16)] + [((rows + TAPS, width), BF16)] * (SIDE - 1),
+        [((rows + s % 2 * TAPS, width), BF16) for s in range(SIDE)],
     )
 
 
@@ -364,28 +363,6 @@
         cost_estimate=lasting(5 if done else 0),
         name="project_late" if done else "project_early",
     )(mine, other, weight, gating, response, *done, *after)
-
-
-def high_and_low(x):
-    high = x.astype(BF16).astype(F32)
-    return high, (x - high).astype(BF16).astype(F32)
-
-
-def folded(x, rows):
-    return jnp.concatenate([x[i : i + rows] for i in range(0, x.shape[0], rows)], 1)
-
-
-def unfolded(x):
-    return jnp.concatenate([x[:, i : i + LANES] for i in range(0, x.shape[1], LANES)], 0)
-
-
-def riding(ref, start, rows):
-    pair = ref[start : start + 2 * rows].astype(F32)
-    return unfolded(pair[:rows] + pair[rows:])
-
-
-def four_sum(parts):
-    return (parts[0] + parts[2]) + (parts[1] + parts[3])
 
 
 def weight_kernel(*refs):
@@ -434,10 +411,7 @@
         weight_kernel,
         "weight_parts",
         [
-            early[0],
-            early[1],
-            block(late[1], rows),
-            early[2],
+            *early,
             own_late,
             *[block(part, 0) for part in late],
             block(gated, 0, length),
@@ -453,88 +427,53 @@
     )
 
 
-def high_and_low(x):
-    high = x.astype(BF16).astype(F32)
-    return high, (x - high).astype(BF16).astype(F32)
-
-
-def folded(x, rows):
-    return jnp.concatenate([x[i : i + rows] for i in range(0, x.shape[0], rows)], 1)
-
-
-def unfolded(x):
-    return jnp.concatenate([x[:, i : i + LANES] for i in range(0, x.shape[1], LANES)], 0)
-
-
-def riding(ref, start, rows):
-    pair = ref[start : start + 2 * rows].astype(F32)
-    return unfolded(pair[:rows] + pair[rows:])
-
-
 def four_sum(parts):
     return (parts[0] + parts[2]) + (parts[1] + parts[3])
 
 
 def first_sum_kernel(*refs):
     _, _, z, _, _ = spot()
-    extra, outs, own_extra, kept = refs[SIDE], refs[SIDE + 1 : -2], refs[-2], refs[-1]
+    outs, kept = refs[SIDE:-1], refs[-1]
     run = kept.shape[0] // SIDE
     total = refs[0][...]
     for ref in refs[1:SIDE]:
         total = total + ref[...].astype(F32)
     for d in range(SIDE):
         kept[aligned((d - z + SIDE) % SIDE, run), :] = total[d * run : (d + 1) * run]
-    high, low = (folded(part, own_extra.shape[0]) for part in high_and_low(extra[...]))
-    own_extra[...] = high + low
     for s, out in enumerate(outs):
-        out[:run] = kept[s * run : (s + 1) * run, :].astype(out.dtype)
-        if s:
-            out[run:] = jnp.concatenate([high, low], 0).astype(BF16)
-
-
-def first_sum(parts, extra, after):
+        out[...] = kept[s * run : (s + 1) * run, :].astype(out.dtype)
+
+
+def first_sum(parts, after):
     rows, width = parts[0].shape
-    below = LANES * extra.shape[0] // width
     run = rows // SIDE
-    *sums, own_extra = once(
+    return once(
         first_sum_kernel,
         "first_sum",
-        [*parts, extra],
-        [((run, width), F32)]
-        + [((run + 2 * below, width), BF16)] * (SIDE - 1)
-        + [((below, width), F32)],
+        parts,
+        [((run, width), F32)] + [((run, width), BF16)] * (SIDE - 1),
         [pltpu.VMEM((rows, width), F32)],
         after,
         1,
     )
-    return sums, own_extra
-
-
-def last_sum(parts, own_extra, filters, scale, filter_scale, after):
+
+
+def last_sum(parts, scale, after):
     rows, width = parts[0].shape
-    below = own_extra.shape[0]
 
     def kernel(*refs):
-        own, others, extra = refs[0], refs[1:SIDE], refs[SIDE]
-        kept, given, filter_out, summed = refs[SIDE + 1 :]
+        kept, given, summed = refs[SIDE:]
         _, _, _, _, core = spot()
-        total = own[...]
-        for ref in others:
-            total = total + ref[:rows].astype(F32)
+        total = refs[0][...]
+        for ref in refs[1:SIDE]:
+            total = total + ref[...].astype(F32)
         summed[...] = total * scale
         kept[...] = summed[:, aligned(core, width // 2)]
         given[...] = summed[:, aligned(1 - core, width // 2)]
-        values = [unfolded(extra[...])] + [riding(ref, rows, below) for ref in others]
-        filter_out[...] = four_sum(values) * filter_scale
 
     half = ((rows, width // 2), F32)
     return once(
-        kernel,
-        "last_sum",
-        [*parts, own_extra],
-        [half, half, (filters.shape, F32)],
-        [pltpu.VMEM((rows, width), F32)],
-        after,
+        kernel, "last_sum", parts, [half, half], [pltpu.VMEM((rows, width), F32)], after
     )
 
 
@@ -571,38 +510,31 @@
     early_other = moved(grads, "core")
     grads = resident(grads)
     early = pack(grads, early_other)
-    early_got = [stepped(early[1], True, 1), stepped(early[3], True, 3)]
-    response, kept, *given = forward(filters, previous, signal, gating)
-    gated = join(kept, [moved(part, "core") for part in given], early_got)
+    early_got = [stepped(early[s], True, s) for s in shifts]
+    response, kept, *given = forward(filters, previous, signal, gating, early_got)
+    gated = join(kept, [moved(part, "core") for part in given], ())
     got = [stepped(gated, True, 1), stepped(gated, True, 3)]
     conv_early, gate_early = project(grads, early_other, weight, gating, response)
 
     late_other = moved(tied(late, conv_early), "core")
-    own_late, *late_sent = relay(late, late_other, *got, early[2])
+    own_late, *late_sent = relay(late, late_other, *got)
     conv_grad, grad_gate = project(
         late, late_other, weight, gating, response, (conv_early, gate_early), (own_late,)
     )
     late_got = [stepped(late_sent[s - 1], True, s) for s in shifts]
     following = shifted(conv_grad[:TAPS], -1)
-    filter_sum = filter_grad(previous, signal, conv_grad, ())
-    parts = weight_parts([early[0], *early_got], own_late, gated, got, late_got, (filter_sum,))
-
-    filter_sum = paired(filter_sum, True, 1)
-    filter_sum = paired(filter_sum, True, 2, (parts[0],))
-    filter_sum = paired(paired(filter_sum, False, 1), False, 2)
+    parts = weight_parts([early[0], *early_got], own_late, gated, got, late_got, (conv_grad,))
+    filter_sum = filter_grad(previous, signal, conv_grad, (parts[0],))
+    filter_sum = four_sum([filter_sum] + [stepped(filter_sum, True, s) for s in shifts])
     parts = [parts[0]] + [stepped(parts[s], False, s) for s in shifts]
-    sums, own_filter = first_sum(parts, filter_sum, (following,))
+    sums = first_sum(parts, (following,))
     grad_input = input_grad(filters, conv_grad, following, (sums[0],))
     line = [[(i, (i + s) % SIDE) for i in range(SIDE)] for s in shifts]
+    filter_sum = paired(paired(filter_sum, False, 1, (sums[0],)), False, 2)
+    filter_sum = four_sum([filter_sum] + [lax.ppermute(filter_sum, "dp", pairs) for pairs in line])
+    grad_filter = filter_sum * (1.0 / math.sqrt(tokens_all * GROUP))
     sums = [sums[0]] + [lax.ppermute(sums[s], "dp", line[s - 1]) for s in shifts]
-    kept, given, grad_filter = last_sum(
-        sums,
-        own_filter,
-        filters,
-        1.0 / math.sqrt(tokens_all),
-        1.0 / math.sqrt(tokens_all * GROUP),
-        (resident(grad_input),),
-    )
+    kept, given = last_sum(sums, 1.0 / math.sqrt(tokens_all), (resident(grad_input),))
     grad_weight = beside(kept, moved(given, "core"))
     return (grad_input[None], grad_gate[None], grad_weight, grad_filter)
 

time: 105 us -> 117 us (1.11)
  starting transfers between devices: 50.7 us -> 58.7 us
  waiting for transfers between devices: 23 us -> 26.3 us
    ppermute x14 -> x16, starting transfers between devices: 22.5 us -> 27.8 us  [in_plane(): return lax.ppermute(x, ('ctx', 'tp'), pairs)]
    ppermute x14 -> x16, waiting for transfers between devices: 16.3 us -> 21.1 us  [in_plane(): return lax.ppermute(x, ('ctx', 'tp'), pairs)]
    ppermute x0 -> x3, starting transfers between devices: none -> 4.3 us  [local(): lax.ppermute(filter_sum, 'dp', pairs)]
    ppermute x3, waiting for transfers between devices: 2.36 us -> 0.01 us  [local(): lax.ppermute(sums[s], 'dp', line[s - 1])]
    ppermute x6, starting transfers between devices: 20.1 us -> 18.2 us  [moved(): return lax.ppermute(x, 'tp', [(i, i ^ step) for i in range(4)])]
    ppermute x2, waiting for transfers between devices: 0.52 us -> 2.33 us  [shifted(): lax.ppermute(x, 'ctx', [(i, i + by) for i in range(devices) if 0 <= i + b...]
  transfers between devices with their start and end apart: 25 -> 30, of which waited for: 11 -> 12; matrix products, arithmetic and copies ran while one was open for 1% -> 1% of each run, Pallas kernels for 22% -> 21%
where the time goes in v7:
time: 117 us; the launch traced here: 116 us
  starting transfers between devices  58.7 us (50%)
  Pallas kernels  28.9 us (25%)
  waiting for transfers between devices  26.3 us (22%)
    ppermute x16, starting transfers between devices, in_plane(): return lax.ppermute(x, ('ctx', 'tp'), pairs)  27.8 us
    ppermute x16, waiting for transfers between devices, in_plane(): return lax.ppermute(x, ('ctx', 'tp'), pairs)  21.1 us
    ppermute x6, starting transfers between devices, moved(): return lax.ppermute(x, 'tp', [(i, i ^ step) for i in range(4)])  18.2 us
    pallas_call x10, Pallas kernels, once(): pl.pallas_call(body, grid=(1,), in_specs=specs + [ANYWHERE] * len(after),...  17.9 us
    pallas_call x2, Pallas kernels, project(): pl.pallas_call(body, grid=(channels // WIDE,), in_specs=[full(mine.shape)...  11 us
    ppermute x2, starting transfers between devices, shifted(): lax.ppermute(x, 'ctx', [(i, i + by) for i in range(devices) if 0 <= i + b...  4.51 us
    ppermute x3, starting transfers between devices, local(): lax.ppermute(filter_sum, 'dp', pairs)  4.3 us
    ppermute x3, starting transfers between devices, local(): lax.ppermute(sums[s], 'dp', line[s - 1])  3.86 us
  transfers between devices with their start and end apart: 30, of which 12 were waited for; matrix products, arithmetic and copies ran while one was open for 1% of the time, Pallas kernels for 21%

profile of v7, /device:TPU:1, one launch (start us, length us, event | category | flops | bytes accessed | tf_op | source)
XLA Modules:
  0.0 116.4 jit_solution(6036350544985289799)
XLA Ops:
  0.6 3.3 %collective-permute-start.1 = (bf16[64,4096]{1,0:T(8,128)(2,1)}, bf16[64,4096]{1,0:T(8,128)(2,1)S(1)}, u32[]{:S(2)}, u32[]{:S(2)}) collective-permute-start(bf16[64,4096]{1,0:T(8,128)(2,1)} %bitcast.8), channel_id=1, source_target_pairs={{0,1},{1,0},{2,3},{3,2},{4,5},{5,4},{6,7},{7,6},{8,9},{9,8},{10,11... | collective-permute-start | bytes 1572872 | tf_op jit(solution)/shard_map/ppermute | solution.py:32
  4.0 5.2 %collective-permute-start = (bf16[64,4096]{1,0:T(8,128)(2,1)}, bf16[64,4096]{1,0:T(8,128)(2,1)S(1)}, u32[]{:S(2)}, u32[]{:S(2)}) collective-permute-start(bf16[64,4096]{1,0:T(8,128)(2,1)} %bitcast.9), channel_id=1, source_target_pairs={{0,2},{1,3},{2,0},{3,1},{4,6},{5,7},{6,4},{7,5},{8,10},{9,11},{10,... | collective-permute-start | bytes 1572872 | tf_op jit(solution)/shard_map/ppermute | solution.py:32
  10.1 3.2 %collective-permute-start.2 = (bf16[128,1024]{1,0:T(8,128)(2,1)S(1)}, bf16[128,1024]{1,0:T(8,128)(2,1)S(1)}, u32[]{:S(2)}, u32[]{:S(2)}) collective-permute-start(bf16[128,1024]{1,0:T(8,128)(2,1)S(1)} %slice_bitcast_fusion), channel_id=1, source_target_pairs={{0,4},{4,8},{8,12},{12,16},{16,20},{20,24},{24,28},{28,32},{32,36}... | collective-permute-start | bytes 786440 | tf_op jit(solution)/shard_map/ppermute | solution.py:54
  13.4 2.0 %pack.1 = (bf16[128,1024]{1,0:T(8,128)(2,1)S(1)}, bf16[128,1024]{1,0:T(8,128)(2,1)S(1)}, bf16[128,1024]{1,0:T(8,128)(2,1)S(1)}, bf16[128,1024]{1,0:T(8,128)(2,1)S(1)}) custom-call(bf16[64,4096]{1,0:T(8,128)(2,1)} %bitcast.10, bf16[64,4096]{1,0:T(8,128)(2,1)S(1)} %collective-permute-done.1.refs_1_), custom_call_target="tpu_custom_call" | custom-call | tf_op jit(solution)/shard_map/pack/pallas_call | solution.py:96
  15.4 1.4 %collective-permute-start.3 = (bf16[128,1024]{1,0:T(8,128)(2,1)S(1)}, bf16[128,1024]{1,0:T(8,128)(2,1)S(1)}, u32[]{:S(2)}, u32[]{:S(2)}) collective-permute-start(bf16[128,1024]{1,0:T(8,128)(2,1)S(1)} %get-tuple-element.32), channel_id=1, source_target_pairs={{0,16},{1,5},{2,18},{3,7},{4,20},{5,9},{6,22},{7,11},{8,24},{9,13}... | collective-permute-start | bytes 786440 | tf_op jit(solution)/shard_map/ppermute | solution.py:45
  16.7 2.2 %collective-permute-start.4 = (bf16[128,1024]{1,0:T(8,128)(2,1)S(1)}, bf16[128,1024]{1,0:T(8,128)(2,1)S(1)}, u32[]{:S(2)}, u32[]{:S(2)}) collective-permute-start(bf16[128,1024]{1,0:T(8,128)(2,1)S(1)} %get-tuple-element.33), channel_id=1, source_target_pairs={{0,32},{1,9},{2,34},{3,11},{4,36},{5,13},{6,38},{7,15},{8,40},{9,1... | collective-permute-start | bytes 786440 | tf_op jit(solution)/shard_map/ppermute | solution.py:45
  18.9 1.2 %collective-permute-start.5 = (bf16[128,1024]{1,0:T(8,128)(2,1)S(1)}, bf16[128,1024]{1,0:T(8,128)(2,1)S(1)}, u32[]{:S(2)}, u32[]{:S(2)}) collective-permute-start(bf16[128,1024]{1,0:T(8,128)(2,1)S(1)} %get-tuple-element.34), channel_id=1, source_target_pairs={{0,48},{1,13},{2,50},{3,15},{4,52},{5,1},{6,54},{7,3},{8,56},{9,5}... | collective-permute-start | bytes 786440 | tf_op jit(solution)/shard_map/ppermute | solution.py:45
  20.1 2.1 %collective-permute-done.3.refs_4_.refs_1_ = bf16[128,1024]{1,0:T(8,128)(2,1)S(1)} collective-permute-done((bf16[128,1024]{1,0:T(8,128)(2,1)S(1)}, bf16[128,1024]{1,0:T(8,128)(2,1)S(1)}, u32[]{:S(2)}, u32[]{:S(2)}) %collective-permute-start.3) | collective-permute-done | bytes 262176 | tf_op jit(solution)/shard_map/ppermute | solution.py:45
  22.2 5.9 %collective-permute-done.4.refs_5_.refs_2_ = bf16[128,1024]{1,0:T(8,128)(2,1)S(1)} collective-permute-done((bf16[128,1024]{1,0:T(8,128)(2,1)S(1)}, bf16[128,1024]{1,0:T(8,128)(2,1)S(1)}, u32[]{:S(2)}, u32[]{:S(2)}) %collective-permute-start.4) | collective-permute-done | bytes 262176 | tf_op jit(solution)/shard_map/ppermute | solution.py:45
  28.1 3.4 %conv_forward.1 = (f32[256,1024]{1,0:T(8,128)S(1)}, bf16[256,512]{1,0:T(8,128)(2,1)S(1)}, bf16[128,512]{1,0:T(8,128)(2,1)S(1)}, bf16[128,512]{1,0:T(8,128)(2,1)S(1)}) custom-call(bf16[64,128]{1,0:T(8,128)(2,1)} %refs_0_.3, bf16[128,1024]{1,0:T(8,128)(2,1)S(1)} %collective-permute-done.2.refs_1_.refs_0_, bf16[256,1024]{1,0:T(8,128)(2,1)} %bitcast.15, ...), custom_call_target="tpu_custom_call" | custom-call | tf_op jit(solution)/shard_map/conv_forward/pallas_call | solution.py:96
  33.2 2.8 %collective-permute-start.10 = (bf16[272,1024]{1,0:T(8,128)(2,1)S(1)}, bf16[272,1024]{1,0:T(8,128)(2,1)S(1)}, u32[]{:S(2)}, u32[]{:S(2)}) collective-permute-start(bf16[272,1024]{1,0:T(8,128)(2,1)S(1)} %join.1.refs_8_), channel_id=1, source_target_pairs={{0,48},{1,13},{2,50},{3,15},{4,52},{5,1},{6,54},{7,3},{8,56},{9,5}... | collective-permute-start | bytes 1671176 | tf_op jit(solution)/shard_map/ppermute | solution.py:45
  36.0 5.2 %project_early.1 = (bf16[128,1024]{1,0:T(8,128)(2,1)S(1)}, bf16[128,1024]{1,0:T(8,128)(2,1)S(1)}) custom-call(bf16[64,4096]{1,0:T(8,128)(2,1)} %bitcast.11, bf16[64,4096]{1,0:T(8,128)(2,1)S(1)} %collective-permute-done.1.refs_1_, bf16[4096,1024]{1,0:T(8,128)(2,1)} %refs_2_.3, bf16[256,1024]{1,0:T(8,128)(2,1)} %bitcast.13, ...), custom_call_target="tpu_custom_call" | custom-call | tf_op jit(solution)/shard_map/project_early/pallas_call | solution.py:352
  41.7 1.5 %collective-permute-done.6.refs_1_ = bf16[64,4096]{1,0:T(8,128)(2,1)S(1)} collective-permute-done((bf16[64,4096]{1,0:T(8,128)(2,1)S(1)}, bf16[64,4096]{1,0:T(8,128)(2,1)S(1)}, u32[]{:S(2)}, u32[]{:S(2)}) %collective-permute-start.6) | collective-permute-done | bytes 524320 | tf_op jit(solution)/shard_map/ppermute | solution.py:32
  43.2 2.6 %collective-permute-done.9.refs_2_.refs_9_ = bf16[272,1024]{1,0:T(8,128)(2,1)S(1)} collective-permute-done((bf16[272,1024]{1,0:T(8,128)(2,1)S(1)}, bf16[272,1024]{1,0:T(8,128)(2,1)S(1)}, u32[]{:S(2)}, u32[]{:S(2)}) %collective-permute-start.9) | collective-permute-done | bytes 557088 | tf_op jit(solution)/shard_map/ppermute | solution.py:45
  47.1 2.7 %collective-permute-start.14 = (bf16[256,1024]{1,0:T(8,128)(2,1)S(1)}, bf16[256,1024]{1,0:T(8,128)(2,1)S(1)}, u32[]{:S(2)}, u32[]{:S(2)}) collective-permute-start(bf16[256,1024]{1,0:T(8,128)(2,1)S(1)} %get-tuple-element.47), channel_id=1, source_target_pairs={{0,48},{1,13},{2,50},{3,15},{4,52},{5,1},{6,54},{7,3},{8,56},{9,5}... | collective-permute-start | bytes 1572872 | tf_op jit(solution)/shard_map/ppermute | solution.py:45
  49.8 5.8 %project_late.1 = (bf16[256,1024]{1,0:T(8,128)(2,1)S(1)}, bf16[256,1024]{1,0:T(8,128)(2,1)}) custom-call(bf16[64,4096]{1,0:T(8,128)(2,1)S(1)} %collective-permute-done.refs_0_, bf16[64,4096]{1,0:T(8,128)(2,1)S(1)} %collective-permute-done.6.refs_1_, bf16[4096,1024]{1,0:T(8,128)(2,1)} %refs_2_.3, bf16[256,1024]{1,0:T(8,128)(2,1)} %bitcast.14, ...), custom_call_target="tpu_custom_call" | custom-call | flops 5000000000 | tf_op jit(solution)/shard_map/project_late/pallas_call | solution.py:352
  55.6 2.5 %collective-permute-done.13.refs_6_ = bf16[128,1024]{1,0:T(8,128)(2,1)S(1)} collective-permute-done((bf16[128,1024]{1,0:T(8,128)(2,1)S(1)}, bf16[128,1024]{1,0:T(8,128)(2,1)S(1)}, u32[]{:S(2)}, u32[]{:S(2)}) %collective-permute-start.13) | collective-permute-done | bytes 262176 | tf_op jit(solution)/shard_map/ppermute | solution.py:45
  58.0 1.4 %collective-permute-done.12.refs_5_.refs_10_ = bf16[256,1024]{1,0:T(8,128)(2,1)S(1)} collective-permute-done((bf16[256,1024]{1,0:T(8,128)(2,1)S(1)}, bf16[256,1024]{1,0:T(8,128)(2,1)S(1)}, u32[]{:S(2)}, u32[]{:S(2)}) %collective-permute-start.12) | collective-permute-done | bytes 524320 | tf_op jit(solution)/shard_map/ppermute | solution.py:45
  59.5 3.1 %weight_parts.1 = (f32[256,1024]{1,0:T(8,128)S(1)}, bf16[256,1024]{1,0:T(8,128)(2,1)S(1)}, bf16[256,1024]{1,0:T(8,128)(2,1)S(1)}, bf16[256,1024]{1,0:T(8,128)(2,1)S(1)}) custom-call(bf16[128,1024]{1,0:T(8,128)(2,1)S(1)} %get-tuple-element.44.refs_0_, bf16[128,1024]{1,0:T(8,128)(2,1)S(1)} %collective-permute-done.3.refs_4_.refs_1_, ...), custom_call_target="tpu_custom_call" | custom-call | flops 4000000000 | tf_op jit(solution)/shard_map/weight_parts/pallas_call | solution.py:96
  62.6 1.5 %collective-permute-start.16 = (bf16[256,1024]{1,0:T(8,128)(2,1)S(1)}, bf16[256,1024]{1,0:T(8,128)(2,1)S(1)}, u32[]{:S(2)}, u32[]{:S(2)}) collective-permute-start(bf16[256,1024]{1,0:T(8,128)(2,1)S(1)} %get-tuple-element.50), channel_id=1, source_target_pairs={{0,8},{1,33},{2,10},{3,35},{4,12},{5,37},{6,14},{7,39},{8,0},{9,41... | collective-permute-start | bytes 1572872 | tf_op jit(solution)/shard_map/ppermute | solution.py:45
  65.3 1.3 %collective-permute-start.11 = (bf16[128,1024]{1,0:T(8,128)(2,1)S(1)}, bf16[128,1024]{1,0:T(8,128)(2,1)S(1)}, u32[]{:S(2)}, u32[]{:S(2)}) collective-permute-start(bf16[128,1024]{1,0:T(8,128)(2,1)S(1)} %slice.11), channel_id=1, source_target_pairs={{4,0},{8,4},{12,8},{16,12},{20,16},{24,20},{28,24},{32,28},{36,32}... | collective-permute-start | bytes 786440 | tf_op jit(solution)/shard_map/ppermute | solution.py:54
  66.6 3.8 %filter_grad.1 = f32[64,128]{1,0:T(8,128)S(1)} custom-call(bf16[128,1024]{1,0:T(8,128)(2,1)S(1)} %collective-permute-done.2.refs_1_.refs_0_, bf16[256,1024]{1,0:T(8,128)(2,1)} %bitcast.16, bf16[256,1024]{1,0:T(8,128)(2,1)S(1)} %get-tuple-element.43.refs_13_.refs_1_.refs_2_, f32[256,1024]{1,0:T(8,128)S(1)} %get-tuple-element.48.refs_0_.refs_3_), custom_call_target="tpu_custom_call" | custom-call | flops 4000000000 | tf_op jit(solution)/shard_map/filter_grad/pallas_call | solution.py:96
  70.4 2.8 %collective-permute-start.22 = (f32[64,128]{1,0:T(8,128)S(1)}, f32[64,128]{1,0:T(8,128)S(1)}, u32[]{:S(2)}, u32[]{:S(2)}) collective-permute-start(f32[64,128]{1,0:T(8,128)S(1)} %filter_grad.1), channel_id=1, source_target_pairs={{0,32},{1,9},{2,34},{3,11},{4,36},{5,13},{6,38},{7,15},{8,40},{9,1... | collective-permute-start | bytes 98312 | tf_op jit(solution)/shard_map/ppermute | solution.py:45
  73.2 2.3 %collective-permute-done.11.refs_4_.refs_2_ = bf16[128,1024]{1,0:T(8,128)(2,1)S(1)} collective-permute-done((bf16[128,1024]{1,0:T(8,128)(2,1)S(1)}, bf16[128,1024]{1,0:T(8,128)(2,1)S(1)}, u32[]{:S(2)}, u32[]{:S(2)}) %collective-permute-start.11) | collective-permute-done | bytes 262176 | tf_op jit(solution)/shard_map/ppermute | solution.py:54
  75.5 5.2 %collective-permute-start.23 = (f32[64,128]{1,0:T(8,128)S(1)}, f32[64,128]{1,0:T(8,128)S(1)}, u32[]{:S(2)}, u32[]{:S(2)}) collective-permute-start(f32[64,128]{1,0:T(8,128)S(1)} %filter_grad.1), channel_id=1, source_target_pairs={{0,16},{1,5},{2,18},{3,7},{4,20},{5,9},{6,22},{7,11},{8,24},{9,13}... | collective-permute-start | bytes 98312 | tf_op jit(solution)/shard_map/ppermute | solution.py:45
  80.7 5.9 %collective-permute-start.24 = (f32[64,128]{1,0:T(8,128)S(1)}, f32[64,128]{1,0:T(8,128)S(1)}, u32[]{:S(2)}, u32[]{:S(2)}) collective-permute-start(f32[64,128]{1,0:T(8,128)S(1)} %filter_grad.1), channel_id=1, source_target_pairs={{0,48},{1,13},{2,50},{3,15},{4,52},{5,1},{6,54},{7,3},{8,56},{9,5}... | collective-permute-start | bytes 98312 | tf_op jit(solution)/shard_map/ppermute | solution.py:45
  89.2 1.6 %collective-permute-start.20 = (bf16[64,1024]{1,0:T(8,128)(2,1)S(1)}, bf16[64,1024]{1,0:T(8,128)(2,1)S(1)}, u32[]{:S(2)}, u32[]{:S(2)}) collective-permute-start(bf16[64,1024]{1,0:T(8,128)(2,1)S(1)} %get-tuple-element.56), channel_id=1, source_target_pairs={{0,192},{64,0},{128,64},{192,128},{1,193},{65,1},{129,65},{193,129... | collective-permute-start | bytes 393224 | tf_op jit(solution)/shard_map/ppermute | solution.py:536
  91.0 2.8 %collective-permute-done.25 = f32[64,128]{1,0:T(8,128)S(1)} collective-permute-done((f32[64,128]{1,0:T(8,128)S(1)}, f32[64,128]{1,0:T(8,128)S(1)}, u32[]{:S(2)}, u32[]{:S(2)}) %collective-permute-start.25) | collective-permute-done | bytes 32800 | tf_op jit(solution)/shard_map/ppermute | solution.py:45
  94.3 3.8 %collective-permute-done.26 = f32[64,128]{1,0:T(8,128)S(1)} collective-permute-done((f32[64,128]{1,0:T(8,128)S(1)}, f32[64,128]{1,0:T(8,128)S(1)}, u32[]{:S(2)}, u32[]{:S(2)}) %collective-permute-start.26) | collective-permute-done | bytes 32800 | tf_op jit(solution)/shard_map/ppermute | solution.py:45
  99.4 3.0 %collective-permute-start.29 = (f32[64,128]{1,0:T(8,128)S(1)}, f32[64,128]{1,0:T(8,128)S(1)}, u32[]{:S(2)}, u32[]{:S(2)}) collective-permute-start(f32[64,128]{1,0:T(8,128)S(1)} %add.28), channel_id=1, source_target_pairs={{0,192},{64,0},{128,64},{192,128},{1,193},{65,1},{129,65},{193,129... | collective-permute-start | bytes 98312 | tf_op jit(solution)/shard_map/ppermute | solution.py:534
  102.5 3.4 %input_grad.1.refs_4_ = bf16[256,1024]{1,0:T(8,128)(2,1)} custom-call(bf16[64,128]{1,0:T(8,128)(2,1)} %refs_0_.3, bf16[256,1024]{1,0:T(8,128)(2,1)S(1)} %get-tuple-element.43.refs_13_.refs_1_.refs_2_, bf16[128,1024]{1,0:T(8,128)(2,1)S(1)} %collective-permute-done.11.refs_4_.refs_2_, f32[64,1024]{1,0:T(8,128)S(1)} %get-tuple-element.52.refs_3_.refs_0_), custom_call_target="tpu_custom_call" | custom-call | tf_op jit(solution)/shard_map/input_grad/pallas_call | solution.py:96
  106.0 8.7 %collective-permute-start.21 = (f32[64,512]{1,0:T(8,128)S(1)}, f32[64,512]{1,0:T(8,128)S(1)}, u32[]{:S(2)}, u32[]{:S(2)}) collective-permute-start(f32[64,512]{1,0:T(8,128)S(1)} %get-tuple-element.58), channel_id=1, source_target_pairs={{0,1},{1,0},{2,3},{3,2},{4,5},{5,4},{6,7},{7,6},{8,9},{9,8},{10,11... | collective-permute-start | bytes 393224 | tf_op jit(solution)/shard_map/ppermute | solution.py:32
  (46 shorter events, 12.1 us)
Async XLA Ops:
  0.6 12.7 %collective-permute-start.1 = (bf16[64,4096]{1,0:T(8,128)(2,1)}, bf16[64,4096]{1,0:T(8,128)(2,1)S(1)}, u32[]{:S(2)}, u32[]{:S(2)}) collective-permute-start(bf16[64,4096]{1,0:T(8,128)(2,1)} %bitcast.8), channel_id=1, source_target_pairs={{0,1},{1,0},{2,3},{3,2},{4,5},{5,4},{6,7},{7,6},{8,9},{9,8},{10,11... | collective-permute-start | bytes 1572872 | tf_op jit(solution)/shard_map/ppermute | solution.py:32
  4.0 37.2 %collective-permute-start = (bf16[64,4096]{1,0:T(8,128)(2,1)}, bf16[64,4096]{1,0:T(8,128)(2,1)S(1)}, u32[]{:S(2)}, u32[]{:S(2)}) collective-permute-start(bf16[64,4096]{1,0:T(8,128)(2,1)} %bitcast.9), channel_id=1, source_target_pairs={{0,2},{1,3},{2,0},{3,1},{4,6},{5,7},{6,4},{7,5},{8,10},{9,11},{10,... | collective-permute-start | bytes 1572872 | tf_op jit(solution)/shard_map/ppermute | solution.py:32
  10.1 10.0 %collective-permute-start.2 = (bf16[128,1024]{1,0:T(8,128)(2,1)S(1)}, bf16[128,1024]{1,0:T(8,128)(2,1)S(1)}, u32[]{:S(2)}, u32[]{:S(2)}) collective-permute-start(bf16[128,1024]{1,0:T(8,128)(2,1)S(1)} %slice_bitcast_fusion), channel_id=1, source_target_pairs={{0,4},{4,8},{8,12},{12,16},{16,20},{20,24},{24,28},{28,32},{32,36}... | collective-permute-start | bytes 786440 | tf_op jit(solution)/shard_map/ppermute | solution.py:54
  15.4 6.9 %collective-permute-start.3 = (bf16[128,1024]{1,0:T(8,128)(2,1)S(1)}, bf16[128,1024]{1,0:T(8,128)(2,1)S(1)}, u32[]{:S(2)}, u32[]{:S(2)}) collective-permute-start(bf16[128,1024]{1,0:T(8,128)(2,1)S(1)} %get-tuple-element.32), channel_id=1, source_target_pairs={{0,16},{1,5},{2,18},{3,7},{4,20},{5,9},{6,22},{7,11},{8,24},{9,13}... | collective-permute-start | bytes 786440 | tf_op jit(solution)/shard_map/ppermute | solution.py:45
  16.7 11.4 %collective-permute-start.4 = (bf16[128,1024]{1,0:T(8,128)(2,1)S(1)}, bf16[128,1024]{1,0:T(8,128)(2,1)S(1)}, u32[]{:S(2)}, u32[]{:S(2)}) collective-permute-start(bf16[128,1024]{1,0:T(8,128)(2,1)S(1)} %get-tuple-element.33), channel_id=1, source_target_pairs={{0,32},{1,9},{2,34},{3,11},{4,36},{5,13},{6,38},{7,15},{8,40},{9,1... | collective-permute-start | bytes 786440 | tf_op jit(solution)/shard_map/ppermute | solution.py:45
  18.9 9.2 %collective-permute-start.5 = (bf16[128,1024]{1,0:T(8,128)(2,1)S(1)}, bf16[128,1024]{1,0:T(8,128)(2,1)S(1)}, u32[]{:S(2)}, u32[]{:S(2)}) collective-permute-start(bf16[128,1024]{1,0:T(8,128)(2,1)S(1)} %get-tuple-element.34), channel_id=1, source_target_pairs={{0,48},{1,13},{2,50},{3,15},{4,52},{5,1},{6,54},{7,3},{8,56},{9,5}... | collective-permute-start | bytes 786440 | tf_op jit(solution)/shard_map/ppermute | solution.py:45
  31.5 1.4 %collective-permute-start.7 = (bf16[128,512]{1,0:T(8,128)(2,1)S(1)}, bf16[128,512]{1,0:T(8,128)(2,1)S(1)}, u32[]{:S(2)}, u32[]{:S(2)}) collective-permute-start(bf16[128,512]{1,0:T(8,128)(2,1)S(1)} %get-tuple-element.40), channel_id=1, source_target_pairs={{0,1},{1,0},{2,3},{3,2},{4,5},{5,4},{6,7},{7,6},{8,9},{9,8},{10,11... | collective-permute-start | bytes 393224 | tf_op jit(solution)/shard_map/ppermute | solution.py:32
  31.6 1.5 %collective-permute-start.8 = (bf16[128,512]{1,0:T(8,128)(2,1)S(1)}, bf16[128,512]{1,0:T(8,128)(2,1)S(1)}, u32[]{:S(2)}, u32[]{:S(2)}) collective-permute-start(bf16[128,512]{1,0:T(8,128)(2,1)S(1)} %get-tuple-element.41), channel_id=1, source_target_pairs={{0,1},{1,0},{2,3},{3,2},{4,5},{5,4},{6,7},{7,6},{8,9},{9,8},{10,11... | collective-permute-start | bytes 393224 | tf_op jit(solution)/shard_map/ppermute | solution.py:32
  33.2 10.0 %collective-permute-start.10 = (bf16[272,1024]{1,0:T(8,128)(2,1)S(1)}, bf16[272,1024]{1,0:T(8,128)(2,1)S(1)}, u32[]{:S(2)}, u32[]{:S(2)}) collective-permute-start(bf16[272,1024]{1,0:T(8,128)(2,1)S(1)} %join.1.refs_8_), channel_id=1, source_target_pairs={{0,48},{1,13},{2,50},{3,15},{4,52},{5,1},{6,54},{7,3},{8,56},{9,5}... | collective-permute-start | bytes 1671176 | tf_op jit(solution)/shard_map/ppermute | solution.py:45
  36.0 9.9 %collective-permute-start.9 = (bf16[272,1024]{1,0:T(8,128)(2,1)S(1)}, bf16[272,1024]{1,0:T(8,128)(2,1)S(1)}, u32[]{:S(2)}, u32[]{:S(2)}) collective-permute-start(bf16[272,1024]{1,0:T(8,128)(2,1)S(1)} %join.1.refs_8_), channel_id=1, source_target_pairs={{0,16},{1,5},{2,18},{3,7},{4,20},{5,9},{6,22},{7,11},{8,24},{9,13}... | collective-permute-start | bytes 1671176 | tf_op jit(solution)/shard_map/ppermute | solution.py:45
  41.2 2.0 %collective-permute-start.6 = (bf16[64,4096]{1,0:T(8,128)(2,1)S(1)}, bf16[64,4096]{1,0:T(8,128)(2,1)S(1)}, u32[]{:S(2)}, u32[]{:S(2)}) collective-permute-start(bf16[64,4096]{1,0:T(8,128)(2,1)S(1)} %collective-permute-done.refs_0_), channel_id=1, source_target_pairs={{0,1},{1,0},{2,3},{3,2},{4,5},{5,4},{6,7},{7,6},{8,9},{9,8},{10,11... | collective-permute-start | bytes 1572872 | tf_op jit(solution)/shard_map/ppermute | solution.py:32
  46.9 12.6 %collective-permute-start.12 = (bf16[256,1024]{1,0:T(8,128)(2,1)S(1)}, bf16[256,1024]{1,0:T(8,128)(2,1)S(1)}, u32[]{:S(2)}, u32[]{:S(2)}) collective-permute-start(bf16[256,1024]{1,0:T(8,128)(2,1)S(1)} %get-tuple-element.45), channel_id=1, source_target_pairs={{0,16},{1,5},{2,18},{3,7},{4,20},{5,9},{6,22},{7,11},{8,24},{9,13}... | collective-permute-start | bytes 1572872 | tf_op jit(solution)/shard_map/ppermute | solution.py:45
  47.1 12.3 %collective-permute-start.14 = (bf16[256,1024]{1,0:T(8,128)(2,1)S(1)}, bf16[256,1024]{1,0:T(8,128)(2,1)S(1)}, u32[]{:S(2)}, u32[]{:S(2)}) collective-permute-start(bf16[256,1024]{1,0:T(8,128)(2,1)S(1)} %get-tuple-element.47), channel_id=1, source_target_pairs={{0,48},{1,13},{2,50},{3,15},{4,52},{5,1},{6,54},{7,3},{8,56},{9,5}... | collective-permute-start | bytes 1572872 | tf_op jit(solution)/shard_map/ppermute | solution.py:45
  49.8 8.2 %collective-permute-start.13 = (bf16[128,1024]{1,0:T(8,128)(2,1)S(1)}, bf16[128,1024]{1,0:T(8,128)(2,1)S(1)}, u32[]{:S(2)}, u32[]{:S(2)}) collective-permute-start(bf16[128,1024]{1,0:T(8,128)(2,1)S(1)} %get-tuple-element.46), channel_id=1, source_target_pairs={{0,32},{1,9},{2,34},{3,11},{4,36},{5,13},{6,38},{7,15},{8,40},{9,1... | collective-permute-start | bytes 786440 | tf_op jit(solution)/shard_map/ppermute | solution.py:45
  62.5 18.1 %collective-permute-start.15 = (bf16[256,1024]{1,0:T(8,128)(2,1)S(1)}, bf16[256,1024]{1,0:T(8,128)(2,1)S(1)}, u32[]{:S(2)}, u32[]{:S(2)}) collective-permute-start(bf16[256,1024]{1,0:T(8,128)(2,1)S(1)} %get-tuple-element.49), channel_id=1, source_target_pairs={{0,4},{1,17},{2,6},{3,19},{4,8},{5,21},{6,10},{7,23},{8,12},{9,25}... | collective-permute-start | bytes 1572872 | tf_op jit(solution)/shard_map/ppermute | solution.py:45
  62.6 23.9 %collective-permute-start.16 = (bf16[256,1024]{1,0:T(8,128)(2,1)S(1)}, bf16[256,1024]{1,0:T(8,128)(2,1)S(1)}, u32[]{:S(2)}, u32[]{:S(2)}) collective-permute-start(bf16[256,1024]{1,0:T(8,128)(2,1)S(1)} %get-tuple-element.50), channel_id=1, source_target_pairs={{0,8},{1,33},{2,10},{3,35},{4,12},{5,37},{6,14},{7,39},{8,0},{9,41... | collective-permute-start | bytes 1572872 | tf_op jit(solution)/shard_map/ppermute | solution.py:45
  64.1 22.5 %collective-permute-start.17 = (bf16[256,1024]{1,0:T(8,128)(2,1)S(1)}, bf16[256,1024]{1,0:T(8,128)(2,1)S(1)}, u32[]{:S(2)}, u32[]{:S(2)}) collective-permute-start(bf16[256,1024]{1,0:T(8,128)(2,1)S(1)} %get-tuple-element.51), channel_id=1, source_target_pairs={{0,12},{1,49},{2,14},{3,51},{4,0},{5,53},{6,2},{7,55},{8,4},{9,57}... | collective-permute-start | bytes 1572872 | tf_op jit(solution)/shard_map/ppermute | solution.py:45
  65.3 10.2 %collective-permute-start.11 = (bf16[128,1024]{1,0:T(8,128)(2,1)S(1)}, bf16[128,1024]{1,0:T(8,128)(2,1)S(1)}, u32[]{:S(2)}, u32[]{:S(2)}) collective-permute-start(bf16[128,1024]{1,0:T(8,128)(2,1)S(1)} %slice.11), channel_id=1, source_target_pairs={{4,0},{8,4},{12,8},{16,12},{20,16},{24,20},{28,24},{32,28},{36,32}... | collective-permute-start | bytes 786440 | tf_op jit(solution)/shard_map/ppermute | solution.py:54
  70.4 18.8 %collective-permute-start.22 = (f32[64,128]{1,0:T(8,128)S(1)}, f32[64,128]{1,0:T(8,128)S(1)}, u32[]{:S(2)}, u32[]{:S(2)}) collective-permute-start(f32[64,128]{1,0:T(8,128)S(1)} %filter_grad.1), channel_id=1, source_target_pairs={{0,32},{1,9},{2,34},{3,11},{4,36},{5,13},{6,38},{7,15},{8,40},{9,1... | collective-permute-start | bytes 98312 | tf_op jit(solution)/shard_map/ppermute | solution.py:45
  75.5 15.4 %collective-permute-start.23 = (f32[64,128]{1,0:T(8,128)S(1)}, f32[64,128]{1,0:T(8,128)S(1)}, u32[]{:S(2)}, u32[]{:S(2)}) collective-permute-start(f32[64,128]{1,0:T(8,128)S(1)} %filter_grad.1), channel_id=1, source_target_pairs={{0,16},{1,5},{2,18},{3,7},{4,20},{5,9},{6,22},{7,11},{8,24},{9,13}... | collective-permute-start | bytes 98312 | tf_op jit(solution)/shard_map/ppermute | solution.py:45
  80.7 10.2 %collective-permute-start.24 = (f32[64,128]{1,0:T(8,128)S(1)}, f32[64,128]{1,0:T(8,128)S(1)}, u32[]{:S(2)}, u32[]{:S(2)}) collective-permute-start(f32[64,128]{1,0:T(8,128)S(1)} %filter_grad.1), channel_id=1, source_target_pairs={{0,48},{1,13},{2,50},{3,15},{4,52},{5,1},{6,54},{7,3},{8,56},{9,5}... | collective-permute-start | bytes 98312 | tf_op jit(solution)/shard_map/ppermute | solution.py:45
  87.0 12.4 %collective-permute-start.18 = (bf16[64,1024]{1,0:T(8,128)(2,1)S(1)}, bf16[64,1024]{1,0:T(8,128)(2,1)S(1)}, u32[]{:S(2)}, u32[]{:S(2)}) collective-permute-start(bf16[64,1024]{1,0:T(8,128)(2,1)S(1)} %get-tuple-element.54), channel_id=1, source_target_pairs={{0,64},{64,128},{128,192},{192,0},{1,65},{65,129},{129,193},{193,1... | collective-permute-start | bytes 393224 | tf_op jit(solution)/shard_map/ppermute | solution.py:536
  88.1 17.8 %collective-permute-start.19 = (bf16[64,1024]{1,0:T(8,128)(2,1)S(1)}, bf16[64,1024]{1,0:T(8,128)(2,1)S(1)}, u32[]{:S(2)}, u32[]{:S(2)}) collective-permute-start(bf16[64,1024]{1,0:T(8,128)(2,1)S(1)} %get-tuple-element.55), channel_id=1, source_target_pairs={{0,128},{64,192},{128,0},{192,64},{1,129},{65,193},{129,1},{193,65... | collective-permute-start | bytes 393224 | tf_op jit(solution)/shard_map/ppermute | solution.py:536
  89.2 16.6 %collective-permute-start.20 = (bf16[64,1024]{1,0:T(8,128)(2,1)S(1)}, bf16[64,1024]{1,0:T(8,128)(2,1)S(1)}, u32[]{:S(2)}, u32[]{:S(2)}) collective-permute-start(bf16[64,1024]{1,0:T(8,128)(2,1)S(1)} %get-tuple-element.56), channel_id=1, source_target_pairs={{0,192},{64,0},{128,64},{192,128},{1,193},{65,1},{129,65},{193,129... | collective-permute-start | bytes 393224 | tf_op jit(solution)/shard_map/ppermute | solution.py:536
  90.9 2.9 %collective-permute-start.25 = (f32[64,128]{1,0:T(8,128)S(1)}, f32[64,128]{1,0:T(8,128)S(1)}, u32[]{:S(2)}, u32[]{:S(2)}) collective-permute-start(f32[64,128]{1,0:T(8,128)S(1)} %add_add_fusion), channel_id=1, source_target_pairs={{0,4},{1,17},{2,6},{3,19},{4,0},{5,21},{6,2},{7,23},{8,12},{9,25},... | collective-permute-start | bytes 98312 | tf_op jit(solution)/shard_map/ppermute | solution.py:45
  93.7 4.4 %collective-permute-start.26 = (f32[64,128]{1,0:T(8,128)S(1)}, f32[64,128]{1,0:T(8,128)S(1)}, u32[]{:S(2)}, u32[]{:S(2)}) collective-permute-start(f32[64,128]{1,0:T(8,128)S(1)} %add.27), channel_id=1, source_target_pairs={{0,8},{1,33},{2,10},{3,35},{4,12},{5,37},{6,14},{7,39},{8,0},{9,41... | collective-permute-start | bytes 98312 | tf_op jit(solution)/shard_map/ppermute | solution.py:45
  98.2 16.5 %collective-permute-start.27 = (f32[64,128]{1,0:T(8,128)S(1)}, f32[64,128]{1,0:T(8,128)S(1)}, u32[]{:S(2)}, u32[]{:S(2)}) collective-permute-start(f32[64,128]{1,0:T(8,128)S(1)} %add.28), channel_id=1, source_target_pairs={{0,128},{64,192},{128,0},{192,64},{1,129},{65,193},{129,1},{193,65... | collective-permute-start | bytes 98312 | tf_op jit(solution)/shard_map/ppermute | solution.py:534
  99.2 15.5 %collective-permute-start.28 = (f32[64,128]{1,0:T(8,128)S(1)}, f32[64,128]{1,0:T(8,128)S(1)}, u32[]{:S(2)}, u32[]{:S(2)}) collective-permute-start(f32[64,128]{1,0:T(8,128)S(1)} %add.28), channel_id=1, source_target_pairs={{0,64},{64,128},{128,192},{192,0},{1,65},{65,129},{129,193},{193,1... | collective-permute-start | bytes 98312 | tf_op jit(solution)/shard_map/ppermute | solution.py:534
  99.4 15.2 %collective-permute-start.29 = (f32[64,128]{1,0:T(8,128)S(1)}, f32[64,128]{1,0:T(8,128)S(1)}, u32[]{:S(2)}, u32[]{:S(2)}) collective-permute-start(f32[64,128]{1,0:T(8,128)S(1)} %add.28), channel_id=1, source_target_pairs={{0,192},{64,0},{128,64},{192,128},{1,193},{65,1},{129,65},{193,129... | collective-permute-start | bytes 98312 | tf_op jit(solution)/shard_map/ppermute | solution.py:534
  106.0 9.6 %collective-permute-start.21 = (f32[64,512]{1,0:T(8,128)S(1)}, f32[64,512]{1,0:T(8,128)S(1)}, u32[]{:S(2)}, u32[]{:S(2)}) collective-permute-start(f32[64,512]{1,0:T(8,128)S(1)} %get-tuple-element.58), channel_id=1, source_target_pairs={{0,1},{1,0},{2,3},{3,2},{4,5},{5,4},{6,7},{7,6},{8,9},{9,8},{10,11... | collective-permute-start | bytes 393224 | tf_op jit(solution)/shard_map/ppermute | solution.py:32

commit v8 on v6

--- a/solution.py
+++ b/solution.py
@@ -364,28 +364,6 @@
         cost_estimate=lasting(5 if done else 0),
         name="project_late" if done else "project_early",
     )(mine, other, weight, gating, response, *done, *after)
-
-
-def high_and_low(x):
-    high = x.astype(BF16).astype(F32)
-    return high, (x - high).astype(BF16).astype(F32)
-
-
-def folded(x, rows):
-    return jnp.concatenate([x[i : i + rows] for i in range(0, x.shape[0], rows)], 1)
-
-
-def unfolded(x):
-    return jnp.concatenate([x[:, i : i + LANES] for i in range(0, x.shape[1], LANES)], 0)
-
-
-def riding(ref, start, rows):
-    pair = ref[start : start + 2 * rows].astype(F32)
-    return unfolded(pair[:rows] + pair[rows:])
-
-
-def four_sum(parts):
-    return (parts[0] + parts[2]) + (parts[1] + parts[3])
 
 
 def weight_kernel(*refs):
@@ -583,15 +561,15 @@
         late, late_other, weight, gating, response, (conv_early, gate_early), (own_late,)
     )
     late_got = [stepped(late_sent[s - 1], True, s) for s in shifts]
-    following = shifted(conv_grad[:TAPS], -1)
     filter_sum = filter_grad(previous, signal, conv_grad, ())
     parts = weight_parts([early[0], *early_got], own_late, gated, got, late_got, (filter_sum,))
 
-    filter_sum = paired(filter_sum, True, 1)
-    filter_sum = paired(filter_sum, True, 2, (parts[0],))
-    filter_sum = paired(paired(filter_sum, False, 1), False, 2)
+    filter_sum = four_sum([filter_sum] + [stepped(filter_sum, True, s) for s in shifts])
+    filter_sum = tied(filter_sum, parts[0])
+    filter_sum = four_sum([filter_sum] + [stepped(filter_sum, False, s) for s in shifts])
     parts = [parts[0]] + [stepped(parts[s], False, s) for s in shifts]
-    sums, own_filter = first_sum(parts, filter_sum, (following,))
+    sums, own_filter = first_sum(parts, filter_sum, ())
+    following = shifted(tied(conv_grad[:TAPS], filter_sum), -1)
     grad_input = input_grad(filters, conv_grad, following, (sums[0],))
     line = [[(i, (i + s) % SIDE) for i in range(SIDE)] for s in shifts]
     sums = [sums[0]] + [lax.ppermute(sums[s], "dp", line[s - 1]) for s in shifts]

time: 105 us -> 102 us (0.971)
  the two profiles are of different devices: /device:TPU:1 before, /device:TPU:2 now
where the time goes in v8:
time: 102 us; the launch traced here: 101 us
  starting transfers between devices  46 us (45%)
  Pallas kernels  27.9 us (27%)
  waiting for transfers between devices  25.2 us (25%)
    ppermute x16, starting transfers between devices, in_plane(): return lax.ppermute(x, ('ctx', 'tp'), pairs)  22.3 us
    pallas_call x10, Pallas kernels, once(): pl.pallas_call(body, grid=(1,), in_specs=specs + [ANYWHERE] * len(after),...  16.9 us
    ppermute x16, waiting for transfers between devices, in_plane(): return lax.ppermute(x, ('ctx', 'tp'), pairs)  12.8 us
    pallas_call x2, Pallas kernels, project(): pl.pallas_call(body, grid=(channels // WIDE,), in_specs=[full(mine.shape)...  11 us
    ppermute x2, starting transfers between devices, shifted(): lax.ppermute(x, 'ctx', [(i, i + by) for i in range(devices) if 0 <= i + b...  10.2 us
    ppermute x6, starting transfers between devices, moved(): return lax.ppermute(x, 'tp', [(i, i ^ step) for i in range(4)])  9.02 us
    ppermute x2, waiting for transfers between devices, shifted(): lax.ppermute(x, 'ctx', [(i, i + by) for i in range(devices) if 0 <= i + b...  5.67 us
    ppermute x3, starting transfers between devices, local(): lax.ppermute(sums[s], 'dp', line[s - 1])  4.46 us
  transfers between devices with their start and end apart: 27, of which 9 were waited for; matrix products, arithmetic and copies ran while one was open for 1% of the time, Pallas kernels for 26%

profile of v8, /device:TPU:2, one launch (start us, length us, event | category | flops | bytes accessed | tf_op | source)
XLA Modules:
  0.0 101.0 jit_solution(12146943763382826977)
XLA Ops:
  0.7 7.3 %collective-permute-start = (bf16[64,4096]{1,0:T(8,128)(2,1)}, bf16[64,4096]{1,0:T(8,128)(2,1)S(1)}, u32[]{:S(2)}, u32[]{:S(2)}) collective-permute-start(bf16[64,4096]{1,0:T(8,128)(2,1)} %bitcast.9), channel_id=1, source_target_pairs={{0,2},{1,3},{2,0},{3,1},{4,6},{5,7},{6,4},{7,5},{8,10},{9,11},{10,... | collective-permute-start | bytes 1572872 | tf_op jit(solution)/shard_map/ppermute | solution.py:32
  8.0 1.0 slice_bitcast_fusion
  9.0 3.5 %collective-permute-start.2 = (bf16[128,1024]{1,0:T(8,128)(2,1)S(1)}, bf16[128,1024]{1,0:T(8,128)(2,1)S(1)}, u32[]{:S(2)}, u32[]{:S(2)}) collective-permute-start(bf16[128,1024]{1,0:T(8,128)(2,1)S(1)} %slice_bitcast_fusion), channel_id=1, source_target_pairs={{0,4},{4,8},{8,12},{12,16},{16,20},{20,24},{24,28},{28,32},{32,36}... | collective-permute-start | bytes 786440 | tf_op jit(solution)/shard_map/ppermute | solution.py:54
  12.5 1.2 %pack.1 = (bf16[128,1024]{1,0:T(8,128)(2,1)S(1)}, bf16[128,1024]{1,0:T(8,128)(2,1)S(1)}, bf16[128,1024]{1,0:T(8,128)(2,1)S(1)}, bf16[128,1024]{1,0:T(8,128)(2,1)S(1)}) custom-call(bf16[64,4096]{1,0:T(8,128)(2,1)} %bitcast.10, bf16[64,4096]{1,0:T(8,128)(2,1)S(1)} %collective-permute-done.1.refs_1_), custom_call_target="tpu_custom_call" | custom-call | tf_op jit(solution)/shard_map/pack/pallas_call | solution.py:96
  13.7 1.6 %collective-permute-start.6 = (bf16[128,1024]{1,0:T(8,128)(2,1)S(1)}, bf16[128,1024]{1,0:T(8,128)(2,1)S(1)}, u32[]{:S(2)}, u32[]{:S(2)}) collective-permute-start(bf16[128,1024]{1,0:T(8,128)(2,1)S(1)} %get-tuple-element.42), channel_id=1, source_target_pairs={{0,16},{1,5},{2,18},{3,7},{4,20},{5,9},{6,22},{7,11},{8,24},{9,13}... | collective-permute-start | bytes 786440 | tf_op jit(solution)/shard_map/ppermute | solution.py:45
  15.8 5.7 %collective-permute-done.2.refs_1_.refs_0_ = bf16[128,1024]{1,0:T(8,128)(2,1)S(1)} collective-permute-done((bf16[128,1024]{1,0:T(8,128)(2,1)S(1)}, bf16[128,1024]{1,0:T(8,128)(2,1)S(1)}, u32[]{:S(2)}, u32[]{:S(2)}) %collective-permute-start.2) | collective-permute-done | bytes 262176 | tf_op jit(solution)/shard_map/ppermute | solution.py:54
  21.4 3.4 %conv_forward.1 = (f32[256,1024]{1,0:T(8,128)S(1)}, bf16[256,512]{1,0:T(8,128)(2,1)S(1)}, bf16[128,512]{1,0:T(8,128)(2,1)S(1)}, bf16[128,512]{1,0:T(8,128)(2,1)S(1)}) custom-call(bf16[64,128]{1,0:T(8,128)(2,1)} %refs_0_.3, bf16[128,1024]{1,0:T(8,128)(2,1)S(1)} %collective-permute-done.2.refs_1_.refs_0_, bf16[256,1024]{1,0:T(8,128)(2,1)} %bitcast.15, ...), custom_call_target="tpu_custom_call" | custom-call | tf_op jit(solution)/shard_map/conv_forward/pallas_call | solution.py:96
  26.5 1.6 %collective-permute-start.8 = (bf16[272,1024]{1,0:T(8,128)(2,1)S(1)}, bf16[272,1024]{1,0:T(8,128)(2,1)S(1)}, u32[]{:S(2)}, u32[]{:S(2)}) collective-permute-start(bf16[272,1024]{1,0:T(8,128)(2,1)S(1)} %join.1.refs_8_), channel_id=1, source_target_pairs={{0,16},{1,5},{2,18},{3,7},{4,20},{5,9},{6,22},{7,11},{8,24},{9,13}... | collective-permute-start | bytes 1671176 | tf_op jit(solution)/shard_map/ppermute | solution.py:45
  28.6 5.2 %project_early.1 = (bf16[128,1024]{1,0:T(8,128)(2,1)S(1)}, bf16[128,1024]{1,0:T(8,128)(2,1)S(1)}) custom-call(bf16[64,4096]{1,0:T(8,128)(2,1)} %bitcast.11, bf16[64,4096]{1,0:T(8,128)(2,1)S(1)} %collective-permute-done.1.refs_1_, bf16[4096,1024]{1,0:T(8,128)(2,1)} %refs_2_.3, bf16[256,1024]{1,0:T(8,128)(2,1)} %bitcast.13, ...), custom_call_target="tpu_custom_call" | custom-call | tf_op jit(solution)/shard_map/project_early/pallas_call | solution.py:353
  33.9 1.1 %collective-permute-start.3 = (bf16[64,4096]{1,0:T(8,128)(2,1)S(1)}, bf16[64,4096]{1,0:T(8,128)(2,1)S(1)}, u32[]{:S(2)}, u32[]{:S(2)}) collective-permute-start(bf16[64,4096]{1,0:T(8,128)(2,1)S(1)} %collective-permute-done.refs_0_), channel_id=1, source_target_pairs={{0,1},{1,0},{2,3},{3,2},{4,5},{5,4},{6,7},{7,6},{8,9},{9,8},{10,11... | collective-permute-start | bytes 1572872 | tf_op jit(solution)/shard_map/ppermute | solution.py:32
  34.9 1.5 %collective-permute-done.3.refs_1_ = bf16[64,4096]{1,0:T(8,128)(2,1)S(1)} collective-permute-done((bf16[64,4096]{1,0:T(8,128)(2,1)S(1)}, bf16[64,4096]{1,0:T(8,128)(2,1)S(1)}, u32[]{:S(2)}, u32[]{:S(2)}) %collective-permute-start.3) | collective-permute-done | bytes 524320 | tf_op jit(solution)/shard_map/ppermute | solution.py:32
  36.5 1.2 %collective-permute-done.9.refs_3_.refs_12_ = bf16[272,1024]{1,0:T(8,128)(2,1)S(1)} collective-permute-done((bf16[272,1024]{1,0:T(8,128)(2,1)S(1)}, bf16[272,1024]{1,0:T(8,128)(2,1)S(1)}, u32[]{:S(2)}, u32[]{:S(2)}) %collective-permute-start.9) | collective-permute-done | bytes 557088 | tf_op jit(solution)/shard_map/ppermute | solution.py:45
  37.8 2.0 %collective-permute-start.13 = (bf16[256,1024]{1,0:T(8,128)(2,1)S(1)}, bf16[256,1024]{1,0:T(8,128)(2,1)S(1)}, u32[]{:S(2)}, u32[]{:S(2)}) collective-permute-start(bf16[256,1024]{1,0:T(8,128)(2,1)S(1)} %get-tuple-element.48), channel_id=1, source_target_pairs={{0,32},{1,9},{2,34},{3,11},{4,36},{5,13},{6,38},{7,15},{8,40},{9,1... | collective-permute-start | bytes 1572872 | tf_op jit(solution)/shard_map/ppermute | solution.py:45
  39.9 2.0 %collective-permute-start.15 = (bf16[256,1024]{1,0:T(8,128)(2,1)S(1)}, bf16[256,1024]{1,0:T(8,128)(2,1)S(1)}, u32[]{:S(2)}, u32[]{:S(2)}) collective-permute-start(bf16[256,1024]{1,0:T(8,128)(2,1)S(1)} %get-tuple-element.50), channel_id=1, source_target_pairs={{0,48},{1,13},{2,50},{3,15},{4,52},{5,1},{6,54},{7,3},{8,56},{9,5}... | collective-permute-start | bytes 1572872 | tf_op jit(solution)/shard_map/ppermute | solution.py:45
  41.9 5.8 %project_late.1 = (bf16[256,1024]{1,0:T(8,128)(2,1)S(1)}, bf16[256,1024]{1,0:T(8,128)(2,1)}) custom-call(bf16[64,4096]{1,0:T(8,128)(2,1)S(1)} %collective-permute-done.refs_0_, bf16[64,4096]{1,0:T(8,128)(2,1)S(1)} %collective-permute-done.3.refs_1_, bf16[4096,1024]{1,0:T(8,128)(2,1)} %refs_2_.3, bf16[256,1024]{1,0:T(8,128)(2,1)} %bitcast.14, ...), custom_call_target="tpu_custom_call" | custom-call | flops 5000000000 | tf_op jit(solution)/shard_map/project_late/pallas_call | solution.py:353
  47.7 3.8 %filter_grad.1.refs_13_ = f32[64,128]{1,0:T(8,128)S(1)} custom-call(bf16[128,1024]{1,0:T(8,128)(2,1)S(1)} %collective-permute-done.2.refs_1_.refs_0_, bf16[256,1024]{1,0:T(8,128)(2,1)} %bitcast.16, bf16[256,1024]{1,0:T(8,128)(2,1)S(1)} %get-tuple-element.46.refs_2_.refs_1_), custom_call_target="tpu_custom_call" | custom-call | flops 4000000000 | tf_op jit(solution)/shard_map/filter_grad/pallas_call | solution.py:96
  51.4 1.7 %collective-permute-start.10 = (f32[64,128]{1,0:T(8,128)S(1)}, f32[64,128]{1,0:T(8,128)S(1)}, u32[]{:S(2)}, u32[]{:S(2)}) collective-permute-start(f32[64,128]{1,0:T(8,128)S(1)} %filter_grad.1.refs_13_), channel_id=1, source_target_pairs={{0,32},{1,9},{2,34},{3,11},{4,36},{5,13},{6,38},{7,15},{8,40},{9,1... | collective-permute-start | bytes 98312 | tf_op jit(solution)/shard_map/ppermute | solution.py:45
  53.1 2.4 %collective-permute-start.11 = (f32[64,128]{1,0:T(8,128)S(1)}, f32[64,128]{1,0:T(8,128)S(1)}, u32[]{:S(2)}, u32[]{:S(2)}) collective-permute-start(f32[64,128]{1,0:T(8,128)S(1)} %filter_grad.1.refs_13_), channel_id=1, source_target_pairs={{0,16},{1,5},{2,18},{3,7},{4,20},{5,9},{6,22},{7,11},{8,24},{9,13}... | collective-permute-start | bytes 98312 | tf_op jit(solution)/shard_map/ppermute | solution.py:45
  55.6 3.1 %weight_parts.1 = (f32[256,1024]{1,0:T(8,128)S(1)}, bf16[256,1024]{1,0:T(8,128)(2,1)S(1)}, bf16[256,1024]{1,0:T(8,128)(2,1)S(1)}, bf16[256,1024]{1,0:T(8,128)(2,1)S(1)}) custom-call(bf16[128,1024]{1,0:T(8,128)(2,1)S(1)} %get-tuple-element.47.refs_0_, bf16[128,1024]{1,0:T(8,128)(2,1)S(1)} %collective-permute-done.6.refs_3_.refs_1_, ...), custom_call_target="tpu_custom_call" | custom-call | flops 4000000000 | tf_op jit(solution)/shard_map/weight_parts/pallas_call | solution.py:96
  58.9 2.9 %collective-permute-start.21 = (bf16[256,1024]{1,0:T(8,128)(2,1)S(1)}, bf16[256,1024]{1,0:T(8,128)(2,1)S(1)}, u32[]{:S(2)}, u32[]{:S(2)}) collective-permute-start(bf16[256,1024]{1,0:T(8,128)(2,1)S(1)} %get-tuple-element.55), channel_id=1, source_target_pairs={{0,8},{1,33},{2,10},{3,35},{4,12},{5,37},{6,14},{7,39},{8,0},{9,41... | collective-permute-start | bytes 1572872 | tf_op jit(solution)/shard_map/ppermute | solution.py:45
  61.8 1.3 %collective-permute-start.22 = (bf16[256,1024]{1,0:T(8,128)(2,1)S(1)}, bf16[256,1024]{1,0:T(8,128)(2,1)S(1)}, u32[]{:S(2)}, u32[]{:S(2)}) collective-permute-start(bf16[256,1024]{1,0:T(8,128)(2,1)S(1)} %get-tuple-element.56), channel_id=1, source_target_pairs={{0,12},{1,49},{2,14},{3,51},{4,0},{5,53},{6,2},{7,55},{8,4},{9,57}... | collective-permute-start | bytes 1572872 | tf_op jit(solution)/shard_map/ppermute | solution.py:45
  63.2 1.8 %collective-permute-start.16 = (f32[64,128]{1,0:T(8,128)S(1)}, f32[64,128]{1,0:T(8,128)S(1)}, u32[]{:S(2)}, u32[]{:S(2)}) collective-permute-start(f32[64,128]{1,0:T(8,128)S(1)} %add_add_fusion.1), channel_id=1, source_target_pairs={{0,8},{1,33},{2,10},{3,35},{4,12},{5,37},{6,14},{7,39},{8,0},{9,41... | collective-permute-start | bytes 98312 | tf_op jit(solution)/shard_map/ppermute | solution.py:45
  65.0 10.0 %collective-permute-done.16 = f32[64,128]{1,0:T(8,128)S(1)} collective-permute-done((f32[64,128]{1,0:T(8,128)S(1)}, f32[64,128]{1,0:T(8,128)S(1)}, u32[]{:S(2)}, u32[]{:S(2)}) %collective-permute-start.16) | collective-permute-done | bytes 32800 | tf_op jit(solution)/shard_map/ppermute | solution.py:45
  75.0 3.6 %collective-permute-start.18 = (f32[64,128]{1,0:T(8,128)S(1)}, f32[64,128]{1,0:T(8,128)S(1)}, u32[]{:S(2)}, u32[]{:S(2)}) collective-permute-start(f32[64,128]{1,0:T(8,128)S(1)} %add_add_fusion.1), channel_id=1, source_target_pairs={{0,12},{1,49},{2,14},{3,51},{4,0},{5,53},{6,2},{7,55},{8,4},{9,57}... | collective-permute-start | bytes 98312 | tf_op jit(solution)/shard_map/ppermute | solution.py:45
  78.7 1.6 %collective-permute-done.18 = f32[64,128]{1,0:T(8,128)S(1)} collective-permute-done((f32[64,128]{1,0:T(8,128)S(1)}, f32[64,128]{1,0:T(8,128)S(1)}, u32[]{:S(2)}, u32[]{:S(2)}) %collective-permute-start.18) | collective-permute-done | bytes 32800 | tf_op jit(solution)/shard_map/ppermute | solution.py:45
  80.3 6.7 %collective-permute-start.19 = (bf16[128,1024]{1,0:T(8,128)(2,1)S(1)}, bf16[128,1024]{1,0:T(8,128)(2,1)S(1)}, u32[]{:S(2)}, u32[]{:S(2)}) collective-permute-start(bf16[128,1024]{1,0:T(8,128)(2,1)S(1)} %slice.11), channel_id=1, source_target_pairs={{4,0},{8,4},{12,8},{16,12},{20,16},{24,20},{28,24},{32,28},{36,32}... | collective-permute-start | bytes 786440 | tf_op jit(solution)/shard_map/ppermute | solution.py:54
  87.5 1.1 %collective-permute-start.23 = (bf16[80,1024]{1,0:T(8,128)(2,1)S(1)}, bf16[80,1024]{1,0:T(8,128)(2,1)S(1)}, u32[]{:S(2)}, u32[]{:S(2)}) collective-permute-start(bf16[80,1024]{1,0:T(8,128)(2,1)S(1)} %get-tuple-element.59), channel_id=1, source_target_pairs={{0,64},{64,128},{128,192},{192,0},{1,65},{65,129},{129,193},{193,1... | collective-permute-start | bytes 491528 | tf_op jit(solution)/shard_map/ppermute | solution.py:575
  88.6 1.5 %collective-permute-start.24 = (bf16[80,1024]{1,0:T(8,128)(2,1)S(1)}, bf16[80,1024]{1,0:T(8,128)(2,1)S(1)}, u32[]{:S(2)}, u32[]{:S(2)}) collective-permute-start(bf16[80,1024]{1,0:T(8,128)(2,1)S(1)} %get-tuple-element.60), channel_id=1, source_target_pairs={{0,128},{64,192},{128,0},{192,64},{1,129},{65,193},{129,1},{193,65... | collective-permute-start | bytes 491528 | tf_op jit(solution)/shard_map/ppermute | solution.py:575
  90.0 1.9 %collective-permute-start.25 = (bf16[80,1024]{1,0:T(8,128)(2,1)S(1)}, bf16[80,1024]{1,0:T(8,128)(2,1)S(1)}, u32[]{:S(2)}, u32[]{:S(2)}) collective-permute-start(bf16[80,1024]{1,0:T(8,128)(2,1)S(1)} %get-tuple-element.61), channel_id=1, source_target_pairs={{0,192},{64,0},{128,64},{192,128},{1,193},{65,1},{129,65},{193,129... | collective-permute-start | bytes 491528 | tf_op jit(solution)/shard_map/ppermute | solution.py:575
  91.9 3.4 %input_grad.1.refs_5_ = bf16[256,1024]{1,0:T(8,128)(2,1)} custom-call(bf16[64,128]{1,0:T(8,128)(2,1)} %refs_0_.3, bf16[256,1024]{1,0:T(8,128)(2,1)S(1)} %get-tuple-element.46.refs_2_.refs_1_, bf16[128,1024]{1,0:T(8,128)(2,1)S(1)} %collective-permute-done.19.refs_2_, f32[64,1024]{1,0:T(8,128)S(1)} %get-tuple-element.57.refs_3_.refs_0_), custom_call_target="tpu_custom_call" | custom-call | tf_op jit(solution)/shard_map/input_grad/pallas_call | solution.py:96
  95.3 2.8 %collective-permute-done.24.refs_2_ = bf16[80,1024]{1,0:T(8,128)(2,1)S(1)} collective-permute-done((bf16[80,1024]{1,0:T(8,128)(2,1)S(1)}, bf16[80,1024]{1,0:T(8,128)(2,1)S(1)}, u32[]{:S(2)}, u32[]{:S(2)}) %collective-permute-start.24) | collective-permute-done | bytes 163872 | tf_op jit(solution)/shard_map/ppermute | solution.py:575
  98.9 1.3 %collective-permute-done.26.refs_1_ = f32[64,512]{1,0:T(8,128)S(1)} collective-permute-done((f32[64,512]{1,0:T(8,128)S(1)}, f32[64,512]{1,0:T(8,128)S(1)}, u32[]{:S(2)}, u32[]{:S(2)}) %collective-permute-start.26) | collective-permute-done | bytes 131104 | tf_op jit(solution)/shard_map/ppermute | solution.py:32
  (38 shorter events, 5.3 us)
Async XLA Ops:
  0.6 11.8 %collective-permute-start.1 = (bf16[64,4096]{1,0:T(8,128)(2,1)}, bf16[64,4096]{1,0:T(8,128)(2,1)S(1)}, u32[]{:S(2)}, u32[]{:S(2)}) collective-permute-start(bf16[64,4096]{1,0:T(8,128)(2,1)} %bitcast.8), channel_id=1, source_target_pairs={{0,1},{1,0},{2,3},{3,2},{4,5},{5,4},{6,7},{7,6},{8,9},{9,8},{10,11... | collective-permute-start | bytes 1572872 | tf_op jit(solution)/shard_map/ppermute | solution.py:32
  0.7 33.1 %collective-permute-start = (bf16[64,4096]{1,0:T(8,128)(2,1)}, bf16[64,4096]{1,0:T(8,128)(2,1)S(1)}, u32[]{:S(2)}, u32[]{:S(2)}) collective-permute-start(bf16[64,4096]{1,0:T(8,128)(2,1)} %bitcast.9), channel_id=1, source_target_pairs={{0,2},{1,3},{2,0},{3,1},{4,6},{5,7},{6,4},{7,5},{8,10},{9,11},{10,... | collective-permute-start | bytes 1572872 | tf_op jit(solution)/shard_map/ppermute | solution.py:32
  9.0 12.5 %collective-permute-start.2 = (bf16[128,1024]{1,0:T(8,128)(2,1)S(1)}, bf16[128,1024]{1,0:T(8,128)(2,1)S(1)}, u32[]{:S(2)}, u32[]{:S(2)}) collective-permute-start(bf16[128,1024]{1,0:T(8,128)(2,1)S(1)} %slice_bitcast_fusion), channel_id=1, source_target_pairs={{0,4},{4,8},{8,12},{12,16},{16,20},{20,24},{24,28},{28,32},{32,36}... | collective-permute-start | bytes 786440 | tf_op jit(solution)/shard_map/ppermute | solution.py:54
  13.7 12.8 %collective-permute-start.6 = (bf16[128,1024]{1,0:T(8,128)(2,1)S(1)}, bf16[128,1024]{1,0:T(8,128)(2,1)S(1)}, u32[]{:S(2)}, u32[]{:S(2)}) collective-permute-start(bf16[128,1024]{1,0:T(8,128)(2,1)S(1)} %get-tuple-element.42), channel_id=1, source_target_pairs={{0,16},{1,5},{2,18},{3,7},{4,20},{5,9},{6,22},{7,11},{8,24},{9,13}... | collective-permute-start | bytes 786440 | tf_op jit(solution)/shard_map/ppermute | solution.py:45
  15.2 11.2 %collective-permute-start.7 = (bf16[128,1024]{1,0:T(8,128)(2,1)S(1)}, bf16[128,1024]{1,0:T(8,128)(2,1)S(1)}, u32[]{:S(2)}, u32[]{:S(2)}) collective-permute-start(bf16[128,1024]{1,0:T(8,128)(2,1)S(1)} %get-tuple-element.43), channel_id=1, source_target_pairs={{0,48},{1,13},{2,50},{3,15},{4,52},{5,1},{6,54},{7,3},{8,56},{9,5}... | collective-permute-start | bytes 786440 | tf_op jit(solution)/shard_map/ppermute | solution.py:45
  24.9 1.4 %collective-permute-start.4 = (bf16[128,512]{1,0:T(8,128)(2,1)S(1)}, bf16[128,512]{1,0:T(8,128)(2,1)S(1)}, u32[]{:S(2)}, u32[]{:S(2)}) collective-permute-start(bf16[128,512]{1,0:T(8,128)(2,1)S(1)} %get-tuple-element.40), channel_id=1, source_target_pairs={{0,1},{1,0},{2,3},{3,2},{4,5},{5,4},{6,7},{7,6},{8,9},{9,8},{10,11... | collective-permute-start | bytes 393224 | tf_op jit(solution)/shard_map/ppermute | solution.py:32
  25.0 1.5 %collective-permute-start.5 = (bf16[128,512]{1,0:T(8,128)(2,1)S(1)}, bf16[128,512]{1,0:T(8,128)(2,1)S(1)}, u32[]{:S(2)}, u32[]{:S(2)}) collective-permute-start(bf16[128,512]{1,0:T(8,128)(2,1)S(1)} %get-tuple-element.41), channel_id=1, source_target_pairs={{0,1},{1,0},{2,3},{3,2},{4,5},{5,4},{6,7},{7,6},{8,9},{9,8},{10,11... | collective-permute-start | bytes 393224 | tf_op jit(solution)/shard_map/ppermute | solution.py:32
  26.5 9.9 %collective-permute-start.8 = (bf16[272,1024]{1,0:T(8,128)(2,1)S(1)}, bf16[272,1024]{1,0:T(8,128)(2,1)S(1)}, u32[]{:S(2)}, u32[]{:S(2)}) collective-permute-start(bf16[272,1024]{1,0:T(8,128)(2,1)S(1)} %join.1.refs_8_), channel_id=1, source_target_pairs={{0,16},{1,5},{2,18},{3,7},{4,20},{5,9},{6,22},{7,11},{8,24},{9,13}... | collective-permute-start | bytes 1671176 | tf_op jit(solution)/shard_map/ppermute | solution.py:45
  28.1 9.5 %collective-permute-start.9 = (bf16[272,1024]{1,0:T(8,128)(2,1)S(1)}, bf16[272,1024]{1,0:T(8,128)(2,1)S(1)}, u32[]{:S(2)}, u32[]{:S(2)}) collective-permute-start(bf16[272,1024]{1,0:T(8,128)(2,1)S(1)} %join.1.refs_8_), channel_id=1, source_target_pairs={{0,48},{1,13},{2,50},{3,15},{4,52},{5,1},{6,54},{7,3},{8,56},{9,5}... | collective-permute-start | bytes 1671176 | tf_op jit(solution)/shard_map/ppermute | solution.py:45
  33.9 2.6 %collective-permute-start.3 = (bf16[64,4096]{1,0:T(8,128)(2,1)S(1)}, bf16[64,4096]{1,0:T(8,128)(2,1)S(1)}, u32[]{:S(2)}, u32[]{:S(2)}) collective-permute-start(bf16[64,4096]{1,0:T(8,128)(2,1)S(1)} %collective-permute-done.refs_0_), channel_id=1, source_target_pairs={{0,1},{1,0},{2,3},{3,2},{4,5},{5,4},{6,7},{7,6},{8,9},{9,8},{10,11... | collective-permute-start | bytes 1572872 | tf_op jit(solution)/shard_map/ppermute | solution.py:32
  37.8 17.7 %collective-permute-start.13 = (bf16[256,1024]{1,0:T(8,128)(2,1)S(1)}, bf16[256,1024]{1,0:T(8,128)(2,1)S(1)}, u32[]{:S(2)}, u32[]{:S(2)}) collective-permute-start(bf16[256,1024]{1,0:T(8,128)(2,1)S(1)} %get-tuple-element.48), channel_id=1, source_target_pairs={{0,32},{1,9},{2,34},{3,11},{4,36},{5,13},{6,38},{7,15},{8,40},{9,1... | collective-permute-start | bytes 1572872 | tf_op jit(solution)/shard_map/ppermute | solution.py:45
  39.9 15.7 %collective-permute-start.14 = (bf16[256,1024]{1,0:T(8,128)(2,1)S(1)}, bf16[256,1024]{1,0:T(8,128)(2,1)S(1)}, u32[]{:S(2)}, u32[]{:S(2)}) collective-permute-start(bf16[256,1024]{1,0:T(8,128)(2,1)S(1)} %get-tuple-element.49), channel_id=1, source_target_pairs={{0,16},{1,5},{2,18},{3,7},{4,20},{5,9},{6,22},{7,11},{8,24},{9,13}... | collective-permute-start | bytes 1572872 | tf_op jit(solution)/shard_map/ppermute | solution.py:45
  39.9 15.6 %collective-permute-start.15 = (bf16[256,1024]{1,0:T(8,128)(2,1)S(1)}, bf16[256,1024]{1,0:T(8,128)(2,1)S(1)}, u32[]{:S(2)}, u32[]{:S(2)}) collective-permute-start(bf16[256,1024]{1,0:T(8,128)(2,1)S(1)} %get-tuple-element.50), channel_id=1, source_target_pairs={{0,48},{1,13},{2,50},{3,15},{4,52},{5,1},{6,54},{7,3},{8,56},{9,5}... | collective-permute-start | bytes 1572872 | tf_op jit(solution)/shard_map/ppermute | solution.py:45
  51.4 10.4 %collective-permute-start.10 = (f32[64,128]{1,0:T(8,128)S(1)}, f32[64,128]{1,0:T(8,128)S(1)}, u32[]{:S(2)}, u32[]{:S(2)}) collective-permute-start(f32[64,128]{1,0:T(8,128)S(1)} %filter_grad.1.refs_13_), channel_id=1, source_target_pairs={{0,32},{1,9},{2,34},{3,11},{4,36},{5,13},{6,38},{7,15},{8,40},{9,1... | collective-permute-start | bytes 98312 | tf_op jit(solution)/shard_map/ppermute | solution.py:45
  53.1 10.0 %collective-permute-start.11 = (f32[64,128]{1,0:T(8,128)S(1)}, f32[64,128]{1,0:T(8,128)S(1)}, u32[]{:S(2)}, u32[]{:S(2)}) collective-permute-start(f32[64,128]{1,0:T(8,128)S(1)} %filter_grad.1.refs_13_), channel_id=1, source_target_pairs={{0,16},{1,5},{2,18},{3,7},{4,20},{5,9},{6,22},{7,11},{8,24},{9,13}... | collective-permute-start | bytes 98312 | tf_op jit(solution)/shard_map/ppermute | solution.py:45
  55.5 7.6 %collective-permute-start.12 = (f32[64,128]{1,0:T(8,128)S(1)}, f32[64,128]{1,0:T(8,128)S(1)}, u32[]{:S(2)}, u32[]{:S(2)}) collective-permute-start(f32[64,128]{1,0:T(8,128)S(1)} %filter_grad.1.refs_13_), channel_id=1, source_target_pairs={{0,48},{1,13},{2,50},{3,15},{4,52},{5,1},{6,54},{7,3},{8,56},{9,5}... | collective-permute-start | bytes 98312 | tf_op jit(solution)/shard_map/ppermute | solution.py:45
  58.7 28.4 %collective-permute-start.20 = (bf16[256,1024]{1,0:T(8,128)(2,1)S(1)}, bf16[256,1024]{1,0:T(8,128)(2,1)S(1)}, u32[]{:S(2)}, u32[]{:S(2)}) collective-permute-start(bf16[256,1024]{1,0:T(8,128)(2,1)S(1)} %get-tuple-element.54), channel_id=1, source_target_pairs={{0,4},{1,17},{2,6},{3,19},{4,8},{5,21},{6,10},{7,23},{8,12},{9,25}... | collective-permute-start | bytes 1572872 | tf_op jit(solution)/shard_map/ppermute | solution.py:45
  58.9 28.1 %collective-permute-start.21 = (bf16[256,1024]{1,0:T(8,128)(2,1)S(1)}, bf16[256,1024]{1,0:T(8,128)(2,1)S(1)}, u32[]{:S(2)}, u32[]{:S(2)}) collective-permute-start(bf16[256,1024]{1,0:T(8,128)(2,1)S(1)} %get-tuple-element.55), channel_id=1, source_target_pairs={{0,8},{1,33},{2,10},{3,35},{4,12},{5,37},{6,14},{7,39},{8,0},{9,41... | collective-permute-start | bytes 1572872 | tf_op jit(solution)/shard_map/ppermute | solution.py:45
  61.8 25.2 %collective-permute-start.22 = (bf16[256,1024]{1,0:T(8,128)(2,1)S(1)}, bf16[256,1024]{1,0:T(8,128)(2,1)S(1)}, u32[]{:S(2)}, u32[]{:S(2)}) collective-permute-start(bf16[256,1024]{1,0:T(8,128)(2,1)S(1)} %get-tuple-element.56), channel_id=1, source_target_pairs={{0,12},{1,49},{2,14},{3,51},{4,0},{5,53},{6,2},{7,55},{8,4},{9,57}... | collective-permute-start | bytes 1572872 | tf_op jit(solution)/shard_map/ppermute | solution.py:45
  63.2 11.9 %collective-permute-start.16 = (f32[64,128]{1,0:T(8,128)S(1)}, f32[64,128]{1,0:T(8,128)S(1)}, u32[]{:S(2)}, u32[]{:S(2)}) collective-permute-start(f32[64,128]{1,0:T(8,128)S(1)} %add_add_fusion.1), channel_id=1, source_target_pairs={{0,8},{1,33},{2,10},{3,35},{4,12},{5,37},{6,14},{7,39},{8,0},{9,41... | collective-permute-start | bytes 98312 | tf_op jit(solution)/shard_map/ppermute | solution.py:45
  65.0 13.7 %collective-permute-start.17 = (f32[64,128]{1,0:T(8,128)S(1)}, f32[64,128]{1,0:T(8,128)S(1)}, u32[]{:S(2)}, u32[]{:S(2)}) collective-permute-start(f32[64,128]{1,0:T(8,128)S(1)} %add_add_fusion.1), channel_id=1, source_target_pairs={{0,4},{1,17},{2,6},{3,19},{4,8},{5,21},{6,10},{7,23},{8,12},{9,25}... | collective-permute-start | bytes 98312 | tf_op jit(solution)/shard_map/ppermute | solution.py:45
  75.0 5.2 %collective-permute-start.18 = (f32[64,128]{1,0:T(8,128)S(1)}, f32[64,128]{1,0:T(8,128)S(1)}, u32[]{:S(2)}, u32[]{:S(2)}) collective-permute-start(f32[64,128]{1,0:T(8,128)S(1)} %add_add_fusion.1), channel_id=1, source_target_pairs={{0,12},{1,49},{2,14},{3,51},{4,0},{5,53},{6,2},{7,55},{8,4},{9,57}... | collective-permute-start | bytes 98312 | tf_op jit(solution)/shard_map/ppermute | solution.py:45
  80.3 11.7 %collective-permute-start.19 = (bf16[128,1024]{1,0:T(8,128)(2,1)S(1)}, bf16[128,1024]{1,0:T(8,128)(2,1)S(1)}, u32[]{:S(2)}, u32[]{:S(2)}) collective-permute-start(bf16[128,1024]{1,0:T(8,128)(2,1)S(1)} %slice.11), channel_id=1, source_target_pairs={{4,0},{8,4},{12,8},{16,12},{20,16},{24,20},{28,24},{32,28},{36,32}... | collective-permute-start | bytes 786440 | tf_op jit(solution)/shard_map/ppermute | solution.py:54
  87.5 7.9 %collective-permute-start.23 = (bf16[80,1024]{1,0:T(8,128)(2,1)S(1)}, bf16[80,1024]{1,0:T(8,128)(2,1)S(1)}, u32[]{:S(2)}, u32[]{:S(2)}) collective-permute-start(bf16[80,1024]{1,0:T(8,128)(2,1)S(1)} %get-tuple-element.59), channel_id=1, source_target_pairs={{0,64},{64,128},{128,192},{192,0},{1,65},{65,129},{129,193},{193,1... | collective-permute-start | bytes 491528 | tf_op jit(solution)/shard_map/ppermute | solution.py:575
  88.6 9.6 %collective-permute-start.24 = (bf16[80,1024]{1,0:T(8,128)(2,1)S(1)}, bf16[80,1024]{1,0:T(8,128)(2,1)S(1)}, u32[]{:S(2)}, u32[]{:S(2)}) collective-permute-start(bf16[80,1024]{1,0:T(8,128)(2,1)S(1)} %get-tuple-element.60), channel_id=1, source_target_pairs={{0,128},{64,192},{128,0},{192,64},{1,129},{65,193},{129,1},{193,65... | collective-permute-start | bytes 491528 | tf_op jit(solution)/shard_map/ppermute | solution.py:575
  90.0 8.1 %collective-permute-start.25 = (bf16[80,1024]{1,0:T(8,128)(2,1)S(1)}, bf16[80,1024]{1,0:T(8,128)(2,1)S(1)}, u32[]{:S(2)}, u32[]{:S(2)}) collective-permute-start(bf16[80,1024]{1,0:T(8,128)(2,1)S(1)} %get-tuple-element.61), channel_id=1, source_target_pairs={{0,192},{64,0},{128,64},{192,128},{1,193},{65,1},{129,65},{193,129... | collective-permute-start | bytes 491528 | tf_op jit(solution)/shard_map/ppermute | solution.py:575
  98.9 1.3 %collective-permute-start.26 = (f32[64,512]{1,0:T(8,128)S(1)}, f32[64,512]{1,0:T(8,128)S(1)}, u32[]{:S(2)}, u32[]{:S(2)}) collective-permute-start(f32[64,512]{1,0:T(8,128)S(1)} %get-tuple-element.64), channel_id=1, source_target_pairs={{0,1},{1,0},{2,3},{3,2},{4,5},{5,4},{6,7},{7,6},{8,9},{9,8},{10,11... | collective-permute-start | bytes 393224 | tf_op jit(solution)/shard_map/ppermute | solution.py:32

commit v9 on v7

--- a/solution.py
+++ b/solution.py
@@ -157,7 +157,7 @@
         out[...] = gated[i * TAPS : (i + 1) * TAPS, aligned(1 - core, kept.shape[1])]
 
 
-def forward(filters, previous, signal, gating, after):
+def forward(filters, previous, signal, gating):
     length, channels = signal.shape
     quarter = ((TAPS, channels // 2), BF16)
     return once(
@@ -169,7 +169,6 @@
             pltpu.VMEM((length, channels), BF16),
             pltpu.VMEM((2, PER_TILE * TAPS, 2 * TAPS), BF16),
         ],
-        after,
     )
 
 
@@ -292,15 +291,16 @@
     )
 
 
-def relay_kernel(mine, other, before, after, *outs):
+def relay_kernel(mine, other, before, after, opposite, *outs):
     pack_into(mine, other, outs)
-    part = outs[0].shape[0]
+    part = opposite.shape[0]
     outs[1][part:] = before[...]
+    outs[2][part:] = opposite[...]
     outs[3][part:] = after[...]
 
 
-def relay(mine, other, got_next, got_last):
-    rows, width = 2 * mine.shape[0], got_next.shape[1]
+def relay(mine, other, got_next, got_last, opposite):
+    rows, width = opposite.shape
     return once(
         relay_kernel,
         "relay",
@@ -309,60 +309,51 @@
             other,
             (got_next, whole((TAPS, width))),
             (got_last, whole((TAPS, width), (1, 0))),
+            opposite,
         ],
-        [((rows + s % 2 * TAPS, width), BF16) for s in range(SIDE)],
-    )
-
-
-def project_kernel(mine, other, weight, gating, response, *refs):
+        [((rows, width), BF16)] + [((rows + TAPS, width), BF16)] * (SIDE - 1),
+    )
+
+
+def project_kernel(early, early_other, late, late_other, weight, gating, response, conv_grad, grad_gate, rows):
     _, _, _, half, core = spot()
-    part = mine.shape[0]
-    rows = refs[-1]
-    conv_grad, grad_gate = refs[-3:-1]
+    part = early.shape[0]
 
     @pl.when(pl.program_id(0) == 0)
     def _():
-        rows[aligned(core, part), :] = mine[...]
-        rows[aligned(1 - core, part), :] = other[...]
-
-    late = len(refs) > 3
-    tokens = aligned(1 - half if late else half, TAPS)
+        for ref, h, c in (
+            (early, half, core),
+            (early_other, half, 1 - core),
+            (late, 1 - half, core),
+            (late_other, 1 - half, 1 - core),
+        ):
+            rows[aligned(2 * h + c, part), :] = ref[...]
+
     made = jnp.dot(rows[...], weight[...], preferred_element_type=F32)
-    made_conv = (made * gating[tokens, :].astype(F32)).astype(BF16)
-    made_gate = (made * response[tokens, :]).astype(BF16)
-    if late:
-        conv_grad[tokens, :] = made_conv
-        grad_gate[tokens, :] = made_gate
-        conv_grad[aligned(half, TAPS), :] = refs[0][...]
-        grad_gate[aligned(half, TAPS), :] = refs[1][...]
-    else:
-        conv_grad[...] = made_conv
-        grad_gate[...] = made_gate
-
-
-def project(mine, other, weight, gating, response, done=(), after=()):
+    conv_grad[...] = (made * gating[...].astype(F32)).astype(BF16)
+    grad_gate[...] = (made * response[...]).astype(BF16)
+
+
+def project(early, early_other, late, late_other, weight, gating, response, after):
     length, channels = gating.shape
     depth = weight.shape[0]
-    made = length if done else 2 * mine.shape[0]
 
     def body(*refs):
-        kept = 5 + len(done)
-        project_kernel(*refs[:kept], *refs[kept + len(after) :])
+        project_kernel(*refs[:7], *refs[7 + len(after) :])
 
     return pl.pallas_call(
         body,
         grid=(channels // WIDE,),
-        in_specs=[full(mine.shape)] * 2
+        in_specs=[full(early.shape)] * 4
         + [tile(depth, WIDE), tile(length, WIDE), tile(length, WIDE)]
-        + [tile(TAPS, WIDE)] * len(done)
         + [ANYWHERE] * len(after),
-        out_specs=[tile(made, WIDE)] * 2,
-        out_shape=[jax.ShapeDtypeStruct((made, channels), BF16)] * 2,
-        scratch_shapes=[pltpu.VMEM((2 * mine.shape[0], depth), BF16)],
-        compiler_params=room(16),
-        cost_estimate=lasting(5 if done else 0),
-        name="project_late" if done else "project_early",
-    )(mine, other, weight, gating, response, *done, *after)
+        out_specs=[tile(length, WIDE)] * 2,
+        out_shape=[jax.ShapeDtypeStruct((length, channels), BF16)] * 2,
+        scratch_shapes=[pltpu.VMEM((length, depth), BF16)],
+        compiler_params=room(20),
+        cost_estimate=lasting(6),
+        name="project",
+    )(early, early_other, late, late_other, weight, gating, response, *after)
 
 
 def weight_kernel(*refs):
@@ -411,7 +402,10 @@
         weight_kernel,
         "weight_parts",
         [
-            *early,
+            early[0],
+            early[1],
+            block(late[1], rows),
+            early[2],
             own_late,
             *[block(part, 0) for part in late],
             block(gated, 0, length),
@@ -427,10 +421,6 @@
     )
 
 
-def four_sum(parts):
-    return (parts[0] + parts[2]) + (parts[1] + parts[3])
-
-
 def first_sum_kernel(*refs):
     _, _, z, _, _ = spot()
     outs, kept = refs[SIDE:-1], refs[-1]
@@ -495,6 +485,10 @@
     return x + in_plane(tied(x, *before), gather, lambda place: place ^ by)
 
 
+def paired_z(x, by):
+    return x + lax.ppermute(x, "dp", [(i, i ^ by) for i in range(SIDE)])
+
+
 def local(conv_input, gate_value, out_grad, out_weight, filters):
     signal, gating, grads = conv_input[0], gate_value[0], out_grad[0]
     length, channels = signal.shape
@@ -510,29 +504,28 @@
     early_other = moved(grads, "core")
     grads = resident(grads)
     early = pack(grads, early_other)
-    early_got = [stepped(early[s], True, s) for s in shifts]
-    response, kept, *given = forward(filters, previous, signal, gating, early_got)
-    gated = join(kept, [moved(part, "core") for part in given], ())
+    early_got = [stepped(early[1], True, 1), stepped(early[3], True, 3)]
+    response, kept, *given = forward(filters, previous, signal, gating)
+    gated = join(kept, [moved(part, "core") for part in given], early_got)
     got = [stepped(gated, True, 1), stepped(gated, True, 3)]
-    conv_early, gate_early = project(grads, early_other, weight, gating, response)
-
-    late_other = moved(tied(late, conv_early), "core")
-    own_late, *late_sent = relay(late, late_other, *got)
+    late_other = moved(tied(late, gated), "core")
+    own_late, *late_sent = relay(late, late_other, *got, early[2])
     conv_grad, grad_gate = project(
-        late, late_other, weight, gating, response, (conv_early, gate_early), (own_late,)
+        grads, early_other, late, late_other, weight, gating, response, (own_late,)
     )
     late_got = [stepped(late_sent[s - 1], True, s) for s in shifts]
-    following = shifted(conv_grad[:TAPS], -1)
-    parts = weight_parts([early[0], *early_got], own_late, gated, got, late_got, (conv_grad,))
-    filter_sum = filter_grad(previous, signal, conv_grad, (parts[0],))
-    filter_sum = four_sum([filter_sum] + [stepped(filter_sum, True, s) for s in shifts])
+    filter_sum = filter_grad(previous, signal, conv_grad, ())
+    parts = weight_parts([early[0], *early_got], own_late, gated, got, late_got, (filter_sum,))
+
+    filter_sum = paired_z(paired_z(tied(filter_sum, parts[0]), 1), 2)
+    following = shifted(tied(conv_grad[:TAPS], filter_sum), -1)
+    filter_sum = paired(paired(filter_sum, True, 1), True, 2)
     parts = [parts[0]] + [stepped(parts[s], False, s) for s in shifts]
-    sums = first_sum(parts, (following,))
+    sums = first_sum(parts, (filter_sum,))
+    filter_sum = paired(paired(filter_sum, False, 1, (sums[0],)), False, 2)
+    grad_filter = filter_sum * (1.0 / math.sqrt(tokens_all * GROUP))
     grad_input = input_grad(filters, conv_grad, following, (sums[0],))
     line = [[(i, (i + s) % SIDE) for i in range(SIDE)] for s in shifts]
-    filter_sum = paired(paired(filter_sum, False, 1, (sums[0],)), False, 2)
-    filter_sum = four_sum([filter_sum] + [lax.ppermute(filter_sum, "dp", pairs) for pairs in line])
-    grad_filter = filter_sum * (1.0 / math.sqrt(tokens_all * GROUP))
     sums = [sums[0]] + [lax.ppermute(sums[s], "dp", line[s - 1]) for s in shifts]
     kept, given = last_sum(sums, 1.0 / math.sqrt(tokens_all), (resident(grad_input),))
     grad_weight = beside(kept, moved(given, "core"))

time: 117 us -> 98.3 us (0.84)
  the two profiles are of different devices: /device:TPU:1 before, /device:TPU:2 now
where the time goes in v9:
time: 98.3 us; the launch traced here: 96.6 us
  starting transfers between devices  38.1 us (39%)
  waiting for transfers between devices  33 us (34%)
  Pallas kernels  22.9 us (23%)
    ppermute x14, starting transfers between devices, in_plane(): return lax.ppermute(x, ('ctx', 'tp'), pairs)  16.4 us
    pallas_call x10, Pallas kernels, once(): pl.pallas_call(body, grid=(1,), in_specs=specs + [ANYWHERE] * len(after),...  16.3 us
    ppermute x14, waiting for transfers between devices, in_plane(): return lax.ppermute(x, ('ctx', 'tp'), pairs)  16.1 us
    ppermute x6, starting transfers between devices, moved(): return lax.ppermute(x, 'tp', [(i, i ^ step) for i in range(4)])  8.06 us
    ppermute x2, starting transfers between devices, shifted(): lax.ppermute(x, 'ctx', [(i, i + by) for i in range(devices) if 0 <= i + b...  6.69 us
    pallas_call x1, Pallas kernels, project(): pl.pallas_call(body, grid=(channels // WIDE,), in_specs=[full(early.shape...  6.59 us
    ppermute x2, waiting for transfers between devices, paired_z(): return x + lax.ppermute(x, 'dp', [(i, i ^ by) for i in range(SIDE)])  6.24 us
    ppermute x2, waiting for transfers between devices, shifted(): lax.ppermute(x, 'ctx', [(i, i + by) for i in range(devices) if 0 <= i + b...  5.67 us
  transfers between devices with their start and end apart: 27, of which 14 were waited for; matrix products, arithmetic and copies ran while one was open for 2% of the time, Pallas kernels for 20%

profile of v9, /device:TPU:2, one launch (start us, length us, event | category | flops | bytes accessed | tf_op | source)
XLA Modules:
  0.0 96.6 jit_solution(5804721104412953485)
XLA Ops:
  0.7 7.3 %collective-permute-start.1 = (bf16[64,4096]{1,0:T(8,128)(2,1)}, bf16[64,4096]{1,0:T(8,128)(2,1)S(1)}, u32[]{:S(2)}, u32[]{:S(2)}) collective-permute-start(bf16[64,4096]{1,0:T(8,128)(2,1)} %bitcast.11), channel_id=1, source_target_pairs={{0,2},{1,3},{2,0},{3,1},{4,6},{5,7},{6,4},{7,5},{8,10},{9,11},{10,... | collective-permute-start | bytes 1572872 | tf_op jit(solution)/shard_map/ppermute | solution.py:32
  9.0 3.5 %collective-permute-start.2 = (bf16[128,1024]{1,0:T(8,128)(2,1)S(1)}, bf16[128,1024]{1,0:T(8,128)(2,1)S(1)}, u32[]{:S(2)}, u32[]{:S(2)}) collective-permute-start(bf16[128,1024]{1,0:T(8,128)(2,1)S(1)} %slice_bitcast_fusion), channel_id=1, source_target_pairs={{0,4},{4,8},{8,12},{12,16},{16,20},{20,24},{24,28},{28,32},{32,36}... | collective-permute-start | bytes 786440 | tf_op jit(solution)/shard_map/ppermute | solution.py:54
  12.5 1.2 %pack.1 = (bf16[128,1024]{1,0:T(8,128)(2,1)S(1)}, bf16[128,1024]{1,0:T(8,128)(2,1)S(1)}, bf16[128,1024]{1,0:T(8,128)(2,1)S(1)}, bf16[128,1024]{1,0:T(8,128)(2,1)S(1)}) custom-call(bf16[64,4096]{1,0:T(8,128)(2,1)} %bitcast.12, bf16[64,4096]{1,0:T(8,128)(2,1)S(1)} %collective-permute-done.refs_1_), custom_call_target="tpu_custom_call" | custom-call | tf_op jit(solution)/shard_map/pack/pallas_call | solution.py:96
  13.7 1.6 %collective-permute-start.5 = (bf16[128,1024]{1,0:T(8,128)(2,1)S(1)}, bf16[128,1024]{1,0:T(8,128)(2,1)S(1)}, u32[]{:S(2)}, u32[]{:S(2)}) collective-permute-start(bf16[128,1024]{1,0:T(8,128)(2,1)S(1)} %get-tuple-element.35), channel_id=1, source_target_pairs={{0,16},{1,5},{2,18},{3,7},{4,20},{5,9},{6,22},{7,11},{8,24},{9,13}... | collective-permute-start | bytes 786440 | tf_op jit(solution)/shard_map/ppermute | solution.py:45
  15.8 5.7 %collective-permute-done.2.refs_1_.refs_0_ = bf16[128,1024]{1,0:T(8,128)(2,1)S(1)} collective-permute-done((bf16[128,1024]{1,0:T(8,128)(2,1)S(1)}, bf16[128,1024]{1,0:T(8,128)(2,1)S(1)}, u32[]{:S(2)}, u32[]{:S(2)}) %collective-permute-start.2) | collective-permute-done | bytes 262176 | tf_op jit(solution)/shard_map/ppermute | solution.py:54
  21.4 3.4 %conv_forward.1 = (f32[256,1024]{1,0:T(8,128)S(1)}, bf16[256,512]{1,0:T(8,128)(2,1)S(1)}, bf16[128,512]{1,0:T(8,128)(2,1)S(1)}, bf16[128,512]{1,0:T(8,128)(2,1)S(1)}) custom-call(bf16[64,128]{1,0:T(8,128)(2,1)} %refs_0_.3, bf16[128,1024]{1,0:T(8,128)(2,1)S(1)} %collective-permute-done.2.refs_1_.refs_0_, bf16[256,1024]{1,0:T(8,128)(2,1)} %bitcast.8, ...), custom_call_target="tpu_custom_call" | custom-call | tf_op jit(solution)/shard_map/conv_forward/pallas_call | solution.py:96
  26.5 1.6 %collective-permute-start.8 = (bf16[272,1024]{1,0:T(8,128)(2,1)S(1)}, bf16[272,1024]{1,0:T(8,128)(2,1)S(1)}, u32[]{:S(2)}, u32[]{:S(2)}) collective-permute-start(bf16[272,1024]{1,0:T(8,128)(2,1)S(1)} %join.1.refs_8_), channel_id=1, source_target_pairs={{0,16},{1,5},{2,18},{3,7},{4,20},{5,9},{6,22},{7,11},{8,24},{9,13}... | collective-permute-start | bytes 1671176 | tf_op jit(solution)/shard_map/ppermute | solution.py:45
  28.6 2.1 %collective-permute-done.1.refs_0_.refs_2_ = bf16[64,4096]{1,0:T(8,128)(2,1)S(1)} collective-permute-done((bf16[64,4096]{1,0:T(8,128)(2,1)}, bf16[64,4096]{1,0:T(8,128)(2,1)S(1)}, u32[]{:S(2)}, u32[]{:S(2)}) %collective-permute-start.1) | collective-permute-done | bytes 524320 | tf_op jit(solution)/shard_map/ppermute | solution.py:32
  30.7 1.9 %collective-permute-done.7.refs_1_.refs_3_ = bf16[64,4096]{1,0:T(8,128)(2,1)S(1)} collective-permute-done((bf16[64,4096]{1,0:T(8,128)(2,1)S(1)}, bf16[64,4096]{1,0:T(8,128)(2,1)S(1)}, u32[]{:S(2)}, u32[]{:S(2)}) %collective-permute-start.7) | collective-permute-done | bytes 524320 | tf_op jit(solution)/shard_map/ppermute | solution.py:32
  32.7 3.5 %collective-permute-done.8.refs_2_.refs_9_ = bf16[272,1024]{1,0:T(8,128)(2,1)S(1)} collective-permute-done((bf16[272,1024]{1,0:T(8,128)(2,1)S(1)}, bf16[272,1024]{1,0:T(8,128)(2,1)S(1)}, u32[]{:S(2)}, u32[]{:S(2)}) %collective-permute-start.8) | collective-permute-done | bytes 557088 | tf_op jit(solution)/shard_map/ppermute | solution.py:45
  36.2 1.5 %collective-permute-done.9.refs_3_.refs_12_ = bf16[272,1024]{1,0:T(8,128)(2,1)S(1)} collective-permute-done((bf16[272,1024]{1,0:T(8,128)(2,1)S(1)}, bf16[272,1024]{1,0:T(8,128)(2,1)S(1)}, u32[]{:S(2)}, u32[]{:S(2)}) %collective-permute-start.9) | collective-permute-done | bytes 557088 | tf_op jit(solution)/shard_map/ppermute | solution.py:45
  37.8 2.0 %collective-permute-start.10 = (bf16[256,1024]{1,0:T(8,128)(2,1)S(1)}, bf16[256,1024]{1,0:T(8,128)(2,1)S(1)}, u32[]{:S(2)}, u32[]{:S(2)}) collective-permute-start(bf16[256,1024]{1,0:T(8,128)(2,1)S(1)} %get-tuple-element.43), channel_id=1, source_target_pairs={{0,32},{1,9},{2,34},{3,11},{4,36},{5,13},{6,38},{7,15},{8,40},{9,1... | collective-permute-start | bytes 1572872 | tf_op jit(solution)/shard_map/ppermute | solution.py:45
  39.9 2.0 %collective-permute-start.12 = (bf16[256,1024]{1,0:T(8,128)(2,1)S(1)}, bf16[256,1024]{1,0:T(8,128)(2,1)S(1)}, u32[]{:S(2)}, u32[]{:S(2)}) collective-permute-start(bf16[256,1024]{1,0:T(8,128)(2,1)S(1)} %get-tuple-element.45), channel_id=1, source_target_pairs={{0,48},{1,13},{2,50},{3,15},{4,52},{5,1},{6,54},{7,3},{8,56},{9,5}... | collective-permute-start | bytes 1572872 | tf_op jit(solution)/shard_map/ppermute | solution.py:45
  41.9 6.6 %project.1 = (bf16[256,1024]{1,0:T(8,128)(2,1)S(1)}, bf16[256,1024]{1,0:T(8,128)(2,1)}) custom-call(bf16[64,4096]{1,0:T(8,128)(2,1)} %bitcast.13, bf16[64,4096]{1,0:T(8,128)(2,1)S(1)} %collective-permute-done.refs_1_, bf16[64,4096]{1,0:T(8,128)(2,1)S(1)} %collective-permute-done.1.refs_0_.refs_2_, ...), custom_call_target="tpu_custom_call" | custom-call | flops 6000000000 | tf_op jit(solution)/shard_map/project/pallas_call | solution.py:344
  48.5 3.8 %filter_grad.1.refs_13_ = f32[64,128]{1,0:T(8,128)S(1)} custom-call(bf16[128,1024]{1,0:T(8,128)(2,1)S(1)} %collective-permute-done.2.refs_1_.refs_0_, bf16[256,1024]{1,0:T(8,128)(2,1)} %bitcast.9, bf16[256,1024]{1,0:T(8,128)(2,1)S(1)} %get-tuple-element.41.refs_2_.refs_1_), custom_call_target="tpu_custom_call" | custom-call | flops 4000000000 | tf_op jit(solution)/shard_map/filter_grad/pallas_call | solution.py:96
  52.3 1.7 %collective-permute-done.11.refs_5_.refs_10_ = bf16[256,1024]{1,0:T(8,128)(2,1)S(1)} collective-permute-done((bf16[256,1024]{1,0:T(8,128)(2,1)S(1)}, bf16[256,1024]{1,0:T(8,128)(2,1)S(1)}, u32[]{:S(2)}, u32[]{:S(2)}) %collective-permute-start.11) | collective-permute-done | bytes 524320 | tf_op jit(solution)/shard_map/ppermute | solution.py:45
  54.2 3.1 %weight_parts.1 = (f32[256,1024]{1,0:T(8,128)S(1)}, bf16[256,1024]{1,0:T(8,128)(2,1)S(1)}, bf16[256,1024]{1,0:T(8,128)(2,1)S(1)}, bf16[256,1024]{1,0:T(8,128)(2,1)S(1)}) custom-call(bf16[128,1024]{1,0:T(8,128)(2,1)S(1)} %get-tuple-element.42.refs_0_, bf16[128,1024]{1,0:T(8,128)(2,1)S(1)} %collective-permute-done.5.refs_3_.refs_1_, ...), custom_call_target="tpu_custom_call" | custom-call | flops 4000000000 | tf_op jit(solution)/shard_map/weight_parts/pallas_call | solution.py:96
  57.5 2.9 %collective-permute-start.17 = (bf16[256,1024]{1,0:T(8,128)(2,1)S(1)}, bf16[256,1024]{1,0:T(8,128)(2,1)S(1)}, u32[]{:S(2)}, u32[]{:S(2)}) collective-permute-start(bf16[256,1024]{1,0:T(8,128)(2,1)S(1)} %get-tuple-element.50), channel_id=1, source_target_pairs={{0,8},{1,33},{2,10},{3,35},{4,12},{5,37},{6,14},{7,39},{8,0},{9,41... | collective-permute-start | bytes 1572872 | tf_op jit(solution)/shard_map/ppermute | solution.py:45
  60.4 1.3 %collective-permute-start.18 = (bf16[256,1024]{1,0:T(8,128)(2,1)S(1)}, bf16[256,1024]{1,0:T(8,128)(2,1)S(1)}, u32[]{:S(2)}, u32[]{:S(2)}) collective-permute-start(bf16[256,1024]{1,0:T(8,128)(2,1)S(1)} %get-tuple-element.51), channel_id=1, source_target_pairs={{0,12},{1,49},{2,14},{3,51},{4,0},{5,53},{6,2},{7,55},{8,4},{9,57}... | collective-permute-start | bytes 1572872 | tf_op jit(solution)/shard_map/ppermute | solution.py:45
  61.8 1.0 %collective-permute-start.13 = (f32[64,128]{1,0:T(8,128)S(1)}, f32[64,128]{1,0:T(8,128)S(1)}, u32[]{:S(2)}, u32[]{:S(2)}) collective-permute-start(f32[64,128]{1,0:T(8,128)S(1)} %filter_grad.1.refs_13_), channel_id=1, source_target_pairs={{0,64},{64,0},{128,192},{192,128},{1,65},{65,1},{129,193},{193,129... | collective-permute-start | bytes 98312 | tf_op jit(solution)/shard_map/ppermute | solution.py:489
  62.8 2.9 %collective-permute-done.13 = f32[64,128]{1,0:T(8,128)S(1)} collective-permute-done((f32[64,128]{1,0:T(8,128)S(1)}, f32[64,128]{1,0:T(8,128)S(1)}, u32[]{:S(2)}, u32[]{:S(2)}) %collective-permute-start.13) | collective-permute-done | bytes 32800 | tf_op jit(solution)/shard_map/ppermute | solution.py:489
  65.7 1.5 %collective-permute-start.14 = (f32[64,128]{1,0:T(8,128)S(1)}, f32[64,128]{1,0:T(8,128)S(1)}, u32[]{:S(2)}, u32[]{:S(2)}) collective-permute-start(f32[64,128]{1,0:T(8,128)S(1)} %add.18), channel_id=1, source_target_pairs={{0,128},{64,192},{128,0},{192,64},{1,129},{65,193},{129,1},{193,65... | collective-permute-start | bytes 98312 | tf_op jit(solution)/shard_map/ppermute | solution.py:489
  67.2 3.3 %collective-permute-done.14 = f32[64,128]{1,0:T(8,128)S(1)} collective-permute-done((f32[64,128]{1,0:T(8,128)S(1)}, f32[64,128]{1,0:T(8,128)S(1)}, u32[]{:S(2)}, u32[]{:S(2)}) %collective-permute-start.14) | collective-permute-done | bytes 32800 | tf_op jit(solution)/shard_map/ppermute | solution.py:489
  71.4 3.2 %collective-permute-start.15 = (bf16[128,1024]{1,0:T(8,128)(2,1)S(1)}, bf16[128,1024]{1,0:T(8,128)(2,1)S(1)}, u32[]{:S(2)}, u32[]{:S(2)}) collective-permute-start(bf16[128,1024]{1,0:T(8,128)(2,1)S(1)} %slice.11), channel_id=1, source_target_pairs={{4,0},{8,4},{12,8},{16,12},{20,16},{24,20},{28,24},{32,28},{36,32}... | collective-permute-start | bytes 786440 | tf_op jit(solution)/shard_map/ppermute | solution.py:54
  74.7 2.1 %collective-permute-start.20 = (f32[64,128]{1,0:T(8,128)S(1)}, f32[64,128]{1,0:T(8,128)S(1)}, u32[]{:S(2)}, u32[]{:S(2)}) collective-permute-start(f32[64,128]{1,0:T(8,128)S(1)} %add.20), channel_id=1, source_target_pairs={{0,32},{1,9},{2,34},{3,11},{4,36},{5,13},{6,38},{7,15},{8,40},{9,1... | collective-permute-start | bytes 98312 | tf_op jit(solution)/shard_map/ppermute | solution.py:45
  76.8 4.2 %collective-permute-done.20 = f32[64,128]{1,0:T(8,128)S(1)} collective-permute-done((f32[64,128]{1,0:T(8,128)S(1)}, f32[64,128]{1,0:T(8,128)S(1)}, u32[]{:S(2)}, u32[]{:S(2)}) %collective-permute-start.20) | collective-permute-done | bytes 32800 | tf_op jit(solution)/shard_map/ppermute | solution.py:45
  81.4 1.1 %collective-permute-start.21 = (bf16[64,1024]{1,0:T(8,128)(2,1)S(1)}, bf16[64,1024]{1,0:T(8,128)(2,1)S(1)}, u32[]{:S(2)}, u32[]{:S(2)}) collective-permute-start(bf16[64,1024]{1,0:T(8,128)(2,1)S(1)} %get-tuple-element.54), channel_id=1, source_target_pairs={{0,64},{64,128},{128,192},{192,0},{1,65},{65,129},{129,193},{193,1... | collective-permute-start | bytes 393224 | tf_op jit(solution)/shard_map/ppermute | solution.py:529
  82.5 1.5 %collective-permute-start.22 = (bf16[64,1024]{1,0:T(8,128)(2,1)S(1)}, bf16[64,1024]{1,0:T(8,128)(2,1)S(1)}, u32[]{:S(2)}, u32[]{:S(2)}) collective-permute-start(bf16[64,1024]{1,0:T(8,128)(2,1)S(1)} %get-tuple-element.55), channel_id=1, source_target_pairs={{0,128},{64,192},{128,0},{192,64},{1,129},{65,193},{129,1},{193,65... | collective-permute-start | bytes 393224 | tf_op jit(solution)/shard_map/ppermute | solution.py:529
  83.9 1.9 %collective-permute-start.23 = (bf16[64,1024]{1,0:T(8,128)(2,1)S(1)}, bf16[64,1024]{1,0:T(8,128)(2,1)S(1)}, u32[]{:S(2)}, u32[]{:S(2)}) collective-permute-start(bf16[64,1024]{1,0:T(8,128)(2,1)S(1)} %get-tuple-element.56), channel_id=1, source_target_pairs={{0,192},{64,0},{128,64},{192,128},{1,193},{65,1},{129,65},{193,129... | collective-permute-start | bytes 393224 | tf_op jit(solution)/shard_map/ppermute | solution.py:529
  85.9 3.9 %collective-permute-done.25 = f32[64,128]{1,0:T(8,128)S(1)} collective-permute-done((f32[64,128]{1,0:T(8,128)S(1)}, f32[64,128]{1,0:T(8,128)S(1)}, u32[]{:S(2)}, u32[]{:S(2)}) %collective-permute-start.25) | collective-permute-done | bytes 32800 | tf_op jit(solution)/shard_map/ppermute | solution.py:45
  90.5 3.4 %input_grad.1.refs_4_ = bf16[256,1024]{1,0:T(8,128)(2,1)} custom-call(bf16[64,128]{1,0:T(8,128)(2,1)} %refs_0_.3, bf16[256,1024]{1,0:T(8,128)(2,1)S(1)} %get-tuple-element.41.refs_2_.refs_1_, bf16[128,1024]{1,0:T(8,128)(2,1)S(1)} %collective-permute-done.15.refs_2_, f32[64,1024]{1,0:T(8,128)S(1)} %get-tuple-element.52.refs_3_.refs_0_), custom_call_target="tpu_custom_call" | custom-call | tf_op jit(solution)/shard_map/input_grad/pallas_call | solution.py:96
  94.1 1.1 %collective-permute-done.26 = f32[64,128]{1,0:T(8,128)S(1)} collective-permute-done((f32[64,128]{1,0:T(8,128)S(1)}, f32[64,128]{1,0:T(8,128)S(1)}, u32[]{:S(2)}, u32[]{:S(2)}) %collective-permute-start.26) | collective-permute-done | bytes 32800 | tf_op jit(solution)/shard_map/ppermute | solution.py:45
  (41 shorter events, 8.1 us)
Async XLA Ops:
  0.6 11.8 %collective-permute-start = (bf16[64,4096]{1,0:T(8,128)(2,1)}, bf16[64,4096]{1,0:T(8,128)(2,1)S(1)}, u32[]{:S(2)}, u32[]{:S(2)}) collective-permute-start(bf16[64,4096]{1,0:T(8,128)(2,1)} %bitcast.10), channel_id=1, source_target_pairs={{0,1},{1,0},{2,3},{3,2},{4,5},{5,4},{6,7},{7,6},{8,9},{9,8},{10,11... | collective-permute-start | bytes 1572872 | tf_op jit(solution)/shard_map/ppermute | solution.py:32
  0.7 30.0 %collective-permute-start.1 = (bf16[64,4096]{1,0:T(8,128)(2,1)}, bf16[64,4096]{1,0:T(8,128)(2,1)S(1)}, u32[]{:S(2)}, u32[]{:S(2)}) collective-permute-start(bf16[64,4096]{1,0:T(8,128)(2,1)} %bitcast.11), channel_id=1, source_target_pairs={{0,2},{1,3},{2,0},{3,1},{4,6},{5,7},{6,4},{7,5},{8,10},{9,11},{10,... | collective-permute-start | bytes 1572872 | tf_op jit(solution)/shard_map/ppermute | solution.py:32
  9.0 12.5 %collective-permute-start.2 = (bf16[128,1024]{1,0:T(8,128)(2,1)S(1)}, bf16[128,1024]{1,0:T(8,128)(2,1)S(1)}, u32[]{:S(2)}, u32[]{:S(2)}) collective-permute-start(bf16[128,1024]{1,0:T(8,128)(2,1)S(1)} %slice_bitcast_fusion), channel_id=1, source_target_pairs={{0,4},{4,8},{8,12},{12,16},{16,20},{20,24},{24,28},{28,32},{32,36}... | collective-permute-start | bytes 786440 | tf_op jit(solution)/shard_map/ppermute | solution.py:54
  13.7 12.8 %collective-permute-start.5 = (bf16[128,1024]{1,0:T(8,128)(2,1)S(1)}, bf16[128,1024]{1,0:T(8,128)(2,1)S(1)}, u32[]{:S(2)}, u32[]{:S(2)}) collective-permute-start(bf16[128,1024]{1,0:T(8,128)(2,1)S(1)} %get-tuple-element.35), channel_id=1, source_target_pairs={{0,16},{1,5},{2,18},{3,7},{4,20},{5,9},{6,22},{7,11},{8,24},{9,13}... | collective-permute-start | bytes 786440 | tf_op jit(solution)/shard_map/ppermute | solution.py:45
  15.2 11.2 %collective-permute-start.6 = (bf16[128,1024]{1,0:T(8,128)(2,1)S(1)}, bf16[128,1024]{1,0:T(8,128)(2,1)S(1)}, u32[]{:S(2)}, u32[]{:S(2)}) collective-permute-start(bf16[128,1024]{1,0:T(8,128)(2,1)S(1)} %get-tuple-element.36), channel_id=1, source_target_pairs={{0,48},{1,13},{2,50},{3,15},{4,52},{5,1},{6,54},{7,3},{8,56},{9,5}... | collective-permute-start | bytes 786440 | tf_op jit(solution)/shard_map/ppermute | solution.py:45
  24.9 1.4 %collective-permute-start.3 = (bf16[128,512]{1,0:T(8,128)(2,1)S(1)}, bf16[128,512]{1,0:T(8,128)(2,1)S(1)}, u32[]{:S(2)}, u32[]{:S(2)}) collective-permute-start(bf16[128,512]{1,0:T(8,128)(2,1)S(1)} %get-tuple-element.33), channel_id=1, source_target_pairs={{0,1},{1,0},{2,3},{3,2},{4,5},{5,4},{6,7},{7,6},{8,9},{9,8},{10,11... | collective-permute-start | bytes 393224 | tf_op jit(solution)/shard_map/ppermute | solution.py:32
  25.0 1.5 %collective-permute-start.4 = (bf16[128,512]{1,0:T(8,128)(2,1)S(1)}, bf16[128,512]{1,0:T(8,128)(2,1)S(1)}, u32[]{:S(2)}, u32[]{:S(2)}) collective-permute-start(bf16[128,512]{1,0:T(8,128)(2,1)S(1)} %get-tuple-element.34), channel_id=1, source_target_pairs={{0,1},{1,0},{2,3},{3,2},{4,5},{5,4},{6,7},{7,6},{8,9},{9,8},{10,11... | collective-permute-start | bytes 393224 | tf_op jit(solution)/shard_map/ppermute | solution.py:32
  26.5 9.6 %collective-permute-start.8 = (bf16[272,1024]{1,0:T(8,128)(2,1)S(1)}, bf16[272,1024]{1,0:T(8,128)(2,1)S(1)}, u32[]{:S(2)}, u32[]{:S(2)}) collective-permute-start(bf16[272,1024]{1,0:T(8,128)(2,1)S(1)} %join.1.refs_8_), channel_id=1, source_target_pairs={{0,16},{1,5},{2,18},{3,7},{4,20},{5,9},{6,22},{7,11},{8,24},{9,13}... | collective-permute-start | bytes 1671176 | tf_op jit(solution)/shard_map/ppermute | solution.py:45
  28.1 9.5 %collective-permute-start.9 = (bf16[272,1024]{1,0:T(8,128)(2,1)S(1)}, bf16[272,1024]{1,0:T(8,128)(2,1)S(1)}, u32[]{:S(2)}, u32[]{:S(2)}) collective-permute-start(bf16[272,1024]{1,0:T(8,128)(2,1)S(1)} %join.1.refs_8_), channel_id=1, source_target_pairs={{0,48},{1,13},{2,50},{3,15},{4,52},{5,1},{6,54},{7,3},{8,56},{9,5}... | collective-permute-start | bytes 1671176 | tf_op jit(solution)/shard_map/ppermute | solution.py:45
  30.7 1.9 %collective-permute-start.7 = (bf16[64,4096]{1,0:T(8,128)(2,1)S(1)}, bf16[64,4096]{1,0:T(8,128)(2,1)S(1)}, u32[]{:S(2)}, u32[]{:S(2)}) collective-permute-start(bf16[64,4096]{1,0:T(8,128)(2,1)S(1)} %collective-permute-done.1.refs_0_.refs_2_), channel_id=1, source_target_pairs={{0,1},{1,0},{2,3},{3,2},{4,5},{5,4},{6,7},{7,6},{8,9},{9,8},{10,11... | collective-permute-start | bytes 1572872 | tf_op jit(solution)/shard_map/ppermute | solution.py:32
  37.8 14.4 %collective-permute-start.10 = (bf16[256,1024]{1,0:T(8,128)(2,1)S(1)}, bf16[256,1024]{1,0:T(8,128)(2,1)S(1)}, u32[]{:S(2)}, u32[]{:S(2)}) collective-permute-start(bf16[256,1024]{1,0:T(8,128)(2,1)S(1)} %get-tuple-element.43), channel_id=1, source_target_pairs={{0,32},{1,9},{2,34},{3,11},{4,36},{5,13},{6,38},{7,15},{8,40},{9,1... | collective-permute-start | bytes 1572872 | tf_op jit(solution)/shard_map/ppermute | solution.py:45
  39.9 14.2 %collective-permute-start.11 = (bf16[256,1024]{1,0:T(8,128)(2,1)S(1)}, bf16[256,1024]{1,0:T(8,128)(2,1)S(1)}, u32[]{:S(2)}, u32[]{:S(2)}) collective-permute-start(bf16[256,1024]{1,0:T(8,128)(2,1)S(1)} %get-tuple-element.44), channel_id=1, source_target_pairs={{0,16},{1,5},{2,18},{3,7},{4,20},{5,9},{6,22},{7,11},{8,24},{9,13}... | collective-permute-start | bytes 1572872 | tf_op jit(solution)/shard_map/ppermute | solution.py:45
  39.9 14.3 %collective-permute-start.12 = (bf16[256,1024]{1,0:T(8,128)(2,1)S(1)}, bf16[256,1024]{1,0:T(8,128)(2,1)S(1)}, u32[]{:S(2)}, u32[]{:S(2)}) collective-permute-start(bf16[256,1024]{1,0:T(8,128)(2,1)S(1)} %get-tuple-element.45), channel_id=1, source_target_pairs={{0,48},{1,13},{2,50},{3,15},{4,52},{5,1},{6,54},{7,3},{8,56},{9,5}... | collective-permute-start | bytes 1572872 | tf_op jit(solution)/shard_map/ppermute | solution.py:45
  57.3 23.6 %collective-permute-start.16 = (bf16[256,1024]{1,0:T(8,128)(2,1)S(1)}, bf16[256,1024]{1,0:T(8,128)(2,1)S(1)}, u32[]{:S(2)}, u32[]{:S(2)}) collective-permute-start(bf16[256,1024]{1,0:T(8,128)(2,1)S(1)} %get-tuple-element.49), channel_id=1, source_target_pairs={{0,4},{1,17},{2,6},{3,19},{4,8},{5,21},{6,10},{7,23},{8,12},{9,25}... | collective-permute-start | bytes 1572872 | tf_op jit(solution)/shard_map/ppermute | solution.py:45
  57.5 23.4 %collective-permute-start.17 = (bf16[256,1024]{1,0:T(8,128)(2,1)S(1)}, bf16[256,1024]{1,0:T(8,128)(2,1)S(1)}, u32[]{:S(2)}, u32[]{:S(2)}) collective-permute-start(bf16[256,1024]{1,0:T(8,128)(2,1)S(1)} %get-tuple-element.50), channel_id=1, source_target_pairs={{0,8},{1,33},{2,10},{3,35},{4,12},{5,37},{6,14},{7,39},{8,0},{9,41... | collective-permute-start | bytes 1572872 | tf_op jit(solution)/shard_map/ppermute | solution.py:45
  60.4 20.5 %collective-permute-start.18 = (bf16[256,1024]{1,0:T(8,128)(2,1)S(1)}, bf16[256,1024]{1,0:T(8,128)(2,1)S(1)}, u32[]{:S(2)}, u32[]{:S(2)}) collective-permute-start(bf16[256,1024]{1,0:T(8,128)(2,1)S(1)} %get-tuple-element.51), channel_id=1, source_target_pairs={{0,12},{1,49},{2,14},{3,51},{4,0},{5,53},{6,2},{7,55},{8,4},{9,57}... | collective-permute-start | bytes 1572872 | tf_op jit(solution)/shard_map/ppermute | solution.py:45
  61.8 3.9 %collective-permute-start.13 = (f32[64,128]{1,0:T(8,128)S(1)}, f32[64,128]{1,0:T(8,128)S(1)}, u32[]{:S(2)}, u32[]{:S(2)}) collective-permute-start(f32[64,128]{1,0:T(8,128)S(1)} %filter_grad.1.refs_13_), channel_id=1, source_target_pairs={{0,64},{64,0},{128,192},{192,128},{1,65},{65,1},{129,193},{193,129... | collective-permute-start | bytes 98312 | tf_op jit(solution)/shard_map/ppermute | solution.py:489
  65.7 4.8 %collective-permute-start.14 = (f32[64,128]{1,0:T(8,128)S(1)}, f32[64,128]{1,0:T(8,128)S(1)}, u32[]{:S(2)}, u32[]{:S(2)}) collective-permute-start(f32[64,128]{1,0:T(8,128)S(1)} %add.18), channel_id=1, source_target_pairs={{0,128},{64,192},{128,0},{192,64},{1,129},{65,193},{129,1},{193,65... | collective-permute-start | bytes 98312 | tf_op jit(solution)/shard_map/ppermute | solution.py:489
  70.5 4.1 %collective-permute-start.19 = (f32[64,128]{1,0:T(8,128)S(1)}, f32[64,128]{1,0:T(8,128)S(1)}, u32[]{:S(2)}, u32[]{:S(2)}) collective-permute-start(f32[64,128]{1,0:T(8,128)S(1)} %add.19), channel_id=1, source_target_pairs={{0,16},{1,5},{2,18},{3,7},{4,20},{5,1},{6,22},{7,3},{8,24},{9,13},... | collective-permute-start | bytes 98312 | tf_op jit(solution)/shard_map/ppermute | solution.py:45
  71.4 19.1 %collective-permute-start.15 = (bf16[128,1024]{1,0:T(8,128)(2,1)S(1)}, bf16[128,1024]{1,0:T(8,128)(2,1)S(1)}, u32[]{:S(2)}, u32[]{:S(2)}) collective-permute-start(bf16[128,1024]{1,0:T(8,128)(2,1)S(1)} %slice.11), channel_id=1, source_target_pairs={{4,0},{8,4},{12,8},{16,12},{20,16},{24,20},{28,24},{32,28},{36,32}... | collective-permute-start | bytes 786440 | tf_op jit(solution)/shard_map/ppermute | solution.py:54
  74.7 6.3 %collective-permute-start.20 = (f32[64,128]{1,0:T(8,128)S(1)}, f32[64,128]{1,0:T(8,128)S(1)}, u32[]{:S(2)}, u32[]{:S(2)}) collective-permute-start(f32[64,128]{1,0:T(8,128)S(1)} %add.20), channel_id=1, source_target_pairs={{0,32},{1,9},{2,34},{3,11},{4,36},{5,13},{6,38},{7,15},{8,40},{9,1... | collective-permute-start | bytes 98312 | tf_op jit(solution)/shard_map/ppermute | solution.py:45
  81.4 12.5 %collective-permute-start.21 = (bf16[64,1024]{1,0:T(8,128)(2,1)S(1)}, bf16[64,1024]{1,0:T(8,128)(2,1)S(1)}, u32[]{:S(2)}, u32[]{:S(2)}) collective-permute-start(bf16[64,1024]{1,0:T(8,128)(2,1)S(1)} %get-tuple-element.54), channel_id=1, source_target_pairs={{0,64},{64,128},{128,192},{192,0},{1,65},{65,129},{129,193},{193,1... | collective-permute-start | bytes 393224 | tf_op jit(solution)/shard_map/ppermute | solution.py:529
  82.5 11.4 %collective-permute-start.22 = (bf16[64,1024]{1,0:T(8,128)(2,1)S(1)}, bf16[64,1024]{1,0:T(8,128)(2,1)S(1)}, u32[]{:S(2)}, u32[]{:S(2)}) collective-permute-start(bf16[64,1024]{1,0:T(8,128)(2,1)S(1)} %get-tuple-element.55), channel_id=1, source_target_pairs={{0,128},{64,192},{128,0},{192,64},{1,129},{65,193},{129,1},{193,65... | collective-permute-start | bytes 393224 | tf_op jit(solution)/shard_map/ppermute | solution.py:529
  83.9 10.0 %collective-permute-start.23 = (bf16[64,1024]{1,0:T(8,128)(2,1)S(1)}, bf16[64,1024]{1,0:T(8,128)(2,1)S(1)}, u32[]{:S(2)}, u32[]{:S(2)}) collective-permute-start(bf16[64,1024]{1,0:T(8,128)(2,1)S(1)} %get-tuple-element.56), channel_id=1, source_target_pairs={{0,192},{64,0},{128,64},{192,128},{1,193},{65,1},{129,65},{193,129... | collective-permute-start | bytes 393224 | tf_op jit(solution)/shard_map/ppermute | solution.py:529
  85.9 3.9 %collective-permute-start.25 = (f32[64,128]{1,0:T(8,128)S(1)}, f32[64,128]{1,0:T(8,128)S(1)}, u32[]{:S(2)}, u32[]{:S(2)}) collective-permute-start(f32[64,128]{1,0:T(8,128)S(1)} %add.21.refs_4_), channel_id=1, source_target_pairs={{0,4},{1,17},{2,6},{3,19},{4,0},{5,21},{6,2},{7,23},{8,12},{9,25},... | collective-permute-start | bytes 98312 | tf_op jit(solution)/shard_map/ppermute | solution.py:45
  89.8 5.4 %collective-permute-start.26 = (f32[64,128]{1,0:T(8,128)S(1)}, f32[64,128]{1,0:T(8,128)S(1)}, u32[]{:S(2)}, u32[]{:S(2)}) collective-permute-start(f32[64,128]{1,0:T(8,128)S(1)} %add.22), channel_id=1, source_target_pairs={{0,8},{1,33},{2,10},{3,35},{4,12},{5,37},{6,14},{7,39},{8,0},{9,41... | collective-permute-start | bytes 98312 | tf_op jit(solution)/shard_map/ppermute | solution.py:45
  94.0 1.8 %collective-permute-start.24 = (f32[64,512]{1,0:T(8,128)S(1)}, f32[64,512]{1,0:T(8,128)S(1)}, u32[]{:S(2)}, u32[]{:S(2)}) collective-permute-start(f32[64,512]{1,0:T(8,128)S(1)} %get-tuple-element.58), channel_id=1, source_target_pairs={{0,1},{1,0},{2,3},{3,2},{4,5},{5,4},{6,7},{7,6},{8,9},{9,8},{10,11... | collective-permute-start | bytes 393224 | tf_op jit(solution)/shard_map/ppermute | solution.py:32

commit v10 on v9

--- a/solution.py
+++ b/solution.py
@@ -514,12 +514,12 @@
         grads, early_other, late, late_other, weight, gating, response, (own_late,)
     )
     late_got = [stepped(late_sent[s - 1], True, s) for s in shifts]
-    filter_sum = filter_grad(previous, signal, conv_grad, ())
+    filter_sum = paired(filter_grad(previous, signal, conv_grad, ()), True, 1)
     parts = weight_parts([early[0], *early_got], own_late, gated, got, late_got, (filter_sum,))
 
     filter_sum = paired_z(paired_z(tied(filter_sum, parts[0]), 1), 2)
     following = shifted(tied(conv_grad[:TAPS], filter_sum), -1)
-    filter_sum = paired(paired(filter_sum, True, 1), True, 2)
+    filter_sum = paired(filter_sum, True, 2)
     parts = [parts[0]] + [stepped(parts[s], False, s) for s in shifts]
     sums = first_sum(parts, (filter_sum,))
     filter_sum = paired(paired(filter_sum, False, 1, (sums[0],)), False, 2)

time: 98.3 us -> 102 us (1.038)
  the two profiles are of different devices: /device:TPU:2 before, /device:TPU:1 now
where the time goes in v10:
time: 102 us
  starting transfers between devices  56.1 us (55%)
  Pallas kernels  24.6 us (24%)
  waiting for transfers between devices  18.9 us (19%)
    ppermute x14, starting transfers between devices, in_plane(): return lax.ppermute(x, ('ctx', 'tp'), pairs)  23.4 us
    ppermute x6, starting transfers between devices, moved(): return lax.ppermute(x, 'tp', [(i, i ^ step) for i in range(4)])  22.4 us
    pallas_call x10, Pallas kernels, once(): pl.pallas_call(body, grid=(1,), in_specs=specs + [ANYWHERE] * len(after),...  18 us
    ppermute x14, waiting for transfers between devices, in_plane(): return lax.ppermute(x, ('ctx', 'tp'), pairs)  10.5 us
    pallas_call x1, Pallas kernels, project(): pl.pallas_call(body, grid=(channels // WIDE,), in_specs=[full(early.shape...  6.59 us
    ppermute x2, waiting for transfers between devices, paired_z(): return x + lax.ppermute(x, 'dp', [(i, i ^ by) for i in range(SIDE)])  4.75 us
    ppermute x2, starting transfers between devices, shifted(): lax.ppermute(x, 'ctx', [(i, i + by) for i in range(devices) if 0 <= i + b...  4.5 us
    ppermute x3, starting transfers between devices, local(): lax.ppermute(sums[s], 'dp', line[s - 1])  3.84 us
  transfers between devices with their start and end apart: 27, of which 11 were waited for; matrix products, arithmetic and copies ran while one was open for 2% of the time, Pallas kernels for 19%

profile of v10, /device:TPU:1, one launch (start us, length us, event | category | flops | bytes accessed | tf_op | source)
XLA Modules:
  0.0 102.1 jit_solution(18437167235189805669)
XLA Ops:
  0.6 3.3 %collective-permute-start = (bf16[64,4096]{1,0:T(8,128)(2,1)}, bf16[64,4096]{1,0:T(8,128)(2,1)S(1)}, u32[]{:S(2)}, u32[]{:S(2)}) collective-permute-start(bf16[64,4096]{1,0:T(8,128)(2,1)} %bitcast.10), channel_id=1, source_target_pairs={{0,1},{1,0},{2,3},{3,2},{4,5},{5,4},{6,7},{7,6},{8,9},{9,8},{10,11... | collective-permute-start | bytes 1572872 | tf_op jit(solution)/shard_map/ppermute | solution.py:32
  4.0 5.2 %collective-permute-start.1 = (bf16[64,4096]{1,0:T(8,128)(2,1)}, bf16[64,4096]{1,0:T(8,128)(2,1)S(1)}, u32[]{:S(2)}, u32[]{:S(2)}) collective-permute-start(bf16[64,4096]{1,0:T(8,128)(2,1)} %bitcast.11), channel_id=1, source_target_pairs={{0,2},{1,3},{2,0},{3,1},{4,6},{5,7},{6,4},{7,5},{8,10},{9,11},{10,... | collective-permute-start | bytes 1572872 | tf_op jit(solution)/shard_map/ppermute | solution.py:32
  10.1 3.2 %collective-permute-start.2 = (bf16[128,1024]{1,0:T(8,128)(2,1)S(1)}, bf16[128,1024]{1,0:T(8,128)(2,1)S(1)}, u32[]{:S(2)}, u32[]{:S(2)}) collective-permute-start(bf16[128,1024]{1,0:T(8,128)(2,1)S(1)} %slice_bitcast_fusion), channel_id=1, source_target_pairs={{0,4},{4,8},{8,12},{12,16},{16,20},{20,24},{24,28},{28,32},{32,36}... | collective-permute-start | bytes 786440 | tf_op jit(solution)/shard_map/ppermute | solution.py:54
  13.4 2.0 %pack.1 = (bf16[128,1024]{1,0:T(8,128)(2,1)S(1)}, bf16[128,1024]{1,0:T(8,128)(2,1)S(1)}, bf16[128,1024]{1,0:T(8,128)(2,1)S(1)}, bf16[128,1024]{1,0:T(8,128)(2,1)S(1)}) custom-call(bf16[64,4096]{1,0:T(8,128)(2,1)} %bitcast.12, bf16[64,4096]{1,0:T(8,128)(2,1)S(1)} %collective-permute-done.refs_1_), custom_call_target="tpu_custom_call" | custom-call | tf_op jit(solution)/shard_map/pack/pallas_call | solution.py:96
  15.4 1.4 %collective-permute-start.5 = (bf16[128,1024]{1,0:T(8,128)(2,1)S(1)}, bf16[128,1024]{1,0:T(8,128)(2,1)S(1)}, u32[]{:S(2)}, u32[]{:S(2)}) collective-permute-start(bf16[128,1024]{1,0:T(8,128)(2,1)S(1)} %get-tuple-element.35), channel_id=1, source_target_pairs={{0,16},{1,5},{2,18},{3,7},{4,20},{5,9},{6,22},{7,11},{8,24},{9,13}... | collective-permute-start | bytes 786440 | tf_op jit(solution)/shard_map/ppermute | solution.py:45
  16.7 1.4 %collective-permute-start.6 = (bf16[128,1024]{1,0:T(8,128)(2,1)S(1)}, bf16[128,1024]{1,0:T(8,128)(2,1)S(1)}, u32[]{:S(2)}, u32[]{:S(2)}) collective-permute-start(bf16[128,1024]{1,0:T(8,128)(2,1)S(1)} %get-tuple-element.36), channel_id=1, source_target_pairs={{0,48},{1,13},{2,50},{3,15},{4,52},{5,1},{6,54},{7,3},{8,56},{9,5}... | collective-permute-start | bytes 786440 | tf_op jit(solution)/shard_map/ppermute | solution.py:45
  18.6 3.4 %conv_forward.1 = (f32[256,1024]{1,0:T(8,128)S(1)}, bf16[256,512]{1,0:T(8,128)(2,1)S(1)}, bf16[128,512]{1,0:T(8,128)(2,1)S(1)}, bf16[128,512]{1,0:T(8,128)(2,1)S(1)}) custom-call(bf16[64,128]{1,0:T(8,128)(2,1)} %refs_0_.3, bf16[128,1024]{1,0:T(8,128)(2,1)S(1)} %collective-permute-done.2.refs_1_.refs_0_, bf16[256,1024]{1,0:T(8,128)(2,1)} %bitcast.8, ...), custom_call_target="tpu_custom_call" | custom-call | tf_op jit(solution)/shard_map/conv_forward/pallas_call | solution.py:96
  22.1 2.1 %collective-permute-start.3 = (bf16[128,512]{1,0:T(8,128)(2,1)S(1)}, bf16[128,512]{1,0:T(8,128)(2,1)S(1)}, u32[]{:S(2)}, u32[]{:S(2)}) collective-permute-start(bf16[128,512]{1,0:T(8,128)(2,1)S(1)} %get-tuple-element.33), channel_id=1, source_target_pairs={{0,1},{1,0},{2,3},{3,2},{4,5},{5,4},{6,7},{7,6},{8,9},{9,8},{10,11... | collective-permute-start | bytes 393224 | tf_op jit(solution)/shard_map/ppermute | solution.py:32
  25.5 2.3 %collective-permute-start.8 = (bf16[272,1024]{1,0:T(8,128)(2,1)S(1)}, bf16[272,1024]{1,0:T(8,128)(2,1)S(1)}, u32[]{:S(2)}, u32[]{:S(2)}) collective-permute-start(bf16[272,1024]{1,0:T(8,128)(2,1)S(1)} %join.1.refs_8_), channel_id=1, source_target_pairs={{0,16},{1,5},{2,18},{3,7},{4,20},{5,9},{6,22},{7,11},{8,24},{9,13}... | collective-permute-start | bytes 1671176 | tf_op jit(solution)/shard_map/ppermute | solution.py:45
  27.8 1.5 %collective-permute-start.9 = (bf16[272,1024]{1,0:T(8,128)(2,1)S(1)}, bf16[272,1024]{1,0:T(8,128)(2,1)S(1)}, u32[]{:S(2)}, u32[]{:S(2)}) collective-permute-start(bf16[272,1024]{1,0:T(8,128)(2,1)S(1)} %join.1.refs_8_), channel_id=1, source_target_pairs={{0,48},{1,13},{2,50},{3,15},{4,52},{5,1},{6,54},{7,3},{8,56},{9,5}... | collective-permute-start | bytes 1671176 | tf_op jit(solution)/shard_map/ppermute | solution.py:45
  29.3 1.6 %collective-permute-start.7 = (bf16[64,4096]{1,0:T(8,128)(2,1)S(1)}, bf16[64,4096]{1,0:T(8,128)(2,1)S(1)}, u32[]{:S(2)}, u32[]{:S(2)}) collective-permute-start(bf16[64,4096]{1,0:T(8,128)(2,1)S(1)} %collective-permute-done.1.refs_0_.refs_2_), channel_id=1, source_target_pairs={{0,1},{1,0},{2,3},{3,2},{4,5},{5,4},{6,7},{7,6},{8,9},{9,8},{10,11... | collective-permute-start | bytes 1572872 | tf_op jit(solution)/shard_map/ppermute | solution.py:32
  31.0 1.5 %collective-permute-done.7.refs_1_.refs_3_ = bf16[64,4096]{1,0:T(8,128)(2,1)S(1)} collective-permute-done((bf16[64,4096]{1,0:T(8,128)(2,1)S(1)}, bf16[64,4096]{1,0:T(8,128)(2,1)S(1)}, u32[]{:S(2)}, u32[]{:S(2)}) %collective-permute-start.7) | collective-permute-done | bytes 524320 | tf_op jit(solution)/shard_map/ppermute | solution.py:32
  32.5 4.0 %collective-permute-done.8.refs_2_.refs_9_ = bf16[272,1024]{1,0:T(8,128)(2,1)S(1)} collective-permute-done((bf16[272,1024]{1,0:T(8,128)(2,1)S(1)}, bf16[272,1024]{1,0:T(8,128)(2,1)S(1)}, u32[]{:S(2)}, u32[]{:S(2)}) %collective-permute-start.8) | collective-permute-done | bytes 557088 | tf_op jit(solution)/shard_map/ppermute | solution.py:45
  37.5 2.7 %collective-permute-start.11 = (bf16[256,1024]{1,0:T(8,128)(2,1)S(1)}, bf16[256,1024]{1,0:T(8,128)(2,1)S(1)}, u32[]{:S(2)}, u32[]{:S(2)}) collective-permute-start(bf16[256,1024]{1,0:T(8,128)(2,1)S(1)} %get-tuple-element.43), channel_id=1, source_target_pairs={{0,32},{1,9},{2,34},{3,11},{4,36},{5,13},{6,38},{7,15},{8,40},{9,1... | collective-permute-start | bytes 1572872 | tf_op jit(solution)/shard_map/ppermute | solution.py:45
  40.9 2.0 %collective-permute-start.13 = (bf16[256,1024]{1,0:T(8,128)(2,1)S(1)}, bf16[256,1024]{1,0:T(8,128)(2,1)S(1)}, u32[]{:S(2)}, u32[]{:S(2)}) collective-permute-start(bf16[256,1024]{1,0:T(8,128)(2,1)S(1)} %get-tuple-element.45), channel_id=1, source_target_pairs={{0,48},{1,13},{2,50},{3,15},{4,52},{5,1},{6,54},{7,3},{8,56},{9,5}... | collective-permute-start | bytes 1572872 | tf_op jit(solution)/shard_map/ppermute | solution.py:45
  42.9 6.6 %project.1 = (bf16[256,1024]{1,0:T(8,128)(2,1)S(1)}, bf16[256,1024]{1,0:T(8,128)(2,1)}) custom-call(bf16[64,4096]{1,0:T(8,128)(2,1)} %bitcast.13, bf16[64,4096]{1,0:T(8,128)(2,1)S(1)} %collective-permute-done.refs_1_, bf16[64,4096]{1,0:T(8,128)(2,1)S(1)} %collective-permute-done.1.refs_0_.refs_2_, ...), custom_call_target="tpu_custom_call" | custom-call | flops 6000000000 | tf_op jit(solution)/shard_map/project/pallas_call | solution.py:344
  49.5 3.8 %filter_grad.1 = f32[64,128]{1,0:T(8,128)S(1)} custom-call(bf16[128,1024]{1,0:T(8,128)(2,1)S(1)} %collective-permute-done.2.refs_1_.refs_0_, bf16[256,1024]{1,0:T(8,128)(2,1)} %bitcast.9, bf16[256,1024]{1,0:T(8,128)(2,1)S(1)} %get-tuple-element.41.refs_2_.refs_1_), custom_call_target="tpu_custom_call" | custom-call | flops 4000000000 | tf_op jit(solution)/shard_map/filter_grad/pallas_call | solution.py:96
  53.4 2.8 %collective-permute-done.10 = f32[64,128]{1,0:T(8,128)S(1)} collective-permute-done((f32[64,128]{1,0:T(8,128)S(1)}, f32[64,128]{1,0:T(8,128)S(1)}, u32[]{:S(2)}, u32[]{:S(2)}) %collective-permute-start.10) | collective-permute-done | bytes 32800 | tf_op jit(solution)/shard_map/ppermute | solution.py:45
  56.2 3.1 %weight_parts.1 = (f32[256,1024]{1,0:T(8,128)S(1)}, bf16[256,1024]{1,0:T(8,128)(2,1)S(1)}, bf16[256,1024]{1,0:T(8,128)(2,1)S(1)}, bf16[256,1024]{1,0:T(8,128)(2,1)S(1)}) custom-call(bf16[128,1024]{1,0:T(8,128)(2,1)S(1)} %get-tuple-element.42.refs_0_, bf16[128,1024]{1,0:T(8,128)(2,1)S(1)} %collective-permute-done.5.refs_3_.refs_1_, ...), custom_call_target="tpu_custom_call" | custom-call | flops 4000000000 | tf_op jit(solution)/shard_map/weight_parts/pallas_call | solution.py:96
  59.2 1.3 %collective-permute-start.17 = (bf16[256,1024]{1,0:T(8,128)(2,1)S(1)}, bf16[256,1024]{1,0:T(8,128)(2,1)S(1)}, u32[]{:S(2)}, u32[]{:S(2)}) collective-permute-start(bf16[256,1024]{1,0:T(8,128)(2,1)S(1)} %get-tuple-element.49), channel_id=1, source_target_pairs={{0,4},{1,17},{2,6},{3,19},{4,8},{5,21},{6,10},{7,23},{8,12},{9,25}... | collective-permute-start | bytes 1572872 | tf_op jit(solution)/shard_map/ppermute | solution.py:45
  60.5 2.5 %collective-permute-start.18 = (bf16[256,1024]{1,0:T(8,128)(2,1)S(1)}, bf16[256,1024]{1,0:T(8,128)(2,1)S(1)}, u32[]{:S(2)}, u32[]{:S(2)}) collective-permute-start(bf16[256,1024]{1,0:T(8,128)(2,1)S(1)} %get-tuple-element.50), channel_id=1, source_target_pairs={{0,8},{1,33},{2,10},{3,35},{4,12},{5,37},{6,14},{7,39},{8,0},{9,41... | collective-permute-start | bytes 1572872 | tf_op jit(solution)/shard_map/ppermute | solution.py:45
  64.9 2.0 %collective-permute-done.14 = f32[64,128]{1,0:T(8,128)S(1)} collective-permute-done((f32[64,128]{1,0:T(8,128)S(1)}, f32[64,128]{1,0:T(8,128)S(1)}, u32[]{:S(2)}, u32[]{:S(2)}) %collective-permute-start.14) | collective-permute-done | bytes 32800 | tf_op jit(solution)/shard_map/ppermute | solution.py:489
  68.1 2.7 %collective-permute-done.15 = f32[64,128]{1,0:T(8,128)S(1)} collective-permute-done((f32[64,128]{1,0:T(8,128)S(1)}, f32[64,128]{1,0:T(8,128)S(1)}, u32[]{:S(2)}, u32[]{:S(2)}) %collective-permute-start.15) | collective-permute-done | bytes 32800 | tf_op jit(solution)/shard_map/ppermute | solution.py:489
  70.9 1.3 %collective-permute-start.16 = (bf16[128,1024]{1,0:T(8,128)(2,1)S(1)}, bf16[128,1024]{1,0:T(8,128)(2,1)S(1)}, u32[]{:S(2)}, u32[]{:S(2)}) collective-permute-start(bf16[128,1024]{1,0:T(8,128)(2,1)S(1)} %slice.11), channel_id=1, source_target_pairs={{4,0},{8,4},{12,8},{16,12},{20,16},{24,20},{28,24},{32,28},{36,32}... | collective-permute-start | bytes 786440 | tf_op jit(solution)/shard_map/ppermute | solution.py:54
  72.1 3.3 %collective-permute-start.20 = (f32[64,128]{1,0:T(8,128)S(1)}, f32[64,128]{1,0:T(8,128)S(1)}, u32[]{:S(2)}, u32[]{:S(2)}) collective-permute-start(f32[64,128]{1,0:T(8,128)S(1)} %add.20), channel_id=1, source_target_pairs={{0,32},{1,9},{2,34},{3,11},{4,36},{5,13},{6,38},{7,15},{8,40},{9,1... | collective-permute-start | bytes 98312 | tf_op jit(solution)/shard_map/ppermute | solution.py:45
  75.4 2.0 %collective-permute-done.20 = f32[64,128]{1,0:T(8,128)S(1)} collective-permute-done((f32[64,128]{1,0:T(8,128)S(1)}, f32[64,128]{1,0:T(8,128)S(1)}, u32[]{:S(2)}, u32[]{:S(2)}) %collective-permute-start.20) | collective-permute-done | bytes 32800 | tf_op jit(solution)/shard_map/ppermute | solution.py:45
  79.9 1.8 %collective-permute-start.23 = (bf16[64,1024]{1,0:T(8,128)(2,1)S(1)}, bf16[64,1024]{1,0:T(8,128)(2,1)S(1)}, u32[]{:S(2)}, u32[]{:S(2)}) collective-permute-start(bf16[64,1024]{1,0:T(8,128)(2,1)S(1)} %get-tuple-element.56), channel_id=1, source_target_pairs={{0,192},{64,0},{128,64},{192,128},{1,193},{65,1},{129,65},{193,129... | collective-permute-start | bytes 393224 | tf_op jit(solution)/shard_map/ppermute | solution.py:529
  81.7 1.3 %collective-permute-start.25 = (f32[64,128]{1,0:T(8,128)S(1)}, f32[64,128]{1,0:T(8,128)S(1)}, u32[]{:S(2)}, u32[]{:S(2)}) collective-permute-start(f32[64,128]{1,0:T(8,128)S(1)} %add.21.refs_4_), channel_id=1, source_target_pairs={{0,4},{1,17},{2,6},{3,19},{4,0},{5,21},{6,2},{7,23},{8,12},{9,25},... | collective-permute-start | bytes 98312 | tf_op jit(solution)/shard_map/ppermute | solution.py:45
  83.0 1.8 %collective-permute-done.25 = f32[64,128]{1,0:T(8,128)S(1)} collective-permute-done((f32[64,128]{1,0:T(8,128)S(1)}, f32[64,128]{1,0:T(8,128)S(1)}, u32[]{:S(2)}, u32[]{:S(2)}) %collective-permute-start.25) | collective-permute-done | bytes 32800 | tf_op jit(solution)/shard_map/ppermute | solution.py:45
  84.8 2.0 %collective-permute-start.26 = (f32[64,128]{1,0:T(8,128)S(1)}, f32[64,128]{1,0:T(8,128)S(1)}, u32[]{:S(2)}, u32[]{:S(2)}) collective-permute-start(f32[64,128]{1,0:T(8,128)S(1)} %add.22), channel_id=1, source_target_pairs={{0,8},{1,33},{2,10},{3,35},{4,12},{5,37},{6,14},{7,39},{8,0},{9,41... | collective-permute-start | bytes 98312 | tf_op jit(solution)/shard_map/ppermute | solution.py:45
  86.8 3.4 %input_grad.1.refs_4_ = bf16[256,1024]{1,0:T(8,128)(2,1)} custom-call(bf16[64,128]{1,0:T(8,128)(2,1)} %refs_0_.3, bf16[256,1024]{1,0:T(8,128)(2,1)S(1)} %get-tuple-element.41.refs_2_.refs_1_, bf16[128,1024]{1,0:T(8,128)(2,1)S(1)} %collective-permute-done.16.refs_2_, f32[64,1024]{1,0:T(8,128)S(1)} %get-tuple-element.52.refs_3_.refs_0_), custom_call_target="tpu_custom_call" | custom-call | tf_op jit(solution)/shard_map/input_grad/pallas_call | solution.py:96
  90.3 10.1 %collective-permute-start.24 = (f32[64,512]{1,0:T(8,128)S(1)}, f32[64,512]{1,0:T(8,128)S(1)}, u32[]{:S(2)}, u32[]{:S(2)}) collective-permute-start(f32[64,512]{1,0:T(8,128)S(1)} %get-tuple-element.58), channel_id=1, source_target_pairs={{0,1},{1,0},{2,3},{3,2},{4,5},{5,4},{6,7},{7,6},{8,9},{9,8},{10,11... | collective-permute-start | bytes 393224 | tf_op jit(solution)/shard_map/ppermute | solution.py:32
  (41 shorter events, 12.1 us)
Async XLA Ops:
  0.6 12.7 %collective-permute-start = (bf16[64,4096]{1,0:T(8,128)(2,1)}, bf16[64,4096]{1,0:T(8,128)(2,1)S(1)}, u32[]{:S(2)}, u32[]{:S(2)}) collective-permute-start(bf16[64,4096]{1,0:T(8,128)(2,1)} %bitcast.10), channel_id=1, source_target_pairs={{0,1},{1,0},{2,3},{3,2},{4,5},{5,4},{6,7},{7,6},{8,9},{9,8},{10,11... | collective-permute-start | bytes 1572872 | tf_op jit(solution)/shard_map/ppermute | solution.py:32
  4.0 25.4 %collective-permute-start.1 = (bf16[64,4096]{1,0:T(8,128)(2,1)}, bf16[64,4096]{1,0:T(8,128)(2,1)S(1)}, u32[]{:S(2)}, u32[]{:S(2)}) collective-permute-start(bf16[64,4096]{1,0:T(8,128)(2,1)} %bitcast.11), channel_id=1, source_target_pairs={{0,2},{1,3},{2,0},{3,1},{4,6},{5,7},{6,4},{7,5},{8,10},{9,11},{10,... | collective-permute-start | bytes 1572872 | tf_op jit(solution)/shard_map/ppermute | solution.py:32
  10.1 8.5 %collective-permute-start.2 = (bf16[128,1024]{1,0:T(8,128)(2,1)S(1)}, bf16[128,1024]{1,0:T(8,128)(2,1)S(1)}, u32[]{:S(2)}, u32[]{:S(2)}) collective-permute-start(bf16[128,1024]{1,0:T(8,128)(2,1)S(1)} %slice_bitcast_fusion), channel_id=1, source_target_pairs={{0,4},{4,8},{8,12},{12,16},{16,20},{20,24},{24,28},{28,32},{32,36}... | collective-permute-start | bytes 786440 | tf_op jit(solution)/shard_map/ppermute | solution.py:54
  15.4 10.1 %collective-permute-start.5 = (bf16[128,1024]{1,0:T(8,128)(2,1)S(1)}, bf16[128,1024]{1,0:T(8,128)(2,1)S(1)}, u32[]{:S(2)}, u32[]{:S(2)}) collective-permute-start(bf16[128,1024]{1,0:T(8,128)(2,1)S(1)} %get-tuple-element.35), channel_id=1, source_target_pairs={{0,16},{1,5},{2,18},{3,7},{4,20},{5,9},{6,22},{7,11},{8,24},{9,13}... | collective-permute-start | bytes 786440 | tf_op jit(solution)/shard_map/ppermute | solution.py:45
  16.7 8.7 %collective-permute-start.6 = (bf16[128,1024]{1,0:T(8,128)(2,1)S(1)}, bf16[128,1024]{1,0:T(8,128)(2,1)S(1)}, u32[]{:S(2)}, u32[]{:S(2)}) collective-permute-start(bf16[128,1024]{1,0:T(8,128)(2,1)S(1)} %get-tuple-element.36), channel_id=1, source_target_pairs={{0,48},{1,13},{2,50},{3,15},{4,52},{5,1},{6,54},{7,3},{8,56},{9,5}... | collective-permute-start | bytes 786440 | tf_op jit(solution)/shard_map/ppermute | solution.py:45
  22.1 3.1 %collective-permute-start.3 = (bf16[128,512]{1,0:T(8,128)(2,1)S(1)}, bf16[128,512]{1,0:T(8,128)(2,1)S(1)}, u32[]{:S(2)}, u32[]{:S(2)}) collective-permute-start(bf16[128,512]{1,0:T(8,128)(2,1)S(1)} %get-tuple-element.33), channel_id=1, source_target_pairs={{0,1},{1,0},{2,3},{3,2},{4,5},{5,4},{6,7},{7,6},{8,9},{9,8},{10,11... | collective-permute-start | bytes 393224 | tf_op jit(solution)/shard_map/ppermute | solution.py:32
  24.1 1.3 %collective-permute-start.4 = (bf16[128,512]{1,0:T(8,128)(2,1)S(1)}, bf16[128,512]{1,0:T(8,128)(2,1)S(1)}, u32[]{:S(2)}, u32[]{:S(2)}) collective-permute-start(bf16[128,512]{1,0:T(8,128)(2,1)S(1)} %get-tuple-element.34), channel_id=1, source_target_pairs={{0,1},{1,0},{2,3},{3,2},{4,5},{5,4},{6,7},{7,6},{8,9},{9,8},{10,11... | collective-permute-start | bytes 393224 | tf_op jit(solution)/shard_map/ppermute | solution.py:32
  25.5 10.9 %collective-permute-start.8 = (bf16[272,1024]{1,0:T(8,128)(2,1)S(1)}, bf16[272,1024]{1,0:T(8,128)(2,1)S(1)}, u32[]{:S(2)}, u32[]{:S(2)}) collective-permute-start(bf16[272,1024]{1,0:T(8,128)(2,1)S(1)} %join.1.refs_8_), channel_id=1, source_target_pairs={{0,16},{1,5},{2,18},{3,7},{4,20},{5,9},{6,22},{7,11},{8,24},{9,13}... | collective-permute-start | bytes 1671176 | tf_op jit(solution)/shard_map/ppermute | solution.py:45
  27.8 8.7 %collective-permute-start.9 = (bf16[272,1024]{1,0:T(8,128)(2,1)S(1)}, bf16[272,1024]{1,0:T(8,128)(2,1)S(1)}, u32[]{:S(2)}, u32[]{:S(2)}) collective-permute-start(bf16[272,1024]{1,0:T(8,128)(2,1)S(1)} %join.1.refs_8_), channel_id=1, source_target_pairs={{0,48},{1,13},{2,50},{3,15},{4,52},{5,1},{6,54},{7,3},{8,56},{9,5}... | collective-permute-start | bytes 1671176 | tf_op jit(solution)/shard_map/ppermute | solution.py:45
  29.3 3.2 %collective-permute-start.7 = (bf16[64,4096]{1,0:T(8,128)(2,1)S(1)}, bf16[64,4096]{1,0:T(8,128)(2,1)S(1)}, u32[]{:S(2)}, u32[]{:S(2)}) collective-permute-start(bf16[64,4096]{1,0:T(8,128)(2,1)S(1)} %collective-permute-done.1.refs_0_.refs_2_), channel_id=1, source_target_pairs={{0,1},{1,0},{2,3},{3,2},{4,5},{5,4},{6,7},{7,6},{8,9},{9,8},{10,11... | collective-permute-start | bytes 1572872 | tf_op jit(solution)/shard_map/ppermute | solution.py:32
  37.5 18.6 %collective-permute-start.11 = (bf16[256,1024]{1,0:T(8,128)(2,1)S(1)}, bf16[256,1024]{1,0:T(8,128)(2,1)S(1)}, u32[]{:S(2)}, u32[]{:S(2)}) collective-permute-start(bf16[256,1024]{1,0:T(8,128)(2,1)S(1)} %get-tuple-element.43), channel_id=1, source_target_pairs={{0,32},{1,9},{2,34},{3,11},{4,36},{5,13},{6,38},{7,15},{8,40},{9,1... | collective-permute-start | bytes 1572872 | tf_op jit(solution)/shard_map/ppermute | solution.py:45
  40.2 15.9 %collective-permute-start.12 = (bf16[256,1024]{1,0:T(8,128)(2,1)S(1)}, bf16[256,1024]{1,0:T(8,128)(2,1)S(1)}, u32[]{:S(2)}, u32[]{:S(2)}) collective-permute-start(bf16[256,1024]{1,0:T(8,128)(2,1)S(1)} %get-tuple-element.44), channel_id=1, source_target_pairs={{0,16},{1,5},{2,18},{3,7},{4,20},{5,9},{6,22},{7,11},{8,24},{9,13}... | collective-permute-start | bytes 1572872 | tf_op jit(solution)/shard_map/ppermute | solution.py:45
  40.9 15.2 %collective-permute-start.13 = (bf16[256,1024]{1,0:T(8,128)(2,1)S(1)}, bf16[256,1024]{1,0:T(8,128)(2,1)S(1)}, u32[]{:S(2)}, u32[]{:S(2)}) collective-permute-start(bf16[256,1024]{1,0:T(8,128)(2,1)S(1)} %get-tuple-element.45), channel_id=1, source_target_pairs={{0,48},{1,13},{2,50},{3,15},{4,52},{5,1},{6,54},{7,3},{8,56},{9,5}... | collective-permute-start | bytes 1572872 | tf_op jit(solution)/shard_map/ppermute | solution.py:45
  53.3 2.9 %collective-permute-start.10 = (f32[64,128]{1,0:T(8,128)S(1)}, f32[64,128]{1,0:T(8,128)S(1)}, u32[]{:S(2)}, u32[]{:S(2)}) collective-permute-start(f32[64,128]{1,0:T(8,128)S(1)} %filter_grad.1), channel_id=1, source_target_pairs={{0,16},{1,5},{2,18},{3,7},{4,20},{5,1},{6,22},{7,3},{8,24},{9,13},... | collective-permute-start | bytes 98312 | tf_op jit(solution)/shard_map/ppermute | solution.py:45
  59.2 18.2 %collective-permute-start.17 = (bf16[256,1024]{1,0:T(8,128)(2,1)S(1)}, bf16[256,1024]{1,0:T(8,128)(2,1)S(1)}, u32[]{:S(2)}, u32[]{:S(2)}) collective-permute-start(bf16[256,1024]{1,0:T(8,128)(2,1)S(1)} %get-tuple-element.49), channel_id=1, source_target_pairs={{0,4},{1,17},{2,6},{3,19},{4,8},{5,21},{6,10},{7,23},{8,12},{9,25}... | collective-permute-start | bytes 1572872 | tf_op jit(solution)/shard_map/ppermute | solution.py:45
  60.5 16.9 %collective-permute-start.18 = (bf16[256,1024]{1,0:T(8,128)(2,1)S(1)}, bf16[256,1024]{1,0:T(8,128)(2,1)S(1)}, u32[]{:S(2)}, u32[]{:S(2)}) collective-permute-start(bf16[256,1024]{1,0:T(8,128)(2,1)S(1)} %get-tuple-element.50), channel_id=1, source_target_pairs={{0,8},{1,33},{2,10},{3,35},{4,12},{5,37},{6,14},{7,39},{8,0},{9,41... | collective-permute-start | bytes 1572872 | tf_op jit(solution)/shard_map/ppermute | solution.py:45
  63.0 14.5 %collective-permute-start.19 = (bf16[256,1024]{1,0:T(8,128)(2,1)S(1)}, bf16[256,1024]{1,0:T(8,128)(2,1)S(1)}, u32[]{:S(2)}, u32[]{:S(2)}) collective-permute-start(bf16[256,1024]{1,0:T(8,128)(2,1)S(1)} %get-tuple-element.51), channel_id=1, source_target_pairs={{0,12},{1,49},{2,14},{3,51},{4,0},{5,53},{6,2},{7,55},{8,4},{9,57}... | collective-permute-start | bytes 1572872 | tf_op jit(solution)/shard_map/ppermute | solution.py:45
  64.1 2.8 %collective-permute-start.14 = (f32[64,128]{1,0:T(8,128)S(1)}, f32[64,128]{1,0:T(8,128)S(1)}, u32[]{:S(2)}, u32[]{:S(2)}) collective-permute-start(f32[64,128]{1,0:T(8,128)S(1)} %add.18.refs_13_), channel_id=1, source_target_pairs={{0,64},{64,0},{128,192},{192,128},{1,65},{65,1},{129,193},{193,129... | collective-permute-start | bytes 98312 | tf_op jit(solution)/shard_map/ppermute | solution.py:489
  66.9 4.0 %collective-permute-start.15 = (f32[64,128]{1,0:T(8,128)S(1)}, f32[64,128]{1,0:T(8,128)S(1)}, u32[]{:S(2)}, u32[]{:S(2)}) collective-permute-start(f32[64,128]{1,0:T(8,128)S(1)} %add.19), channel_id=1, source_target_pairs={{0,128},{64,192},{128,0},{192,64},{1,129},{65,193},{129,1},{193,65... | collective-permute-start | bytes 98312 | tf_op jit(solution)/shard_map/ppermute | solution.py:489
  70.9 15.9 %collective-permute-start.16 = (bf16[128,1024]{1,0:T(8,128)(2,1)S(1)}, bf16[128,1024]{1,0:T(8,128)(2,1)S(1)}, u32[]{:S(2)}, u32[]{:S(2)}) collective-permute-start(bf16[128,1024]{1,0:T(8,128)(2,1)S(1)} %slice.11), channel_id=1, source_target_pairs={{4,0},{8,4},{12,8},{16,12},{20,16},{24,20},{28,24},{32,28},{36,32}... | collective-permute-start | bytes 786440 | tf_op jit(solution)/shard_map/ppermute | solution.py:54
  72.1 5.3 %collective-permute-start.20 = (f32[64,128]{1,0:T(8,128)S(1)}, f32[64,128]{1,0:T(8,128)S(1)}, u32[]{:S(2)}, u32[]{:S(2)}) collective-permute-start(f32[64,128]{1,0:T(8,128)S(1)} %add.20), channel_id=1, source_target_pairs={{0,32},{1,9},{2,34},{3,11},{4,36},{5,13},{6,38},{7,15},{8,40},{9,1... | collective-permute-start | bytes 98312 | tf_op jit(solution)/shard_map/ppermute | solution.py:45
  77.9 12.3 %collective-permute-start.21 = (bf16[64,1024]{1,0:T(8,128)(2,1)S(1)}, bf16[64,1024]{1,0:T(8,128)(2,1)S(1)}, u32[]{:S(2)}, u32[]{:S(2)}) collective-permute-start(bf16[64,1024]{1,0:T(8,128)(2,1)S(1)} %get-tuple-element.54), channel_id=1, source_target_pairs={{0,64},{64,128},{128,192},{192,0},{1,65},{65,129},{129,193},{193,1... | collective-permute-start | bytes 393224 | tf_op jit(solution)/shard_map/ppermute | solution.py:529
  78.9 11.3 %collective-permute-start.22 = (bf16[64,1024]{1,0:T(8,128)(2,1)S(1)}, bf16[64,1024]{1,0:T(8,128)(2,1)S(1)}, u32[]{:S(2)}, u32[]{:S(2)}) collective-permute-start(bf16[64,1024]{1,0:T(8,128)(2,1)S(1)} %get-tuple-element.55), channel_id=1, source_target_pairs={{0,128},{64,192},{128,0},{192,64},{1,129},{65,193},{129,1},{193,65... | collective-permute-start | bytes 393224 | tf_op jit(solution)/shard_map/ppermute | solution.py:529
  79.9 10.3 %collective-permute-start.23 = (bf16[64,1024]{1,0:T(8,128)(2,1)S(1)}, bf16[64,1024]{1,0:T(8,128)(2,1)S(1)}, u32[]{:S(2)}, u32[]{:S(2)}) collective-permute-start(bf16[64,1024]{1,0:T(8,128)(2,1)S(1)} %get-tuple-element.56), channel_id=1, source_target_pairs={{0,192},{64,0},{128,64},{192,128},{1,193},{65,1},{129,65},{193,129... | collective-permute-start | bytes 393224 | tf_op jit(solution)/shard_map/ppermute | solution.py:529
  81.7 3.1 %collective-permute-start.25 = (f32[64,128]{1,0:T(8,128)S(1)}, f32[64,128]{1,0:T(8,128)S(1)}, u32[]{:S(2)}, u32[]{:S(2)}) collective-permute-start(f32[64,128]{1,0:T(8,128)S(1)} %add.21.refs_4_), channel_id=1, source_target_pairs={{0,4},{1,17},{2,6},{3,19},{4,0},{5,21},{6,2},{7,23},{8,12},{9,25},... | collective-permute-start | bytes 98312 | tf_op jit(solution)/shard_map/ppermute | solution.py:45
  84.8 15.6 %collective-permute-start.26 = (f32[64,128]{1,0:T(8,128)S(1)}, f32[64,128]{1,0:T(8,128)S(1)}, u32[]{:S(2)}, u32[]{:S(2)}) collective-permute-start(f32[64,128]{1,0:T(8,128)S(1)} %add.22), channel_id=1, source_target_pairs={{0,8},{1,33},{2,10},{3,35},{4,12},{5,37},{6,14},{7,39},{8,0},{9,41... | collective-permute-start | bytes 98312 | tf_op jit(solution)/shard_map/ppermute | solution.py:45
  90.3 11.1 %collective-permute-start.24 = (f32[64,512]{1,0:T(8,128)S(1)}, f32[64,512]{1,0:T(8,128)S(1)}, u32[]{:S(2)}, u32[]{:S(2)}) collective-permute-start(f32[64,512]{1,0:T(8,128)S(1)} %get-tuple-element.58), channel_id=1, source_target_pairs={{0,1},{1,0},{2,3},{3,2},{4,5},{5,4},{6,7},{7,6},{8,9},{9,8},{10,11... | collective-permute-start | bytes 393224 | tf_op jit(solution)/shard_map/ppermute | solution.py:32

commit v11 on v9

--- a/solution.py
+++ b/solution.py
@@ -519,12 +519,13 @@
 
     filter_sum = paired_z(paired_z(tied(filter_sum, parts[0]), 1), 2)
     following = shifted(tied(conv_grad[:TAPS], filter_sum), -1)
-    filter_sum = paired(paired(filter_sum, True, 1), True, 2)
+    filter_sum = paired(filter_sum, True, 1)
     parts = [parts[0]] + [stepped(parts[s], False, s) for s in shifts]
     sums = first_sum(parts, (filter_sum,))
-    filter_sum = paired(paired(filter_sum, False, 1, (sums[0],)), False, 2)
+    grad_input = input_grad(filters, conv_grad, following, (sums[0],))
+    filter_sum = paired(filter_sum, True, 2, (sums[0],))
+    filter_sum = paired(paired(filter_sum, False, 1, (resident(grad_input),)), False, 2)
     grad_filter = filter_sum * (1.0 / math.sqrt(tokens_all * GROUP))
-    grad_input = input_grad(filters, conv_grad, following, (sums[0],))
     line = [[(i, (i + s) % SIDE) for i in range(SIDE)] for s in shifts]
     sums = [sums[0]] + [lax.ppermute(sums[s], "dp", line[s - 1]) for s in shifts]
     kept, given = last_sum(sums, 1.0 / math.sqrt(tokens_all), (resident(grad_input),))

time: 98.3 us -> 101 us (1.027)
  waiting for transfers between devices: 33 us -> 36.4 us
    ppermute x14, waiting for transfers between devices: 16.1 us -> 19.5 us  [in_plane(): return lax.ppermute(x, ('ctx', 'tp'), pairs)]
  transfers between devices with their start and end apart: 27 -> 27, of which waited for: 14 -> 15; matrix products, arithmetic and copies ran while one was open for 2% -> 2% of each run, Pallas kernels for 20% -> 19%
where the time goes in v11:
time: 101 us; the launch traced here: 99.9 us
  starting transfers between devices  38.1 us (38%)
  waiting for transfers between devices  36.4 us (36%)
  Pallas kernels  22.9 us (23%)
    ppermute x14, waiting for transfers between devices, in_plane(): return lax.ppermute(x, ('ctx', 'tp'), pairs)  19.5 us
    ppermute x14, starting transfers between devices, in_plane(): return lax.ppermute(x, ('ctx', 'tp'), pairs)  16.6 us
    pallas_call x10, Pallas kernels, once(): pl.pallas_call(body, grid=(1,), in_specs=specs + [ANYWHERE] * len(after),...  16.3 us
    ppermute x6, starting transfers between devices, moved(): return lax.ppermute(x, 'tp', [(i, i ^ step) for i in range(4)])  8.06 us
    pallas_call x1, Pallas kernels, project(): pl.pallas_call(body, grid=(channels // WIDE,), in_specs=[full(early.shape...  6.59 us
    ppermute x2, starting transfers between devices, shifted(): lax.ppermute(x, 'ctx', [(i, i + by) for i in range(devices) if 0 <= i + b...  6.53 us
    ppermute x2, waiting for transfers between devices, paired_z(): return x + lax.ppermute(x, 'dp', [(i, i ^ by) for i in range(SIDE)])  6.21 us
    ppermute x2, waiting for transfers between devices, shifted(): lax.ppermute(x, 'ctx', [(i, i + by) for i in range(devices) if 0 <= i + b...  5.67 us
  transfers between devices with their start and end apart: 27, of which 15 were waited for; matrix products, arithmetic and copies ran while one was open for 2% of the time, Pallas kernels for 19%

profile of v11, /device:TPU:2, one launch (start us, length us, event | category | flops | bytes accessed | tf_op | source)
XLA Modules:
  0.0 99.9 jit_solution(12014921210289927420)
XLA Ops:
  0.7 7.3 %collective-permute-start.1 = (bf16[64,4096]{1,0:T(8,128)(2,1)}, bf16[64,4096]{1,0:T(8,128)(2,1)S(1)}, u32[]{:S(2)}, u32[]{:S(2)}) collective-permute-start(bf16[64,4096]{1,0:T(8,128)(2,1)} %bitcast.11), channel_id=1, source_target_pairs={{0,2},{1,3},{2,0},{3,1},{4,6},{5,7},{6,4},{7,5},{8,10},{9,11},{10,... | collective-permute-start | bytes 1572872 | tf_op jit(solution)/shard_map/ppermute | solution.py:32
  9.0 3.5 %collective-permute-start.2 = (bf16[128,1024]{1,0:T(8,128)(2,1)S(1)}, bf16[128,1024]{1,0:T(8,128)(2,1)S(1)}, u32[]{:S(2)}, u32[]{:S(2)}) collective-permute-start(bf16[128,1024]{1,0:T(8,128)(2,1)S(1)} %slice_bitcast_fusion), channel_id=1, source_target_pairs={{0,4},{4,8},{8,12},{12,16},{16,20},{20,24},{24,28},{28,32},{32,36}... | collective-permute-start | bytes 786440 | tf_op jit(solution)/shard_map/ppermute | solution.py:54
  12.5 1.2 %pack.1 = (bf16[128,1024]{1,0:T(8,128)(2,1)S(1)}, bf16[128,1024]{1,0:T(8,128)(2,1)S(1)}, bf16[128,1024]{1,0:T(8,128)(2,1)S(1)}, bf16[128,1024]{1,0:T(8,128)(2,1)S(1)}) custom-call(bf16[64,4096]{1,0:T(8,128)(2,1)} %bitcast.12, bf16[64,4096]{1,0:T(8,128)(2,1)S(1)} %collective-permute-done.refs_1_), custom_call_target="tpu_custom_call" | custom-call | tf_op jit(solution)/shard_map/pack/pallas_call | solution.py:96
  13.7 1.6 %collective-permute-start.5 = (bf16[128,1024]{1,0:T(8,128)(2,1)S(1)}, bf16[128,1024]{1,0:T(8,128)(2,1)S(1)}, u32[]{:S(2)}, u32[]{:S(2)}) collective-permute-start(bf16[128,1024]{1,0:T(8,128)(2,1)S(1)} %get-tuple-element.36), channel_id=1, source_target_pairs={{0,16},{1,5},{2,18},{3,7},{4,20},{5,9},{6,22},{7,11},{8,24},{9,13}... | collective-permute-start | bytes 786440 | tf_op jit(solution)/shard_map/ppermute | solution.py:45
  15.8 5.7 %collective-permute-done.2.refs_1_.refs_0_ = bf16[128,1024]{1,0:T(8,128)(2,1)S(1)} collective-permute-done((bf16[128,1024]{1,0:T(8,128)(2,1)S(1)}, bf16[128,1024]{1,0:T(8,128)(2,1)S(1)}, u32[]{:S(2)}, u32[]{:S(2)}) %collective-permute-start.2) | collective-permute-done | bytes 262176 | tf_op jit(solution)/shard_map/ppermute | solution.py:54
  21.4 3.4 %conv_forward.1 = (f32[256,1024]{1,0:T(8,128)S(1)}, bf16[256,512]{1,0:T(8,128)(2,1)S(1)}, bf16[128,512]{1,0:T(8,128)(2,1)S(1)}, bf16[128,512]{1,0:T(8,128)(2,1)S(1)}) custom-call(bf16[64,128]{1,0:T(8,128)(2,1)} %refs_0_.3, bf16[128,1024]{1,0:T(8,128)(2,1)S(1)} %collective-permute-done.2.refs_1_.refs_0_, bf16[256,1024]{1,0:T(8,128)(2,1)} %bitcast.8, ...), custom_call_target="tpu_custom_call" | custom-call | tf_op jit(solution)/shard_map/conv_forward/pallas_call | solution.py:96
  26.5 1.6 %collective-permute-start.8 = (bf16[272,1024]{1,0:T(8,128)(2,1)S(1)}, bf16[272,1024]{1,0:T(8,128)(2,1)S(1)}, u32[]{:S(2)}, u32[]{:S(2)}) collective-permute-start(bf16[272,1024]{1,0:T(8,128)(2,1)S(1)} %join.1.refs_8_), channel_id=1, source_target_pairs={{0,16},{1,5},{2,18},{3,7},{4,20},{5,9},{6,22},{7,11},{8,24},{9,13}... | collective-permute-start | bytes 1671176 | tf_op jit(solution)/shard_map/ppermute | solution.py:45
  28.6 2.1 %collective-permute-done.1.refs_0_.refs_2_ = bf16[64,4096]{1,0:T(8,128)(2,1)S(1)} collective-permute-done((bf16[64,4096]{1,0:T(8,128)(2,1)}, bf16[64,4096]{1,0:T(8,128)(2,1)S(1)}, u32[]{:S(2)}, u32[]{:S(2)}) %collective-permute-start.1) | collective-permute-done | bytes 524320 | tf_op jit(solution)/shard_map/ppermute | solution.py:32
  30.7 1.9 %collective-permute-done.7.refs_1_.refs_3_ = bf16[64,4096]{1,0:T(8,128)(2,1)S(1)} collective-permute-done((bf16[64,4096]{1,0:T(8,128)(2,1)S(1)}, bf16[64,4096]{1,0:T(8,128)(2,1)S(1)}, u32[]{:S(2)}, u32[]{:S(2)}) %collective-permute-start.7) | collective-permute-done | bytes 524320 | tf_op jit(solution)/shard_map/ppermute | solution.py:32
  32.7 3.5 %collective-permute-done.8.refs_2_.refs_9_ = bf16[272,1024]{1,0:T(8,128)(2,1)S(1)} collective-permute-done((bf16[272,1024]{1,0:T(8,128)(2,1)S(1)}, bf16[272,1024]{1,0:T(8,128)(2,1)S(1)}, u32[]{:S(2)}, u32[]{:S(2)}) %collective-permute-start.8) | collective-permute-done | bytes 557088 | tf_op jit(solution)/shard_map/ppermute | solution.py:45
  36.2 1.5 %collective-permute-done.9.refs_3_.refs_12_ = bf16[272,1024]{1,0:T(8,128)(2,1)S(1)} collective-permute-done((bf16[272,1024]{1,0:T(8,128)(2,1)S(1)}, bf16[272,1024]{1,0:T(8,128)(2,1)S(1)}, u32[]{:S(2)}, u32[]{:S(2)}) %collective-permute-start.9) | collective-permute-done | bytes 557088 | tf_op jit(solution)/shard_map/ppermute | solution.py:45
  37.8 2.0 %collective-permute-start.10 = (bf16[256,1024]{1,0:T(8,128)(2,1)S(1)}, bf16[256,1024]{1,0:T(8,128)(2,1)S(1)}, u32[]{:S(2)}, u32[]{:S(2)}) collective-permute-start(bf16[256,1024]{1,0:T(8,128)(2,1)S(1)} %get-tuple-element.44), channel_id=1, source_target_pairs={{0,32},{1,9},{2,34},{3,11},{4,36},{5,13},{6,38},{7,15},{8,40},{9,1... | collective-permute-start | bytes 1572872 | tf_op jit(solution)/shard_map/ppermute | solution.py:45
  39.9 2.0 %collective-permute-start.12 = (bf16[256,1024]{1,0:T(8,128)(2,1)S(1)}, bf16[256,1024]{1,0:T(8,128)(2,1)S(1)}, u32[]{:S(2)}, u32[]{:S(2)}) collective-permute-start(bf16[256,1024]{1,0:T(8,128)(2,1)S(1)} %get-tuple-element.46), channel_id=1, source_target_pairs={{0,48},{1,13},{2,50},{3,15},{4,52},{5,1},{6,54},{7,3},{8,56},{9,5}... | collective-permute-start | bytes 1572872 | tf_op jit(solution)/shard_map/ppermute | solution.py:45
  41.9 6.6 %project.1 = (bf16[256,1024]{1,0:T(8,128)(2,1)S(1)}, bf16[256,1024]{1,0:T(8,128)(2,1)}) custom-call(bf16[64,4096]{1,0:T(8,128)(2,1)} %bitcast.13, bf16[64,4096]{1,0:T(8,128)(2,1)S(1)} %collective-permute-done.refs_1_, bf16[64,4096]{1,0:T(8,128)(2,1)S(1)} %collective-permute-done.1.refs_0_.refs_2_, ...), custom_call_target="tpu_custom_call" | custom-call | flops 6000000000 | tf_op jit(solution)/shard_map/project/pallas_call | solution.py:344
  48.5 3.8 %filter_grad.1.refs_13_ = f32[64,128]{1,0:T(8,128)S(1)} custom-call(bf16[128,1024]{1,0:T(8,128)(2,1)S(1)} %collective-permute-done.2.refs_1_.refs_0_, bf16[256,1024]{1,0:T(8,128)(2,1)} %bitcast.9, bf16[256,1024]{1,0:T(8,128)(2,1)S(1)} %get-tuple-element.42.refs_2_.refs_1_), custom_call_target="tpu_custom_call" | custom-call | flops 4000000000 | tf_op jit(solution)/shard_map/filter_grad/pallas_call | solution.py:96
  52.3 1.7 %collective-permute-done.11.refs_5_.refs_10_ = bf16[256,1024]{1,0:T(8,128)(2,1)S(1)} collective-permute-done((bf16[256,1024]{1,0:T(8,128)(2,1)S(1)}, bf16[256,1024]{1,0:T(8,128)(2,1)S(1)}, u32[]{:S(2)}, u32[]{:S(2)}) %collective-permute-start.11) | collective-permute-done | bytes 524320 | tf_op jit(solution)/shard_map/ppermute | solution.py:45
  54.2 3.1 %weight_parts.1 = (f32[256,1024]{1,0:T(8,128)S(1)}, bf16[256,1024]{1,0:T(8,128)(2,1)S(1)}, bf16[256,1024]{1,0:T(8,128)(2,1)S(1)}, bf16[256,1024]{1,0:T(8,128)(2,1)S(1)}) custom-call(bf16[128,1024]{1,0:T(8,128)(2,1)S(1)} %get-tuple-element.43.refs_0_, bf16[128,1024]{1,0:T(8,128)(2,1)S(1)} %collective-permute-done.5.refs_3_.refs_1_, ...), custom_call_target="tpu_custom_call" | custom-call | flops 4000000000 | tf_op jit(solution)/shard_map/weight_parts/pallas_call | solution.py:96
  57.5 2.9 %collective-permute-start.17 = (bf16[256,1024]{1,0:T(8,128)(2,1)S(1)}, bf16[256,1024]{1,0:T(8,128)(2,1)S(1)}, u32[]{:S(2)}, u32[]{:S(2)}) collective-permute-start(bf16[256,1024]{1,0:T(8,128)(2,1)S(1)} %get-tuple-element.51), channel_id=1, source_target_pairs={{0,8},{1,33},{2,10},{3,35},{4,12},{5,37},{6,14},{7,39},{8,0},{9,41... | collective-permute-start | bytes 1572872 | tf_op jit(solution)/shard_map/ppermute | solution.py:45
  60.4 1.3 %collective-permute-start.18 = (bf16[256,1024]{1,0:T(8,128)(2,1)S(1)}, bf16[256,1024]{1,0:T(8,128)(2,1)S(1)}, u32[]{:S(2)}, u32[]{:S(2)}) collective-permute-start(bf16[256,1024]{1,0:T(8,128)(2,1)S(1)} %get-tuple-element.52), channel_id=1, source_target_pairs={{0,12},{1,49},{2,14},{3,51},{4,0},{5,53},{6,2},{7,55},{8,4},{9,57}... | collective-permute-start | bytes 1572872 | tf_op jit(solution)/shard_map/ppermute | solution.py:45
  62.8 2.9 %collective-permute-done.13 = f32[64,128]{1,0:T(8,128)S(1)} collective-permute-done((f32[64,128]{1,0:T(8,128)S(1)}, f32[64,128]{1,0:T(8,128)S(1)}, u32[]{:S(2)}, u32[]{:S(2)}) %collective-permute-start.13) | collective-permute-done | bytes 32800 | tf_op jit(solution)/shard_map/ppermute | solution.py:489
  65.7 1.5 %collective-permute-start.14 = (f32[64,128]{1,0:T(8,128)S(1)}, f32[64,128]{1,0:T(8,128)S(1)}, u32[]{:S(2)}, u32[]{:S(2)}) collective-permute-start(f32[64,128]{1,0:T(8,128)S(1)} %add.18), channel_id=1, source_target_pairs={{0,128},{64,192},{128,0},{192,64},{1,129},{65,193},{129,1},{193,65... | collective-permute-start | bytes 98312 | tf_op jit(solution)/shard_map/ppermute | solution.py:489
  67.2 3.3 %collective-permute-done.14 = f32[64,128]{1,0:T(8,128)S(1)} collective-permute-done((f32[64,128]{1,0:T(8,128)S(1)}, f32[64,128]{1,0:T(8,128)S(1)}, u32[]{:S(2)}, u32[]{:S(2)}) %collective-permute-start.14) | collective-permute-done | bytes 32800 | tf_op jit(solution)/shard_map/ppermute | solution.py:489
  70.5 3.0 %collective-permute-start.15 = (bf16[128,1024]{1,0:T(8,128)(2,1)S(1)}, bf16[128,1024]{1,0:T(8,128)(2,1)S(1)}, u32[]{:S(2)}, u32[]{:S(2)}) collective-permute-start(bf16[128,1024]{1,0:T(8,128)(2,1)S(1)} %slice.11), channel_id=1, source_target_pairs={{4,0},{8,4},{12,8},{16,12},{20,16},{24,20},{28,24},{32,28},{36,32}... | collective-permute-start | bytes 786440 | tf_op jit(solution)/shard_map/ppermute | solution.py:54
  73.7 5.2 %collective-permute-done.19 = f32[64,128]{1,0:T(8,128)S(1)} collective-permute-done((f32[64,128]{1,0:T(8,128)S(1)}, f32[64,128]{1,0:T(8,128)S(1)}, u32[]{:S(2)}, u32[]{:S(2)}) %collective-permute-start.19) | collective-permute-done | bytes 32800 | tf_op jit(solution)/shard_map/ppermute | solution.py:45
  79.3 1.1 %collective-permute-start.20 = (bf16[64,1024]{1,0:T(8,128)(2,1)S(1)}, bf16[64,1024]{1,0:T(8,128)(2,1)S(1)}, u32[]{:S(2)}, u32[]{:S(2)}) collective-permute-start(bf16[64,1024]{1,0:T(8,128)(2,1)S(1)} %get-tuple-element.55), channel_id=1, source_target_pairs={{0,64},{64,128},{128,192},{192,0},{1,65},{65,129},{129,193},{193,1... | collective-permute-start | bytes 393224 | tf_op jit(solution)/shard_map/ppermute | solution.py:530
  80.4 1.5 %collective-permute-start.21 = (bf16[64,1024]{1,0:T(8,128)(2,1)S(1)}, bf16[64,1024]{1,0:T(8,128)(2,1)S(1)}, u32[]{:S(2)}, u32[]{:S(2)}) collective-permute-start(bf16[64,1024]{1,0:T(8,128)(2,1)S(1)} %get-tuple-element.56), channel_id=1, source_target_pairs={{0,128},{64,192},{128,0},{192,64},{1,129},{65,193},{129,1},{193,65... | collective-permute-start | bytes 393224 | tf_op jit(solution)/shard_map/ppermute | solution.py:530
  81.9 1.9 %collective-permute-start.22 = (bf16[64,1024]{1,0:T(8,128)(2,1)S(1)}, bf16[64,1024]{1,0:T(8,128)(2,1)S(1)}, u32[]{:S(2)}, u32[]{:S(2)}) collective-permute-start(bf16[64,1024]{1,0:T(8,128)(2,1)S(1)} %get-tuple-element.57), channel_id=1, source_target_pairs={{0,192},{64,0},{128,64},{192,128},{1,193},{65,1},{129,65},{193,129... | collective-permute-start | bytes 393224 | tf_op jit(solution)/shard_map/ppermute | solution.py:530
  84.3 3.4 %input_grad.1.refs_4_ = bf16[256,1024]{1,0:T(8,128)(2,1)} custom-call(bf16[64,128]{1,0:T(8,128)(2,1)} %refs_0_.3, bf16[256,1024]{1,0:T(8,128)(2,1)S(1)} %get-tuple-element.42.refs_2_.refs_1_, bf16[128,1024]{1,0:T(8,128)(2,1)S(1)} %collective-permute-done.15.refs_2_, f32[64,1024]{1,0:T(8,128)S(1)} %get-tuple-element.53.refs_3_.refs_0_), custom_call_target="tpu_custom_call" | custom-call | tf_op jit(solution)/shard_map/input_grad/pallas_call | solution.py:96
  87.7 1.5 %collective-permute-done.24 = f32[64,128]{1,0:T(8,128)S(1)} collective-permute-done((f32[64,128]{1,0:T(8,128)S(1)}, f32[64,128]{1,0:T(8,128)S(1)}, u32[]{:S(2)}, u32[]{:S(2)}) %collective-permute-start.24) | collective-permute-done | bytes 32800 | tf_op jit(solution)/shard_map/ppermute | solution.py:45
  89.2 3.9 %collective-permute-done.25 = f32[64,128]{1,0:T(8,128)S(1)} collective-permute-done((f32[64,128]{1,0:T(8,128)S(1)}, f32[64,128]{1,0:T(8,128)S(1)}, u32[]{:S(2)}, u32[]{:S(2)}) %collective-permute-start.25) | collective-permute-done | bytes 32800 | tf_op jit(solution)/shard_map/ppermute | solution.py:45
  93.1 3.1 %collective-permute-start.26 = (f32[64,128]{1,0:T(8,128)S(1)}, f32[64,128]{1,0:T(8,128)S(1)}, u32[]{:S(2)}, u32[]{:S(2)}) collective-permute-start(f32[64,128]{1,0:T(8,128)S(1)} %add.22), channel_id=1, source_target_pairs={{0,8},{1,33},{2,10},{3,35},{4,12},{5,37},{6,14},{7,39},{8,0},{9,41... | collective-permute-start | bytes 98312 | tf_op jit(solution)/shard_map/ppermute | solution.py:45
  96.5 2.0 %collective-permute-done.26 = f32[64,128]{1,0:T(8,128)S(1)} collective-permute-done((f32[64,128]{1,0:T(8,128)S(1)}, f32[64,128]{1,0:T(8,128)S(1)}, u32[]{:S(2)}, u32[]{:S(2)}) %collective-permute-start.26) | collective-permute-done | bytes 32800 | tf_op jit(solution)/shard_map/ppermute | solution.py:45
  (41 shorter events, 8.2 us)
Async XLA Ops:
  0.6 11.8 %collective-permute-start = (bf16[64,4096]{1,0:T(8,128)(2,1)}, bf16[64,4096]{1,0:T(8,128)(2,1)S(1)}, u32[]{:S(2)}, u32[]{:S(2)}) collective-permute-start(bf16[64,4096]{1,0:T(8,128)(2,1)} %bitcast.10), channel_id=1, source_target_pairs={{0,1},{1,0},{2,3},{3,2},{4,5},{5,4},{6,7},{7,6},{8,9},{9,8},{10,11... | collective-permute-start | bytes 1572872 | tf_op jit(solution)/shard_map/ppermute | solution.py:32
  0.7 30.0 %collective-permute-start.1 = (bf16[64,4096]{1,0:T(8,128)(2,1)}, bf16[64,4096]{1,0:T(8,128)(2,1)S(1)}, u32[]{:S(2)}, u32[]{:S(2)}) collective-permute-start(bf16[64,4096]{1,0:T(8,128)(2,1)} %bitcast.11), channel_id=1, source_target_pairs={{0,2},{1,3},{2,0},{3,1},{4,6},{5,7},{6,4},{7,5},{8,10},{9,11},{10,... | collective-permute-start | bytes 1572872 | tf_op jit(solution)/shard_map/ppermute | solution.py:32
  9.0 12.5 %collective-permute-start.2 = (bf16[128,1024]{1,0:T(8,128)(2,1)S(1)}, bf16[128,1024]{1,0:T(8,128)(2,1)S(1)}, u32[]{:S(2)}, u32[]{:S(2)}) collective-permute-start(bf16[128,1024]{1,0:T(8,128)(2,1)S(1)} %slice_bitcast_fusion), channel_id=1, source_target_pairs={{0,4},{4,8},{8,12},{12,16},{16,20},{20,24},{24,28},{28,32},{32,36}... | collective-permute-start | bytes 786440 | tf_op jit(solution)/shard_map/ppermute | solution.py:54
  13.7 12.8 %collective-permute-start.5 = (bf16[128,1024]{1,0:T(8,128)(2,1)S(1)}, bf16[128,1024]{1,0:T(8,128)(2,1)S(1)}, u32[]{:S(2)}, u32[]{:S(2)}) collective-permute-start(bf16[128,1024]{1,0:T(8,128)(2,1)S(1)} %get-tuple-element.36), channel_id=1, source_target_pairs={{0,16},{1,5},{2,18},{3,7},{4,20},{5,9},{6,22},{7,11},{8,24},{9,13}... | collective-permute-start | bytes 786440 | tf_op jit(solution)/shard_map/ppermute | solution.py:45
  15.2 11.2 %collective-permute-start.6 = (bf16[128,1024]{1,0:T(8,128)(2,1)S(1)}, bf16[128,1024]{1,0:T(8,128)(2,1)S(1)}, u32[]{:S(2)}, u32[]{:S(2)}) collective-permute-start(bf16[128,1024]{1,0:T(8,128)(2,1)S(1)} %get-tuple-element.37), channel_id=1, source_target_pairs={{0,48},{1,13},{2,50},{3,15},{4,52},{5,1},{6,54},{7,3},{8,56},{9,5}... | collective-permute-start | bytes 786440 | tf_op jit(solution)/shard_map/ppermute | solution.py:45
  24.9 1.4 %collective-permute-start.3 = (bf16[128,512]{1,0:T(8,128)(2,1)S(1)}, bf16[128,512]{1,0:T(8,128)(2,1)S(1)}, u32[]{:S(2)}, u32[]{:S(2)}) collective-permute-start(bf16[128,512]{1,0:T(8,128)(2,1)S(1)} %get-tuple-element.34), channel_id=1, source_target_pairs={{0,1},{1,0},{2,3},{3,2},{4,5},{5,4},{6,7},{7,6},{8,9},{9,8},{10,11... | collective-permute-start | bytes 393224 | tf_op jit(solution)/shard_map/ppermute | solution.py:32
  25.0 1.5 %collective-permute-start.4 = (bf16[128,512]{1,0:T(8,128)(2,1)S(1)}, bf16[128,512]{1,0:T(8,128)(2,1)S(1)}, u32[]{:S(2)}, u32[]{:S(2)}) collective-permute-start(bf16[128,512]{1,0:T(8,128)(2,1)S(1)} %get-tuple-element.35), channel_id=1, source_target_pairs={{0,1},{1,0},{2,3},{3,2},{4,5},{5,4},{6,7},{7,6},{8,9},{9,8},{10,11... | collective-permute-start | bytes 393224 | tf_op jit(solution)/shard_map/ppermute | solution.py:32
  26.5 9.6 %collective-permute-start.8 = (bf16[272,1024]{1,0:T(8,128)(2,1)S(1)}, bf16[272,1024]{1,0:T(8,128)(2,1)S(1)}, u32[]{:S(2)}, u32[]{:S(2)}) collective-permute-start(bf16[272,1024]{1,0:T(8,128)(2,1)S(1)} %join.1.refs_8_), channel_id=1, source_target_pairs={{0,16},{1,5},{2,18},{3,7},{4,20},{5,9},{6,22},{7,11},{8,24},{9,13}... | collective-permute-start | bytes 1671176 | tf_op jit(solution)/shard_map/ppermute | solution.py:45
  28.1 9.5 %collective-permute-start.9 = (bf16[272,1024]{1,0:T(8,128)(2,1)S(1)}, bf16[272,1024]{1,0:T(8,128)(2,1)S(1)}, u32[]{:S(2)}, u32[]{:S(2)}) collective-permute-start(bf16[272,1024]{1,0:T(8,128)(2,1)S(1)} %join.1.refs_8_), channel_id=1, source_target_pairs={{0,48},{1,13},{2,50},{3,15},{4,52},{5,1},{6,54},{7,3},{8,56},{9,5}... | collective-permute-start | bytes 1671176 | tf_op jit(solution)/shard_map/ppermute | solution.py:45
  30.7 1.9 %collective-permute-start.7 = (bf16[64,4096]{1,0:T(8,128)(2,1)S(1)}, bf16[64,4096]{1,0:T(8,128)(2,1)S(1)}, u32[]{:S(2)}, u32[]{:S(2)}) collective-permute-start(bf16[64,4096]{1,0:T(8,128)(2,1)S(1)} %collective-permute-done.1.refs_0_.refs_2_), channel_id=1, source_target_pairs={{0,1},{1,0},{2,3},{3,2},{4,5},{5,4},{6,7},{7,6},{8,9},{9,8},{10,11... | collective-permute-start | bytes 1572872 | tf_op jit(solution)/shard_map/ppermute | solution.py:32
  37.8 14.4 %collective-permute-start.10 = (bf16[256,1024]{1,0:T(8,128)(2,1)S(1)}, bf16[256,1024]{1,0:T(8,128)(2,1)S(1)}, u32[]{:S(2)}, u32[]{:S(2)}) collective-permute-start(bf16[256,1024]{1,0:T(8,128)(2,1)S(1)} %get-tuple-element.44), channel_id=1, source_target_pairs={{0,32},{1,9},{2,34},{3,11},{4,36},{5,13},{6,38},{7,15},{8,40},{9,1... | collective-permute-start | bytes 1572872 | tf_op jit(solution)/shard_map/ppermute | solution.py:45
  39.9 14.2 %collective-permute-start.11 = (bf16[256,1024]{1,0:T(8,128)(2,1)S(1)}, bf16[256,1024]{1,0:T(8,128)(2,1)S(1)}, u32[]{:S(2)}, u32[]{:S(2)}) collective-permute-start(bf16[256,1024]{1,0:T(8,128)(2,1)S(1)} %get-tuple-element.45), channel_id=1, source_target_pairs={{0,16},{1,5},{2,18},{3,7},{4,20},{5,9},{6,22},{7,11},{8,24},{9,13}... | collective-permute-start | bytes 1572872 | tf_op jit(solution)/shard_map/ppermute | solution.py:45
  39.9 14.3 %collective-permute-start.12 = (bf16[256,1024]{1,0:T(8,128)(2,1)S(1)}, bf16[256,1024]{1,0:T(8,128)(2,1)S(1)}, u32[]{:S(2)}, u32[]{:S(2)}) collective-permute-start(bf16[256,1024]{1,0:T(8,128)(2,1)S(1)} %get-tuple-element.46), channel_id=1, source_target_pairs={{0,48},{1,13},{2,50},{3,15},{4,52},{5,1},{6,54},{7,3},{8,56},{9,5}... | collective-permute-start | bytes 1572872 | tf_op jit(solution)/shard_map/ppermute | solution.py:45
  57.3 21.5 %collective-permute-start.16 = (bf16[256,1024]{1,0:T(8,128)(2,1)S(1)}, bf16[256,1024]{1,0:T(8,128)(2,1)S(1)}, u32[]{:S(2)}, u32[]{:S(2)}) collective-permute-start(bf16[256,1024]{1,0:T(8,128)(2,1)S(1)} %get-tuple-element.50), channel_id=1, source_target_pairs={{0,4},{1,17},{2,6},{3,19},{4,8},{5,21},{6,10},{7,23},{8,12},{9,25}... | collective-permute-start | bytes 1572872 | tf_op jit(solution)/shard_map/ppermute | solution.py:45
  57.5 21.3 %collective-permute-start.17 = (bf16[256,1024]{1,0:T(8,128)(2,1)S(1)}, bf16[256,1024]{1,0:T(8,128)(2,1)S(1)}, u32[]{:S(2)}, u32[]{:S(2)}) collective-permute-start(bf16[256,1024]{1,0:T(8,128)(2,1)S(1)} %get-tuple-element.51), channel_id=1, source_target_pairs={{0,8},{1,33},{2,10},{3,35},{4,12},{5,37},{6,14},{7,39},{8,0},{9,41... | collective-permute-start | bytes 1572872 | tf_op jit(solution)/shard_map/ppermute | solution.py:45
  60.4 18.4 %collective-permute-start.18 = (bf16[256,1024]{1,0:T(8,128)(2,1)S(1)}, bf16[256,1024]{1,0:T(8,128)(2,1)S(1)}, u32[]{:S(2)}, u32[]{:S(2)}) collective-permute-start(bf16[256,1024]{1,0:T(8,128)(2,1)S(1)} %get-tuple-element.52), channel_id=1, source_target_pairs={{0,12},{1,49},{2,14},{3,51},{4,0},{5,53},{6,2},{7,55},{8,4},{9,57}... | collective-permute-start | bytes 1572872 | tf_op jit(solution)/shard_map/ppermute | solution.py:45
  61.8 3.9 %collective-permute-start.13 = (f32[64,128]{1,0:T(8,128)S(1)}, f32[64,128]{1,0:T(8,128)S(1)}, u32[]{:S(2)}, u32[]{:S(2)}) collective-permute-start(f32[64,128]{1,0:T(8,128)S(1)} %filter_grad.1.refs_13_), channel_id=1, source_target_pairs={{0,64},{64,0},{128,192},{192,128},{1,65},{65,1},{129,193},{193,129... | collective-permute-start | bytes 98312 | tf_op jit(solution)/shard_map/ppermute | solution.py:489
  65.7 4.8 %collective-permute-start.14 = (f32[64,128]{1,0:T(8,128)S(1)}, f32[64,128]{1,0:T(8,128)S(1)}, u32[]{:S(2)}, u32[]{:S(2)}) collective-permute-start(f32[64,128]{1,0:T(8,128)S(1)} %add.18), channel_id=1, source_target_pairs={{0,128},{64,192},{128,0},{192,64},{1,129},{65,193},{129,1},{193,65... | collective-permute-start | bytes 98312 | tf_op jit(solution)/shard_map/ppermute | solution.py:489
  70.5 13.8 %collective-permute-start.15 = (bf16[128,1024]{1,0:T(8,128)(2,1)S(1)}, bf16[128,1024]{1,0:T(8,128)(2,1)S(1)}, u32[]{:S(2)}, u32[]{:S(2)}) collective-permute-start(bf16[128,1024]{1,0:T(8,128)(2,1)S(1)} %slice.11), channel_id=1, source_target_pairs={{4,0},{8,4},{12,8},{16,12},{20,16},{24,20},{28,24},{32,28},{36,32}... | collective-permute-start | bytes 786440 | tf_op jit(solution)/shard_map/ppermute | solution.py:54
  73.6 5.3 %collective-permute-start.19 = (f32[64,128]{1,0:T(8,128)S(1)}, f32[64,128]{1,0:T(8,128)S(1)}, u32[]{:S(2)}, u32[]{:S(2)}) collective-permute-start(f32[64,128]{1,0:T(8,128)S(1)} %add.19), channel_id=1, source_target_pairs={{0,16},{1,5},{2,18},{3,7},{4,20},{5,1},{6,22},{7,3},{8,24},{9,13},... | collective-permute-start | bytes 98312 | tf_op jit(solution)/shard_map/ppermute | solution.py:45
  79.3 16.9 %collective-permute-start.20 = (bf16[64,1024]{1,0:T(8,128)(2,1)S(1)}, bf16[64,1024]{1,0:T(8,128)(2,1)S(1)}, u32[]{:S(2)}, u32[]{:S(2)}) collective-permute-start(bf16[64,1024]{1,0:T(8,128)(2,1)S(1)} %get-tuple-element.55), channel_id=1, source_target_pairs={{0,64},{64,128},{128,192},{192,0},{1,65},{65,129},{129,193},{193,1... | collective-permute-start | bytes 393224 | tf_op jit(solution)/shard_map/ppermute | solution.py:530
  80.4 15.9 %collective-permute-start.21 = (bf16[64,1024]{1,0:T(8,128)(2,1)S(1)}, bf16[64,1024]{1,0:T(8,128)(2,1)S(1)}, u32[]{:S(2)}, u32[]{:S(2)}) collective-permute-start(bf16[64,1024]{1,0:T(8,128)(2,1)S(1)} %get-tuple-element.56), channel_id=1, source_target_pairs={{0,128},{64,192},{128,0},{192,64},{1,129},{65,193},{129,1},{193,65... | collective-permute-start | bytes 393224 | tf_op jit(solution)/shard_map/ppermute | solution.py:530
  81.9 14.4 %collective-permute-start.22 = (bf16[64,1024]{1,0:T(8,128)(2,1)S(1)}, bf16[64,1024]{1,0:T(8,128)(2,1)S(1)}, u32[]{:S(2)}, u32[]{:S(2)}) collective-permute-start(bf16[64,1024]{1,0:T(8,128)(2,1)S(1)} %get-tuple-element.57), channel_id=1, source_target_pairs={{0,192},{64,0},{128,64},{192,128},{1,193},{65,1},{129,65},{193,129... | collective-permute-start | bytes 393224 | tf_op jit(solution)/shard_map/ppermute | solution.py:530
  83.7 5.4 %collective-permute-start.24 = (f32[64,128]{1,0:T(8,128)S(1)}, f32[64,128]{1,0:T(8,128)S(1)}, u32[]{:S(2)}, u32[]{:S(2)}) collective-permute-start(f32[64,128]{1,0:T(8,128)S(1)} %add.20.refs_4_), channel_id=1, source_target_pairs={{0,32},{1,9},{2,34},{3,11},{4,36},{5,13},{6,38},{7,15},{8,40},{9,1... | collective-permute-start | bytes 98312 | tf_op jit(solution)/shard_map/ppermute | solution.py:45
  89.2 3.9 %collective-permute-start.25 = (f32[64,128]{1,0:T(8,128)S(1)}, f32[64,128]{1,0:T(8,128)S(1)}, u32[]{:S(2)}, u32[]{:S(2)}) collective-permute-start(f32[64,128]{1,0:T(8,128)S(1)} %add.21), channel_id=1, source_target_pairs={{0,4},{1,17},{2,6},{3,19},{4,0},{5,21},{6,2},{7,23},{8,12},{9,25},... | collective-permute-start | bytes 98312 | tf_op jit(solution)/shard_map/ppermute | solution.py:45
  93.1 5.4 %collective-permute-start.26 = (f32[64,128]{1,0:T(8,128)S(1)}, f32[64,128]{1,0:T(8,128)S(1)}, u32[]{:S(2)}, u32[]{:S(2)}) collective-permute-start(f32[64,128]{1,0:T(8,128)S(1)} %add.22), channel_id=1, source_target_pairs={{0,8},{1,33},{2,10},{3,35},{4,12},{5,37},{6,14},{7,39},{8,0},{9,41... | collective-permute-start | bytes 98312 | tf_op jit(solution)/shard_map/ppermute | solution.py:45
  96.4 2.8 %collective-permute-start.23 = (f32[64,512]{1,0:T(8,128)S(1)}, f32[64,512]{1,0:T(8,128)S(1)}, u32[]{:S(2)}, u32[]{:S(2)}) collective-permute-start(f32[64,512]{1,0:T(8,128)S(1)} %get-tuple-element.59), channel_id=1, source_target_pairs={{0,1},{1,0},{2,3},{3,2},{4,5},{5,4},{6,7},{7,6},{8,9},{9,8},{10,11... | collective-permute-start | bytes 393224 | tf_op jit(solution)/shard_map/ppermute | solution.py:32

commit v12 on v11

--- a/solution.py
+++ b/solution.py
@@ -520,11 +520,14 @@
     filter_sum = paired_z(paired_z(tied(filter_sum, parts[0]), 1), 2)
     following = shifted(tied(conv_grad[:TAPS], filter_sum), -1)
     filter_sum = paired(filter_sum, True, 1)
+    padded = jnp.pad(filter_sum, ((0, 3 * filter_sum.shape[0]), (0, 0)))
+    padded = in_plane(padded, True, lambda place: place ^ 2)
+    filter_sum = filter_sum + padded[: filter_sum.shape[0]]
     parts = [parts[0]] + [stepped(parts[s], False, s) for s in shifts]
-    sums = first_sum(parts, (filter_sum,))
+    sums = first_sum(parts, ())
     grad_input = input_grad(filters, conv_grad, following, (sums[0],))
-    filter_sum = paired(filter_sum, True, 2, (sums[0],))
-    filter_sum = paired(paired(filter_sum, False, 1, (resident(grad_input),)), False, 2)
+    filter_sum = paired(filter_sum, False, 1, (sums[0],))
+    filter_sum = paired(filter_sum, False, 2, (resident(grad_input),))
     grad_filter = filter_sum * (1.0 / math.sqrt(tokens_all * GROUP))
     line = [[(i, (i + s) % SIDE) for i in range(SIDE)] for s in shifts]
     sums = [sums[0]] + [lax.ppermute(sums[s], "dp", line[s - 1]) for s in shifts]

time: 101 us -> 96.5 us (0.955)
  waiting for transfers between devices: 36.4 us -> 30.6 us
  starting transfers between devices: 38.1 us -> 40.1 us
    ppermute x14, waiting for transfers between devices: 19.5 us -> 13.7 us  [in_plane(): return lax.ppermute(x, ('ctx', 'tp'), pairs)]
    ppermute x14, starting transfers between devices: 16.6 us -> 19.3 us  [in_plane(): return lax.ppermute(x, ('ctx', 'tp'), pairs)]
  transfers between devices with their start and end apart: 27 -> 27, of which waited for: 15 -> 13; matrix products, arithmetic and copies ran while one was open for 2% -> 2% of each run, Pallas kernels for 19% -> 20%
where the time goes in v12:
time: 96.5 us; the launch traced here: 96.1 us
  starting transfers between devices  40.1 us (42%)
  waiting for transfers between devices  30.6 us (32%)
  Pallas kernels  22.9 us (24%)
  local copies, waits for them, and re-layouts  1 us (1%)
    ppermute x14, starting transfers between devices, in_plane(): return lax.ppermute(x, ('ctx', 'tp'), pairs)  19.3 us
    pallas_call x10, Pallas kernels, once(): pl.pallas_call(body, grid=(1,), in_specs=specs + [ANYWHERE] * len(after),...  16.3 us
    ppermute x14, waiting for transfers between devices, in_plane(): return lax.ppermute(x, ('ctx', 'tp'), pairs)  13.7 us
    ppermute x6, starting transfers between devices, moved(): return lax.ppermute(x, 'tp', [(i, i ^ step) for i in range(4)])  8.06 us
    pallas_call x1, Pallas kernels, project(): pl.pallas_call(body, grid=(channels // WIDE,), in_specs=[full(early.shape...  6.59 us
    ppermute x2, waiting for transfers between devices, paired_z(): return x + lax.ppermute(x, 'dp', [(i, i ^ by) for i in range(SIDE)])  6.24 us
    ppermute x2, starting transfers between devices, shifted(): lax.ppermute(x, 'ctx', [(i, i + by) for i in range(devices) if 0 <= i + b...  5.86 us
    ppermute x2, waiting for transfers between devices, shifted(): lax.ppermute(x, 'ctx', [(i, i + by) for i in range(devices) if 0 <= i + b...  5.67 us
  transfers between devices with their start and end apart: 27, of which 13 were waited for; matrix products, arithmetic and copies ran while one was open for 2% of the time, Pallas kernels for 20%

profile of v12, /device:TPU:2, one launch (start us, length us, event | category | flops | bytes accessed | tf_op | source)
XLA Modules:
  0.0 96.1 jit_solution(15438094653029417539)
XLA Ops:
  0.7 7.3 %collective-permute-start.1 = (bf16[64,4096]{1,0:T(8,128)(2,1)}, bf16[64,4096]{1,0:T(8,128)(2,1)S(1)}, u32[]{:S(2)}, u32[]{:S(2)}) collective-permute-start(bf16[64,4096]{1,0:T(8,128)(2,1)} %bitcast.11), channel_id=1, source_target_pairs={{0,2},{1,3},{2,0},{3,1},{4,6},{5,7},{6,4},{7,5},{8,10},{9,11},{10,... | collective-permute-start | bytes 1572872 | tf_op jit(solution)/shard_map/ppermute | solution.py:32
  9.0 3.5 %collective-permute-start.2 = (bf16[128,1024]{1,0:T(8,128)(2,1)S(1)}, bf16[128,1024]{1,0:T(8,128)(2,1)S(1)}, u32[]{:S(2)}, u32[]{:S(2)}) collective-permute-start(bf16[128,1024]{1,0:T(8,128)(2,1)S(1)} %slice_bitcast_fusion), channel_id=1, source_target_pairs={{0,4},{4,8},{8,12},{12,16},{16,20},{20,24},{24,28},{28,32},{32,36}... | collective-permute-start | bytes 786440 | tf_op jit(solution)/shard_map/ppermute | solution.py:54
  12.5 1.2 %pack.1 = (bf16[128,1024]{1,0:T(8,128)(2,1)S(1)}, bf16[128,1024]{1,0:T(8,128)(2,1)S(1)}, bf16[128,1024]{1,0:T(8,128)(2,1)S(1)}, bf16[128,1024]{1,0:T(8,128)(2,1)S(1)}) custom-call(bf16[64,4096]{1,0:T(8,128)(2,1)} %bitcast.12, bf16[64,4096]{1,0:T(8,128)(2,1)S(1)} %collective-permute-done.refs_1_), custom_call_target="tpu_custom_call" | custom-call | tf_op jit(solution)/shard_map/pack/pallas_call | solution.py:96
  13.7 1.6 %collective-permute-start.5 = (bf16[128,1024]{1,0:T(8,128)(2,1)S(1)}, bf16[128,1024]{1,0:T(8,128)(2,1)S(1)}, u32[]{:S(2)}, u32[]{:S(2)}) collective-permute-start(bf16[128,1024]{1,0:T(8,128)(2,1)S(1)} %get-tuple-element.36), channel_id=1, source_target_pairs={{0,16},{1,5},{2,18},{3,7},{4,20},{5,9},{6,22},{7,11},{8,24},{9,13}... | collective-permute-start | bytes 786440 | tf_op jit(solution)/shard_map/ppermute | solution.py:45
  15.8 5.7 %collective-permute-done.2.refs_1_.refs_0_ = bf16[128,1024]{1,0:T(8,128)(2,1)S(1)} collective-permute-done((bf16[128,1024]{1,0:T(8,128)(2,1)S(1)}, bf16[128,1024]{1,0:T(8,128)(2,1)S(1)}, u32[]{:S(2)}, u32[]{:S(2)}) %collective-permute-start.2) | collective-permute-done | bytes 262176 | tf_op jit(solution)/shard_map/ppermute | solution.py:54
  21.4 3.4 %conv_forward.1 = (f32[256,1024]{1,0:T(8,128)S(1)}, bf16[256,512]{1,0:T(8,128)(2,1)S(1)}, bf16[128,512]{1,0:T(8,128)(2,1)S(1)}, bf16[128,512]{1,0:T(8,128)(2,1)S(1)}) custom-call(bf16[64,128]{1,0:T(8,128)(2,1)} %refs_0_.3, bf16[128,1024]{1,0:T(8,128)(2,1)S(1)} %collective-permute-done.2.refs_1_.refs_0_, bf16[256,1024]{1,0:T(8,128)(2,1)} %bitcast.8, ...), custom_call_target="tpu_custom_call" | custom-call | tf_op jit(solution)/shard_map/conv_forward/pallas_call | solution.py:96
  26.5 1.6 %collective-permute-start.8 = (bf16[272,1024]{1,0:T(8,128)(2,1)S(1)}, bf16[272,1024]{1,0:T(8,128)(2,1)S(1)}, u32[]{:S(2)}, u32[]{:S(2)}) collective-permute-start(bf16[272,1024]{1,0:T(8,128)(2,1)S(1)} %join.1.refs_8_), channel_id=1, source_target_pairs={{0,16},{1,5},{2,18},{3,7},{4,20},{5,9},{6,22},{7,11},{8,24},{9,13}... | collective-permute-start | bytes 1671176 | tf_op jit(solution)/shard_map/ppermute | solution.py:45
  28.6 2.1 %collective-permute-done.1.refs_0_.refs_2_ = bf16[64,4096]{1,0:T(8,128)(2,1)S(1)} collective-permute-done((bf16[64,4096]{1,0:T(8,128)(2,1)}, bf16[64,4096]{1,0:T(8,128)(2,1)S(1)}, u32[]{:S(2)}, u32[]{:S(2)}) %collective-permute-start.1) | collective-permute-done | bytes 524320 | tf_op jit(solution)/shard_map/ppermute | solution.py:32
  30.7 1.9 %collective-permute-done.7.refs_1_.refs_3_ = bf16[64,4096]{1,0:T(8,128)(2,1)S(1)} collective-permute-done((bf16[64,4096]{1,0:T(8,128)(2,1)S(1)}, bf16[64,4096]{1,0:T(8,128)(2,1)S(1)}, u32[]{:S(2)}, u32[]{:S(2)}) %collective-permute-start.7) | collective-permute-done | bytes 524320 | tf_op jit(solution)/shard_map/ppermute | solution.py:32
  32.7 3.5 %collective-permute-done.8.refs_2_.refs_9_ = bf16[272,1024]{1,0:T(8,128)(2,1)S(1)} collective-permute-done((bf16[272,1024]{1,0:T(8,128)(2,1)S(1)}, bf16[272,1024]{1,0:T(8,128)(2,1)S(1)}, u32[]{:S(2)}, u32[]{:S(2)}) %collective-permute-start.8) | collective-permute-done | bytes 557088 | tf_op jit(solution)/shard_map/ppermute | solution.py:45
  36.2 1.5 %collective-permute-done.9.refs_3_.refs_12_ = bf16[272,1024]{1,0:T(8,128)(2,1)S(1)} collective-permute-done((bf16[272,1024]{1,0:T(8,128)(2,1)S(1)}, bf16[272,1024]{1,0:T(8,128)(2,1)S(1)}, u32[]{:S(2)}, u32[]{:S(2)}) %collective-permute-start.9) | collective-permute-done | bytes 557088 | tf_op jit(solution)/shard_map/ppermute | solution.py:45
  37.8 2.0 %collective-permute-start.10 = (bf16[256,1024]{1,0:T(8,128)(2,1)S(1)}, bf16[256,1024]{1,0:T(8,128)(2,1)S(1)}, u32[]{:S(2)}, u32[]{:S(2)}) collective-permute-start(bf16[256,1024]{1,0:T(8,128)(2,1)S(1)} %get-tuple-element.44), channel_id=1, source_target_pairs={{0,32},{1,9},{2,34},{3,11},{4,36},{5,13},{6,38},{7,15},{8,40},{9,1... | collective-permute-start | bytes 1572872 | tf_op jit(solution)/shard_map/ppermute | solution.py:45
  39.9 2.0 %collective-permute-start.12 = (bf16[256,1024]{1,0:T(8,128)(2,1)S(1)}, bf16[256,1024]{1,0:T(8,128)(2,1)S(1)}, u32[]{:S(2)}, u32[]{:S(2)}) collective-permute-start(bf16[256,1024]{1,0:T(8,128)(2,1)S(1)} %get-tuple-element.46), channel_id=1, source_target_pairs={{0,48},{1,13},{2,50},{3,15},{4,52},{5,1},{6,54},{7,3},{8,56},{9,5}... | collective-permute-start | bytes 1572872 | tf_op jit(solution)/shard_map/ppermute | solution.py:45
  41.9 6.6 %project.1 = (bf16[256,1024]{1,0:T(8,128)(2,1)S(1)}, bf16[256,1024]{1,0:T(8,128)(2,1)}) custom-call(bf16[64,4096]{1,0:T(8,128)(2,1)} %bitcast.13, bf16[64,4096]{1,0:T(8,128)(2,1)S(1)} %collective-permute-done.refs_1_, bf16[64,4096]{1,0:T(8,128)(2,1)S(1)} %collective-permute-done.1.refs_0_.refs_2_, ...), custom_call_target="tpu_custom_call" | custom-call | flops 6000000000 | tf_op jit(solution)/shard_map/project/pallas_call | solution.py:344
  48.5 3.8 %filter_grad.1.refs_13_ = f32[64,128]{1,0:T(8,128)S(1)} custom-call(bf16[128,1024]{1,0:T(8,128)(2,1)S(1)} %collective-permute-done.2.refs_1_.refs_0_, bf16[256,1024]{1,0:T(8,128)(2,1)} %bitcast.9, bf16[256,1024]{1,0:T(8,128)(2,1)S(1)} %get-tuple-element.42.refs_2_.refs_1_), custom_call_target="tpu_custom_call" | custom-call | flops 4000000000 | tf_op jit(solution)/shard_map/filter_grad/pallas_call | solution.py:96
  52.3 1.7 %collective-permute-done.11.refs_5_.refs_10_ = bf16[256,1024]{1,0:T(8,128)(2,1)S(1)} collective-permute-done((bf16[256,1024]{1,0:T(8,128)(2,1)S(1)}, bf16[256,1024]{1,0:T(8,128)(2,1)S(1)}, u32[]{:S(2)}, u32[]{:S(2)}) %collective-permute-start.11) | collective-permute-done | bytes 524320 | tf_op jit(solution)/shard_map/ppermute | solution.py:45
  54.2 3.1 %weight_parts.1 = (f32[256,1024]{1,0:T(8,128)S(1)}, bf16[256,1024]{1,0:T(8,128)(2,1)S(1)}, bf16[256,1024]{1,0:T(8,128)(2,1)S(1)}, bf16[256,1024]{1,0:T(8,128)(2,1)S(1)}) custom-call(bf16[128,1024]{1,0:T(8,128)(2,1)S(1)} %get-tuple-element.43.refs_0_, bf16[128,1024]{1,0:T(8,128)(2,1)S(1)} %collective-permute-done.5.refs_3_.refs_1_, ...), custom_call_target="tpu_custom_call" | custom-call | flops 4000000000 | tf_op jit(solution)/shard_map/weight_parts/pallas_call | solution.py:96
  57.5 2.9 %collective-permute-start.17 = (bf16[256,1024]{1,0:T(8,128)(2,1)S(1)}, bf16[256,1024]{1,0:T(8,128)(2,1)S(1)}, u32[]{:S(2)}, u32[]{:S(2)}) collective-permute-start(bf16[256,1024]{1,0:T(8,128)(2,1)S(1)} %get-tuple-element.51), channel_id=1, source_target_pairs={{0,8},{1,33},{2,10},{3,35},{4,12},{5,37},{6,14},{7,39},{8,0},{9,41... | collective-permute-start | bytes 1572872 | tf_op jit(solution)/shard_map/ppermute | solution.py:45
  60.4 1.3 %collective-permute-start.18 = (bf16[256,1024]{1,0:T(8,128)(2,1)S(1)}, bf16[256,1024]{1,0:T(8,128)(2,1)S(1)}, u32[]{:S(2)}, u32[]{:S(2)}) collective-permute-start(bf16[256,1024]{1,0:T(8,128)(2,1)S(1)} %get-tuple-element.52), channel_id=1, source_target_pairs={{0,12},{1,49},{2,14},{3,51},{4,0},{5,53},{6,2},{7,55},{8,4},{9,57}... | collective-permute-start | bytes 1572872 | tf_op jit(solution)/shard_map/ppermute | solution.py:45
  62.8 2.9 %collective-permute-done.13 = f32[64,128]{1,0:T(8,128)S(1)} collective-permute-done((f32[64,128]{1,0:T(8,128)S(1)}, f32[64,128]{1,0:T(8,128)S(1)}, u32[]{:S(2)}, u32[]{:S(2)}) %collective-permute-start.13) | collective-permute-done | bytes 32800 | tf_op jit(solution)/shard_map/ppermute | solution.py:489
  65.7 1.5 %collective-permute-start.14 = (f32[64,128]{1,0:T(8,128)S(1)}, f32[64,128]{1,0:T(8,128)S(1)}, u32[]{:S(2)}, u32[]{:S(2)}) collective-permute-start(f32[64,128]{1,0:T(8,128)S(1)} %add.20), channel_id=1, source_target_pairs={{0,128},{64,192},{128,0},{192,64},{1,129},{65,193},{129,1},{193,65... | collective-permute-start | bytes 98312 | tf_op jit(solution)/shard_map/ppermute | solution.py:489
  67.2 3.3 %collective-permute-done.14 = f32[64,128]{1,0:T(8,128)S(1)} collective-permute-done((f32[64,128]{1,0:T(8,128)S(1)}, f32[64,128]{1,0:T(8,128)S(1)}, u32[]{:S(2)}, u32[]{:S(2)}) %collective-permute-start.14) | collective-permute-done | bytes 32800 | tf_op jit(solution)/shard_map/ppermute | solution.py:489
  71.4 3.0 %collective-permute-done.23 = f32[64,128]{1,0:T(8,128)S(1)} collective-permute-done((f32[64,128]{1,0:T(8,128)S(1)}, f32[64,128]{1,0:T(8,128)S(1)}, u32[]{:S(2)}, u32[]{:S(2)}) %collective-permute-start.23) | collective-permute-done | bytes 32800 | tf_op jit(solution)/shard_map/ppermute | solution.py:45
  74.5 2.4 %collective-permute-start.24 = (f32[256,128]{1,0:T(8,128)S(1)}, f32[256,128]{1,0:T(8,128)S(1)}, u32[]{:S(2)}, u32[]{:S(2)}) collective-permute-start(f32[256,128]{1,0:T(8,128)S(1)} %pad.4), channel_id=1, source_target_pairs={{0,32},{1,9},{2,34},{3,11},{4,36},{5,13},{6,38},{7,15},{8,40},{9,1... | collective-permute-start | bytes 393224 | tf_op jit(solution)/shard_map/ppermute | solution.py:45
  76.9 2.4 %collective-permute-start.15 = (bf16[128,1024]{1,0:T(8,128)(2,1)S(1)}, bf16[128,1024]{1,0:T(8,128)(2,1)S(1)}, u32[]{:S(2)}, u32[]{:S(2)}) collective-permute-start(bf16[128,1024]{1,0:T(8,128)(2,1)S(1)} %slice.14), channel_id=1, source_target_pairs={{4,0},{8,4},{12,8},{16,12},{20,16},{24,20},{28,24},{32,28},{36,32}... | collective-permute-start | bytes 786440 | tf_op jit(solution)/shard_map/ppermute | solution.py:54
  79.7 1.1 %collective-permute-start.19 = (bf16[64,1024]{1,0:T(8,128)(2,1)S(1)}, bf16[64,1024]{1,0:T(8,128)(2,1)S(1)}, u32[]{:S(2)}, u32[]{:S(2)}) collective-permute-start(bf16[64,1024]{1,0:T(8,128)(2,1)S(1)} %get-tuple-element.55), channel_id=1, source_target_pairs={{0,64},{64,128},{128,192},{192,0},{1,65},{65,129},{129,193},{193,1... | collective-permute-start | bytes 393224 | tf_op jit(solution)/shard_map/ppermute | solution.py:533
  80.8 1.5 %collective-permute-start.20 = (bf16[64,1024]{1,0:T(8,128)(2,1)S(1)}, bf16[64,1024]{1,0:T(8,128)(2,1)S(1)}, u32[]{:S(2)}, u32[]{:S(2)}) collective-permute-start(bf16[64,1024]{1,0:T(8,128)(2,1)S(1)} %get-tuple-element.56), channel_id=1, source_target_pairs={{0,128},{64,192},{128,0},{192,64},{1,129},{65,193},{129,1},{193,65... | collective-permute-start | bytes 393224 | tf_op jit(solution)/shard_map/ppermute | solution.py:533
  82.3 1.9 %collective-permute-start.21 = (bf16[64,1024]{1,0:T(8,128)(2,1)S(1)}, bf16[64,1024]{1,0:T(8,128)(2,1)S(1)}, u32[]{:S(2)}, u32[]{:S(2)}) collective-permute-start(bf16[64,1024]{1,0:T(8,128)(2,1)S(1)} %get-tuple-element.57), channel_id=1, source_target_pairs={{0,192},{64,0},{128,64},{192,128},{1,193},{65,1},{129,65},{193,129... | collective-permute-start | bytes 393224 | tf_op jit(solution)/shard_map/ppermute | solution.py:533
  84.2 1.6 %collective-permute-start.25 = (f32[64,128]{1,0:T(8,128)S(1)}, f32[64,128]{1,0:T(8,128)S(1)}, u32[]{:S(2)}, u32[]{:S(2)}) collective-permute-start(f32[64,128]{1,0:T(8,128)S(1)} %slice_add_fusion), channel_id=1, source_target_pairs={{0,4},{1,17},{2,6},{3,19},{4,0},{5,21},{6,2},{7,23},{8,12},{9,25},... | collective-permute-start | bytes 98312 | tf_op jit(solution)/shard_map/ppermute | solution.py:45
  85.9 3.4 %input_grad.1.refs_4_ = bf16[256,1024]{1,0:T(8,128)(2,1)} custom-call(bf16[64,128]{1,0:T(8,128)(2,1)} %refs_0_.3, bf16[256,1024]{1,0:T(8,128)(2,1)S(1)} %get-tuple-element.42.refs_2_.refs_1_, bf16[128,1024]{1,0:T(8,128)(2,1)S(1)} %collective-permute-done.15.refs_2_, f32[64,1024]{1,0:T(8,128)S(1)} %get-tuple-element.53.refs_3_.refs_0_), custom_call_target="tpu_custom_call" | custom-call | tf_op jit(solution)/shard_map/input_grad/pallas_call | solution.py:96
  89.3 1.6 %collective-permute-start.26 = (f32[64,128]{1,0:T(8,128)S(1)}, f32[64,128]{1,0:T(8,128)S(1)}, u32[]{:S(2)}, u32[]{:S(2)}) collective-permute-start(f32[64,128]{1,0:T(8,128)S(1)} %add.24), channel_id=1, source_target_pairs={{0,8},{1,33},{2,10},{3,35},{4,12},{5,37},{6,14},{7,39},{8,0},{9,41... | collective-permute-start | bytes 98312 | tf_op jit(solution)/shard_map/ppermute | solution.py:45
  91.1 3.7 %collective-permute-done.26 = f32[64,128]{1,0:T(8,128)S(1)} collective-permute-done((f32[64,128]{1,0:T(8,128)S(1)}, f32[64,128]{1,0:T(8,128)S(1)}, u32[]{:S(2)}, u32[]{:S(2)}) %collective-permute-start.26) | collective-permute-done | bytes 32800 | tf_op jit(solution)/shard_map/ppermute | solution.py:45
  (42 shorter events, 8.5 us)
Async XLA Ops:
  0.6 11.8 %collective-permute-start = (bf16[64,4096]{1,0:T(8,128)(2,1)}, bf16[64,4096]{1,0:T(8,128)(2,1)S(1)}, u32[]{:S(2)}, u32[]{:S(2)}) collective-permute-start(bf16[64,4096]{1,0:T(8,128)(2,1)} %bitcast.10), channel_id=1, source_target_pairs={{0,1},{1,0},{2,3},{3,2},{4,5},{5,4},{6,7},{7,6},{8,9},{9,8},{10,11... | collective-permute-start | bytes 1572872 | tf_op jit(solution)/shard_map/ppermute | solution.py:32
  0.7 30.0 %collective-permute-start.1 = (bf16[64,4096]{1,0:T(8,128)(2,1)}, bf16[64,4096]{1,0:T(8,128)(2,1)S(1)}, u32[]{:S(2)}, u32[]{:S(2)}) collective-permute-start(bf16[64,4096]{1,0:T(8,128)(2,1)} %bitcast.11), channel_id=1, source_target_pairs={{0,2},{1,3},{2,0},{3,1},{4,6},{5,7},{6,4},{7,5},{8,10},{9,11},{10,... | collective-permute-start | bytes 1572872 | tf_op jit(solution)/shard_map/ppermute | solution.py:32
  9.0 12.5 %collective-permute-start.2 = (bf16[128,1024]{1,0:T(8,128)(2,1)S(1)}, bf16[128,1024]{1,0:T(8,128)(2,1)S(1)}, u32[]{:S(2)}, u32[]{:S(2)}) collective-permute-start(bf16[128,1024]{1,0:T(8,128)(2,1)S(1)} %slice_bitcast_fusion), channel_id=1, source_target_pairs={{0,4},{4,8},{8,12},{12,16},{16,20},{20,24},{24,28},{28,32},{32,36}... | collective-permute-start | bytes 786440 | tf_op jit(solution)/shard_map/ppermute | solution.py:54
  13.7 12.8 %collective-permute-start.5 = (bf16[128,1024]{1,0:T(8,128)(2,1)S(1)}, bf16[128,1024]{1,0:T(8,128)(2,1)S(1)}, u32[]{:S(2)}, u32[]{:S(2)}) collective-permute-start(bf16[128,1024]{1,0:T(8,128)(2,1)S(1)} %get-tuple-element.36), channel_id=1, source_target_pairs={{0,16},{1,5},{2,18},{3,7},{4,20},{5,9},{6,22},{7,11},{8,24},{9,13}... | collective-permute-start | bytes 786440 | tf_op jit(solution)/shard_map/ppermute | solution.py:45
  15.2 11.2 %collective-permute-start.6 = (bf16[128,1024]{1,0:T(8,128)(2,1)S(1)}, bf16[128,1024]{1,0:T(8,128)(2,1)S(1)}, u32[]{:S(2)}, u32[]{:S(2)}) collective-permute-start(bf16[128,1024]{1,0:T(8,128)(2,1)S(1)} %get-tuple-element.37), channel_id=1, source_target_pairs={{0,48},{1,13},{2,50},{3,15},{4,52},{5,1},{6,54},{7,3},{8,56},{9,5}... | collective-permute-start | bytes 786440 | tf_op jit(solution)/shard_map/ppermute | solution.py:45
  24.9 1.4 %collective-permute-start.3 = (bf16[128,512]{1,0:T(8,128)(2,1)S(1)}, bf16[128,512]{1,0:T(8,128)(2,1)S(1)}, u32[]{:S(2)}, u32[]{:S(2)}) collective-permute-start(bf16[128,512]{1,0:T(8,128)(2,1)S(1)} %get-tuple-element.34), channel_id=1, source_target_pairs={{0,1},{1,0},{2,3},{3,2},{4,5},{5,4},{6,7},{7,6},{8,9},{9,8},{10,11... | collective-permute-start | bytes 393224 | tf_op jit(solution)/shard_map/ppermute | solution.py:32
  25.0 1.5 %collective-permute-start.4 = (bf16[128,512]{1,0:T(8,128)(2,1)S(1)}, bf16[128,512]{1,0:T(8,128)(2,1)S(1)}, u32[]{:S(2)}, u32[]{:S(2)}) collective-permute-start(bf16[128,512]{1,0:T(8,128)(2,1)S(1)} %get-tuple-element.35), channel_id=1, source_target_pairs={{0,1},{1,0},{2,3},{3,2},{4,5},{5,4},{6,7},{7,6},{8,9},{9,8},{10,11... | collective-permute-start | bytes 393224 | tf_op jit(solution)/shard_map/ppermute | solution.py:32
  26.5 9.6 %collective-permute-start.8 = (bf16[272,1024]{1,0:T(8,128)(2,1)S(1)}, bf16[272,1024]{1,0:T(8,128)(2,1)S(1)}, u32[]{:S(2)}, u32[]{:S(2)}) collective-permute-start(bf16[272,1024]{1,0:T(8,128)(2,1)S(1)} %join.1.refs_8_), channel_id=1, source_target_pairs={{0,16},{1,5},{2,18},{3,7},{4,20},{5,9},{6,22},{7,11},{8,24},{9,13}... | collective-permute-start | bytes 1671176 | tf_op jit(solution)/shard_map/ppermute | solution.py:45
  28.1 9.5 %collective-permute-start.9 = (bf16[272,1024]{1,0:T(8,128)(2,1)S(1)}, bf16[272,1024]{1,0:T(8,128)(2,1)S(1)}, u32[]{:S(2)}, u32[]{:S(2)}) collective-permute-start(bf16[272,1024]{1,0:T(8,128)(2,1)S(1)} %join.1.refs_8_), channel_id=1, source_target_pairs={{0,48},{1,13},{2,50},{3,15},{4,52},{5,1},{6,54},{7,3},{8,56},{9,5}... | collective-permute-start | bytes 1671176 | tf_op jit(solution)/shard_map/ppermute | solution.py:45
  30.7 1.9 %collective-permute-start.7 = (bf16[64,4096]{1,0:T(8,128)(2,1)S(1)}, bf16[64,4096]{1,0:T(8,128)(2,1)S(1)}, u32[]{:S(2)}, u32[]{:S(2)}) collective-permute-start(bf16[64,4096]{1,0:T(8,128)(2,1)S(1)} %collective-permute-done.1.refs_0_.refs_2_), channel_id=1, source_target_pairs={{0,1},{1,0},{2,3},{3,2},{4,5},{5,4},{6,7},{7,6},{8,9},{9,8},{10,11... | collective-permute-start | bytes 1572872 | tf_op jit(solution)/shard_map/ppermute | solution.py:32
  37.8 14.4 %collective-permute-start.10 = (bf16[256,1024]{1,0:T(8,128)(2,1)S(1)}, bf16[256,1024]{1,0:T(8,128)(2,1)S(1)}, u32[]{:S(2)}, u32[]{:S(2)}) collective-permute-start(bf16[256,1024]{1,0:T(8,128)(2,1)S(1)} %get-tuple-element.44), channel_id=1, source_target_pairs={{0,32},{1,9},{2,34},{3,11},{4,36},{5,13},{6,38},{7,15},{8,40},{9,1... | collective-permute-start | bytes 1572872 | tf_op jit(solution)/shard_map/ppermute | solution.py:45
  39.9 14.2 %collective-permute-start.11 = (bf16[256,1024]{1,0:T(8,128)(2,1)S(1)}, bf16[256,1024]{1,0:T(8,128)(2,1)S(1)}, u32[]{:S(2)}, u32[]{:S(2)}) collective-permute-start(bf16[256,1024]{1,0:T(8,128)(2,1)S(1)} %get-tuple-element.45), channel_id=1, source_target_pairs={{0,16},{1,5},{2,18},{3,7},{4,20},{5,9},{6,22},{7,11},{8,24},{9,13}... | collective-permute-start | bytes 1572872 | tf_op jit(solution)/shard_map/ppermute | solution.py:45
  39.9 14.3 %collective-permute-start.12 = (bf16[256,1024]{1,0:T(8,128)(2,1)S(1)}, bf16[256,1024]{1,0:T(8,128)(2,1)S(1)}, u32[]{:S(2)}, u32[]{:S(2)}) collective-permute-start(bf16[256,1024]{1,0:T(8,128)(2,1)S(1)} %get-tuple-element.46), channel_id=1, source_target_pairs={{0,48},{1,13},{2,50},{3,15},{4,52},{5,1},{6,54},{7,3},{8,56},{9,5}... | collective-permute-start | bytes 1572872 | tf_op jit(solution)/shard_map/ppermute | solution.py:45
  57.3 22.0 %collective-permute-start.16 = (bf16[256,1024]{1,0:T(8,128)(2,1)S(1)}, bf16[256,1024]{1,0:T(8,128)(2,1)S(1)}, u32[]{:S(2)}, u32[]{:S(2)}) collective-permute-start(bf16[256,1024]{1,0:T(8,128)(2,1)S(1)} %get-tuple-element.50), channel_id=1, source_target_pairs={{0,4},{1,17},{2,6},{3,19},{4,8},{5,21},{6,10},{7,23},{8,12},{9,25}... | collective-permute-start | bytes 1572872 | tf_op jit(solution)/shard_map/ppermute | solution.py:45
  57.5 21.7 %collective-permute-start.17 = (bf16[256,1024]{1,0:T(8,128)(2,1)S(1)}, bf16[256,1024]{1,0:T(8,128)(2,1)S(1)}, u32[]{:S(2)}, u32[]{:S(2)}) collective-permute-start(bf16[256,1024]{1,0:T(8,128)(2,1)S(1)} %get-tuple-element.51), channel_id=1, source_target_pairs={{0,8},{1,33},{2,10},{3,35},{4,12},{5,37},{6,14},{7,39},{8,0},{9,41... | collective-permute-start | bytes 1572872 | tf_op jit(solution)/shard_map/ppermute | solution.py:45
  60.4 18.9 %collective-permute-start.18 = (bf16[256,1024]{1,0:T(8,128)(2,1)S(1)}, bf16[256,1024]{1,0:T(8,128)(2,1)S(1)}, u32[]{:S(2)}, u32[]{:S(2)}) collective-permute-start(bf16[256,1024]{1,0:T(8,128)(2,1)S(1)} %get-tuple-element.52), channel_id=1, source_target_pairs={{0,12},{1,49},{2,14},{3,51},{4,0},{5,53},{6,2},{7,55},{8,4},{9,57}... | collective-permute-start | bytes 1572872 | tf_op jit(solution)/shard_map/ppermute | solution.py:45
  61.8 3.9 %collective-permute-start.13 = (f32[64,128]{1,0:T(8,128)S(1)}, f32[64,128]{1,0:T(8,128)S(1)}, u32[]{:S(2)}, u32[]{:S(2)}) collective-permute-start(f32[64,128]{1,0:T(8,128)S(1)} %filter_grad.1.refs_13_), channel_id=1, source_target_pairs={{0,64},{64,0},{128,192},{192,128},{1,65},{65,1},{129,193},{193,129... | collective-permute-start | bytes 98312 | tf_op jit(solution)/shard_map/ppermute | solution.py:489
  65.7 4.8 %collective-permute-start.14 = (f32[64,128]{1,0:T(8,128)S(1)}, f32[64,128]{1,0:T(8,128)S(1)}, u32[]{:S(2)}, u32[]{:S(2)}) collective-permute-start(f32[64,128]{1,0:T(8,128)S(1)} %add.20), channel_id=1, source_target_pairs={{0,128},{64,192},{128,0},{192,64},{1,129},{65,193},{129,1},{193,65... | collective-permute-start | bytes 98312 | tf_op jit(solution)/shard_map/ppermute | solution.py:489
  70.5 3.9 %collective-permute-start.23 = (f32[64,128]{1,0:T(8,128)S(1)}, f32[64,128]{1,0:T(8,128)S(1)}, u32[]{:S(2)}, u32[]{:S(2)}) collective-permute-start(f32[64,128]{1,0:T(8,128)S(1)} %add.21), channel_id=1, source_target_pairs={{0,16},{1,5},{2,18},{3,7},{4,20},{5,1},{6,22},{7,3},{8,24},{9,13},... | collective-permute-start | bytes 98312 | tf_op jit(solution)/shard_map/ppermute | solution.py:45
  74.5 9.7 %collective-permute-start.24 = (f32[256,128]{1,0:T(8,128)S(1)}, f32[256,128]{1,0:T(8,128)S(1)}, u32[]{:S(2)}, u32[]{:S(2)}) collective-permute-start(f32[256,128]{1,0:T(8,128)S(1)} %pad.4), channel_id=1, source_target_pairs={{0,32},{1,9},{2,34},{3,11},{4,36},{5,13},{6,38},{7,15},{8,40},{9,1... | collective-permute-start | bytes 393224 | tf_op jit(solution)/shard_map/ppermute | solution.py:45
  76.9 9.0 %collective-permute-start.15 = (bf16[128,1024]{1,0:T(8,128)(2,1)S(1)}, bf16[128,1024]{1,0:T(8,128)(2,1)S(1)}, u32[]{:S(2)}, u32[]{:S(2)}) collective-permute-start(bf16[128,1024]{1,0:T(8,128)(2,1)S(1)} %slice.14), channel_id=1, source_target_pairs={{4,0},{8,4},{12,8},{16,12},{20,16},{24,20},{28,24},{32,28},{36,32}... | collective-permute-start | bytes 786440 | tf_op jit(solution)/shard_map/ppermute | solution.py:54
  79.7 11.2 %collective-permute-start.19 = (bf16[64,1024]{1,0:T(8,128)(2,1)S(1)}, bf16[64,1024]{1,0:T(8,128)(2,1)S(1)}, u32[]{:S(2)}, u32[]{:S(2)}) collective-permute-start(bf16[64,1024]{1,0:T(8,128)(2,1)S(1)} %get-tuple-element.55), channel_id=1, source_target_pairs={{0,64},{64,128},{128,192},{192,0},{1,65},{65,129},{129,193},{193,1... | collective-permute-start | bytes 393224 | tf_op jit(solution)/shard_map/ppermute | solution.py:533
  80.8 10.1 %collective-permute-start.20 = (bf16[64,1024]{1,0:T(8,128)(2,1)S(1)}, bf16[64,1024]{1,0:T(8,128)(2,1)S(1)}, u32[]{:S(2)}, u32[]{:S(2)}) collective-permute-start(bf16[64,1024]{1,0:T(8,128)(2,1)S(1)} %get-tuple-element.56), channel_id=1, source_target_pairs={{0,128},{64,192},{128,0},{192,64},{1,129},{65,193},{129,1},{193,65... | collective-permute-start | bytes 393224 | tf_op jit(solution)/shard_map/ppermute | solution.py:533
  82.3 8.6 %collective-permute-start.21 = (bf16[64,1024]{1,0:T(8,128)(2,1)S(1)}, bf16[64,1024]{1,0:T(8,128)(2,1)S(1)}, u32[]{:S(2)}, u32[]{:S(2)}) collective-permute-start(bf16[64,1024]{1,0:T(8,128)(2,1)S(1)} %get-tuple-element.57), channel_id=1, source_target_pairs={{0,192},{64,0},{128,64},{192,128},{1,193},{65,1},{129,65},{193,129... | collective-permute-start | bytes 393224 | tf_op jit(solution)/shard_map/ppermute | solution.py:533
  84.2 5.1 %collective-permute-start.25 = (f32[64,128]{1,0:T(8,128)S(1)}, f32[64,128]{1,0:T(8,128)S(1)}, u32[]{:S(2)}, u32[]{:S(2)}) collective-permute-start(f32[64,128]{1,0:T(8,128)S(1)} %slice_add_fusion), channel_id=1, source_target_pairs={{0,4},{1,17},{2,6},{3,19},{4,0},{5,21},{6,2},{7,23},{8,12},{9,25},... | collective-permute-start | bytes 98312 | tf_op jit(solution)/shard_map/ppermute | solution.py:45
  89.3 5.5 %collective-permute-start.26 = (f32[64,128]{1,0:T(8,128)S(1)}, f32[64,128]{1,0:T(8,128)S(1)}, u32[]{:S(2)}, u32[]{:S(2)}) collective-permute-start(f32[64,128]{1,0:T(8,128)S(1)} %add.24), channel_id=1, source_target_pairs={{0,8},{1,33},{2,10},{3,35},{4,12},{5,37},{6,14},{7,39},{8,0},{9,41... | collective-permute-start | bytes 98312 | tf_op jit(solution)/shard_map/ppermute | solution.py:45
  91.0 4.4 %collective-permute-start.22 = (f32[64,512]{1,0:T(8,128)S(1)}, f32[64,512]{1,0:T(8,128)S(1)}, u32[]{:S(2)}, u32[]{:S(2)}) collective-permute-start(f32[64,512]{1,0:T(8,128)S(1)} %get-tuple-element.59), channel_id=1, source_target_pairs={{0,1},{1,0},{2,3},{3,2},{4,5},{5,4},{6,7},{7,6},{8,9},{9,8},{10,11... | collective-permute-start | bytes 393224 | tf_op jit(solution)/shard_map/ppermute | solution.py:32

commit v13 on v12

--- a/solution.py
+++ b/solution.py
@@ -207,7 +207,7 @@
     return once(
         input_grad_kernel,
         "input_grad",
-        [filters, conv_grad, following],
+        [filters, conv_grad, (following, whole((TAPS, conv_grad.shape[1])))],
         [(conv_grad.shape, BF16)],
         [pltpu.VMEM((2, PER_TILE * TAPS, 2 * TAPS), BF16)],
         after,
@@ -518,7 +518,7 @@
     parts = weight_parts([early[0], *early_got], own_late, gated, got, late_got, (filter_sum,))
 
     filter_sum = paired_z(paired_z(tied(filter_sum, parts[0]), 1), 2)
-    following = shifted(tied(conv_grad[:TAPS], filter_sum), -1)
+    following = shifted(tied(conv_grad[: TAPS + 64], filter_sum), -1)
     filter_sum = paired(filter_sum, True, 1)
     padded = jnp.pad(filter_sum, ((0, 3 * filter_sum.shape[0]), (0, 0)))
     padded = in_plane(padded, True, lambda place: place ^ 2)

time: 96.5 us -> 99.8 us (1.034)
  the two profiles are of different devices: /device:TPU:2 before, /device:TPU:20 now
where the time goes in v13:
time: 99.8 us; the launch traced here: 99.4 us
  starting transfers between devices  44.8 us (45%)
  waiting for transfers between devices  29.3 us (29%)
  Pallas kernels  22.9 us (23%)
  local copies, waits for them, and re-layouts  1 us (1%)
    ppermute x14, starting transfers between devices, in_plane(): return lax.ppermute(x, ('ctx', 'tp'), pairs)  23.8 us
    pallas_call x10, Pallas kernels, once(): pl.pallas_call(body, grid=(1,), in_specs=specs + [ANYWHERE] * len(after),...  16.3 us
    ppermute x14, waiting for transfers between devices, in_plane(): return lax.ppermute(x, ('ctx', 'tp'), pairs)  12.2 us
    ppermute x6, starting transfers between devices, moved(): return lax.ppermute(x, 'tp', [(i, i ^ step) for i in range(4)])  8.06 us
    pallas_call x1, Pallas kernels, project(): pl.pallas_call(body, grid=(channels // WIDE,), in_specs=[full(early.shape...  6.59 us
    ppermute x6, waiting for transfers between devices, moved(): return lax.ppermute(x, 'tp', [(i, i ^ step) for i in range(4)])  6.45 us
    ppermute x2, waiting for transfers between devices, paired_z(): return x + lax.ppermute(x, 'dp', [(i, i ^ by) for i in range(SIDE)])  6.08 us
    ppermute x2, starting transfers between devices, shifted(): lax.ppermute(x, 'ctx', [(i, i + by) for i in range(devices) if 0 <= i + b...  5.77 us
  transfers between devices with their start and end apart: 27, of which 12 were waited for; matrix products, arithmetic and copies ran while one was open for 2% of the time, Pallas kernels for 19%

profile of v13, /device:TPU:20, one launch (start us, length us, event | category | flops | bytes accessed | tf_op | source)
XLA Modules:
  0.0 99.4 jit_solution(13977918507368697313)
XLA Ops:
  0.7 7.3 %collective-permute-start.1 = (bf16[64,4096]{1,0:T(8,128)(2,1)}, bf16[64,4096]{1,0:T(8,128)(2,1)S(1)}, u32[]{:S(2)}, u32[]{:S(2)}) collective-permute-start(bf16[64,4096]{1,0:T(8,128)(2,1)} %bitcast.11), channel_id=1, source_target_pairs={{0,2},{1,3},{2,0},{3,1},{4,6},{5,7},{6,4},{7,5},{8,10},{9,11},{10,... | collective-permute-start | bytes 1572872 | tf_op jit(solution)/shard_map/ppermute | solution.py:32
  8.0 1.0 slice_bitcast_fusion
  9.0 3.2 %collective-permute-start.2 = (bf16[128,1024]{1,0:T(8,128)(2,1)S(1)}, bf16[128,1024]{1,0:T(8,128)(2,1)S(1)}, u32[]{:S(2)}, u32[]{:S(2)}) collective-permute-start(bf16[128,1024]{1,0:T(8,128)(2,1)S(1)} %slice_bitcast_fusion), channel_id=1, source_target_pairs={{0,4},{4,8},{8,12},{12,16},{16,20},{20,24},{24,28},{28,32},{32,36}... | collective-permute-start | bytes 786440 | tf_op jit(solution)/shard_map/ppermute | solution.py:54
  12.2 1.2 %pack.1 = (bf16[128,1024]{1,0:T(8,128)(2,1)S(1)}, bf16[128,1024]{1,0:T(8,128)(2,1)S(1)}, bf16[128,1024]{1,0:T(8,128)(2,1)S(1)}, bf16[128,1024]{1,0:T(8,128)(2,1)S(1)}) custom-call(bf16[64,4096]{1,0:T(8,128)(2,1)} %bitcast.12, bf16[64,4096]{1,0:T(8,128)(2,1)S(1)} %collective-permute-done.refs_1_), custom_call_target="tpu_custom_call" | custom-call | tf_op jit(solution)/shard_map/pack/pallas_call | solution.py:96
  13.4 1.3 %collective-permute-start.5 = (bf16[128,1024]{1,0:T(8,128)(2,1)S(1)}, bf16[128,1024]{1,0:T(8,128)(2,1)S(1)}, u32[]{:S(2)}, u32[]{:S(2)}) collective-permute-start(bf16[128,1024]{1,0:T(8,128)(2,1)S(1)} %get-tuple-element.36), channel_id=1, source_target_pairs={{0,16},{1,5},{2,18},{3,7},{4,20},{5,9},{6,22},{7,11},{8,24},{9,13}... | collective-permute-start | bytes 786440 | tf_op jit(solution)/shard_map/ppermute | solution.py:45
  15.5 4.5 %collective-permute-done.2.refs_1_.refs_0_ = bf16[128,1024]{1,0:T(8,128)(2,1)S(1)} collective-permute-done((bf16[128,1024]{1,0:T(8,128)(2,1)S(1)}, bf16[128,1024]{1,0:T(8,128)(2,1)S(1)}, u32[]{:S(2)}, u32[]{:S(2)}) %collective-permute-start.2) | collective-permute-done | bytes 262176 | tf_op jit(solution)/shard_map/ppermute | solution.py:54
  20.0 3.4 %conv_forward.1 = (f32[256,1024]{1,0:T(8,128)S(1)}, bf16[256,512]{1,0:T(8,128)(2,1)S(1)}, bf16[128,512]{1,0:T(8,128)(2,1)S(1)}, bf16[128,512]{1,0:T(8,128)(2,1)S(1)}) custom-call(bf16[64,128]{1,0:T(8,128)(2,1)} %refs_0_.3, bf16[128,1024]{1,0:T(8,128)(2,1)S(1)} %collective-permute-done.2.refs_1_.refs_0_, bf16[256,1024]{1,0:T(8,128)(2,1)} %bitcast.8, ...), custom_call_target="tpu_custom_call" | custom-call | tf_op jit(solution)/shard_map/conv_forward/pallas_call | solution.py:96
  25.1 1.3 %collective-permute-start.8 = (bf16[272,1024]{1,0:T(8,128)(2,1)S(1)}, bf16[272,1024]{1,0:T(8,128)(2,1)S(1)}, u32[]{:S(2)}, u32[]{:S(2)}) collective-permute-start(bf16[272,1024]{1,0:T(8,128)(2,1)S(1)} %join.1.refs_8_), channel_id=1, source_target_pairs={{0,16},{1,5},{2,18},{3,7},{4,20},{5,9},{6,22},{7,11},{8,24},{9,13}... | collective-permute-start | bytes 1671176 | tf_op jit(solution)/shard_map/ppermute | solution.py:45
  27.2 3.5 %collective-permute-done.1.refs_0_.refs_2_ = bf16[64,4096]{1,0:T(8,128)(2,1)S(1)} collective-permute-done((bf16[64,4096]{1,0:T(8,128)(2,1)}, bf16[64,4096]{1,0:T(8,128)(2,1)S(1)}, u32[]{:S(2)}, u32[]{:S(2)}) %collective-permute-start.1) | collective-permute-done | bytes 524320 | tf_op jit(solution)/shard_map/ppermute | solution.py:32
  30.7 1.9 %collective-permute-done.7.refs_1_.refs_3_ = bf16[64,4096]{1,0:T(8,128)(2,1)S(1)} collective-permute-done((bf16[64,4096]{1,0:T(8,128)(2,1)S(1)}, bf16[64,4096]{1,0:T(8,128)(2,1)S(1)}, u32[]{:S(2)}, u32[]{:S(2)}) %collective-permute-start.7) | collective-permute-done | bytes 524320 | tf_op jit(solution)/shard_map/ppermute | solution.py:32
  32.7 2.1 %collective-permute-done.8.refs_2_.refs_9_ = bf16[272,1024]{1,0:T(8,128)(2,1)S(1)} collective-permute-done((bf16[272,1024]{1,0:T(8,128)(2,1)S(1)}, bf16[272,1024]{1,0:T(8,128)(2,1)S(1)}, u32[]{:S(2)}, u32[]{:S(2)}) %collective-permute-start.8) | collective-permute-done | bytes 557088 | tf_op jit(solution)/shard_map/ppermute | solution.py:45
  34.7 1.2 %collective-permute-done.9.refs_3_.refs_12_ = bf16[272,1024]{1,0:T(8,128)(2,1)S(1)} collective-permute-done((bf16[272,1024]{1,0:T(8,128)(2,1)S(1)}, bf16[272,1024]{1,0:T(8,128)(2,1)S(1)}, u32[]{:S(2)}, u32[]{:S(2)}) %collective-permute-start.9) | collective-permute-done | bytes 557088 | tf_op jit(solution)/shard_map/ppermute | solution.py:45
  37.0 2.1 %collective-permute-start.11 = (bf16[256,1024]{1,0:T(8,128)(2,1)S(1)}, bf16[256,1024]{1,0:T(8,128)(2,1)S(1)}, u32[]{:S(2)}, u32[]{:S(2)}) collective-permute-start(bf16[256,1024]{1,0:T(8,128)(2,1)S(1)} %get-tuple-element.45), channel_id=1, source_target_pairs={{0,16},{1,5},{2,18},{3,7},{4,20},{5,9},{6,22},{7,11},{8,24},{9,13}... | collective-permute-start | bytes 1572872 | tf_op jit(solution)/shard_map/ppermute | solution.py:45
  39.4 6.6 %project.1 = (bf16[256,1024]{1,0:T(8,128)(2,1)S(1)}, bf16[256,1024]{1,0:T(8,128)(2,1)}) custom-call(bf16[64,4096]{1,0:T(8,128)(2,1)} %bitcast.13, bf16[64,4096]{1,0:T(8,128)(2,1)S(1)} %collective-permute-done.refs_1_, bf16[64,4096]{1,0:T(8,128)(2,1)S(1)} %collective-permute-done.1.refs_0_.refs_2_, ...), custom_call_target="tpu_custom_call" | custom-call | flops 6000000000 | tf_op jit(solution)/shard_map/project/pallas_call | solution.py:344
  46.0 3.8 %filter_grad.1.refs_13_ = f32[64,128]{1,0:T(8,128)S(1)} custom-call(bf16[128,1024]{1,0:T(8,128)(2,1)S(1)} %collective-permute-done.2.refs_1_.refs_0_, bf16[256,1024]{1,0:T(8,128)(2,1)} %bitcast.9, bf16[256,1024]{1,0:T(8,128)(2,1)S(1)} %get-tuple-element.42.refs_2_.refs_1_), custom_call_target="tpu_custom_call" | custom-call | flops 4000000000 | tf_op jit(solution)/shard_map/filter_grad/pallas_call | solution.py:96
  49.7 2.4 %collective-permute-done.11.refs_5_.refs_10_ = bf16[256,1024]{1,0:T(8,128)(2,1)S(1)} collective-permute-done((bf16[256,1024]{1,0:T(8,128)(2,1)S(1)}, bf16[256,1024]{1,0:T(8,128)(2,1)S(1)}, u32[]{:S(2)}, u32[]{:S(2)}) %collective-permute-start.11) | collective-permute-done | bytes 524320 | tf_op jit(solution)/shard_map/ppermute | solution.py:45
  52.1 3.1 %weight_parts.1 = (f32[256,1024]{1,0:T(8,128)S(1)}, bf16[256,1024]{1,0:T(8,128)(2,1)S(1)}, bf16[256,1024]{1,0:T(8,128)(2,1)S(1)}, bf16[256,1024]{1,0:T(8,128)(2,1)S(1)}) custom-call(bf16[128,1024]{1,0:T(8,128)(2,1)S(1)} %get-tuple-element.43.refs_0_, bf16[128,1024]{1,0:T(8,128)(2,1)S(1)} %collective-permute-done.5.refs_3_.refs_1_, ...), custom_call_target="tpu_custom_call" | custom-call | flops 4000000000 | tf_op jit(solution)/shard_map/weight_parts/pallas_call | solution.py:96
  55.2 1.4 %collective-permute-start.16 = (bf16[256,1024]{1,0:T(8,128)(2,1)S(1)}, bf16[256,1024]{1,0:T(8,128)(2,1)S(1)}, u32[]{:S(2)}, u32[]{:S(2)}) collective-permute-start(bf16[256,1024]{1,0:T(8,128)(2,1)S(1)} %get-tuple-element.50), channel_id=1, source_target_pairs={{0,4},{1,17},{2,6},{3,19},{4,8},{5,21},{6,10},{7,23},{8,12},{9,25}... | collective-permute-start | bytes 1572872 | tf_op jit(solution)/shard_map/ppermute | solution.py:45
  57.2 2.3 %collective-permute-start.18 = (bf16[256,1024]{1,0:T(8,128)(2,1)S(1)}, bf16[256,1024]{1,0:T(8,128)(2,1)S(1)}, u32[]{:S(2)}, u32[]{:S(2)}) collective-permute-start(bf16[256,1024]{1,0:T(8,128)(2,1)S(1)} %get-tuple-element.52), channel_id=1, source_target_pairs={{0,12},{1,49},{2,14},{3,51},{4,0},{5,53},{6,2},{7,55},{8,4},{9,57}... | collective-permute-start | bytes 1572872 | tf_op jit(solution)/shard_map/ppermute | solution.py:45
  59.5 1.0 %collective-permute-start.13 = (f32[64,128]{1,0:T(8,128)S(1)}, f32[64,128]{1,0:T(8,128)S(1)}, u32[]{:S(2)}, u32[]{:S(2)}) collective-permute-start(f32[64,128]{1,0:T(8,128)S(1)} %filter_grad.1.refs_13_), channel_id=1, source_target_pairs={{0,64},{64,0},{128,192},{192,128},{1,65},{65,1},{129,193},{193,129... | collective-permute-start | bytes 98312 | tf_op jit(solution)/shard_map/ppermute | solution.py:489
  60.5 2.9 %collective-permute-done.13 = f32[64,128]{1,0:T(8,128)S(1)} collective-permute-done((f32[64,128]{1,0:T(8,128)S(1)}, f32[64,128]{1,0:T(8,128)S(1)}, u32[]{:S(2)}, u32[]{:S(2)}) %collective-permute-start.13) | collective-permute-done | bytes 32800 | tf_op jit(solution)/shard_map/ppermute | solution.py:489
  63.4 1.6 %collective-permute-start.14 = (f32[64,128]{1,0:T(8,128)S(1)}, f32[64,128]{1,0:T(8,128)S(1)}, u32[]{:S(2)}, u32[]{:S(2)}) collective-permute-start(f32[64,128]{1,0:T(8,128)S(1)} %add.20), channel_id=1, source_target_pairs={{0,128},{64,192},{128,0},{192,64},{1,129},{65,193},{129,1},{193,65... | collective-permute-start | bytes 98312 | tf_op jit(solution)/shard_map/ppermute | solution.py:489
  65.0 3.2 %collective-permute-done.14 = f32[64,128]{1,0:T(8,128)S(1)} collective-permute-done((f32[64,128]{1,0:T(8,128)S(1)}, f32[64,128]{1,0:T(8,128)S(1)}, u32[]{:S(2)}, u32[]{:S(2)}) %collective-permute-start.14) | collective-permute-done | bytes 32800 | tf_op jit(solution)/shard_map/ppermute | solution.py:489
  68.2 2.6 %collective-permute-start.23 = (f32[64,128]{1,0:T(8,128)S(1)}, f32[64,128]{1,0:T(8,128)S(1)}, u32[]{:S(2)}, u32[]{:S(2)}) collective-permute-start(f32[64,128]{1,0:T(8,128)S(1)} %add.21), channel_id=1, source_target_pairs={{0,16},{1,5},{2,18},{3,7},{4,20},{5,1},{6,22},{7,3},{8,24},{9,13},... | collective-permute-start | bytes 98312 | tf_op jit(solution)/shard_map/ppermute | solution.py:45
  70.8 2.6 %collective-permute-start.15 = (bf16[192,1024]{1,0:T(8,128)(2,1)S(1)}, bf16[192,1024]{1,0:T(8,128)(2,1)S(1)}, u32[]{:S(2)}, u32[]{:S(2)}) collective-permute-start(bf16[192,1024]{1,0:T(8,128)(2,1)S(1)} %slice.14), channel_id=1, source_target_pairs={{4,0},{8,4},{12,8},{16,12},{20,16},{24,20},{28,24},{32,28},{36,32}... | collective-permute-start | bytes 1179656 | tf_op jit(solution)/shard_map/ppermute | solution.py:54
  74.6 1.1 %collective-permute-start.19 = (bf16[64,1024]{1,0:T(8,128)(2,1)S(1)}, bf16[64,1024]{1,0:T(8,128)(2,1)S(1)}, u32[]{:S(2)}, u32[]{:S(2)}) collective-permute-start(bf16[64,1024]{1,0:T(8,128)(2,1)S(1)} %get-tuple-element.55), channel_id=1, source_target_pairs={{0,64},{64,128},{128,192},{192,0},{1,65},{65,129},{129,193},{193,1... | collective-permute-start | bytes 393224 | tf_op jit(solution)/shard_map/ppermute | solution.py:533
  75.7 1.5 %collective-permute-start.20 = (bf16[64,1024]{1,0:T(8,128)(2,1)S(1)}, bf16[64,1024]{1,0:T(8,128)(2,1)S(1)}, u32[]{:S(2)}, u32[]{:S(2)}) collective-permute-start(bf16[64,1024]{1,0:T(8,128)(2,1)S(1)} %get-tuple-element.56), channel_id=1, source_target_pairs={{0,128},{64,192},{128,0},{192,64},{1,129},{65,193},{129,1},{193,65... | collective-permute-start | bytes 393224 | tf_op jit(solution)/shard_map/ppermute | solution.py:533
  77.2 1.9 %collective-permute-start.21 = (bf16[64,1024]{1,0:T(8,128)(2,1)S(1)}, bf16[64,1024]{1,0:T(8,128)(2,1)S(1)}, u32[]{:S(2)}, u32[]{:S(2)}) collective-permute-start(bf16[64,1024]{1,0:T(8,128)(2,1)S(1)} %get-tuple-element.57), channel_id=1, source_target_pairs={{0,192},{64,0},{128,64},{192,128},{1,193},{65,1},{129,65},{193,129... | collective-permute-start | bytes 393224 | tf_op jit(solution)/shard_map/ppermute | solution.py:533
  79.1 1.3 %collective-permute-done.24 = f32[256,128]{1,0:T(8,128)S(1)} collective-permute-done((f32[256,128]{1,0:T(8,128)S(1)}, f32[256,128]{1,0:T(8,128)S(1)}, u32[]{:S(2)}, u32[]{:S(2)}) %collective-permute-start.24) | collective-permute-done | bytes 131104 | tf_op jit(solution)/shard_map/ppermute | solution.py:45
  80.4 8.7 %collective-permute-start.25 = (f32[64,128]{1,0:T(8,128)S(1)}, f32[64,128]{1,0:T(8,128)S(1)}, u32[]{:S(2)}, u32[]{:S(2)}) collective-permute-start(f32[64,128]{1,0:T(8,128)S(1)} %slice_add_fusion), channel_id=1, source_target_pairs={{0,4},{1,17},{2,6},{3,19},{4,0},{5,21},{6,2},{7,23},{8,12},{9,25},... | collective-permute-start | bytes 98312 | tf_op jit(solution)/shard_map/ppermute | solution.py:45
  89.1 3.4 %input_grad.1.refs_4_ = bf16[256,1024]{1,0:T(8,128)(2,1)} custom-call(bf16[64,128]{1,0:T(8,128)(2,1)} %refs_0_.3, bf16[256,1024]{1,0:T(8,128)(2,1)S(1)} %get-tuple-element.42.refs_2_.refs_1_, bf16[192,1024]{1,0:T(8,128)(2,1)S(1)} %collective-permute-done.15.refs_2_, f32[64,1024]{1,0:T(8,128)S(1)} %get-tuple-element.53.refs_3_.refs_0_), custom_call_target="tpu_custom_call" | custom-call | tf_op jit(solution)/shard_map/input_grad/pallas_call | solution.py:96
  92.9 5.2 %collective-permute-done.26 = f32[64,128]{1,0:T(8,128)S(1)} collective-permute-done((f32[64,128]{1,0:T(8,128)S(1)}, f32[64,128]{1,0:T(8,128)S(1)}, u32[]{:S(2)}, u32[]{:S(2)}) %collective-permute-start.26) | collective-permute-done | bytes 32800 | tf_op jit(solution)/shard_map/ppermute | solution.py:45
  (42 shorter events, 8.2 us)
Async XLA Ops:
  0.6 11.6 %collective-permute-start = (bf16[64,4096]{1,0:T(8,128)(2,1)}, bf16[64,4096]{1,0:T(8,128)(2,1)S(1)}, u32[]{:S(2)}, u32[]{:S(2)}) collective-permute-start(bf16[64,4096]{1,0:T(8,128)(2,1)} %bitcast.10), channel_id=1, source_target_pairs={{0,1},{1,0},{2,3},{3,2},{4,5},{5,4},{6,7},{7,6},{8,9},{9,8},{10,11... | collective-permute-start | bytes 1572872 | tf_op jit(solution)/shard_map/ppermute | solution.py:32
  0.7 30.0 %collective-permute-start.1 = (bf16[64,4096]{1,0:T(8,128)(2,1)}, bf16[64,4096]{1,0:T(8,128)(2,1)S(1)}, u32[]{:S(2)}, u32[]{:S(2)}) collective-permute-start(bf16[64,4096]{1,0:T(8,128)(2,1)} %bitcast.11), channel_id=1, source_target_pairs={{0,2},{1,3},{2,0},{3,1},{4,6},{5,7},{6,4},{7,5},{8,10},{9,11},{10,... | collective-permute-start | bytes 1572872 | tf_op jit(solution)/shard_map/ppermute | solution.py:32
  9.0 11.0 %collective-permute-start.2 = (bf16[128,1024]{1,0:T(8,128)(2,1)S(1)}, bf16[128,1024]{1,0:T(8,128)(2,1)S(1)}, u32[]{:S(2)}, u32[]{:S(2)}) collective-permute-start(bf16[128,1024]{1,0:T(8,128)(2,1)S(1)} %slice_bitcast_fusion), channel_id=1, source_target_pairs={{0,4},{4,8},{8,12},{12,16},{16,20},{20,24},{24,28},{28,32},{32,36}... | collective-permute-start | bytes 786440 | tf_op jit(solution)/shard_map/ppermute | solution.py:54
  13.4 11.7 %collective-permute-start.5 = (bf16[128,1024]{1,0:T(8,128)(2,1)S(1)}, bf16[128,1024]{1,0:T(8,128)(2,1)S(1)}, u32[]{:S(2)}, u32[]{:S(2)}) collective-permute-start(bf16[128,1024]{1,0:T(8,128)(2,1)S(1)} %get-tuple-element.36), channel_id=1, source_target_pairs={{0,16},{1,5},{2,18},{3,7},{4,20},{5,9},{6,22},{7,11},{8,24},{9,13}... | collective-permute-start | bytes 786440 | tf_op jit(solution)/shard_map/ppermute | solution.py:45
  14.7 10.4 %collective-permute-start.6 = (bf16[128,1024]{1,0:T(8,128)(2,1)S(1)}, bf16[128,1024]{1,0:T(8,128)(2,1)S(1)}, u32[]{:S(2)}, u32[]{:S(2)}) collective-permute-start(bf16[128,1024]{1,0:T(8,128)(2,1)S(1)} %get-tuple-element.37), channel_id=1, source_target_pairs={{0,48},{1,13},{2,50},{3,15},{4,52},{5,1},{6,54},{7,3},{8,56},{9,5}... | collective-permute-start | bytes 786440 | tf_op jit(solution)/shard_map/ppermute | solution.py:45
  23.4 1.4 %collective-permute-start.3 = (bf16[128,512]{1,0:T(8,128)(2,1)S(1)}, bf16[128,512]{1,0:T(8,128)(2,1)S(1)}, u32[]{:S(2)}, u32[]{:S(2)}) collective-permute-start(bf16[128,512]{1,0:T(8,128)(2,1)S(1)} %get-tuple-element.34), channel_id=1, source_target_pairs={{0,1},{1,0},{2,3},{3,2},{4,5},{5,4},{6,7},{7,6},{8,9},{9,8},{10,11... | collective-permute-start | bytes 393224 | tf_op jit(solution)/shard_map/ppermute | solution.py:32
  23.5 1.5 %collective-permute-start.4 = (bf16[128,512]{1,0:T(8,128)(2,1)S(1)}, bf16[128,512]{1,0:T(8,128)(2,1)S(1)}, u32[]{:S(2)}, u32[]{:S(2)}) collective-permute-start(bf16[128,512]{1,0:T(8,128)(2,1)S(1)} %get-tuple-element.35), channel_id=1, source_target_pairs={{0,1},{1,0},{2,3},{3,2},{4,5},{5,4},{6,7},{7,6},{8,9},{9,8},{10,11... | collective-permute-start | bytes 393224 | tf_op jit(solution)/shard_map/ppermute | solution.py:32
  25.1 9.6 %collective-permute-start.8 = (bf16[272,1024]{1,0:T(8,128)(2,1)S(1)}, bf16[272,1024]{1,0:T(8,128)(2,1)S(1)}, u32[]{:S(2)}, u32[]{:S(2)}) collective-permute-start(bf16[272,1024]{1,0:T(8,128)(2,1)S(1)} %join.1.refs_8_), channel_id=1, source_target_pairs={{0,16},{1,5},{2,18},{3,7},{4,20},{5,9},{6,22},{7,11},{8,24},{9,13}... | collective-permute-start | bytes 1671176 | tf_op jit(solution)/shard_map/ppermute | solution.py:45
  26.4 9.5 %collective-permute-start.9 = (bf16[272,1024]{1,0:T(8,128)(2,1)S(1)}, bf16[272,1024]{1,0:T(8,128)(2,1)S(1)}, u32[]{:S(2)}, u32[]{:S(2)}) collective-permute-start(bf16[272,1024]{1,0:T(8,128)(2,1)S(1)} %join.1.refs_8_), channel_id=1, source_target_pairs={{0,48},{1,13},{2,50},{3,15},{4,52},{5,1},{6,54},{7,3},{8,56},{9,5}... | collective-permute-start | bytes 1671176 | tf_op jit(solution)/shard_map/ppermute | solution.py:45
  30.7 1.9 %collective-permute-start.7 = (bf16[64,4096]{1,0:T(8,128)(2,1)S(1)}, bf16[64,4096]{1,0:T(8,128)(2,1)S(1)}, u32[]{:S(2)}, u32[]{:S(2)}) collective-permute-start(bf16[64,4096]{1,0:T(8,128)(2,1)S(1)} %collective-permute-done.1.refs_0_.refs_2_), channel_id=1, source_target_pairs={{0,1},{1,0},{2,3},{3,2},{4,5},{5,4},{6,7},{7,6},{8,9},{9,8},{10,11... | collective-permute-start | bytes 1572872 | tf_op jit(solution)/shard_map/ppermute | solution.py:32
  36.1 13.6 %collective-permute-start.10 = (bf16[256,1024]{1,0:T(8,128)(2,1)S(1)}, bf16[256,1024]{1,0:T(8,128)(2,1)S(1)}, u32[]{:S(2)}, u32[]{:S(2)}) collective-permute-start(bf16[256,1024]{1,0:T(8,128)(2,1)S(1)} %get-tuple-element.44), channel_id=1, source_target_pairs={{0,32},{1,9},{2,34},{3,11},{4,36},{5,13},{6,38},{7,15},{8,40},{9,1... | collective-permute-start | bytes 1572872 | tf_op jit(solution)/shard_map/ppermute | solution.py:45
  37.0 15.1 %collective-permute-start.11 = (bf16[256,1024]{1,0:T(8,128)(2,1)S(1)}, bf16[256,1024]{1,0:T(8,128)(2,1)S(1)}, u32[]{:S(2)}, u32[]{:S(2)}) collective-permute-start(bf16[256,1024]{1,0:T(8,128)(2,1)S(1)} %get-tuple-element.45), channel_id=1, source_target_pairs={{0,16},{1,5},{2,18},{3,7},{4,20},{5,9},{6,22},{7,11},{8,24},{9,13}... | collective-permute-start | bytes 1572872 | tf_op jit(solution)/shard_map/ppermute | solution.py:45
  39.1 13.0 %collective-permute-start.12 = (bf16[256,1024]{1,0:T(8,128)(2,1)S(1)}, bf16[256,1024]{1,0:T(8,128)(2,1)S(1)}, u32[]{:S(2)}, u32[]{:S(2)}) collective-permute-start(bf16[256,1024]{1,0:T(8,128)(2,1)S(1)} %get-tuple-element.46), channel_id=1, source_target_pairs={{0,48},{1,13},{2,50},{3,15},{4,52},{5,1},{6,54},{7,3},{8,56},{9,5}... | collective-permute-start | bytes 1572872 | tf_op jit(solution)/shard_map/ppermute | solution.py:45
  55.2 18.9 %collective-permute-start.16 = (bf16[256,1024]{1,0:T(8,128)(2,1)S(1)}, bf16[256,1024]{1,0:T(8,128)(2,1)S(1)}, u32[]{:S(2)}, u32[]{:S(2)}) collective-permute-start(bf16[256,1024]{1,0:T(8,128)(2,1)S(1)} %get-tuple-element.50), channel_id=1, source_target_pairs={{0,4},{1,17},{2,6},{3,19},{4,8},{5,21},{6,10},{7,23},{8,12},{9,25}... | collective-permute-start | bytes 1572872 | tf_op jit(solution)/shard_map/ppermute | solution.py:45
  56.6 17.6 %collective-permute-start.17 = (bf16[256,1024]{1,0:T(8,128)(2,1)S(1)}, bf16[256,1024]{1,0:T(8,128)(2,1)S(1)}, u32[]{:S(2)}, u32[]{:S(2)}) collective-permute-start(bf16[256,1024]{1,0:T(8,128)(2,1)S(1)} %get-tuple-element.51), channel_id=1, source_target_pairs={{0,8},{1,33},{2,10},{3,35},{4,12},{5,37},{6,14},{7,39},{8,0},{9,41... | collective-permute-start | bytes 1572872 | tf_op jit(solution)/shard_map/ppermute | solution.py:45
  57.2 17.0 %collective-permute-start.18 = (bf16[256,1024]{1,0:T(8,128)(2,1)S(1)}, bf16[256,1024]{1,0:T(8,128)(2,1)S(1)}, u32[]{:S(2)}, u32[]{:S(2)}) collective-permute-start(bf16[256,1024]{1,0:T(8,128)(2,1)S(1)} %get-tuple-element.52), channel_id=1, source_target_pairs={{0,12},{1,49},{2,14},{3,51},{4,0},{5,53},{6,2},{7,55},{8,4},{9,57}... | collective-permute-start | bytes 1572872 | tf_op jit(solution)/shard_map/ppermute | solution.py:45
  59.5 3.9 %collective-permute-start.13 = (f32[64,128]{1,0:T(8,128)S(1)}, f32[64,128]{1,0:T(8,128)S(1)}, u32[]{:S(2)}, u32[]{:S(2)}) collective-permute-start(f32[64,128]{1,0:T(8,128)S(1)} %filter_grad.1.refs_13_), channel_id=1, source_target_pairs={{0,64},{64,0},{128,192},{192,128},{1,65},{65,1},{129,193},{193,129... | collective-permute-start | bytes 98312 | tf_op jit(solution)/shard_map/ppermute | solution.py:489
  63.4 4.8 %collective-permute-start.14 = (f32[64,128]{1,0:T(8,128)S(1)}, f32[64,128]{1,0:T(8,128)S(1)}, u32[]{:S(2)}, u32[]{:S(2)}) collective-permute-start(f32[64,128]{1,0:T(8,128)S(1)} %add.20), channel_id=1, source_target_pairs={{0,128},{64,192},{128,0},{192,64},{1,129},{65,193},{129,1},{193,65... | collective-permute-start | bytes 98312 | tf_op jit(solution)/shard_map/ppermute | solution.py:489
  68.2 5.2 %collective-permute-start.23 = (f32[64,128]{1,0:T(8,128)S(1)}, f32[64,128]{1,0:T(8,128)S(1)}, u32[]{:S(2)}, u32[]{:S(2)}) collective-permute-start(f32[64,128]{1,0:T(8,128)S(1)} %add.21), channel_id=1, source_target_pairs={{0,16},{1,5},{2,18},{3,7},{4,20},{5,1},{6,22},{7,3},{8,24},{9,13},... | collective-permute-start | bytes 98312 | tf_op jit(solution)/shard_map/ppermute | solution.py:45
  70.8 18.3 %collective-permute-start.15 = (bf16[192,1024]{1,0:T(8,128)(2,1)S(1)}, bf16[192,1024]{1,0:T(8,128)(2,1)S(1)}, u32[]{:S(2)}, u32[]{:S(2)}) collective-permute-start(bf16[192,1024]{1,0:T(8,128)(2,1)S(1)} %slice.14), channel_id=1, source_target_pairs={{4,0},{8,4},{12,8},{16,12},{20,16},{24,20},{28,24},{32,28},{36,32}... | collective-permute-start | bytes 1179656 | tf_op jit(solution)/shard_map/ppermute | solution.py:54
  73.5 6.9 %collective-permute-start.24 = (f32[256,128]{1,0:T(8,128)S(1)}, f32[256,128]{1,0:T(8,128)S(1)}, u32[]{:S(2)}, u32[]{:S(2)}) collective-permute-start(f32[256,128]{1,0:T(8,128)S(1)} %pad.4), channel_id=1, source_target_pairs={{0,32},{1,9},{2,34},{3,11},{4,36},{5,13},{6,38},{7,15},{8,40},{9,1... | collective-permute-start | bytes 393224 | tf_op jit(solution)/shard_map/ppermute | solution.py:45
  74.6 18.1 %collective-permute-start.19 = (bf16[64,1024]{1,0:T(8,128)(2,1)S(1)}, bf16[64,1024]{1,0:T(8,128)(2,1)S(1)}, u32[]{:S(2)}, u32[]{:S(2)}) collective-permute-start(bf16[64,1024]{1,0:T(8,128)(2,1)S(1)} %get-tuple-element.55), channel_id=1, source_target_pairs={{0,64},{64,128},{128,192},{192,0},{1,65},{65,129},{129,193},{193,1... | collective-permute-start | bytes 393224 | tf_op jit(solution)/shard_map/ppermute | solution.py:533
  75.7 17.0 %collective-permute-start.20 = (bf16[64,1024]{1,0:T(8,128)(2,1)S(1)}, bf16[64,1024]{1,0:T(8,128)(2,1)S(1)}, u32[]{:S(2)}, u32[]{:S(2)}) collective-permute-start(bf16[64,1024]{1,0:T(8,128)(2,1)S(1)} %get-tuple-element.56), channel_id=1, source_target_pairs={{0,128},{64,192},{128,0},{192,64},{1,129},{65,193},{129,1},{193,65... | collective-permute-start | bytes 393224 | tf_op jit(solution)/shard_map/ppermute | solution.py:533
  77.2 15.5 %collective-permute-start.21 = (bf16[64,1024]{1,0:T(8,128)(2,1)S(1)}, bf16[64,1024]{1,0:T(8,128)(2,1)S(1)}, u32[]{:S(2)}, u32[]{:S(2)}) collective-permute-start(bf16[64,1024]{1,0:T(8,128)(2,1)S(1)} %get-tuple-element.57), channel_id=1, source_target_pairs={{0,192},{64,0},{128,64},{192,128},{1,193},{65,1},{129,65},{193,129... | collective-permute-start | bytes 393224 | tf_op jit(solution)/shard_map/ppermute | solution.py:533
  80.4 12.2 %collective-permute-start.25 = (f32[64,128]{1,0:T(8,128)S(1)}, f32[64,128]{1,0:T(8,128)S(1)}, u32[]{:S(2)}, u32[]{:S(2)}) collective-permute-start(f32[64,128]{1,0:T(8,128)S(1)} %slice_add_fusion), channel_id=1, source_target_pairs={{0,4},{1,17},{2,6},{3,19},{4,0},{5,21},{6,2},{7,23},{8,12},{9,25},... | collective-permute-start | bytes 98312 | tf_op jit(solution)/shard_map/ppermute | solution.py:45
  92.6 5.5 %collective-permute-start.26 = (f32[64,128]{1,0:T(8,128)S(1)}, f32[64,128]{1,0:T(8,128)S(1)}, u32[]{:S(2)}, u32[]{:S(2)}) collective-permute-start(f32[64,128]{1,0:T(8,128)S(1)} %add.24), channel_id=1, source_target_pairs={{0,8},{1,33},{2,10},{3,35},{4,12},{5,37},{6,14},{7,39},{8,0},{9,41... | collective-permute-start | bytes 98312 | tf_op jit(solution)/shard_map/ppermute | solution.py:45
  92.8 5.9 %collective-permute-start.22 = (f32[64,512]{1,0:T(8,128)S(1)}, f32[64,512]{1,0:T(8,128)S(1)}, u32[]{:S(2)}, u32[]{:S(2)}) collective-permute-start(f32[64,512]{1,0:T(8,128)S(1)} %get-tuple-element.59), channel_id=1, source_target_pairs={{0,1},{1,0},{2,3},{3,2},{4,5},{5,4},{6,7},{7,6},{8,9},{9,8},{10,11... | collective-permute-start | bytes 393224 | tf_op jit(solution)/shard_map/ppermute | solution.py:32

commit v14 on v12

--- a/solution.py
+++ b/solution.py
@@ -520,7 +520,7 @@
     filter_sum = paired_z(paired_z(tied(filter_sum, parts[0]), 1), 2)
     following = shifted(tied(conv_grad[:TAPS], filter_sum), -1)
     filter_sum = paired(filter_sum, True, 1)
-    padded = jnp.pad(filter_sum, ((0, 3 * filter_sum.shape[0]), (0, 0)))
+    padded = jnp.pad(filter_sum, ((0, 2 * filter_sum.shape[0]), (0, 0)))
     padded = in_plane(padded, True, lambda place: place ^ 2)
     filter_sum = filter_sum + padded[: filter_sum.shape[0]]
     parts = [parts[0]] + [stepped(parts[s], False, s) for s in shifts]

time: 96.5 us -> 96.5 us (level)
  no operation moved by 1% of the time
where the time goes in v14:
time: 96.5 us; the launch traced here: 96.1 us
  starting transfers between devices  40.1 us (42%)
  waiting for transfers between devices  30.6 us (32%)
  Pallas kernels  22.9 us (24%)
  local copies, waits for them, and re-layouts  0.99 us (1%)
    ppermute x14, starting transfers between devices, in_plane(): return lax.ppermute(x, ('ctx', 'tp'), pairs)  19.3 us
    pallas_call x10, Pallas kernels, once(): pl.pallas_call(body, grid=(1,), in_specs=specs + [ANYWHERE] * len(after),...  16.3 us
    ppermute x14, waiting for transfers between devices, in_plane(): return lax.ppermute(x, ('ctx', 'tp'), pairs)  13.7 us
    ppermute x6, starting transfers between devices, moved(): return lax.ppermute(x, 'tp', [(i, i ^ step) for i in range(4)])  8.06 us
    pallas_call x1, Pallas kernels, project(): pl.pallas_call(body, grid=(channels // WIDE,), in_specs=[full(early.shape...  6.59 us
    ppermute x2, waiting for transfers between devices, paired_z(): return x + lax.ppermute(x, 'dp', [(i, i ^ by) for i in range(SIDE)])  6.24 us
    ppermute x2, starting transfers between devices, shifted(): lax.ppermute(x, 'ctx', [(i, i + by) for i in range(devices) if 0 <= i + b...  5.86 us
    ppermute x2, waiting for transfers between devices, shifted(): lax.ppermute(x, 'ctx', [(i, i + by) for i in range(devices) if 0 <= i + b...  5.67 us
  transfers between devices with their start and end apart: 27, of which 13 were waited for; matrix products, arithmetic and copies ran while one was open for 2% of the time, Pallas kernels for 20%

profile of v14, /device:TPU:2, one launch (start us, length us, event | category | flops | bytes accessed | tf_op | source)
XLA Modules:
  0.0 96.1 jit_solution(7946840883650796407)
XLA Ops:
  0.7 7.3 %collective-permute-start.1 = (bf16[64,4096]{1,0:T(8,128)(2,1)}, bf16[64,4096]{1,0:T(8,128)(2,1)S(1)}, u32[]{:S(2)}, u32[]{:S(2)}) collective-permute-start(bf16[64,4096]{1,0:T(8,128)(2,1)} %bitcast.11), channel_id=1, source_target_pairs={{0,2},{1,3},{2,0},{3,1},{4,6},{5,7},{6,4},{7,5},{8,10},{9,11},{10,... | collective-permute-start | bytes 1572872 | tf_op jit(solution)/shard_map/ppermute | solution.py:32
  9.0 3.5 %collective-permute-start.2 = (bf16[128,1024]{1,0:T(8,128)(2,1)S(1)}, bf16[128,1024]{1,0:T(8,128)(2,1)S(1)}, u32[]{:S(2)}, u32[]{:S(2)}) collective-permute-start(bf16[128,1024]{1,0:T(8,128)(2,1)S(1)} %slice_bitcast_fusion), channel_id=1, source_target_pairs={{0,4},{4,8},{8,12},{12,16},{16,20},{20,24},{24,28},{28,32},{32,36}... | collective-permute-start | bytes 786440 | tf_op jit(solution)/shard_map/ppermute | solution.py:54
  12.5 1.2 %pack.1 = (bf16[128,1024]{1,0:T(8,128)(2,1)S(1)}, bf16[128,1024]{1,0:T(8,128)(2,1)S(1)}, bf16[128,1024]{1,0:T(8,128)(2,1)S(1)}, bf16[128,1024]{1,0:T(8,128)(2,1)S(1)}) custom-call(bf16[64,4096]{1,0:T(8,128)(2,1)} %bitcast.12, bf16[64,4096]{1,0:T(8,128)(2,1)S(1)} %collective-permute-done.refs_1_), custom_call_target="tpu_custom_call" | custom-call | tf_op jit(solution)/shard_map/pack/pallas_call | solution.py:96
  13.7 1.6 %collective-permute-start.5 = (bf16[128,1024]{1,0:T(8,128)(2,1)S(1)}, bf16[128,1024]{1,0:T(8,128)(2,1)S(1)}, u32[]{:S(2)}, u32[]{:S(2)}) collective-permute-start(bf16[128,1024]{1,0:T(8,128)(2,1)S(1)} %get-tuple-element.36), channel_id=1, source_target_pairs={{0,16},{1,5},{2,18},{3,7},{4,20},{5,9},{6,22},{7,11},{8,24},{9,13}... | collective-permute-start | bytes 786440 | tf_op jit(solution)/shard_map/ppermute | solution.py:45
  15.8 5.7 %collective-permute-done.2.refs_1_.refs_0_ = bf16[128,1024]{1,0:T(8,128)(2,1)S(1)} collective-permute-done((bf16[128,1024]{1,0:T(8,128)(2,1)S(1)}, bf16[128,1024]{1,0:T(8,128)(2,1)S(1)}, u32[]{:S(2)}, u32[]{:S(2)}) %collective-permute-start.2) | collective-permute-done | bytes 262176 | tf_op jit(solution)/shard_map/ppermute | solution.py:54
  21.4 3.4 %conv_forward.1 = (f32[256,1024]{1,0:T(8,128)S(1)}, bf16[256,512]{1,0:T(8,128)(2,1)S(1)}, bf16[128,512]{1,0:T(8,128)(2,1)S(1)}, bf16[128,512]{1,0:T(8,128)(2,1)S(1)}) custom-call(bf16[64,128]{1,0:T(8,128)(2,1)} %refs_0_.3, bf16[128,1024]{1,0:T(8,128)(2,1)S(1)} %collective-permute-done.2.refs_1_.refs_0_, bf16[256,1024]{1,0:T(8,128)(2,1)} %bitcast.8, ...), custom_call_target="tpu_custom_call" | custom-call | tf_op jit(solution)/shard_map/conv_forward/pallas_call | solution.py:96
  26.5 1.6 %collective-permute-start.8 = (bf16[272,1024]{1,0:T(8,128)(2,1)S(1)}, bf16[272,1024]{1,0:T(8,128)(2,1)S(1)}, u32[]{:S(2)}, u32[]{:S(2)}) collective-permute-start(bf16[272,1024]{1,0:T(8,128)(2,1)S(1)} %join.1.refs_8_), channel_id=1, source_target_pairs={{0,16},{1,5},{2,18},{3,7},{4,20},{5,9},{6,22},{7,11},{8,24},{9,13}... | collective-permute-start | bytes 1671176 | tf_op jit(solution)/shard_map/ppermute | solution.py:45
  28.6 2.1 %collective-permute-done.1.refs_0_.refs_2_ = bf16[64,4096]{1,0:T(8,128)(2,1)S(1)} collective-permute-done((bf16[64,4096]{1,0:T(8,128)(2,1)}, bf16[64,4096]{1,0:T(8,128)(2,1)S(1)}, u32[]{:S(2)}, u32[]{:S(2)}) %collective-permute-start.1) | collective-permute-done | bytes 524320 | tf_op jit(solution)/shard_map/ppermute | solution.py:32
  30.7 1.9 %collective-permute-done.7.refs_1_.refs_3_ = bf16[64,4096]{1,0:T(8,128)(2,1)S(1)} collective-permute-done((bf16[64,4096]{1,0:T(8,128)(2,1)S(1)}, bf16[64,4096]{1,0:T(8,128)(2,1)S(1)}, u32[]{:S(2)}, u32[]{:S(2)}) %collective-permute-start.7) | collective-permute-done | bytes 524320 | tf_op jit(solution)/shard_map/ppermute | solution.py:32
  32.7 3.5 %collective-permute-done.8.refs_2_.refs_9_ = bf16[272,1024]{1,0:T(8,128)(2,1)S(1)} collective-permute-done((bf16[272,1024]{1,0:T(8,128)(2,1)S(1)}, bf16[272,1024]{1,0:T(8,128)(2,1)S(1)}, u32[]{:S(2)}, u32[]{:S(2)}) %collective-permute-start.8) | collective-permute-done | bytes 557088 | tf_op jit(solution)/shard_map/ppermute | solution.py:45
  36.2 1.5 %collective-permute-done.9.refs_3_.refs_12_ = bf16[272,1024]{1,0:T(8,128)(2,1)S(1)} collective-permute-done((bf16[272,1024]{1,0:T(8,128)(2,1)S(1)}, bf16[272,1024]{1,0:T(8,128)(2,1)S(1)}, u32[]{:S(2)}, u32[]{:S(2)}) %collective-permute-start.9) | collective-permute-done | bytes 557088 | tf_op jit(solution)/shard_map/ppermute | solution.py:45
  37.8 2.0 %collective-permute-start.10 = (bf16[256,1024]{1,0:T(8,128)(2,1)S(1)}, bf16[256,1024]{1,0:T(8,128)(2,1)S(1)}, u32[]{:S(2)}, u32[]{:S(2)}) collective-permute-start(bf16[256,1024]{1,0:T(8,128)(2,1)S(1)} %get-tuple-element.44), channel_id=1, source_target_pairs={{0,32},{1,9},{2,34},{3,11},{4,36},{5,13},{6,38},{7,15},{8,40},{9,1... | collective-permute-start | bytes 1572872 | tf_op jit(solution)/shard_map/ppermute | solution.py:45
  39.9 2.0 %collective-permute-start.12 = (bf16[256,1024]{1,0:T(8,128)(2,1)S(1)}, bf16[256,1024]{1,0:T(8,128)(2,1)S(1)}, u32[]{:S(2)}, u32[]{:S(2)}) collective-permute-start(bf16[256,1024]{1,0:T(8,128)(2,1)S(1)} %get-tuple-element.46), channel_id=1, source_target_pairs={{0,48},{1,13},{2,50},{3,15},{4,52},{5,1},{6,54},{7,3},{8,56},{9,5}... | collective-permute-start | bytes 1572872 | tf_op jit(solution)/shard_map/ppermute | solution.py:45
  41.9 6.6 %project.1 = (bf16[256,1024]{1,0:T(8,128)(2,1)S(1)}, bf16[256,1024]{1,0:T(8,128)(2,1)}) custom-call(bf16[64,4096]{1,0:T(8,128)(2,1)} %bitcast.13, bf16[64,4096]{1,0:T(8,128)(2,1)S(1)} %collective-permute-done.refs_1_, bf16[64,4096]{1,0:T(8,128)(2,1)S(1)} %collective-permute-done.1.refs_0_.refs_2_, ...), custom_call_target="tpu_custom_call" | custom-call | flops 6000000000 | tf_op jit(solution)/shard_map/project/pallas_call | solution.py:344
  48.5 3.8 %filter_grad.1.refs_13_ = f32[64,128]{1,0:T(8,128)S(1)} custom-call(bf16[128,1024]{1,0:T(8,128)(2,1)S(1)} %collective-permute-done.2.refs_1_.refs_0_, bf16[256,1024]{1,0:T(8,128)(2,1)} %bitcast.9, bf16[256,1024]{1,0:T(8,128)(2,1)S(1)} %get-tuple-element.42.refs_2_.refs_1_), custom_call_target="tpu_custom_call" | custom-call | flops 4000000000 | tf_op jit(solution)/shard_map/filter_grad/pallas_call | solution.py:96
  52.3 1.7 %collective-permute-done.11.refs_5_.refs_10_ = bf16[256,1024]{1,0:T(8,128)(2,1)S(1)} collective-permute-done((bf16[256,1024]{1,0:T(8,128)(2,1)S(1)}, bf16[256,1024]{1,0:T(8,128)(2,1)S(1)}, u32[]{:S(2)}, u32[]{:S(2)}) %collective-permute-start.11) | collective-permute-done | bytes 524320 | tf_op jit(solution)/shard_map/ppermute | solution.py:45
  54.2 3.1 %weight_parts.1 = (f32[256,1024]{1,0:T(8,128)S(1)}, bf16[256,1024]{1,0:T(8,128)(2,1)S(1)}, bf16[256,1024]{1,0:T(8,128)(2,1)S(1)}, bf16[256,1024]{1,0:T(8,128)(2,1)S(1)}) custom-call(bf16[128,1024]{1,0:T(8,128)(2,1)S(1)} %get-tuple-element.43.refs_0_, bf16[128,1024]{1,0:T(8,128)(2,1)S(1)} %collective-permute-done.5.refs_3_.refs_1_, ...), custom_call_target="tpu_custom_call" | custom-call | flops 4000000000 | tf_op jit(solution)/shard_map/weight_parts/pallas_call | solution.py:96
  57.5 2.9 %collective-permute-start.17 = (bf16[256,1024]{1,0:T(8,128)(2,1)S(1)}, bf16[256,1024]{1,0:T(8,128)(2,1)S(1)}, u32[]{:S(2)}, u32[]{:S(2)}) collective-permute-start(bf16[256,1024]{1,0:T(8,128)(2,1)S(1)} %get-tuple-element.51), channel_id=1, source_target_pairs={{0,8},{1,33},{2,10},{3,35},{4,12},{5,37},{6,14},{7,39},{8,0},{9,41... | collective-permute-start | bytes 1572872 | tf_op jit(solution)/shard_map/ppermute | solution.py:45
  60.4 1.3 %collective-permute-start.18 = (bf16[256,1024]{1,0:T(8,128)(2,1)S(1)}, bf16[256,1024]{1,0:T(8,128)(2,1)S(1)}, u32[]{:S(2)}, u32[]{:S(2)}) collective-permute-start(bf16[256,1024]{1,0:T(8,128)(2,1)S(1)} %get-tuple-element.52), channel_id=1, source_target_pairs={{0,12},{1,49},{2,14},{3,51},{4,0},{5,53},{6,2},{7,55},{8,4},{9,57}... | collective-permute-start | bytes 1572872 | tf_op jit(solution)/shard_map/ppermute | solution.py:45
  62.8 2.9 %collective-permute-done.13 = f32[64,128]{1,0:T(8,128)S(1)} collective-permute-done((f32[64,128]{1,0:T(8,128)S(1)}, f32[64,128]{1,0:T(8,128)S(1)}, u32[]{:S(2)}, u32[]{:S(2)}) %collective-permute-start.13) | collective-permute-done | bytes 32800 | tf_op jit(solution)/shard_map/ppermute | solution.py:489
  65.7 1.5 %collective-permute-start.14 = (f32[64,128]{1,0:T(8,128)S(1)}, f32[64,128]{1,0:T(8,128)S(1)}, u32[]{:S(2)}, u32[]{:S(2)}) collective-permute-start(f32[64,128]{1,0:T(8,128)S(1)} %add.20), channel_id=1, source_target_pairs={{0,128},{64,192},{128,0},{192,64},{1,129},{65,193},{129,1},{193,65... | collective-permute-start | bytes 98312 | tf_op jit(solution)/shard_map/ppermute | solution.py:489
  67.2 3.3 %collective-permute-done.14 = f32[64,128]{1,0:T(8,128)S(1)} collective-permute-done((f32[64,128]{1,0:T(8,128)S(1)}, f32[64,128]{1,0:T(8,128)S(1)}, u32[]{:S(2)}, u32[]{:S(2)}) %collective-permute-start.14) | collective-permute-done | bytes 32800 | tf_op jit(solution)/shard_map/ppermute | solution.py:489
  71.4 3.0 %collective-permute-done.23 = f32[64,128]{1,0:T(8,128)S(1)} collective-permute-done((f32[64,128]{1,0:T(8,128)S(1)}, f32[64,128]{1,0:T(8,128)S(1)}, u32[]{:S(2)}, u32[]{:S(2)}) %collective-permute-start.23) | collective-permute-done | bytes 32800 | tf_op jit(solution)/shard_map/ppermute | solution.py:45
  74.5 2.4 %collective-permute-start.24 = (f32[192,128]{1,0:T(8,128)S(1)}, f32[192,128]{1,0:T(8,128)S(1)}, u32[]{:S(2)}, u32[]{:S(2)}) collective-permute-start(f32[192,128]{1,0:T(8,128)S(1)} %pad.4), channel_id=1, source_target_pairs={{0,32},{1,9},{2,34},{3,11},{4,36},{5,13},{6,38},{7,15},{8,40},{9,1... | collective-permute-start | bytes 294920 | tf_op jit(solution)/shard_map/ppermute | solution.py:45
  76.9 2.4 %collective-permute-start.15 = (bf16[128,1024]{1,0:T(8,128)(2,1)S(1)}, bf16[128,1024]{1,0:T(8,128)(2,1)S(1)}, u32[]{:S(2)}, u32[]{:S(2)}) collective-permute-start(bf16[128,1024]{1,0:T(8,128)(2,1)S(1)} %slice.14), channel_id=1, source_target_pairs={{4,0},{8,4},{12,8},{16,12},{20,16},{24,20},{28,24},{32,28},{36,32}... | collective-permute-start | bytes 786440 | tf_op jit(solution)/shard_map/ppermute | solution.py:54
  79.7 1.1 %collective-permute-start.19 = (bf16[64,1024]{1,0:T(8,128)(2,1)S(1)}, bf16[64,1024]{1,0:T(8,128)(2,1)S(1)}, u32[]{:S(2)}, u32[]{:S(2)}) collective-permute-start(bf16[64,1024]{1,0:T(8,128)(2,1)S(1)} %get-tuple-element.55), channel_id=1, source_target_pairs={{0,64},{64,128},{128,192},{192,0},{1,65},{65,129},{129,193},{193,1... | collective-permute-start | bytes 393224 | tf_op jit(solution)/shard_map/ppermute | solution.py:533
  80.8 1.5 %collective-permute-start.20 = (bf16[64,1024]{1,0:T(8,128)(2,1)S(1)}, bf16[64,1024]{1,0:T(8,128)(2,1)S(1)}, u32[]{:S(2)}, u32[]{:S(2)}) collective-permute-start(bf16[64,1024]{1,0:T(8,128)(2,1)S(1)} %get-tuple-element.56), channel_id=1, source_target_pairs={{0,128},{64,192},{128,0},{192,64},{1,129},{65,193},{129,1},{193,65... | collective-permute-start | bytes 393224 | tf_op jit(solution)/shard_map/ppermute | solution.py:533
  82.3 1.9 %collective-permute-start.21 = (bf16[64,1024]{1,0:T(8,128)(2,1)S(1)}, bf16[64,1024]{1,0:T(8,128)(2,1)S(1)}, u32[]{:S(2)}, u32[]{:S(2)}) collective-permute-start(bf16[64,1024]{1,0:T(8,128)(2,1)S(1)} %get-tuple-element.57), channel_id=1, source_target_pairs={{0,192},{64,0},{128,64},{192,128},{1,193},{65,1},{129,65},{193,129... | collective-permute-start | bytes 393224 | tf_op jit(solution)/shard_map/ppermute | solution.py:533
  84.2 1.6 %collective-permute-start.25 = (f32[64,128]{1,0:T(8,128)S(1)}, f32[64,128]{1,0:T(8,128)S(1)}, u32[]{:S(2)}, u32[]{:S(2)}) collective-permute-start(f32[64,128]{1,0:T(8,128)S(1)} %slice_add_fusion), channel_id=1, source_target_pairs={{0,4},{1,17},{2,6},{3,19},{4,0},{5,21},{6,2},{7,23},{8,12},{9,25},... | collective-permute-start | bytes 98312 | tf_op jit(solution)/shard_map/ppermute | solution.py:45
  85.9 3.4 %input_grad.1.refs_4_ = bf16[256,1024]{1,0:T(8,128)(2,1)} custom-call(bf16[64,128]{1,0:T(8,128)(2,1)} %refs_0_.3, bf16[256,1024]{1,0:T(8,128)(2,1)S(1)} %get-tuple-element.42.refs_2_.refs_1_, bf16[128,1024]{1,0:T(8,128)(2,1)S(1)} %collective-permute-done.15.refs_2_, f32[64,1024]{1,0:T(8,128)S(1)} %get-tuple-element.53.refs_3_.refs_0_), custom_call_target="tpu_custom_call" | custom-call | tf_op jit(solution)/shard_map/input_grad/pallas_call | solution.py:96
  89.3 1.6 %collective-permute-start.26 = (f32[64,128]{1,0:T(8,128)S(1)}, f32[64,128]{1,0:T(8,128)S(1)}, u32[]{:S(2)}, u32[]{:S(2)}) collective-permute-start(f32[64,128]{1,0:T(8,128)S(1)} %add.24), channel_id=1, source_target_pairs={{0,8},{1,33},{2,10},{3,35},{4,12},{5,37},{6,14},{7,39},{8,0},{9,41... | collective-permute-start | bytes 98312 | tf_op jit(solution)/shard_map/ppermute | solution.py:45
  91.1 3.7 %collective-permute-done.26 = f32[64,128]{1,0:T(8,128)S(1)} collective-permute-done((f32[64,128]{1,0:T(8,128)S(1)}, f32[64,128]{1,0:T(8,128)S(1)}, u32[]{:S(2)}, u32[]{:S(2)}) %collective-permute-start.26) | collective-permute-done | bytes 32800 | tf_op jit(solution)/shard_map/ppermute | solution.py:45
  (42 shorter events, 8.5 us)
Async XLA Ops:
  0.6 11.8 %collective-permute-start = (bf16[64,4096]{1,0:T(8,128)(2,1)}, bf16[64,4096]{1,0:T(8,128)(2,1)S(1)}, u32[]{:S(2)}, u32[]{:S(2)}) collective-permute-start(bf16[64,4096]{1,0:T(8,128)(2,1)} %bitcast.10), channel_id=1, source_target_pairs={{0,1},{1,0},{2,3},{3,2},{4,5},{5,4},{6,7},{7,6},{8,9},{9,8},{10,11... | collective-permute-start | bytes 1572872 | tf_op jit(solution)/shard_map/ppermute | solution.py:32
  0.7 30.0 %collective-permute-start.1 = (bf16[64,4096]{1,0:T(8,128)(2,1)}, bf16[64,4096]{1,0:T(8,128)(2,1)S(1)}, u32[]{:S(2)}, u32[]{:S(2)}) collective-permute-start(bf16[64,4096]{1,0:T(8,128)(2,1)} %bitcast.11), channel_id=1, source_target_pairs={{0,2},{1,3},{2,0},{3,1},{4,6},{5,7},{6,4},{7,5},{8,10},{9,11},{10,... | collective-permute-start | bytes 1572872 | tf_op jit(solution)/shard_map/ppermute | solution.py:32
  9.0 12.5 %collective-permute-start.2 = (bf16[128,1024]{1,0:T(8,128)(2,1)S(1)}, bf16[128,1024]{1,0:T(8,128)(2,1)S(1)}, u32[]{:S(2)}, u32[]{:S(2)}) collective-permute-start(bf16[128,1024]{1,0:T(8,128)(2,1)S(1)} %slice_bitcast_fusion), channel_id=1, source_target_pairs={{0,4},{4,8},{8,12},{12,16},{16,20},{20,24},{24,28},{28,32},{32,36}... | collective-permute-start | bytes 786440 | tf_op jit(solution)/shard_map/ppermute | solution.py:54
  13.7 12.8 %collective-permute-start.5 = (bf16[128,1024]{1,0:T(8,128)(2,1)S(1)}, bf16[128,1024]{1,0:T(8,128)(2,1)S(1)}, u32[]{:S(2)}, u32[]{:S(2)}) collective-permute-start(bf16[128,1024]{1,0:T(8,128)(2,1)S(1)} %get-tuple-element.36), channel_id=1, source_target_pairs={{0,16},{1,5},{2,18},{3,7},{4,20},{5,9},{6,22},{7,11},{8,24},{9,13}... | collective-permute-start | bytes 786440 | tf_op jit(solution)/shard_map/ppermute | solution.py:45
  15.2 11.2 %collective-permute-start.6 = (bf16[128,1024]{1,0:T(8,128)(2,1)S(1)}, bf16[128,1024]{1,0:T(8,128)(2,1)S(1)}, u32[]{:S(2)}, u32[]{:S(2)}) collective-permute-start(bf16[128,1024]{1,0:T(8,128)(2,1)S(1)} %get-tuple-element.37), channel_id=1, source_target_pairs={{0,48},{1,13},{2,50},{3,15},{4,52},{5,1},{6,54},{7,3},{8,56},{9,5}... | collective-permute-start | bytes 786440 | tf_op jit(solution)/shard_map/ppermute | solution.py:45
  24.9 1.4 %collective-permute-start.3 = (bf16[128,512]{1,0:T(8,128)(2,1)S(1)}, bf16[128,512]{1,0:T(8,128)(2,1)S(1)}, u32[]{:S(2)}, u32[]{:S(2)}) collective-permute-start(bf16[128,512]{1,0:T(8,128)(2,1)S(1)} %get-tuple-element.34), channel_id=1, source_target_pairs={{0,1},{1,0},{2,3},{3,2},{4,5},{5,4},{6,7},{7,6},{8,9},{9,8},{10,11... | collective-permute-start | bytes 393224 | tf_op jit(solution)/shard_map/ppermute | solution.py:32
  25.0 1.5 %collective-permute-start.4 = (bf16[128,512]{1,0:T(8,128)(2,1)S(1)}, bf16[128,512]{1,0:T(8,128)(2,1)S(1)}, u32[]{:S(2)}, u32[]{:S(2)}) collective-permute-start(bf16[128,512]{1,0:T(8,128)(2,1)S(1)} %get-tuple-element.35), channel_id=1, source_target_pairs={{0,1},{1,0},{2,3},{3,2},{4,5},{5,4},{6,7},{7,6},{8,9},{9,8},{10,11... | collective-permute-start | bytes 393224 | tf_op jit(solution)/shard_map/ppermute | solution.py:32
  26.5 9.6 %collective-permute-start.8 = (bf16[272,1024]{1,0:T(8,128)(2,1)S(1)}, bf16[272,1024]{1,0:T(8,128)(2,1)S(1)}, u32[]{:S(2)}, u32[]{:S(2)}) collective-permute-start(bf16[272,1024]{1,0:T(8,128)(2,1)S(1)} %join.1.refs_8_), channel_id=1, source_target_pairs={{0,16},{1,5},{2,18},{3,7},{4,20},{5,9},{6,22},{7,11},{8,24},{9,13}... | collective-permute-start | bytes 1671176 | tf_op jit(solution)/shard_map/ppermute | solution.py:45
  28.1 9.5 %collective-permute-start.9 = (bf16[272,1024]{1,0:T(8,128)(2,1)S(1)}, bf16[272,1024]{1,0:T(8,128)(2,1)S(1)}, u32[]{:S(2)}, u32[]{:S(2)}) collective-permute-start(bf16[272,1024]{1,0:T(8,128)(2,1)S(1)} %join.1.refs_8_), channel_id=1, source_target_pairs={{0,48},{1,13},{2,50},{3,15},{4,52},{5,1},{6,54},{7,3},{8,56},{9,5}... | collective-permute-start | bytes 1671176 | tf_op jit(solution)/shard_map/ppermute | solution.py:45
  30.7 1.9 %collective-permute-start.7 = (bf16[64,4096]{1,0:T(8,128)(2,1)S(1)}, bf16[64,4096]{1,0:T(8,128)(2,1)S(1)}, u32[]{:S(2)}, u32[]{:S(2)}) collective-permute-start(bf16[64,4096]{1,0:T(8,128)(2,1)S(1)} %collective-permute-done.1.refs_0_.refs_2_), channel_id=1, source_target_pairs={{0,1},{1,0},{2,3},{3,2},{4,5},{5,4},{6,7},{7,6},{8,9},{9,8},{10,11... | collective-permute-start | bytes 1572872 | tf_op jit(solution)/shard_map/ppermute | solution.py:32
  37.8 14.4 %collective-permute-start.10 = (bf16[256,1024]{1,0:T(8,128)(2,1)S(1)}, bf16[256,1024]{1,0:T(8,128)(2,1)S(1)}, u32[]{:S(2)}, u32[]{:S(2)}) collective-permute-start(bf16[256,1024]{1,0:T(8,128)(2,1)S(1)} %get-tuple-element.44), channel_id=1, source_target_pairs={{0,32},{1,9},{2,34},{3,11},{4,36},{5,13},{6,38},{7,15},{8,40},{9,1... | collective-permute-start | bytes 1572872 | tf_op jit(solution)/shard_map/ppermute | solution.py:45
  39.9 14.2 %collective-permute-start.11 = (bf16[256,1024]{1,0:T(8,128)(2,1)S(1)}, bf16[256,1024]{1,0:T(8,128)(2,1)S(1)}, u32[]{:S(2)}, u32[]{:S(2)}) collective-permute-start(bf16[256,1024]{1,0:T(8,128)(2,1)S(1)} %get-tuple-element.45), channel_id=1, source_target_pairs={{0,16},{1,5},{2,18},{3,7},{4,20},{5,9},{6,22},{7,11},{8,24},{9,13}... | collective-permute-start | bytes 1572872 | tf_op jit(solution)/shard_map/ppermute | solution.py:45
  39.9 14.3 %collective-permute-start.12 = (bf16[256,1024]{1,0:T(8,128)(2,1)S(1)}, bf16[256,1024]{1,0:T(8,128)(2,1)S(1)}, u32[]{:S(2)}, u32[]{:S(2)}) collective-permute-start(bf16[256,1024]{1,0:T(8,128)(2,1)S(1)} %get-tuple-element.46), channel_id=1, source_target_pairs={{0,48},{1,13},{2,50},{3,15},{4,52},{5,1},{6,54},{7,3},{8,56},{9,5}... | collective-permute-start | bytes 1572872 | tf_op jit(solution)/shard_map/ppermute | solution.py:45
  57.3 22.0 %collective-permute-start.16 = (bf16[256,1024]{1,0:T(8,128)(2,1)S(1)}, bf16[256,1024]{1,0:T(8,128)(2,1)S(1)}, u32[]{:S(2)}, u32[]{:S(2)}) collective-permute-start(bf16[256,1024]{1,0:T(8,128)(2,1)S(1)} %get-tuple-element.50), channel_id=1, source_target_pairs={{0,4},{1,17},{2,6},{3,19},{4,8},{5,21},{6,10},{7,23},{8,12},{9,25}... | collective-permute-start | bytes 1572872 | tf_op jit(solution)/shard_map/ppermute | solution.py:45
  57.5 21.7 %collective-permute-start.17 = (bf16[256,1024]{1,0:T(8,128)(2,1)S(1)}, bf16[256,1024]{1,0:T(8,128)(2,1)S(1)}, u32[]{:S(2)}, u32[]{:S(2)}) collective-permute-start(bf16[256,1024]{1,0:T(8,128)(2,1)S(1)} %get-tuple-element.51), channel_id=1, source_target_pairs={{0,8},{1,33},{2,10},{3,35},{4,12},{5,37},{6,14},{7,39},{8,0},{9,41... | collective-permute-start | bytes 1572872 | tf_op jit(solution)/shard_map/ppermute | solution.py:45
  60.4 18.9 %collective-permute-start.18 = (bf16[256,1024]{1,0:T(8,128)(2,1)S(1)}, bf16[256,1024]{1,0:T(8,128)(2,1)S(1)}, u32[]{:S(2)}, u32[]{:S(2)}) collective-permute-start(bf16[256,1024]{1,0:T(8,128)(2,1)S(1)} %get-tuple-element.52), channel_id=1, source_target_pairs={{0,12},{1,49},{2,14},{3,51},{4,0},{5,53},{6,2},{7,55},{8,4},{9,57}... | collective-permute-start | bytes 1572872 | tf_op jit(solution)/shard_map/ppermute | solution.py:45
  61.8 3.9 %collective-permute-start.13 = (f32[64,128]{1,0:T(8,128)S(1)}, f32[64,128]{1,0:T(8,128)S(1)}, u32[]{:S(2)}, u32[]{:S(2)}) collective-permute-start(f32[64,128]{1,0:T(8,128)S(1)} %filter_grad.1.refs_13_), channel_id=1, source_target_pairs={{0,64},{64,0},{128,192},{192,128},{1,65},{65,1},{129,193},{193,129... | collective-permute-start | bytes 98312 | tf_op jit(solution)/shard_map/ppermute | solution.py:489
  65.7 4.8 %collective-permute-start.14 = (f32[64,128]{1,0:T(8,128)S(1)}, f32[64,128]{1,0:T(8,128)S(1)}, u32[]{:S(2)}, u32[]{:S(2)}) collective-permute-start(f32[64,128]{1,0:T(8,128)S(1)} %add.20), channel_id=1, source_target_pairs={{0,128},{64,192},{128,0},{192,64},{1,129},{65,193},{129,1},{193,65... | collective-permute-start | bytes 98312 | tf_op jit(solution)/shard_map/ppermute | solution.py:489
  70.5 3.9 %collective-permute-start.23 = (f32[64,128]{1,0:T(8,128)S(1)}, f32[64,128]{1,0:T(8,128)S(1)}, u32[]{:S(2)}, u32[]{:S(2)}) collective-permute-start(f32[64,128]{1,0:T(8,128)S(1)} %add.21), channel_id=1, source_target_pairs={{0,16},{1,5},{2,18},{3,7},{4,20},{5,1},{6,22},{7,3},{8,24},{9,13},... | collective-permute-start | bytes 98312 | tf_op jit(solution)/shard_map/ppermute | solution.py:45
  74.5 9.7 %collective-permute-start.24 = (f32[192,128]{1,0:T(8,128)S(1)}, f32[192,128]{1,0:T(8,128)S(1)}, u32[]{:S(2)}, u32[]{:S(2)}) collective-permute-start(f32[192,128]{1,0:T(8,128)S(1)} %pad.4), channel_id=1, source_target_pairs={{0,32},{1,9},{2,34},{3,11},{4,36},{5,13},{6,38},{7,15},{8,40},{9,1... | collective-permute-start | bytes 294920 | tf_op jit(solution)/shard_map/ppermute | solution.py:45
  76.9 9.0 %collective-permute-start.15 = (bf16[128,1024]{1,0:T(8,128)(2,1)S(1)}, bf16[128,1024]{1,0:T(8,128)(2,1)S(1)}, u32[]{:S(2)}, u32[]{:S(2)}) collective-permute-start(bf16[128,1024]{1,0:T(8,128)(2,1)S(1)} %slice.14), channel_id=1, source_target_pairs={{4,0},{8,4},{12,8},{16,12},{20,16},{24,20},{28,24},{32,28},{36,32}... | collective-permute-start | bytes 786440 | tf_op jit(solution)/shard_map/ppermute | solution.py:54
  79.7 11.2 %collective-permute-start.19 = (bf16[64,1024]{1,0:T(8,128)(2,1)S(1)}, bf16[64,1024]{1,0:T(8,128)(2,1)S(1)}, u32[]{:S(2)}, u32[]{:S(2)}) collective-permute-start(bf16[64,1024]{1,0:T(8,128)(2,1)S(1)} %get-tuple-element.55), channel_id=1, source_target_pairs={{0,64},{64,128},{128,192},{192,0},{1,65},{65,129},{129,193},{193,1... | collective-permute-start | bytes 393224 | tf_op jit(solution)/shard_map/ppermute | solution.py:533
  80.8 10.1 %collective-permute-start.20 = (bf16[64,1024]{1,0:T(8,128)(2,1)S(1)}, bf16[64,1024]{1,0:T(8,128)(2,1)S(1)}, u32[]{:S(2)}, u32[]{:S(2)}) collective-permute-start(bf16[64,1024]{1,0:T(8,128)(2,1)S(1)} %get-tuple-element.56), channel_id=1, source_target_pairs={{0,128},{64,192},{128,0},{192,64},{1,129},{65,193},{129,1},{193,65... | collective-permute-start | bytes 393224 | tf_op jit(solution)/shard_map/ppermute | solution.py:533
  82.3 8.6 %collective-permute-start.21 = (bf16[64,1024]{1,0:T(8,128)(2,1)S(1)}, bf16[64,1024]{1,0:T(8,128)(2,1)S(1)}, u32[]{:S(2)}, u32[]{:S(2)}) collective-permute-start(bf16[64,1024]{1,0:T(8,128)(2,1)S(1)} %get-tuple-element.57), channel_id=1, source_target_pairs={{0,192},{64,0},{128,64},{192,128},{1,193},{65,1},{129,65},{193,129... | collective-permute-start | bytes 393224 | tf_op jit(solution)/shard_map/ppermute | solution.py:533
  84.2 5.1 %collective-permute-start.25 = (f32[64,128]{1,0:T(8,128)S(1)}, f32[64,128]{1,0:T(8,128)S(1)}, u32[]{:S(2)}, u32[]{:S(2)}) collective-permute-start(f32[64,128]{1,0:T(8,128)S(1)} %slice_add_fusion), channel_id=1, source_target_pairs={{0,4},{1,17},{2,6},{3,19},{4,0},{5,21},{6,2},{7,23},{8,12},{9,25},... | collective-permute-start | bytes 98312 | tf_op jit(solution)/shard_map/ppermute | solution.py:45
  89.3 5.5 %collective-permute-start.26 = (f32[64,128]{1,0:T(8,128)S(1)}, f32[64,128]{1,0:T(8,128)S(1)}, u32[]{:S(2)}, u32[]{:S(2)}) collective-permute-start(f32[64,128]{1,0:T(8,128)S(1)} %add.24), channel_id=1, source_target_pairs={{0,8},{1,33},{2,10},{3,35},{4,12},{5,37},{6,14},{7,39},{8,0},{9,41... | collective-permute-start | bytes 98312 | tf_op jit(solution)/shard_map/ppermute | solution.py:45
  91.0 4.4 %collective-permute-start.22 = (f32[64,512]{1,0:T(8,128)S(1)}, f32[64,512]{1,0:T(8,128)S(1)}, u32[]{:S(2)}, u32[]{:S(2)}) collective-permute-start(f32[64,512]{1,0:T(8,128)S(1)} %get-tuple-element.59), channel_id=1, source_target_pairs={{0,1},{1,0},{2,3},{3,2},{4,5},{5,4},{6,7},{7,6},{8,9},{9,8},{10,11... | collective-permute-start | bytes 393224 | tf_op jit(solution)/shard_map/ppermute | solution.py:32
